TPU v7x, 32 devices: a whole 2x2x4 slice. The times are simulated.
32 devices in a mesh: dp: 4 (over x, core), seq: 2 (over y), tensor: 4 (over z).
Axes of the slice: x: 2, y: 2, z: 4, core: 2. Of those that a mesh axis runs over, the one named last changes fastest.
Arguments:
- hidden: bfloat16 [8, 2048, 1536], P('dp', ('seq', 'tensor')), may hold values from -6 to 6
- cotangent: bfloat16 [8, 2048, 1536], P('dp', ('seq', 'tensor')), may hold values from -6 to 6
- norm_gain: bfloat16 [1536], replicated, may hold values from 0.5 to 1.5
- w_z: bfloat16 [1536, 3072], P(('dp', 'seq'), 'tensor'), may hold values from -0.15625 to 0.15625
- w_x: bfloat16 [1536, 3072], P(('dp', 'seq'), 'tensor'), may hold values from -0.15625 to 0.15625
- w_bc: bfloat16 [1536, 256], P(('dp', 'seq')), may hold values from -0.15625 to 0.15625
- w_dt: bfloat16 [1536, 48], P(('dp', 'seq'), 'tensor'), may hold values from -0.15625 to 0.15625
- conv_x: bfloat16 [4, 3072], P(None, 'tensor'), may hold values from -3 to 3
- conv_x_bias: bfloat16 [3072], P('tensor'), may hold values from -0.5 to 0.5
- conv_bc: bfloat16 [4, 256], replicated, may hold values from -3 to 3
- conv_bc_bias: bfloat16 [256], replicated, may hold values from -0.5 to 0.5
- dt_bias: float32 [48], P('tensor'), may hold values from -7 to -2
- a_log: float32 [48], P('tensor'), may hold values from 0 to 2.77
- d_skip: float32 [48], P('tensor'), may hold values from 0.5 to 1.5
- inner_gain: bfloat16 [3072], P('tensor'), may hold values from 0.5 to 1.5
- w_out: bfloat16 [3072, 1536], P('tensor', ('dp', 'seq')), may hold values from -0.109375 to 0.109375
Outputs:
- output: bfloat16 [8, 2048, 1536], P('dp', ('seq', 'tensor'))
- grad_hidden: float32 [8, 2048, 1536], P('dp', ('seq', 'tensor'))
- grad_norm_gain: float32 [1536], replicated
- grad_w_z: float32 [1536, 3072], P(('dp', 'seq'), 'tensor')
- grad_w_x: float32 [1536, 3072], P(('dp', 'seq'), 'tensor')
- grad_w_bc: float32 [1536, 256], P(('dp', 'seq'))
- grad_w_dt: float32 [1536, 48], P(('dp', 'seq'), 'tensor')
- grad_conv_x: float32 [4, 3072], P(None, 'tensor')
- grad_conv_x_bias: float32 [3072], P('tensor')
- grad_conv_bc: float32 [4, 256], replicated
- grad_conv_bc_bias: float32 [256], replicated
- grad_dt_bias: float32 [48], P('tensor')
- grad_a_log: float32 [48], P('tensor')
- grad_d_skip: float32 [48], P('tensor')
- grad_inner_gain: float32 [3072], P('tensor')
- grad_w_out: float32 [3072, 1536], P('tensor', ('dp', 'seq'))
All inputs are finite; a program needn't handle non-finite values.
Results may differ from a plain program's by a relative error of at most 0.014.
Values may be sent and summed in bfloat16 or wider, within the bound.
No kernel may reach another device: no remote copies, remote signals or barrier semaphores. Data moves between devices by JAX's collectives and lax.ppermute only.
A program may use at most 136 MiB of HBM per device.

v0:
```python
import jax
import jax.numpy as jnp
from jax import lax
from jax.sharding import PartitionSpec as P

BLOCK = 256
MICRO = 2


EPS = 1e-05
scan_mode = lax.Precision.HIGH


def from_behind(value, axis, by):
    devices = lax.axis_size(axis)
    pairs = [(i, i + by) for i in range(devices) if 0 <= i + by < devices]
    return lax.ppermute(value, axis, pairs)


def carried_in(part, axis, combine, identity):
    place = lax.axis_index(axis)
    gathered = jax.tree.map(lambda a: lax.all_gather(a, axis), part)
    state = jax.tree.map(lambda a, e: jnp.zeros_like(a) + jnp.asarray(e, a.dtype), part, identity)

    def carried_one(hop, state):
        return combine(
            state, jax.tree.map(lambda a: lax.dynamic_index_in_dim(a, hop, 0, False), gathered)
        )

    return lax.fori_loop(0, place, carried_one, state)


def prefix(value, axis, join, neutral):
    count = lax.axis_size(axis)
    place = lax.axis_index(axis)
    ahead = count - 1 - place
    gathered = jax.tree.map(
        lambda a, kind: lax.all_gather(a.astype(kind), axis),
        value,
        jax.tree.map(lambda a: jnp.bfloat16 if a.dtype == jnp.float32 else a.dtype, value),
    )
    state = jax.tree.map(lambda a, e: jnp.zeros_like(a) + jnp.asarray(e, a.dtype), value, neutral)

    def prefix_one(hop, state):
        source = count - 1 - hop
        return join(
            state,
            jax.tree.map(
                lambda a, own: lax.dynamic_index_in_dim(a, source, 0, False).astype(own.dtype),
                gathered,
                value,
            ),
        )

    return lax.fori_loop(0, ahead, prefix_one, state)


def norm_rows(values, weight):
    scale = lax.rsqrt(jnp.mean(values * values, axis=-1, keepdims=True) + EPS)
    return values * scale * weight


def conv_apply(extended, conv_weight, conv_bias):
    width = conv_weight.shape[0]
    length = extended.shape[0] - width + 1
    total = conv_bias + conv_weight[0] * extended[0:length]
    for offset in range(1, width):
        total = total + conv_weight[offset] * extended[offset : offset + length]
    return jax.nn.silu(total)


def local_scan(inputs_x, state_b, state_c, step_raw, bias_step, log_rate, skip_gain):
    length, groups, heads, width = inputs_x.shape
    blocks = length // BLOCK
    step = jax.nn.softplus(step_raw + bias_step)
    log_decay = step * -jnp.exp(log_rate)
    decay_blk = jnp.transpose(log_decay.reshape(blocks, BLOCK, groups, heads), (2, 3, 0, 1))
    step_blk = jnp.transpose(step.reshape(blocks, BLOCK, groups, heads), (2, 3, 0, 1))
    cumul = jnp.cumsum(decay_blk, axis=-1)
    block_sum = cumul[..., -1]
    before = jnp.cumsum(block_sum, axis=-1) - block_sum
    xs_blk = inputs_x.reshape(blocks, BLOCK, groups, heads, width)
    b_blk = state_b.reshape(blocks, BLOCK, groups, -1)
    c_blk = state_c.reshape(blocks, BLOCK, groups, -1)
    scores = jnp.einsum("ktgn,ksgn->gkts", c_blk, b_blk, precision=scan_mode)
    row_pos = lax.broadcasted_iota(jnp.int32, (BLOCK, BLOCK), 0)
    col_pos = lax.broadcasted_iota(jnp.int32, (BLOCK, BLOCK), 1)
    causal = row_pos >= col_pos
    diff = cumul[..., :, None] - cumul[..., None, :]
    decay = jnp.where(causal, jnp.exp(jnp.where(causal, diff, 0.0)), 0.0)
    weights = scores[:, None] * decay * step_blk[..., None, :]
    intra = jnp.einsum("ghkts,ksghp->ktghp", weights, xs_blk, precision=scan_mode)
    tail = jnp.exp(block_sum[..., None] - cumul) * step_blk
    ends = jnp.einsum("ghks,ksghp,ksgn->gkhpn", tail, xs_blk, b_blk, precision=scan_mode)
    total = jnp.sum(block_sum, axis=-1)
    starts = jnp.concatenate([before, total[..., None]], axis=-1)
    after = starts[..., :, None] - before[..., None, :] - block_sum[..., None, :]
    upper = lax.broadcasted_iota(jnp.int32, (blocks + 1, blocks), 0) > lax.broadcasted_iota(
        jnp.int32, (blocks + 1, blocks), 1
    )
    carry_decay = jnp.where(upper, jnp.exp(jnp.where(upper, after, 0.0)), 0.0)
    entering = jnp.einsum("ghqk,gkhpn->gqhpn", carry_decay, ends, precision=scan_mode)
    carried = jnp.einsum("ktgn,gkhpn->ktghp", c_blk, entering[:, :blocks], precision=scan_mode)
    carried = carried * jnp.transpose(jnp.exp(cumul), (2, 3, 0, 1))[..., None]
    output = (intra + carried).reshape(length, groups, heads, width) + skip_gain[:, None] * inputs_x
    position_decay = jnp.transpose(cumul + before[..., None], (2, 3, 0, 1)).reshape(
        length, groups, heads
    )
    return (output, jnp.exp(total), entering[:, blocks], position_decay)


def state_inject(state_c, position_decay, entering):
    applied = jnp.einsum("tgn,ghpn->tghp", state_c, entering, precision=scan_mode)
    return applied * jnp.exp(position_decay)[..., None]


def chain_join(earlier, later):
    return (earlier[0] * later[0], later[0][..., None, None] * earlier[1] + later[1])


def spread_part(values, size, offset):
    full = jnp.zeros(values.shape[:-1] + (size,), jnp.float32)
    return lax.dynamic_update_slice_in_dim(full, values, offset * values.shape[-1], values.ndim - 1)


def own_part(values, size, offset):
    return lax.dynamic_slice_in_dim(values, offset * size, size, values.ndim - 1)


def per_device(
    hidden,
    cotangent,
    norm_gain,
    w_z,
    w_x,
    w_bc,
    w_dt,
    conv_x,
    conv_x_bias,
    conv_bc,
    conv_bc_bias,
    dt_bias,
    a_log,
    d_skip,
    inner_gain,
    w_out,
):
    f32 = jnp.float32
    bf16 = jnp.bfloat16
    tensor_count = lax.axis_size("tensor")
    tensor_index = lax.axis_index("tensor")
    local_seqs, own_len, model_width = hidden.shape
    group = local_seqs // MICRO
    inner_local = w_z.shape[1]
    heads_local = dt_bias.shape[0]
    head_width = inner_local // heads_local
    state_width = w_bc.shape[1] // 2
    inner_full = inner_local * tensor_count
    heads_full = heads_local * tensor_count
    rim_rows = conv_x.shape[0] - 1
    conv_weight = jnp.concatenate([conv_x, conv_bc], axis=1).astype(f32)
    conv_bias = jnp.concatenate([conv_x_bias, conv_bc_bias]).astype(f32)
    gain_in = norm_gain.astype(f32)
    gain_out = inner_gain.astype(f32)
    acc_z = jnp.zeros((model_width, inner_local), f32)
    acc_x = jnp.zeros((model_width, inner_local), f32)
    acc_bc = jnp.zeros((model_width, 2 * state_width), f32)
    acc_dt = jnp.zeros((model_width, heads_local), f32)
    acc_out = jnp.zeros((inner_local, model_width), f32)
    acc_norm_gain = jnp.zeros_like(gain_in)
    acc_conv_w = jnp.zeros_like(conv_weight)
    acc_conv_b = jnp.zeros_like(conv_bias)
    acc_bias_step = jnp.zeros_like(dt_bias)
    acc_log_rate = jnp.zeros_like(a_log)
    acc_skip = jnp.zeros_like(d_skip)
    acc_gain_out = jnp.zeros_like(gain_out)
    output_list = []
    grad_list = []
    for micro_step in range(MICRO):
        first_row = micro_step * group
        own_in = jnp.transpose(hidden[first_row : first_row + group], (1, 0, 2)).astype(f32)
        own_cot = jnp.transpose(cotangent[first_row : first_row + group], (1, 0, 2))
        normed_f, norm_back = jax.vjp(norm_rows, own_in, gain_in)
        normed_own = normed_f.astype(bf16)
        normed, cot_all = (
            lax.all_gather(normed_own, "tensor", axis=0, tiled=True),
            lax.all_gather(own_cot, "tensor", axis=0, tiled=True),
        )
        full_z, full_x, full_bc, full_dt, full_out = (
            lax.all_gather(w_z, ("dp", "seq"), axis=0, tiled=True),
            lax.all_gather(w_x, ("dp", "seq"), axis=0, tiled=True),
            lax.all_gather(w_bc, ("dp", "seq"), axis=0, tiled=True),
            lax.all_gather(w_dt, ("dp", "seq"), axis=0, tiled=True),
            lax.all_gather(w_out, ("dp", "seq"), axis=1, tiled=True),
        )
        gate_in = jnp.einsum("tgd,df->tgf", normed, full_z, preferred_element_type=f32).astype(bf16)
        mix_x = jnp.einsum("tgd,df->tgf", normed, full_x, preferred_element_type=f32)
        mix_bc = jnp.einsum("tgd,df->tgf", normed, full_bc, preferred_element_type=f32)
        mix_in = jnp.concatenate([mix_x, mix_bc], axis=-1).astype(bf16)
        step_in = jnp.einsum("tgd,df->tgf", normed, full_dt, preferred_element_type=f32).astype(
            bf16
        )
        span_len = mix_in.shape[0]
        prior = from_behind(mix_in[span_len - rim_rows :], "seq", 1)
        extended = jnp.concatenate([prior, mix_in], axis=0).astype(f32)
        act, conv_back = jax.vjp(conv_apply, extended, conv_weight, conv_bias)
        xs_f = (
            act[..., :inner_local]
            .astype(bf16)
            .astype(f32)
            .reshape(span_len, group, heads_local, head_width)
        )
        b_f = act[..., inner_local : inner_local + state_width].astype(bf16).astype(f32)
        c_f = act[..., inner_local + state_width :].astype(bf16).astype(f32)
        scan_out, scan_back = jax.vjp(
            local_scan, xs_f, b_f, c_f, step_in.astype(f32), dt_bias, a_log, d_skip
        )
        ssd_out, decay_all, local_end, position_decay = scan_out
        chain_ident = (jnp.ones_like(decay_all), jnp.zeros_like(local_end))
        decay_before, state_in = carried_in((decay_all, local_end), "seq", chain_join, chain_ident)
        injected, inject_back = jax.vjp(state_inject, c_f, position_decay, state_in)
        y_flat = (ssd_out + injected).reshape(span_len, group, inner_local)
        gate_f = gate_in.astype(f32)
        gated = y_flat * jax.nn.silu(gate_f)
        square_sum = lax.psum(jnp.sum(gated * gated, axis=-1), "tensor")
        inner_scale = lax.rsqrt(square_sum / inner_full + EPS)[..., None]
        mixed = (gated * inner_scale * gain_out).astype(bf16)
        branch = lax.psum_scatter(
            jnp.einsum("tgf,fd->tgd", mixed, full_out, preferred_element_type=f32),
            "tensor",
            scatter_dimension=0,
            tiled=True,
        )
        output_list.append(jnp.transpose((own_in + branch).astype(bf16), (1, 0, 2)))
        back_z, back_x, back_bc, back_dt, back_out = (
            lax.all_gather(w_z, ("dp", "seq"), axis=0, tiled=True),
            lax.all_gather(w_x, ("dp", "seq"), axis=0, tiled=True),
            lax.all_gather(w_bc, ("dp", "seq"), axis=0, tiled=True),
            lax.all_gather(w_dt, ("dp", "seq"), axis=0, tiled=True),
            lax.all_gather(w_out, ("dp", "seq"), axis=1, tiled=True),
        )
        acc_out = acc_out + jnp.einsum("tgf,tgd->fd", mixed, cot_all, preferred_element_type=f32)
        grad_mixed = jnp.einsum("tgd,fd->tgf", cot_all, back_out, preferred_element_type=f32)
        scaled_grad = grad_mixed * gain_out
        acc_gain_out = acc_gain_out + jnp.sum(grad_mixed * gated * inner_scale, axis=(0, 1))
        crossed = lax.psum(jnp.sum(scaled_grad * gated, axis=-1), "tensor")
        grad_gated = inner_scale * scaled_grad - gated * (
            inner_scale * inner_scale * inner_scale
        ) * (crossed[..., None] / inner_full)
        gate_sigmoid = jax.nn.sigmoid(gate_f)
        grad_mixer = (grad_gated * jax.nn.silu(gate_f)).reshape(
            span_len, group, heads_local, head_width
        )
        grad_gate = (
            grad_gated * y_flat * gate_sigmoid * (1.0 + gate_f * (1.0 - gate_sigmoid))
        ).astype(bf16)
        grad_c_inject, grad_position, grad_state_in = inject_back(grad_mixer)
        chain_back_ident = (jnp.ones_like(decay_all), jnp.zeros_like(grad_state_in))
        later_grad = prefix((decay_all, grad_state_in), "seq", chain_join, chain_back_ident)[1]
        grad_decay = jnp.sum(later_grad * state_in, axis=(-2, -1))
        grad_xs, grad_b, grad_c, grad_step, grad_bias, grad_rate, grad_skip = scan_back(
            (grad_mixer, grad_decay, later_grad, grad_position)
        )
        acc_bias_step = acc_bias_step + grad_bias
        acc_log_rate = acc_log_rate + grad_rate
        acc_skip = acc_skip + grad_skip
        grad_states = lax.psum(jnp.concatenate([grad_b, grad_c + grad_c_inject], axis=-1), "tensor")
        grad_act = jnp.concatenate(
            [
                grad_xs.reshape(span_len, group, inner_local).astype(bf16).astype(f32),
                grad_states.astype(bf16).astype(f32),
            ],
            axis=-1,
        )
        grad_ext, grad_conv_w, grad_conv_b = conv_back(grad_act)
        acc_conv_w = acc_conv_w + grad_conv_w
        acc_conv_b = acc_conv_b + grad_conv_b
        returned = from_behind(grad_ext[:rim_rows], "seq", -1)
        grad_mix_f = grad_ext[rim_rows:]
        grad_mix = jnp.concatenate(
            [grad_mix_f[: span_len - rim_rows], grad_mix_f[span_len - rim_rows :] + returned],
            axis=0,
        ).astype(bf16)
        grad_xr = grad_mix[..., :inner_local]
        grad_bc = grad_mix[..., inner_local:]
        grad_step_low = grad_step.astype(bf16)
        acc_z = acc_z + jnp.einsum("tgd,tgf->df", normed, grad_gate, preferred_element_type=f32)
        acc_x = acc_x + jnp.einsum("tgd,tgf->df", normed, grad_xr, preferred_element_type=f32)
        acc_bc = acc_bc + jnp.einsum("tgd,tgf->df", normed, grad_bc, preferred_element_type=f32)
        acc_dt = acc_dt + jnp.einsum(
            "tgd,tgf->df", normed, grad_step_low, preferred_element_type=f32
        )
        summed = jnp.einsum("tgf,df->tgd", grad_gate, back_z, preferred_element_type=f32)
        summed = summed + jnp.einsum("tgf,df->tgd", grad_xr, back_x, preferred_element_type=f32)
        grad_normed = lax.psum_scatter(
            summed + jnp.einsum("tgf,df->tgd", grad_step_low, back_dt, preferred_element_type=f32),
            "tensor",
            scatter_dimension=0,
            tiled=True,
        )
        own_bc = lax.dynamic_slice_in_dim(grad_bc, tensor_index * own_len, own_len, 0)
        grad_normed = grad_normed + jnp.einsum(
            "tgf,df->tgd", own_bc, back_bc, preferred_element_type=f32
        )
        grad_input, grad_gain_part = norm_back(grad_normed)
        acc_norm_gain = acc_norm_gain + grad_gain_part
        grad_list.append(jnp.transpose(own_cot.astype(f32) + grad_input, (1, 0, 2)))
    outputs = jnp.concatenate(output_list, axis=0)
    grad_hidden = jnp.concatenate(grad_list, axis=0)
    grad_w_z, grad_w_x, grad_w_bc, grad_w_dt, grad_w_out = (
        lax.psum_scatter(acc_z, ("dp", "seq"), scatter_dimension=0, tiled=True),
        lax.psum_scatter(acc_x, ("dp", "seq"), scatter_dimension=0, tiled=True),
        lax.psum_scatter(acc_bc, ("dp", "seq"), scatter_dimension=0, tiled=True),
        lax.psum_scatter(acc_dt, ("dp", "seq"), scatter_dimension=0, tiled=True),
        lax.psum_scatter(acc_out, ("dp", "seq"), scatter_dimension=1, tiled=True),
    )
    keep_first = (tensor_index == 0).astype(f32)
    summed_small = lax.psum(
        (
            spread_part(acc_gain_out, inner_full, tensor_index),
            spread_part(acc_conv_w[:, :inner_local], inner_full, tensor_index),
            spread_part(acc_conv_b[:inner_local], inner_full, tensor_index),
            spread_part(acc_bias_step, heads_full, tensor_index),
            spread_part(acc_log_rate, heads_full, tensor_index),
            spread_part(acc_skip, heads_full, tensor_index),
            acc_conv_w[:, inner_local:] * keep_first,
            acc_conv_b[inner_local:] * keep_first,
            acc_norm_gain,
        ),
        ("dp", "seq", "tensor"),
    )
    grad_inner_gain = own_part(summed_small[0], inner_local, tensor_index)
    grad_conv_x = own_part(summed_small[1], inner_local, tensor_index)
    grad_conv_x_bias = own_part(summed_small[2], inner_local, tensor_index)
    grad_dt_bias = own_part(summed_small[3], heads_local, tensor_index)
    grad_a_log = own_part(summed_small[4], heads_local, tensor_index)
    grad_d_skip = own_part(summed_small[5], heads_local, tensor_index)
    return (
        outputs,
        grad_hidden,
        summed_small[8],
        grad_w_z,
        grad_w_x,
        grad_w_bc,
        grad_w_dt,
        grad_conv_x,
        grad_conv_x_bias,
        summed_small[6],
        summed_small[7],
        grad_dt_bias,
        grad_a_log,
        grad_d_skip,
        grad_inner_gain,
        grad_w_out,
    )


def solution(mesh):
    placed = (
        P("dp", ("seq", "tensor"), None),
        P("dp", ("seq", "tensor"), None),
        P(),
        P(("dp", "seq"), "tensor"),
        P(("dp", "seq"), "tensor"),
        P(("dp", "seq"), None),
        P(("dp", "seq"), "tensor"),
        P(None, "tensor"),
        P("tensor"),
        P(),
        P(),
        P("tensor"),
        P("tensor"),
        P("tensor"),
        P("tensor"),
        P("tensor", ("dp", "seq")),
    )
    return jax.shard_map(
        per_device,
        mesh=mesh,
        in_specs=placed,
        out_specs=(
            P("dp", ("seq", "tensor"), None),
            P("dp", ("seq", "tensor"), None),
            P(),
            P(("dp", "seq"), "tensor"),
            P(("dp", "seq"), "tensor"),
            P(("dp", "seq"), None),
            P(("dp", "seq"), "tensor"),
            P(None, "tensor"),
            P("tensor"),
            P(),
            P(),
            P("tensor"),
            P("tensor"),
            P("tensor"),
            P("tensor"),
            P("tensor", ("dp", "seq")),
        ),
        check_vma=False,
    )
```

profile of v0, /device:TPU:0, one launch (start us, length us, event | category | flops | bytes accessed | tf_op | source)
XLA Modules:
  0.0 1708.6 jit_solution(3913252572098837683)
XLA Ops:
  22.0 18.4 %all-gather.8 = bf16[8,192,12]{1,2,0:T(8,128)(2,1)S(1)} all-gather(bf16[1,192,12]{1,2,0:T(8,128)(2,1)S(1)} %bitcast.1077), channel_id=1, replica_groups=mesh['dp'=4,'seq'=2,'tensor'=4] {'dp','seq'}, dimensions={0}, use_global_device_ids=true | all-gather | bytes 41472 | tf_op jit(solution)/shard_map/all_gather | solution.py:193
  40.5 19.9 %all_gather.78 = bf16[1536,256]{1,0:T(8,128)(2,1)} all-gather(bf16[192,256]{1,0:T(8,128)(2,1)S(1)} %copy-done.154), channel_id=1, replica_groups=mesh['dp'=4,'seq'=2,'tensor'=4] {'dp','seq'}, dimensions={0}, use_global_device_ids=true | all-gather | bytes 884736 | tf_op jit(solution)/shard_map/all_gather | solution.py:192
  62.2 18.1 %all-gather.25.cloned.1.call-done = bf16[1024,1,1536]{2,0,1:T(8,128)(2,1)} async-done(((bf16[256,1,1536]{2,0,1:T(8,128)(2,1)}), bf16[1024,1,1536]{2,0,1:T(8,128)(2,1)}) %all-gather.25.cloned.1.call-update) | async-done | bytes 3145744 | tf_op jit(solution)/shard_map/all_gather | solution.py:186
  88.7 55.9 %all-gather.17.cloned.1.call-done = bf16[1024,1,1536]{2,0,1:T(8,128)(2,1)} async-done(((bf16[256,1,1536]{2,0,1:T(8,128)(2,1)}), bf16[1024,1,1536]{2,0,1:T(8,128)(2,1)}) %all-gather.17.cloned.1.call-update) | async-done | bytes 3145744 | tf_op jit(solution)/shard_map/all_gather | solution.py:186
  162.9 11.3 all-gather.19.cloned.1.call-done
  174.2 4.4 fusion.173
  201.1 7.1 all-gather.23.cloned.1.call-done
  208.2 65.0 %all-gather.29.cloned.1.call-done = bf16[1,1024,1536]{2,1,0:T(8,128)(2,1)} async-done(((bf16[1,256,1536]{2,1,0:T(8,128)(2,1)}), bf16[1,1024,1536]{2,1,0:T(8,128)(2,1)}) %all-gather.29.cloned.1.call-update) | async-done | bytes 3145744 | tf_op jit(solution)/shard_map/all_gather | solution.py:187
  273.1 6.9 fusion.79
  280.6 5.6 all-reduce.31
  297.1 5.0 all-reduce.30
  315.3 9.5 multiply_convert_fusion.1
  350.5 4.1 reshape.2414
  372.1 13.9 all_gather.81
  388.6 6.4 fusion.61
  397.2 8.5 all_gather.86
  411.8 6.4 fusion.60
  421.3 11.4 fusion.82
  432.8 7.8 multiply_reduce_fusion.17
  440.6 5.2 multiply_reduce_fusion.16
  445.7 9.7 all-reduce.29
  459.3 10.4 multiply_reduce_fusion.13
  469.6 10.9 all-reduce.28
  482.0 9.6 fusion.53
  494.3 5.9 fusion.63
  506.5 4.5 fusion.81
  518.9 9.0 all-gather.3
  535.3 5.5 fusion.509
  549.1 8.3 bitcast_add_fusion.3
  557.4 5.1 reshape_reshape.9
  562.5 4.5 fusion.64
  572.9 6.4 all-gather.5
  586.4 5.5 fusion.510
  600.3 8.6 bitcast_add_fusion.2
  608.8 6.4 fusion.75
  627.9 25.9 %fusion.9 = (f32[12,4,256]{2,0,1:T(8,128)S(1)}, f32[12,4,256]{2,0,1:T(8,128)S(1)}, f32[12,4,256]{2,0,1:T(8,128)S(1)}, f32[4,256,256]{2,1,0:T(8,128)}, f32[4,256,...) fusion(f32[4,256,256]{2,1,0:T(8,128)} %copy-done.109, ...), kind=kOutput, calls=%fused_computation.29 | convolution fusion | flops 1301733376 | bytes 22052864 | tf_op jit(solution)/shard_map/transpose(jvp(ghkts,ksghp->ktghp))/dot_general | solution.py:92
  655.3 11.2 reduce-window.34
  683.2 11.4 reduce-window.36
  728.7 65.5 %all-reduce.36 = (bf16[1024,1,256]{0,2,1:T(8,128)(2,1)}, bf16[1024,1,256]{0,2,1:T(8,128)(2,1)}) all-reduce(f32[1024,1,256]{0,2,1:T(8,128)} %pad_maximum_fusion.3, f32[1024,1,256]{0,2,1:T(8,128)} %pad_maximum_fusion.2), channel_id=1, replica_groups=mesh['dp'=4,'seq'=2,'tensor'=4] {'tensor'}, use_global_device_ids=true, to_apply=%region_46.48 | all-reduce | flops 524288 | bytes 3145728 | tf_op jit(solution)/shard_map/psum | solution.py:267
  794.3 5.6 fusion.191
  801.2 8.8 multiply_reduce_fusion.9
  810.0 7.5 multiply_reduce_fusion.5
  817.6 10.4 broadcast_multiply_fusion
  833.9 5.0 pad_add_fusion
  841.4 4.9 fusion.526
  867.9 4.1 pad_add_fusion.1
  886.9 8.2 convolution_bitcast_fusion
  895.8 8.1 convolution_bitcast_fusion.1
  913.4 55.4 %reduce-scatter.18.cloned.1.call-done = f32[256,1,1536]{2,0,1:T(8,128)} async-done(((f32[1024,1,1536]{2,0,1:T(8,128)}), f32[256,1,1536]{2,0,1:T(8,128)}) %reduce-scatter.18.cloned.1.call-update) | async-done | bytes 1572880 | tf_op jit(solution)/shard_map/reduce_scatter | solution.py:295
  972.1 110.2 %reduce-scatter.16.cloned.1.call-done = f32[256,1,1536]{2,0,1:T(8,128)} async-done(((f32[1024,1,1536]{2,0,1:T(8,128)}), f32[256,1,1536]{2,0,1:T(8,128)}) %reduce-scatter.16.cloned.1.call-update) | async-done | bytes 1572880 | tf_op jit(solution)/shard_map/reduce_scatter | solution.py:295
  1082.4 4.7 fusion.182
  1092.1 6.2 fusion.95
  1098.3 5.1 convolution_add_fusion
  1103.4 4.2 fusion.121
  1107.7 4.4 convolution_add_fusion.2
  1112.4 4.3 fusion.119
  1116.7 5.5 convolution_add_fusion.1
  1124.0 110.1 %reduce-scatter.14.cloned.1.call-done = f32[256,1,1536]{2,0,1:T(8,128)} async-done(((f32[1024,1,1536]{2,0,1:T(8,128)}), f32[256,1,1536]{2,0,1:T(8,128)}) %reduce-scatter.14.cloned.1.call-update) | async-done | bytes 1572880 | tf_op jit(solution)/shard_map/reduce_scatter | solution.py:228
  1234.1 113.4 %reduce-scatter.12.cloned.1.call-done = f32[256,1,1536]{2,0,1:T(8,128)} async-done(((f32[1024,1,1536]{2,0,1:T(8,128)}), f32[256,1,1536]{2,0,1:T(8,128)}) %reduce-scatter.12.cloned.1.call-update) | async-done | bytes 1572880 | tf_op jit(solution)/shard_map/reduce_scatter | solution.py:228
  1354.5 126.0 %all-reduce.35.cloned.1.call-done = (f32[1536]{0:T(1024)}, f32[4,3072]{1,0:T(4,128)}, f32[3072]{0:T(1024)}, f32[4,256]{1,0:T(4,128)}, f32[256]{0:T(256)}, /*inde...) async-done(((f32[1536]{0:T(1024)}, f32[4,3072]{1,0:T(4,128)}, f32[3072]{0:T(1024)}, f32[4,256]{1,0:T(4,128)}, f32[256]{0:T(256)}, /*index=5*/f32[48]{0:T(128)}, ...) | async-done | bytes 85584 | tf_op jit(solution)/shard_map/psum | solution.py:318
  1488.2 35.8 %reduce-scatter.24.cloned.1.call-done = f32[192,256]{1,0:T(8,128)} async-done(((f32[1536,256]{1,0:T(8,128)}), f32[192,256]{1,0:T(8,128)}) %reduce-scatter.24.cloned.1.call-update) | async-done | bytes 196624 | tf_op jit(solution)/shard_map/reduce_scatter | solution.py:313
  1524.0 58.2 %reduce-scatter.26.cloned.1.call-done = f32[768,192]{0,1:T(8,128)} async-done(((f32[768,1536]{0,1:T(8,128)}), f32[768,192]{0,1:T(8,128)}) %reduce-scatter.26.cloned.1.call-update) | async-done | bytes 589840 | tf_op jit(solution)/shard_map/reduce_scatter | solution.py:315
  1582.2 57.8 %reduce-scatter.20.cloned.1.call-done = f32[192,768]{1,0:T(8,128)} async-done(((f32[1536,768]{1,0:T(8,128)}), f32[192,768]{1,0:T(8,128)}) %reduce-scatter.20.cloned.1.call-update) | async-done | bytes 589840 | tf_op jit(solution)/shard_map/reduce_scatter | solution.py:311
  1640.0 58.2 %reduce-scatter.22.cloned.1.call-done = f32[192,768]{1,0:T(8,128)} async-done(((f32[1536,768]{1,0:T(8,128)}), f32[192,768]{1,0:T(8,128)}) %reduce-scatter.22.cloned.1.call-update) | async-done | bytes 589840 | tf_op jit(solution)/shard_map/reduce_scatter | solution.py:312
  (852 shorter events, 358.8 us)
Async XLA Ops:
  7.2 73.1 %all-gather.25.cloned.1.call-start = ((), (), s32[]{:S(2)}) async-start(), calls=%async_computation.14 | async-start | bytes 3932160 | tf_op jit(solution)/shard_map/all_gather | solution.py:186
  13.9 130.7 %all-gather.17.cloned.1.call-start = ((), (), s32[]{:S(2)}) async-start(), calls=%async_computation.9 | async-start | bytes 3932160 | tf_op jit(solution)/shard_map/all_gather | solution.py:186
  14.7 25.8 %copy-start.154 = (bf16[192,256]{1,0:T(8,128)(2,1)S(1)}, bf16[192,256]{1,0:T(8,128)(2,1)}, u32[]{:S(2)}) copy-start(bf16[192,256]{1,0:T(8,128)(2,1)} %param.30) | copy-start | bytes 294916
  14.7 159.5 %all-gather.19.cloned.1.call-start = ((), (), s32[]{:S(2)}) async-start(), calls=%async_computation.10 | async-start | bytes 2654208 | tf_op jit(solution)/shard_map/all_gather | solution.py:191
  15.4 192.7 %all-gather.23.cloned.1.call-start = ((), (), s32[]{:S(2)}) async-start(), calls=%async_computation.12 | async-start | bytes 2654208 | tf_op jit(solution)/shard_map/all_gather | solution.py:194
  16.0 44.4 %copy-start.249 = (u32[32]{0:T(128)S(1)}, u32[32]{0:T(128)}, u32[]{:S(2)}) copy-start(u32[32]{0:T(128)} %constant.212) | copy-start | bytes 388
  16.0 45.6 %copy-start.234 = (bf16[768]{0:T(1024)(128)(2,1)S(1)}, bf16[768]{0:T(1024)(128)(2,1)}, u32[]{:S(2)}) copy-start(bf16[768]{0:T(1024)(128)(2,1)} %param.33) | copy-start | bytes 4612
  16.0 45.6 %copy-start.240 = (bf16[256]{0:T(256)(128)(2,1)S(1)}, bf16[256]{0:T(256)(128)(2,1)}, u32[]{:S(2)}) copy-start(bf16[256]{0:T(256)(128)(2,1)} %param.35) | copy-start | bytes 1540
  16.1 64.2 %copy-start.219 = (f32[12]{0:T(128)S(1)}, f32[12]{0:T(128)}, u32[]{:S(2)}) copy-start(f32[12]{0:T(128)} %param.36) | copy-start | bytes 148
  16.1 257.0 %all-gather.29.cloned.1.call-start = ((), (), s32[]{:S(2)}) async-start(), calls=%async_computation.23 | async-start | bytes 3932160 | tf_op jit(solution)/shard_map/all_gather | solution.py:187
  17.4 415.3 %all-gather.21.cloned.1.call-start = ((), (), s32[]{:S(2)}) async-start(), calls=%async_computation.11 | async-start | bytes 2654208 | tf_op jit(solution)/shard_map/all_gather | solution.py:190
  18.0 441.2 %all-gather.27.cloned.1.call-start = ((), (), s32[]{:S(2)}) async-start(), calls=%async_computation.22 | async-start | bytes 3932160 | tf_op jit(solution)/shard_map/all_gather | solution.py:187
  18.8 950.0 %reduce-scatter.18.cloned.1.call-start = ((), (), s32[]{:S(2)}) async-start(), calls=%async_computation.17 | async-start | bytes 7864320 | tf_op jit(solution)/shard_map/reduce_scatter | solution.py:295
  20.0 124.6 %copy-start.208 = (f32[12]{0:T(128)}, f32[12]{0:T(128)S(1)}, u32[]{:S(2)}) copy-start(f32[12]{0:T(128)S(1)} %exponential_negate_fusion) | copy-start | bytes 148
  40.5 104.2 %copy-start.104 = (bf16[1536,12]{0,1:T(8,128)(2,1)}, bf16[1536,12]{0,1:T(8,128)(2,1)S(1)}, u32[]{:S(2)}) copy-start(bf16[1536,12]{0,1:T(8,128)(2,1)S(1)} %reshape.2510) | copy-start | bytes 110596
  87.3 102.0 %copy-start.95 = (f32[1,12,4,256]{3,1,2,0:T(8,128)}, f32[1,12,4,256]{3,1,2,0:T(8,128)S(1)}, u32[]{:S(2)}) copy-start(f32[1,12,4,256]{3,1,2,0:T(8,128)S(1)} %get-tuple-element.528) | copy-start | bytes 147460
  88.7 71.2 %copy-start.19 = (bf16[1024,1,1536]{2,0,1:T(8,128)(2,1)S(1)}, bf16[1024,1,1536]{2,0,1:T(8,128)(2,1)}, u32[]{:S(2)}) copy-start(bf16[1024,1,1536]{2,0,1:T(8,128)(2,1)} %all-gather.25.cloned.1.call-done) | copy-start | bytes 9437188
  152.2 40.0 %copy-start.96 = (f32[1,12,4,256]{3,1,2,0:T(8,128)}, f32[1,12,4,256]{3,1,2,0:T(8,128)S(1)}, u32[]{:S(2)}) copy-start(f32[1,12,4,256]{3,1,2,0:T(8,128)S(1)} %get-tuple-element.522) | copy-start | bytes 147460
  154.5 133.1 %copy-start.101 = (f32[4,256,1,12]{1,0,2,3:T(4,128)}, f32[4,256,1,12]{1,0,2,3:T(4,128)S(1)}, u32[]{:S(2)}) copy-start(f32[4,256,1,12]{1,0,2,3:T(4,128)S(1)} %reshape.2423) | copy-start | bytes 147460
  157.0 132.1 %copy-start.102 = (f32[4,256,1,12]{1,0,2,3:T(4,128)}, f32[4,256,1,12]{1,0,2,3:T(4,128)S(1)}, u32[]{:S(2)}) copy-start(f32[4,256,1,12]{1,0,2,3:T(4,128)S(1)} %reshape.2403) | copy-start | bytes 147460
  178.6 15.2 copy-start.17
  181.0 128.9 %collective-permute-start.1 = (bf16[3,1,1024]{0,2,1:T(8,128)(2,1)}, bf16[3,1,1024]{0,2,1:T(8,128)(2,1)}, u32[]{:S(2)}, u32[]{:S(2)}) collective-permute-start(bf16[3,1,1024]{0,2,1:T(8,128)(2,1)} %pad_maximum_fusion.6), channel_id=1, source_target_pairs={{0,4},{1,5},{2,6},{3,7},{8,12},{9,13},{10,14},{11,15},{16,20},{17,... | collective-permute-start | bytes 18440 | tf_op jit(solution)/shard_map/ppermute | solution.py:17
  201.0 78.9 %copy-start.221 = (f32[12]{0:T(128)S(1)}, f32[12]{0:T(128)}, u32[]{:S(2)}) copy-start(f32[12]{0:T(128)} %get-tuple-element.443) | copy-start | bytes 148
  201.1 78.9 %copy-start.223 = (f32[1,12,4]{1,2,0:T(4,128)S(1)}, f32[1,12,4]{1,2,0:T(4,128)}, u32[]{:S(2)}) copy-start(f32[1,12,4]{1,2,0:T(4,128)} %bitcast_subtract_fusion.3) | copy-start | bytes 580
  201.1 79.5 %copy-start.251 = (bf16[24]{0:T(256)(128)(2,1)S(1)}, bf16[24]{0:T(256)(128)(2,1)}, u32[]{:S(2)}) copy-start(bf16[24]{0:T(256)(128)(2,1)} %copy-done.250) | copy-start | bytes 148
  201.1 85.8 %copy-start.149 = (f32[12,4]{0,1:T(4,128)S(1)}, f32[12,4]{0,1:T(4,128)}, u32[]{:S(2)}) copy-start(f32[12,4]{0,1:T(4,128)} %copy-done.148) | copy-start | bytes 580
  201.1 87.2 %copy-start.129 = (f32[12,4,2,128]{3,2,1,0:T(2,128)S(1)}, f32[12,4,2,128]{3,2,1,0:T(2,128)}, u32[]{:S(2)}) copy-start(f32[12,4,2,128]{3,2,1,0:T(2,128)} %copy-done.128) | copy-start | bytes 147460
  201.1 104.3 %copy-start.135 = (f32[4,256,1,12]{1,3,0,2:T(8,128)S(1)}, f32[4,256,1,12]{1,3,0,2:T(8,128)}, u32[]{:S(2)}) copy-start(f32[4,256,1,12]{1,3,0,2:T(8,128)} %get-tuple-element.561) | copy-start | bytes 147460
  289.1 48.7 %copy-start.140 = (f32[12,4]{1,0:T(8,128)}, f32[12,4]{1,0:T(8,128)S(1)}, u32[]{:S(2)}) copy-start(f32[12,4]{1,0:T(8,128)S(1)} %copy.666) | copy-start | bytes 580
  292.8 64.4 %copy-start.144 = (f32[12,5]{1,0:T(8,128)}, f32[12,5]{1,0:T(8,128)S(1)}, u32[]{:S(2)}) copy-start(f32[12,5]{1,0:T(8,128)S(1)} %copy.690) | copy-start | bytes 724
  295.8 42.0 %copy-start.142 = (f32[12,4]{1,0:T(8,128)}, f32[12,4]{1,0:T(8,128)S(1)}, u32[]{:S(2)}) copy-start(f32[12,4]{1,0:T(8,128)S(1)} %copy.665) | copy-start | bytes 580
  305.4 32.4 %copy-start.146 = (f32[12,5]{1,0:T(8,128)}, f32[12,5]{1,0:T(8,128)S(1)}, u32[]{:S(2)}) copy-start(f32[12,5]{1,0:T(8,128)S(1)} %copy.664) | copy-start | bytes 724
  306.1 7.9 collective-permute-start
  366.5 22.0 %copy-start.76 = (bf16[4,256,128,1]{2,1,3,0:T(8,128)(2,1)}, bf16[4,256,128,1]{2,1,3,0:T(8,128)(2,1)S(1)}, u32[]{:S(2)}) copy-start(bf16[4,256,128,1]{2,1,3,0:T(8,128)(2,1)S(1)} %copy.784) | copy-start | bytes 786436
  372.1 15.4 copy-start.54
  445.7 36.2 %copy-start.59 = (f32[1024,768]{0,1:T(8,128)}, f32[1024,768]{0,1:T(8,128)S(1)}, u32[]{:S(2)}) copy-start(f32[1024,768]{0,1:T(8,128)S(1)} %get-tuple-element.526) | copy-start | bytes 9437188
  481.9 12.4 copy-start.70
  627.9 26.0 %copy-start.97 = (f32[1,12,4,256]{3,1,2,0:T(8,128)S(1)}, f32[1,12,4,256]{3,1,2,0:T(8,128)}, u32[]{:S(2)}) copy-start(f32[1,12,4,256]{3,1,2,0:T(8,128)} %copy-done.96) | copy-start | bytes 147460
  627.9 26.0 %copy-start.103 = (f32[4,256,1,12]{1,0,2,3:T(4,128)S(1)}, f32[4,256,1,12]{1,0,2,3:T(4,128)}, u32[]{:S(2)}) copy-start(f32[4,256,1,12]{1,0,2,3:T(4,128)} %copy-done.102) | copy-start | bytes 147460
  627.9 26.0 %copy-start.126 = (f32[4,256,12]{1,0,2:T(4,128)S(1)}, f32[4,256,12]{1,0,2:T(4,128)}, u32[]{:S(2)}) copy-start(f32[4,256,12]{1,0,2:T(4,128)} %multiply_reduce_fusion.11) | copy-start | bytes 147460
  627.9 26.0 %copy-start.127 = (f32[4,256,1,12]{1,0,3,2:T(4,128)S(1)}, f32[4,256,1,12]{1,0,3,2:T(4,128)}, u32[]{:S(2)}) copy-start(f32[4,256,1,12]{1,0,3,2:T(4,128)} %broadcast_in_dim.237) | copy-start | bytes 147460
  627.9 26.0 %copy-start.130 = (f32[4,256,12]{1,2,0:T(8,128)S(1)}, f32[4,256,12]{1,2,0:T(8,128)}, u32[]{:S(2)}) copy-start(f32[4,256,12]{1,2,0:T(8,128)} %fusion.81) | copy-start | bytes 147460
  627.9 26.0 %copy-start.153 = (f32[1,12,4,1]{3,1,2,0:T(8,128)S(1)}, f32[1,12,4,1]{3,1,2,0:T(8,128)}, u32[]{:S(2)}) copy-start(f32[1,12,4,1]{3,1,2,0:T(8,128)} %copy.734) | copy-start | bytes 580
  627.9 47.2 %copy-start.150 = (f32[12,4]{0,1:T(4,128)S(1)}, f32[12,4]{0,1:T(4,128)}, u32[]{:S(2)}) copy-start(f32[12,4]{0,1:T(4,128)} %copy-done.148) | copy-start | bytes 580
  627.9 47.2 %copy-start.194 = (f32[12,4]{0,1:T(4,128)S(1)}, f32[12,4]{0,1:T(4,128)}, u32[]{:S(2)}) copy-start(f32[12,4]{0,1:T(4,128)} %get-tuple-element.444) | copy-start | bytes 580
  727.6 66.6 %copy-start.201 = (f32[768]{0:T(1024)S(1)}, f32[768]{0:T(1024)}, u32[]{:S(2)}) copy-start(f32[768]{0:T(1024)} %mul.1193) | copy-start | bytes 9220
  833.9 12.5 copy-start.131
  833.9 12.5 copy-start.132
  839.3 11.3 collective-permute-start.3
  858.4 224.0 %reduce-scatter.16.cloned.1.call-start = ((), (), s32[]{:S(2)}) async-start(), calls=%async_computation.16 | async-start | bytes 7864320 | tf_op jit(solution)/shard_map/reduce_scatter | solution.py:295
  860.4 12.7 collective-permute-start.2
  882.0 240.2 %reduce-scatter.28.cloned.1.call-start = ((), (), s32[]{:S(2)}) async-start(), calls=%async_computation.24 | async-start | bytes 884736
  886.6 347.4 %reduce-scatter.14.cloned.1.call-start = ((), (), s32[]{:S(2)}) async-start(), calls=%async_computation.15 | async-start | bytes 7864320 | tf_op jit(solution)/shard_map/reduce_scatter | solution.py:228
  895.1 452.4 %reduce-scatter.12.cloned.1.call-start = ((), (), s32[]{:S(2)}) async-start(), calls=%async_computation.13 | async-start | bytes 7864320 | tf_op jit(solution)/shard_map/reduce_scatter | solution.py:228
  904.1 576.4 %all-reduce.35.cloned.1.call-start = ((), (), s32[]{:S(2)}) async-start(), calls=%async_computation.25 | async-start | bytes 177152 | tf_op jit(solution)/shard_map/psum | solution.py:318
  913.3 169.1 %copy-start.156 = (f32[1536]{0:T(1024)S(1)}, f32[1536]{0:T(1024)}, u32[]{:S(2)}) copy-start(f32[1536]{0:T(1024)} %copy-done.155) | copy-start | bytes 18436
  913.3 169.1 %copy-start.212 = (f32[256]{0:T(256)S(1)}, f32[256]{0:T(256)}, u32[]{:S(2)}) copy-start(f32[256]{0:T(256)} %copy-done.211) | copy-start | bytes 3076
  913.4 169.0 %copy-start.214 = (f32[256]{0:T(256)S(1)}, f32[256]{0:T(256)}, u32[]{:S(2)}) copy-start(f32[256]{0:T(256)} %copy-done.213) | copy-start | bytes 3076
  1087.7 436.3 %reduce-scatter.24.cloned.1.call-start = ((), (), s32[]{:S(2)}) async-start(), calls=%async_computation.20 | async-start | bytes 1769472 | tf_op jit(solution)/shard_map/reduce_scatter | solution.py:313
  1091.6 490.6 %reduce-scatter.26.cloned.1.call-start = ((), (), s32[]{:S(2)}) async-start(), calls=%async_computation.21 | async-start | bytes 5308416 | tf_op jit(solution)/shard_map/reduce_scatter | solution.py:315
  1103.4 536.6 %reduce-scatter.20.cloned.1.call-start = ((), (), s32[]{:S(2)}) async-start(), calls=%async_computation.18 | async-start | bytes 5308416 | tf_op jit(solution)/shard_map/reduce_scatter | solution.py:311
  1112.1 586.0 %reduce-scatter.22.cloned.1.call-start = ((), (), s32[]{:S(2)}) async-start(), calls=%async_computation.19 | async-start | bytes 5308416 | tf_op jit(solution)/shard_map/reduce_scatter | solution.py:312
  1122.2 225.3 %copy-start.51 = (bf16[2,256,1536]{2,1,0:T(8,128)(2,1)S(1)}, bf16[2,256,1536]{2,1,0:T(8,128)(2,1)}, u32[]{:S(2)}) copy-start(bf16[2,256,1536]{2,1,0:T(8,128)(2,1)} %param.25) | copy-start | bytes 4718596
  1122.2 225.3 %copy-start.68 = (bf16[2,256,1536]{2,1,0:T(8,128)(2,1)S(1)}, bf16[2,256,1536]{2,1,0:T(8,128)(2,1)}, u32[]{:S(2)}) copy-start(bf16[2,256,1536]{2,1,0:T(8,128)(2,1)} %param.26) | copy-start | bytes 4718596
  (213 other events, 942.2 us)
Sparse Core Ops, SparseCore 0:
  14.1 66.1 all-gather.24
  82.4 62.1 all-gather.16
  146.5 27.6 all-gather.18
  175.9 32.1 all-gather.22
  209.6 63.4 all-gather.28
  274.8 27.7 all-gather.20
  304.2 63.5 all-gather.26
  858.5 110.2 reduce-scatter.17
  971.1 111.2 reduce-scatter.15
  1085.4 35.5 reduce-scatter.27
  1123.3 110.7 reduce-scatter.13
  1236.2 111.2 reduce-scatter.11
  1355.1 125.3 all-reduce.34
  1484.6 39.4 reduce-scatter.23
  1528.3 53.8 reduce-scatter.25
  1586.1 53.8 reduce-scatter.19
  1644.3 53.8 reduce-scatter.21
where the time goes:
time: 1720 us; the launch traced here: 1710 us
  waiting for transfers between devices  888 us (52%)
  matrix products  272 us (16%)
  other arithmetic  199 us (12%)
  blocking collectives  173 us (10%)
  local copies, waits for them, and re-layouts  146 us (8%)
  between operations  17.7 us (1%)
    reduce_scatter x2, waiting for transfers between devices, per_device(): lax.psum_scatter(jnp.einsum('tgf,fd->tgd', mixed, full_out, preferred_ele...  223 us
    reduce_scatter x2, waiting for transfers between devices, per_device(): lax.psum_scatter(summed + jnp.einsum('tgf,df->tgd', grad_step_low, back_d...  166 us
    psum x1, waiting for transfers between devices, per_device(): lax.psum((spread_part(acc_gain_out, inner_full, tensor_index), spread_par...  126 us
    all_gather x2, waiting for transfers between devices, per_device(): lax.all_gather(normed_own, 'tensor', axis=0, tiled=True)  74 us
    psum x1, blocking collectives, per_device(): lax.psum(jnp.concatenate([grad_b, grad_c + grad_c_inject], axis=-1), 'ten...  65.5 us
    all_gather x2, waiting for transfers between devices, per_device(): lax.all_gather(own_cot, 'tensor', axis=0, tiled=True)  65 us
    dot_general x6, matrix products, local_scan(): jnp.einsum('ghkts,ksghp->ktghp', weights, xs_blk, precision=scan_mode)  62.1 us
    reduce_scatter x1, waiting for transfers between devices, per_device(): lax.psum_scatter(acc_out, ('dp', 'seq'), scatter_dimension=1, tiled=True)  58.2 us
  transfers between devices with their start and end apart: 21, of which 16 were waited for; matrix products, arithmetic and copies ran while one was open for 18% of the time, Pallas kernels for 0%

commit v1 on v0

v1 whole, which is shorter than its diff:
```python
import functools

import jax
import jax.numpy as jnp
from jax import lax
from jax.experimental import pallas as pl
from jax.experimental.pallas import tpu as pltpu
from jax.sharding import Mesh
from jax.sharding import PartitionSpec as P

CHUNK = 256
HALF = CHUNK // 2
LANES = 128
STRIP = 256
RIM = 16
EPS = 1e-05
F32 = jnp.float32
BF16 = jnp.bfloat16
VMEM_BYTES = 48 * 1024 * 1024


def dot(left, right):
    return lax.dot_general(left, right, (((1,), (0,)), ((), ())), preferred_element_type=F32)


def dot_nt(left, right):
    return lax.dot_general(left, right, (((1,), (1,)), ((), ())), preferred_element_type=F32)


def pieces(value, count):
    terms = []
    for _ in range(count):
        term = value.astype(BF16)
        terms.append(term)
        value = value - term.astype(F32)
    return terms


def spread_heads(value, spread):
    return sum(dot(term, spread) for term in pieces(value, 2))


def gather_heads(value, spread):
    return sum(dot_nt(term, spread) for term in pieces(value, 2))


def running_sum(value, mask):
    return sum(dot(mask, term) for term in pieces(value, 3))


def iota2(rows, cols, dim):
    return lax.broadcasted_iota(jnp.int32, (rows, cols), dim)


def turned(value):
    return jnp.transpose(value.astype(F32)).astype(BF16)


def strips(width):
    return [slice(at, at + STRIP) for at in range(0, width, STRIP)]


def conv_pre(ext, taps, cols):
    total = taps[4:5, cols] + taps[0:1, cols] * ext[pl.ds(RIM - 3, CHUNK), cols]
    for k in range(1, 4):
        total = total + taps[k : k + 1, cols] * ext[pl.ds(RIM - 3 + k, CHUNK), cols]
    return total


def softplus(value):
    return jnp.maximum(value, 0.0) + jnp.log1p(jnp.exp(-jnp.abs(value)))


def state_kernel(
    mix_ref, halo_ref, step_ref, taps_ref, heads_ref, spread_ref,
    xbc_ref, sum_ref, dt_ref, end_ref, total_ref, ext,
):
    inner = spread_ref.shape[1]
    place = pl.program_id(1)

    @pl.when(place == 0)
    def _():
        ext[0:RIM, :] = halo_ref[0].astype(F32)
        end_ref[...] = jnp.zeros_like(end_ref)
        total_ref[...] = jnp.zeros_like(total_ref)

    @pl.when(place > 0)
    def _():
        ext[0:RIM, :] = ext[CHUNK : CHUNK + RIM, :]

    dt = softplus(step_ref[0].astype(F32) + heads_ref[0:1, :])
    lower = (iota2(CHUNK, CHUNK, 0) >= iota2(CHUNK, CHUNK, 1)).astype(F32).astype(BF16)
    cumul = running_sum(dt * heads_ref[1:2, :], lower)
    sum_ref[0] = cumul
    dt_ref[0] = dt
    last = cumul[CHUNK - 1 : CHUNK, :]
    total_ref[0] += jnp.broadcast_to(last, total_ref.shape[1:])
    tail = jnp.exp(last - cumul) * dt
    decay = jnp.broadcast_to(jnp.exp(last), (8, LANES))
    b_turned = None
    for cols in reversed(strips(xbc_ref.shape[2])):
        ext[RIM:, cols] = mix_ref[0, :, cols].astype(F32)
        pre = conv_pre(ext, taps_ref, cols)
        act = (pre * jax.nn.sigmoid(pre)).astype(BF16)
        xbc_ref[0, :, cols] = act
        if cols.start >= inner:
            b_turned = turned(act[:, 0:LANES])
        else:
            held = spread_ref[:, cols]
            weighted = (act.astype(F32) * spread_heads(tail, held)).astype(BF16)
            kept = end_ref[0, :, cols] * spread_heads(decay, held)[0:1, :]
            end_ref[0, :, cols] = kept + dot(b_turned, weighted)


def scan_kernel(
    xbc_ref, sum_ref, dt_ref, start_ref, gate_ref, gm_ref, rows_ref, spread_ref,
    y_ref, mixed_ref, enter_ref, stat_ref, state,
):
    inner = spread_ref.shape[1]

    @pl.when(pl.program_id(1) == 0)
    def _():
        state[...] = start_ref[0]

    cumul = sum_ref[0]
    dt = dt_ref[0]
    across = jnp.transpose(cumul)
    last = cumul[CHUNK - 1 : CHUNK, :]
    tail = jnp.exp(last - cumul) * dt
    reach = jnp.exp(cumul)
    decay = jnp.broadcast_to(jnp.exp(last), (8, LANES))
    b_low = xbc_ref[0, :, inner : inner + LANES]
    c_low = xbc_ref[0, :, inner + LANES :]
    b_turned = turned(b_low)
    score = dot_nt(c_low, b_low)
    causal = iota2(HALF, HALF, 0) >= iota2(HALF, HALF, 1)
    first = iota2(1, LANES, 1) < LANES // 2
    squares = jnp.zeros((CHUNK, STRIP), F32)
    crossed = jnp.zeros((CHUNK, STRIP), F32)
    for cols in strips(inner):
        held = spread_ref[:, cols]
        x = xbc_ref[0, :, cols].astype(F32)
        u = x * spread_heads(dt, held)
        weighted = (x * spread_heads(tail, held)).astype(BF16)
        entering = state[:, cols].astype(BF16)
        enter_ref[0, 0, :, cols] = entering
        carried = dot(c_low, entering) * spread_heads(reach, held)
        state[:, cols] = state[:, cols] * spread_heads(decay, held)[0:1, :] + dot(b_turned, weighted)
        for pair in range(STRIP // LANES):
            lanes = slice(pair * LANES, (pair + 1) * LANES)
            top = carried[0:HALF, lanes]
            bottom = carried[HALF:, lanes]
            for side in range(2):
                head = (cols.start + pair * LANES) // (LANES // 2) + side
                mine = jnp.where(first if side == 0 else ~first, u[:, lanes], 0.0).astype(BF16)
                column = cumul[:, head : head + 1]
                row = across[head : head + 1, :]
                corner = jnp.where(causal, jnp.exp(column[0:HALF] - row[:, 0:HALF]), 0.0)
                top = top + dot((score[0:HALF, 0:HALF] * corner).astype(BF16), mine[0:HALF])
                left = jnp.exp(column[HALF:] - row[:, 0:HALF])
                right = jnp.where(causal, jnp.exp(column[HALF:] - row[:, HALF:]), 0.0)
                bottom = bottom + dot((score[HALF:, 0:HALF] * left).astype(BF16), mine[0:HALF])
                bottom = bottom + dot((score[HALF:, HALF:] * right).astype(BF16), mine[HALF:])
            into = slice(cols.start + pair * LANES, cols.start + (pair + 1) * LANES)
            y_ref[0, 0:HALF, into] = top
            y_ref[0, HALF:, into] = bottom
        y = y_ref[0, :, cols] + rows_ref[0:1, cols] * x
        gate = gate_ref[0, :, cols].astype(F32)
        gated = y * gate * jax.nn.sigmoid(gate)
        gained = gated * rows_ref[1:2, cols]
        mixed_ref[0, :, cols] = gained.astype(BF16)
        squares = squares + gated * gated
        crossed = crossed + gained * gm_ref[0, :, cols]
    ones = jnp.ones((8, STRIP), BF16)
    square_row = sum(dot_nt(ones, term) for term in pieces(squares, 3))
    cross_row = sum(dot_nt(ones, term) for term in pieces(crossed, 3))
    stat_ref[0] = jnp.where(iota2(8, CHUNK, 0) == 0, square_row, cross_row)


def gate_kernel(
    inner_full, y_ref, xbc_ref, gate_ref, gm_ref, stat_ref, sum_ref, rows_ref, spread_ref,
    gy_ref, gz_ref, mixed_ref, back_ref, gain_ref,
):
    inner = spread_ref.shape[1]

    @pl.when(pl.program_id(1) == 0)
    def _():
        back_ref[...] = jnp.zeros_like(back_ref)

    @pl.when((pl.program_id(0) == 0) & (pl.program_id(1) == 0))
    def _():
        gain_ref[...] = jnp.zeros_like(gain_ref)

    stats = jnp.transpose(stat_ref[0])
    scale = lax.rsqrt(stats[:, 0:1] / inner_full + EPS)
    bent = scale * scale * scale * (stats[:, 1:2] / inner_full)
    cumul = sum_ref[0]
    reach = jnp.exp(cumul)
    decay = jnp.broadcast_to(jnp.exp(cumul[CHUNK - 1 : CHUNK, :]), (8, LANES))
    c_turned = turned(xbc_ref[0, :, inner + LANES :])
    for cols in strips(inner):
        held = spread_ref[:, cols]
        x = xbc_ref[0, :, cols].astype(F32)
        y = y_ref[0, :, cols] + rows_ref[0:1, cols] * x
        gate = gate_ref[0, :, cols].astype(F32)
        sigmoid = jax.nn.sigmoid(gate)
        silu = gate * sigmoid
        gated = y * silu
        scaled = gated * scale
        gm = gm_ref[0, :, cols]
        gain = rows_ref[1:2, cols]
        gg = scale * gm * gain - gated * bent
        gy = (gg * silu).astype(BF16)
        gy_ref[0, :, cols] = gy
        gz_ref[0, :, cols] = (gg * y * sigmoid * (1.0 + gate * (1.0 - sigmoid))).astype(BF16)
        mixed_ref[0, :, cols] = (scaled * gain).astype(BF16)
        gain_ref[:, cols] += jnp.broadcast_to(jnp.sum(gm * scaled, axis=0, keepdims=True), (8, STRIP))
        reached = (gy.astype(F32) * spread_heads(reach, held)).astype(BF16)
        kept = back_ref[0, :, cols] * spread_heads(decay, held)[0:1, :]
        back_ref[0, :, cols] = kept + dot(c_turned, reached)


def adjoint_kernel(
    xbc_ref, sum_ref, dt_ref, gy_ref, y_ref, enter_ref, gin_ref, mix_ref, before_ref, halo_ref,
    step_ref, taps_ref, heads_ref, rows_ref, spread_ref,
    gmix_ref, rim_ref, gtaps_ref, gheads_ref, gskip_ref, back, ext, gpre, pulled,
):
    inner = spread_ref.shape[1]
    chunks = pl.num_programs(1)
    order = pl.program_id(1)

    @pl.when((pl.program_id(0) == 0) & (order == 0))
    def _():
        gtaps_ref[...] = jnp.zeros_like(gtaps_ref)
        gheads_ref[...] = jnp.zeros_like(gheads_ref)
        gskip_ref[...] = jnp.zeros_like(gskip_ref)

    @pl.when(order == 0)
    def _():
        back[...] = gin_ref[0]
        gpre[CHUNK:, :] = jnp.zeros((8, gpre.shape[1]), F32)

    @pl.when(order > 0)
    def _():
        gpre[CHUNK:, :] = gpre[0:8, :]

    @pl.when(order == chunks - 1)
    def _():
        ext[0:RIM, :] = halo_ref[0].astype(F32)

    @pl.when(order < chunks - 1)
    def _():
        ext[0:RIM, :] = before_ref[0].astype(F32)

    cumul = sum_ref[0]
    dt = dt_ref[0]
    across = jnp.transpose(cumul)
    last = cumul[CHUNK - 1 : CHUNK, :]
    fade = jnp.exp(last - cumul)
    reach = jnp.exp(cumul)
    decay = jnp.broadcast_to(jnp.exp(last), (8, LANES))
    b_low = xbc_ref[0, :, inner : inner + LANES]
    c_low = xbc_ref[0, :, inner + LANES :]
    c_turned = turned(c_low)
    score = dot_nt(b_low, c_low)
    causal = iota2(HALF, HALF, 0) <= iota2(HALF, HALF, 1)
    first = iota2(1, LANES, 1) < LANES // 2
    pulled[...] = jnp.zeros_like(pulled)
    gb = jnp.zeros((CHUNK, LANES), F32)
    gc = jnp.zeros((CHUNK, LANES), F32)
    between = jnp.zeros((CHUNK, LANES), F32)
    arrived = jnp.zeros((CHUNK, LANES), F32)
    direct = jnp.zeros((CHUNK, LANES), F32)
    joined = jnp.zeros((8, LANES), F32)

    def conv_part(cols, gact):
        ext[RIM:, cols] = mix_ref[0, :, cols].astype(F32)
        pre = conv_pre(ext, taps_ref, cols)
        sigmoid = jax.nn.sigmoid(pre)
        gp = gact.astype(BF16).astype(F32) * sigmoid * (1.0 + pre * (1.0 - sigmoid))
        gpre[0:CHUNK, cols] = gp
        rim_ref[0, :, cols] = gp[0:8, :]
        total = taps_ref[3:4, cols] * gp
        for k in range(3):
            total = total + taps_ref[k : k + 1, cols] * gpre[pl.ds(3 - k, CHUNK), cols]
            gtaps_ref[k : k + 1, cols] += jnp.sum(
                gp * ext[pl.ds(RIM - 3 + k, CHUNK), cols], axis=0, keepdims=True
            )
        gtaps_ref[3:4, cols] += jnp.sum(gp * ext[RIM:, cols], axis=0, keepdims=True)
        gtaps_ref[4:5, cols] += jnp.sum(gp, axis=0, keepdims=True)
        gmix_ref[0, :, cols] = total.astype(BF16)

    for cols in strips(inner):
        held = spread_ref[:, cols]
        x = xbc_ref[0, :, cols].astype(F32)
        dt_wide = spread_heads(dt, held)
        fade_wide = spread_heads(fade, held)
        u = x * dt_wide
        u_low = u.astype(BF16)
        weighted = (u * fade_wide).astype(BF16)
        gy_low = gy_ref[0, :, cols]
        gy = gy_low.astype(F32)
        reached = (gy * spread_heads(reach, held)).astype(BF16)
        later = back[:, cols]
        later_low = later.astype(BF16)
        entered = enter_ref[0, 0, :, cols]
        gb = gb + dot_nt(weighted, later_low)
        gc = gc + dot_nt(reached, entered)
        gu_carried = dot(b_low, later_low) * fade_wide
        sums = jnp.sum(later * entered.astype(F32), axis=0, keepdims=True)
        joined = joined + gather_heads(jnp.broadcast_to(sums, (8, STRIP)), held)
        back[:, cols] = later * spread_heads(decay, held)[0:1, :] + dot(c_turned, reached)
        parts = []
        for pair in range(STRIP // LANES):
            lanes = slice(pair * LANES, (pair + 1) * LANES)
            top = gu_carried[0:HALF, lanes]
            bottom = gu_carried[HALF:, lanes]
            gy_pair = gy_low[:, lanes]
            for side in range(2):
                head = (cols.start + pair * LANES) // (LANES // 2) + side
                keep = first if side == 0 else ~first
                gy_mine = jnp.where(keep, gy[:, lanes], 0.0).astype(BF16)
                u_mine = jnp.where(keep, u[:, lanes], 0.0).astype(BF16)
                column = cumul[:, head : head + 1]
                row = across[head : head + 1, :]
                corner = jnp.where(causal, jnp.exp(row[:, 0:HALF] - column[0:HALF]), 0.0)
                side_right = jnp.exp(row[:, HALF:] - column[0:HALF])
                low_right = jnp.where(causal, jnp.exp(row[:, HALF:] - column[HALF:]), 0.0)
                top = top + dot((score[0:HALF, 0:HALF] * corner).astype(BF16), gy_mine[0:HALF])
                top = top + dot((score[0:HALF, HALF:] * side_right).astype(BF16), gy_mine[HALF:])
                bottom = bottom + dot((score[HALF:, HALF:] * low_right).astype(BF16), gy_mine[HALF:])
                upper = dot_nt(u_mine[0:HALF], gy_pair)
                pulled[0:HALF, 0:HALF] += upper[:, 0:HALF] * corner
                pulled[0:HALF, HALF:] += upper[:, HALF:] * side_right
                pulled[HALF:, HALF:] += dot_nt(u_mine[HALF:], gy_pair[HALF:]) * low_right
            parts.append(jnp.concatenate([top, bottom], axis=0))
        gu = jnp.concatenate(parts, axis=1)
        u_kept = u_low.astype(F32)
        between = between + gather_heads(gy * y_ref[0, :, cols] - u_kept * gu, held)
        arrived = arrived + gather_heads(u_kept * gu_carried, held)
        direct = direct + gather_heads(x * gu, held)
        gskip_ref[:, cols] += jnp.broadcast_to(jnp.sum(gy * x, axis=0, keepdims=True), (8, STRIP))
        conv_part(cols, dt_wide * gu + rows_ref[0:1, cols] * gy)

    pulled_low = pulled[...].astype(BF16)
    gb = gb + dot(pulled_low, c_low)
    gc = gc + dot(jnp.transpose(pulled[...]).astype(BF16), b_low)
    conv_part(slice(inner, inner + 2 * LANES), jnp.concatenate([gb, gc], axis=1))

    upper = (iota2(CHUNK, CHUNK, 0) <= iota2(CHUNK, CHUNK, 1)).astype(F32).astype(BF16)
    whole = jnp.sum(arrived, axis=0, keepdims=True) + decay[0:1, :] * joined[0:1, :]
    glg = running_sum(between, upper) + whole
    rate = heads_ref[1:2, :]
    gdt = direct + rate * glg
    raw = step_ref[0].astype(F32) + heads_ref[0:1, :]
    gsi = gdt * jax.nn.sigmoid(raw) * heads_ref[2:3, :]
    gmix_ref[0, :, inner + 2 * LANES :] = gsi.astype(BF16)
    gheads_ref[0:1, :] += jnp.sum(gsi, axis=0, keepdims=True)
    gheads_ref[1:2, :] += jnp.sum(glg * dt * rate, axis=0, keepdims=True)


def tall(width, part, order=lambda i: i, column=0):
    return pl.BlockSpec((None, 1, CHUNK, width), lambda g, i: (part, g, order(i), column))


def flat(width, order=lambda i: i, column=0):
    return pl.BlockSpec((1, CHUNK, width), lambda g, i: (g, order(i), column))


def whole(*shape):
    return pl.BlockSpec((1,) + shape, lambda g, i: (g,) + (0,) * len(shape))


def fixed(shape):
    return pl.BlockSpec(shape, lambda g, i: (0,) * len(shape))


def shaped(shape, dtype=F32):
    return jax.ShapeDtypeStruct(shape, dtype)


def run(kernel, grid, ins, outs, scratch, flops, moved, into=None, after=()):
    into = {k: v for k, v in (into or {}).items() if v is not None}
    count = len(ins)
    extra = list(after) + list(into.values())

    def body(*refs):
        kernel(*refs[:count], *refs[count + len(extra) :])

    steps = grid[0] * grid[1]
    return pl.pallas_call(
        body,
        grid=grid,
        in_specs=[spec for _, spec in ins] + [pl.BlockSpec(memory_space=pl.ANY)] * len(extra),
        out_specs=[spec for _, spec in outs],
        out_shape=[shape for shape, _ in outs],
        scratch_shapes=scratch,
        input_output_aliases={count + len(after) + n: k for n, k in enumerate(into)},
        compiler_params=pltpu.CompilerParams(
            dimension_semantics=("arbitrary", "arbitrary"), vmem_limit_bytes=VMEM_BYTES
        ),
        cost_estimate=pl.CostEstimate(
            flops=steps * flops, bytes_accessed=steps * moved, transcendentals=0
        ),
    )(*[array for array, _ in ins], *extra)


def local_states(xw, halo, taps, heads, spread, after):
    groups, length, _ = xw.shape
    inner = spread.shape[1]
    width = inner + 2 * LANES
    return run(
        state_kernel,
        (groups, length // CHUNK),
        [
            (xw, flat(width)),
            (halo, whole(RIM, width)),
            (xw, flat(LANES, column=width // LANES)),
            (taps, fixed(taps.shape)),
            (heads, fixed(heads.shape)),
            (spread, fixed(spread.shape)),
        ],
        [
            (shaped((groups, length, width), BF16), flat(width)),
            (shaped((groups, length, LANES)), flat(LANES)),
            (shaped((groups, length, LANES)), flat(LANES)),
            (shaped((groups, LANES, inner)), whole(LANES, inner)),
            (shaped((groups, 8, LANES)), whole(8, LANES)),
        ],
        [pltpu.VMEM((RIM + CHUNK, width), F32)],
        1_500_000_000,
        2_000_000,
        None,
        after,
    )


def mixer(part, xbc, cumul, dt, start, gate, gm, rows, spread, gained, after):
    groups, length, width = xbc.shape
    inner = spread.shape[1]
    chunks = length // CHUNK
    return run(
        scan_kernel,
        (groups, chunks),
        [
            (xbc, flat(width)),
            (cumul, flat(LANES)),
            (dt, flat(LANES)),
            (start, whole(LANES, inner)),
            (gate, tall(inner, part)),
            (gm, tall(inner, part)),
            (rows, fixed(rows.shape)),
            (spread, fixed(spread.shape)),
        ],
        [
            (shaped((groups, length, inner)), flat(inner)),
            (shaped(gate.shape, BF16), tall(inner, part)),
            (
                shaped((groups, chunks, LANES, inner), BF16),
                pl.BlockSpec((1, 1, LANES, inner), lambda g, i: (g, i, 0, 0)),
            ),
            (shaped((groups, 8, length)), pl.BlockSpec((1, 8, CHUNK), lambda g, i: (g, 0, i))),
        ],
        [pltpu.VMEM((LANES, inner), F32)],
        2_500_000_000,
        4_000_000,
        {1: gained},
        after,
    )


def gate_back(part, inner_full, y, xbc, gate, gm, stats, cumul, rows, spread, gz, mixed, after):
    groups, length, width = xbc.shape
    inner = spread.shape[1]
    chunks = length // CHUNK
    back = lambda i: chunks - 1 - i
    return run(
        functools.partial(gate_kernel, float(inner_full)),
        (groups, chunks),
        [
            (y, flat(inner, back)),
            (xbc, flat(width, back)),
            (gate, tall(inner, part, back)),
            (gm, tall(inner, part, back)),
            (stats, pl.BlockSpec((1, 8, CHUNK), lambda g, i: (g, 0, back(i)))),
            (cumul, flat(LANES, back)),
            (rows, fixed(rows.shape)),
            (spread, fixed(spread.shape)),
        ],
        [
            (shaped((groups, length, inner), BF16), flat(inner, back)),
            (shaped(gate.shape, BF16), tall(inner, part, back)),
            (shaped(gate.shape, BF16), tall(inner, part, back)),
            (shaped((groups, LANES, inner)), whole(LANES, inner)),
            (shaped((8, inner)), fixed((8, inner))),
        ],
        [],
        1_500_000_000,
        4_500_000,
        {1: gz, 2: mixed},
        after,
    )


def adjoint(xbc, cumul, dt, gy, y, enter, gin, xw, halo, taps, heads, rows, spread, after):
    groups, length, width = xbc.shape
    inner = spread.shape[1]
    chunks = length // CHUNK
    back = lambda i: chunks - 1 - i
    per = CHUNK // RIM
    return run(
        adjoint_kernel,
        (groups, chunks),
        [
            (xbc, flat(width, back)),
            (cumul, flat(LANES, back)),
            (dt, flat(LANES, back)),
            (gy, flat(inner, back)),
            (y, flat(inner, back)),
            (enter, pl.BlockSpec((1, 1, LANES, inner), lambda g, i: (g, back(i), 0, 0))),
            (gin, whole(LANES, inner)),
            (xw, flat(width, back)),
            (
                xw,
                pl.BlockSpec(
                    (1, RIM, width), lambda g, i: (g, jnp.maximum(back(i) * per - 1, 0), 0)
                ),
            ),
            (halo, whole(RIM, width)),
            (xw, flat(LANES, back, width // LANES)),
            (taps, fixed(taps.shape)),
            (heads, fixed(heads.shape)),
            (rows, fixed(rows.shape)),
            (spread, fixed(spread.shape)),
        ],
        [
            (shaped((groups, length, width + LANES), BF16), flat(width + LANES, back)),
            (shaped((groups, 8, width)), whole(8, width)),
            (shaped((8, width)), fixed((8, width))),
            (shaped((8, LANES)), fixed((8, LANES))),
            (shaped((8, inner)), fixed((8, inner))),
        ],
        [
            pltpu.VMEM((LANES, inner), F32),
            pltpu.VMEM((RIM + CHUNK, width), F32),
            pltpu.VMEM((CHUNK + 8, width), F32),
            pltpu.VMEM((CHUNK, CHUNK), F32),
        ],
        8_000_000_000,
        6_000_000,
        None,
        after,
    )


def place_kernel(at_ref, first, first_y, second, second_x, full_ref):
    step = pl.program_id(0)
    for number, ref in enumerate((first, first_y, second, second_x)):

        @pl.when(step // 2 == number)
        def _(ref=ref):
            full_ref[0, 0, 0] = ref[0]


def place_row(number, step, at):
    x, core, y = at[0], at[1], at[2]
    later = number // 2
    side = number % 2
    row = x + jnp.where(later == 0, step, side)
    column = y + jnp.where(later == 0, side, step)
    return row % 2, jnp.where(later == 0, core, 1 - core), column % 2, 0, 0


def place(first, first_y, second, second_x):
    _, rows, columns = first.shape
    at = jnp.stack([lax.axis_index(name) for name in ("x", "core", "y")]).astype(jnp.int32)

    def piece(number):
        return pl.BlockSpec(
            (1, rows, columns), lambda i, at: (jnp.clip(i - 2 * number, 0, 1), 0, 0)
        )

    full = pl.pallas_call(
        place_kernel,
        grid_spec=pltpu.PrefetchScalarGridSpec(
            num_scalar_prefetch=1,
            grid=(8,),
            in_specs=[piece(number) for number in range(4)],
            out_specs=pl.BlockSpec(
                (1, 1, 1, rows, columns), lambda i, at: place_row(i // 2, i % 2, at)
            ),
        ),
        out_shape=shaped((2, 2, 2, rows, columns), first.dtype),
        compiler_params=pltpu.CompilerParams(
            dimension_semantics=("arbitrary",), vmem_limit_bytes=VMEM_BYTES
        ),
        cost_estimate=pl.CostEstimate(
            flops=0, bytes_accessed=32 * rows * columns, transcendentals=0
        ),
    )(at, first, first_y, second, second_x)
    return full.reshape(8 * rows, columns)


def swap(value, axis):
    return lax.ppermute(value, axis, [(0, 1), (1, 0)])


def sum_axis(value, axis):
    if lax.axis_size(axis) == 2:
        return value + swap(value, axis)
    return lax.psum(value, axis)


def cut(value, axis, dim):
    size = value.shape[dim] // 2
    at = lax.axis_index(axis)
    kept = lax.dynamic_slice_in_dim(value, at * size, size, dim)
    return kept, lax.dynamic_slice_in_dim(value, (1 - at) * size, size, dim)


def added(kept, got, dtype=BF16):
    return (kept.astype(F32) + got.astype(F32)).astype(dtype)


def ordered_pair(own, other):
    low = lax.axis_index("zq") == 0
    return jnp.where(low, jnp.concatenate([own, other]), jnp.concatenate([other, own]))


def hold(value, *before):
    return lax.optimization_barrier((value,) + before)[0]


def shift(value, by):
    blocks = lax.axis_size(("y", "zp"))
    pairs = [(i, i + by) for i in range(blocks) if 0 <= i + by < blocks]
    return lax.ppermute(value, ("y", "zp"), pairs)


def coarse(value):
    return lax.reduce_precision(value, 8, 7)


def weight(log, inner):
    heads = inner // (LANES // 2)
    return jnp.repeat(jnp.exp(log[:, :, 0:heads]), LANES // 2, axis=2)


def pack_states(ends, totals):
    groups, _, inner = ends.shape
    high = coarse(totals)
    middle = coarse(totals - high)
    low = coarse(totals - high - middle)
    logs = jnp.concatenate([high, middle, low, jnp.zeros((groups, RIM - 3, LANES), F32)], axis=1)
    logs = jnp.pad(logs, ((0, 0), (0, 0), (0, inner - LANES)))
    return jnp.concatenate([ends, logs], axis=1).astype(BF16)


def within_row(packed, ends, totals, way):
    columns = lax.axis_size("zp")
    groups, states, inner = ends.shape
    entering = jnp.zeros(ends.shape, F32)
    passed = jnp.zeros((groups, 1, LANES), F32)
    for by in range(1, columns):
        pairs = [(i, i + by * way) for i in range(columns) if 0 <= i + by * way < columns]
        got = lax.ppermute(packed, "zp", pairs).astype(F32)
        entering = entering + weight(passed, inner) * got[:, 0:states]
        passed = passed + jnp.sum(got[:, states : states + 3, 0:LANES], axis=1, keepdims=True)
    leaving = (ends + weight(totals, inner) * entering).astype(BF16)
    return entering, passed, leaving


def across_rows(entering, passed, leaving, ends, totals, way):
    rows, columns = lax.axis_size("y"), lax.axis_size("zp")
    inner = ends.shape[2]
    edge = columns - 1 if way == 1 else 0
    total = entering
    for step in range(rows - 1):
        if step > 0:
            leaving = (ends + weight(totals, inner) * total).astype(BF16)
        got = jnp.zeros(ends.shape, F32)
        for to in range(columns):
            pairs = [
                (row * columns + edge, (row + way) * columns + to)
                for row in range(rows)
                if 0 <= row + way < rows
            ]
            got = got + lax.ppermute(leaving, ("y", "zp"), pairs).astype(F32)
        total = entering + weight(passed, inner) * got
    return total


def all_pairs():
    return all(lax.axis_size(name) == 2 for name in ("x", "y", "zp"))


NEAR = [(0, 1), (3, 2), (1, 3), (2, 0)]
FAR = [(1, 2), (2, 1)]
HOME = [(to, source) for source, to in NEAR]


def fetched(piece, near, far):
    at_home = lax.axis_index("core") == lax.axis_index("zp")
    return jnp.where(at_home, piece, near), jnp.where(at_home, near, far)


def fetch(piece):
    return lax.ppermute(piece, ("core", "zp"), NEAR), lax.ppermute(piece, ("core", "zp"), FAR)


def gather_slice(piece):
    owners = lax.axis_size("zp")
    rows = lax.all_gather(piece, ("x", "core", "y"), axis=0, tiled=True)
    parts = lax.all_gather(rows, "zp")
    return lax.dynamic_slice_in_dim(parts, lax.axis_index("core") * (owners // 2), owners // 2, 0)


def reduce_slice(parts):
    owners = lax.axis_size("zp")
    full = jnp.zeros((owners,) + parts.shape[1:], parts.dtype)
    full = lax.dynamic_update_slice_in_dim(
        full, parts, lax.axis_index("core") * (owners // 2), axis=0
    )
    mine = lax.psum_scatter(full, "zp", scatter_dimension=0, tiled=True)[0]
    mine = lax.psum_scatter(mine, ("x", "core", "y"), scatter_dimension=0, tiled=True)
    return mine.astype(F32)


def cut_rows(full):
    rows, columns = full.shape[0] // 8, full.shape[1]
    full = full.reshape(2, 2, 2, rows, columns)
    core = lax.axis_index("core")
    same = cut(lax.dynamic_index_in_dim(full, core, 1, False), "x", 0)
    cross = cut(lax.dynamic_index_in_dim(full, 1 - core, 1, False), "y", 1)
    return same[0][0], cross[0][:, 0], same[1][0], cross[1][:, 0]


def cut_again(same, cross):
    same, cross = cut(same, "y", 0), cut(cross, "x", 0)
    return same[0][0], cross[0][0], same[1][0], cross[1][0]


def home_parts(same, cross):
    at_home = lax.axis_index("core") == lax.axis_index("zp")
    return jnp.where(at_home, cross, same), cross


def at_owner(near, far, same):
    at_home = lax.axis_index("core") == lax.axis_index("zp")
    return near.astype(F32) + jnp.where(at_home, same.astype(F32), far.astype(F32))


def own_of_slice(value):
    owners = lax.axis_size("zp")
    core, part = lax.axis_index("core"), lax.axis_index("zp")
    other = swap(value, "core")
    share = value.shape[-1] // (owners // 2)
    wanted = jnp.where(part // (owners // 2) == core, value, other)
    return lax.dynamic_slice_in_dim(wanted, (part % (owners // 2)) * share, share, value.ndim - 1)


def slice_of_own(value, after):
    owners = lax.axis_size("zp")
    core = lax.axis_index("core")
    if owners == 2:
        other = hold(swap(value, "zp"), after)
        return jnp.where(core == lax.axis_index("zp"), value, other)[None]
    parts = lax.all_gather(value, "zp")
    return lax.dynamic_slice_in_dim(parts, core * (owners // 2), owners // 2, 0)


def per_device(
    hidden,
    cotangent,
    norm_gain,
    w_z,
    w_x,
    w_bc,
    w_dt,
    conv_x,
    conv_x_bias,
    conv_bc,
    conv_bc_bias,
    dt_bias,
    a_log,
    d_skip,
    inner_gain,
    w_out,
):
    micro, own_len, model = hidden.shape
    owners = lax.axis_size("zp")
    share = w_x.shape[1]
    own_heads = w_dt.shape[1]
    inner_full = share * 2 * owners
    states2 = w_bc.shape[1]
    halves = owners // 2
    inner = share * halves
    heads = own_heads * halves
    head_width = inner // heads
    width = inner + states2

    def matmul(left, right, contract, dtype=F32):
        return lax.dot_general(
            left, right, (contract, ((), ())), preferred_element_type=F32
        ).astype(dtype)

    def spliced(parts, sizes):
        if halves == 1:
            return parts[0]
        columns, at = [], 0
        for size, copies in sizes:
            columns += [parts[k][:, at : at + size] for k in range(halves if copies else 1)]
            at += size
        return jnp.concatenate(columns, axis=1)

    parts = range(micro)

    own = hidden.astype(F32)
    gain_in = norm_gain.astype(F32)
    r0 = lax.rsqrt(jnp.mean(own * own, axis=-1, keepdims=True) + EPS)
    filler = LANES // halves - own_heads
    own_first = jnp.concatenate(
        [w_x, w_bc, w_dt, jnp.zeros((w_dt.shape[0], filler), BF16)], axis=1
    )
    own_second = jnp.concatenate([w_z, jnp.transpose(w_out)], axis=1)
    normed_own = (own * r0 * gain_in).astype(BF16)
    fast = all_pairs()
    if fast:
        got = fetch(own_first)
    normed_got = [swap(normed_own[part], "zq") for part in parts]
    if fast:
        same, cross = fetched(own_first, *got)
        first, second = [jnp.stack([same, swap(same, "x")]), jnp.stack([cross, swap(cross, "y")])]
        own_second = hold(own_second, same, cross)
        got = fetch(own_second)
        rest = swap(first, "y"), swap(second, "x")
    near = [ordered_pair(normed_own[0], hold(normed_got[0], *((first, second) if fast else ())))]
    far = [swap(near[0], "core")]
    if fast:
        same, cross = fetched(own_second, *hold(got, near[0]))
        moved = swap(same, "x"), swap(cross, "y")
        w_first = place(first, rest[0], second, rest[1])
        same, cross, *moved = hold((same, cross, *moved), w_first)
        first, second = jnp.stack([same, moved[0]]), jnp.stack([cross, moved[1]])
        got_second = first, swap(first, "y"), second, swap(second, "x")
    else:
        w_first = spliced(
            gather_slice(own_first), ((share, 1), (states2, 0), (own_heads, 1), (filler, 1))
        )
    for part in parts[1:]:
        near.append(ordered_pair(normed_own[part], hold(normed_got[part], near[part - 1])))
        far.append(swap(near[part], "core"))
    normed = jnp.stack([jnp.stack(pair) for pair in zip(near, far)])
    cot_own = hold(cotangent, near[-1])
    cot_got = swap(cot_own, "zq")

    per_head = jnp.concatenate([dt_bias, a_log, d_skip])
    per_head = jnp.pad(per_head, (0, share - 3 * own_heads))
    small = jnp.concatenate([conv_x, conv_x_bias[None], inner_gain[None]], axis=0).astype(F32)
    small = jnp.concatenate([small, per_head[None], jnp.zeros((1, share), F32)])
    small = slice_of_own(small, w_first)
    channel_rows = jnp.concatenate([small[k, 0:6] for k in range(halves)], axis=1)
    head_rows = jnp.concatenate(
        [small[k, 6, 0 : 3 * own_heads].reshape(3, own_heads) for k in range(halves)], axis=1
    )
    conv_shared = jnp.concatenate([conv_bc, conv_bc_bias[None]], axis=0).astype(F32)
    taps = jnp.pad(jnp.concatenate([channel_rows[0:5], conv_shared], axis=1), ((0, 3), (0, 0)))
    head_in = jnp.stack([head_rows[0], -jnp.exp(head_rows[1]), jnp.ones((heads,), F32)])
    head_in = jnp.pad(head_in, ((0, 5), (0, LANES - heads)))
    rows = jnp.stack([jnp.repeat(head_rows[2], head_width), channel_rows[5]])
    rows = jnp.pad(rows, ((0, 6), (0, 0)))
    spread = (
        lax.broadcasted_iota(jnp.int32, (LANES, inner), 1) // head_width
        == lax.broadcasted_iota(jnp.int32, (LANES, inner), 0)
    ).astype(BF16)

    scans = []
    for part in parts:
        xw = matmul(normed[part], w_first, ((2,), (0,)), BF16)
        scans.append((xw, shift(xw[:, -RIM:, 0:width], 1)))
    local, packed = [], []
    for part in parts:
        local.append(local_states(*scans[part], taps, head_in, spread, packed[-1:]))
        packed.append(pack_states(local[part][3], local[part][4][:, 0:1]))
        if part == 0:
            cot_got = hold(cot_got, packed[0])
            cot_near = jnp.stack(
                [ordered_pair(cotangent[k], cot_got[k]) for k in parts]
            )
            cot_far = swap(cot_near, "core")
    if fast:
        got_second = hold(got_second, packed[-1])
        w_second = place(*got_second)
    else:
        w_second = spliced(
            gather_slice(hold(own_second, packed[-1])), ((share, 1), (share, 1))
        )
    w_gate, w_down = w_second[:, 0:inner], w_second[:, inner:]
    gate = matmul(normed, w_gate, ((3,), (0,)), BF16)
    totals = [local[part][4][:, 0:1] for part in parts]
    rowwise = [within_row(packed[part], local[part][3], totals[part], 1) for part in parts]
    w_down, _, cot_far = hold((w_down, cot_near, cot_far), gate, rowwise[0][2])
    cot = jnp.stack([cot_near, cot_far], axis=1)
    gm = matmul(cot, w_down, ((3,), (0,)))
    gained, mixes, stats = None, [], []
    for part in parts:
        xbc, cumul, dt = local[part][0:3]
        start = across_rows(*rowwise[part], local[part][3], totals[part], 1)
        y, gained, enter, stat = mixer(
            part, xbc, cumul, dt, start, gate, gm, rows, spread, gained,
            [r[2] for r in rowwise[part + 1 :]],
        )
        mixes.append((y, enter))
        stat = stat + jnp.flip(swap(stat, "core"), 0)
        stats.append(sum_axis(stat, "zq"))
    branch = matmul(gained, w_down, ((3,), (1,)), BF16)
    gz = mixed = None
    gates, packed = [], []
    for part in parts:
        xbc, cumul = local[part][0:2]
        gy, gz, mixed, back_end, g_gain = gate_back(
            part, inner_full, mixes[part][0], xbc, gate, gm, stats[part], cumul, rows, spread,
            gz, mixed, [branch] + packed[-1:],
        )
        gates.append((gy, back_end, g_gain))
        packed.append(pack_states(back_end, totals[part]))

    tokens = ((0, 1, 2), (0, 1, 2))
    branch = added(branch[:, 0], swap(branch[:, 1], "core"))
    branch_kept, branch_sent = cut(branch, "zq", 1)
    mixed = hold(mixed, *packed)
    g_down = matmul(cot, mixed, tokens, BF16)
    g_gate = matmul(normed, hold(gz, g_down), tokens, BF16)
    rowwise = [within_row(packed[part], gates[part][1], totals[part], -1) for part in parts]
    gz = hold(gz, g_gate, rowwise[0][2])
    g_normed_gate = matmul(gz, w_gate, ((3,), (1,)))
    gins = [across_rows(*rowwise[part], gates[part][1], totals[part], -1) for part in parts]
    wait_for = [branch_sent, g_normed_gate, rowwise[-1][2]]
    if fast:
        second = cut_rows(hold(jnp.concatenate([g_gate, g_down], axis=1), gins[0]))
        moved = swap(second[2], "x"), swap(second[3], "y")
        wait_for += second[2:]
    branch_got = swap(branch_sent, "zq")

    g_first, heads_out, norm_sums = 0.0, [], []
    for part in parts:
        xbc, cumul, dt = local[part][0:3]
        gmix, rim, *sums = adjoint(
            xbc, cumul, dt, gates[part][0], mixes[part][0], mixes[part][1], gins[part],
            *scans[part], taps, head_in, rows, spread, wait_for,
        )
        heads_out.append(sums)
        ahead = shift(rim, -1)
        if fast and part == 0:
            moved = hold(moved, gmix)
            second = cut_again(added(second[0], moved[0]), added(second[1], moved[1]))
            moved = swap(second[2], "y"), swap(second[3], "x")
        if part == micro - 1:
            branch_got = hold(branch_got, gmix)
            branch_own = added(branch_kept, branch_got, F32)
        fix = jnp.stack(
            [sum(taps[k, :] * ahead[:, r - k] for k in range(r + 1)) for r in range(3)], axis=1
        )
        length = gmix.shape[1]
        last = gmix[:, length - RIM :].astype(F32)
        last = last + jnp.pad(fix, ((0, 0), (RIM - 3, 0), (0, LANES)))
        gmix = lax.dynamic_update_slice_in_dim(gmix, last.astype(BF16), length - RIM, 1)

        def for_weights(gmix, g_first):
            return g_first + matmul(normed[part], gmix, ((0, 1), (0, 1)))

        def for_tokens(gmix):
            total = g_normed_gate[part] + matmul(gmix, w_first, ((2,), (1,)))
            return total.astype(BF16)

        if part < micro - 1:
            total = for_tokens(gmix)
            other = swap(total[1], "core")
            g_first = for_weights(hold(gmix, total), g_first)
            total, other, _ = hold((total[0], other), g_first) + (None,)
            norm_sums.append(cut(added(total, other), "zq", 0))
            wait_for = [g_first, norm_sums[-1][1]]
            if fast:
                moved = hold(moved, g_first)
                same, cross = added(second[0], moved[0]), added(second[1], moved[1])
                sent = home_parts(same, cross)
                wait_for += sent
                got = (
                    lax.ppermute(sent[0], ("core", "zp"), HOME),
                    lax.ppermute(sent[1], ("core", "zp"), FAR),
                )
        else:
            g_first = for_weights(gmix, g_first).astype(BF16)
            if fast:
                first = cut_rows(g_first)
                moved_first = swap(first[2], "x"), swap(first[3], "y")
                gmix = hold(gmix, *first[2:])
            total = for_tokens(gmix)
            norm_sums.append(cut(added(total[0], swap(total[1], "core")), "zq", 0))

    if fast:
        g_second = at_owner(*hold(got, g_first), same)
        first = cut_again(added(first[0], moved_first[0]), added(first[1], moved_first[1]))
        moved = swap(first[2], "y"), swap(first[3], "x")
        same, cross = added(first[0], moved[0]), added(first[1], moved[1])
        sent = home_parts(same, cross)
        g_first = at_owner(
            lax.ppermute(sent[0], ("core", "zp"), HOME),
            lax.ppermute(sent[1], ("core", "zp"), FAR),
            same,
        )
    else:
        g_second = reduce_slice(
            jnp.stack(
                [
                    jnp.concatenate(pair, axis=1)
                    for pair in zip(
                        jnp.split(g_gate, halves, axis=1), jnp.split(g_down, halves, axis=1)
                    )
                ]
            )
        )
        g_first = reduce_slice(
            jnp.concatenate(
                [
                    jnp.stack(jnp.split(g_first[:, 0:inner], halves, axis=1)),
                    jnp.concatenate(
                        [
                            g_first[None, :, inner:width],
                            jnp.zeros((halves - 1, model, states2), BF16),
                        ]
                    ),
                    jnp.stack(jnp.split(g_first[:, width : width + heads], halves, axis=1)),
                ],
                axis=2,
            )
        )
    g_bc = g_first[:, share : share + states2]
    g_bc = sum_axis(sum_axis(g_bc, "zp"), "zq")

    own_squares, g_hidden, g_norm_gain = [], [], 0.0
    for part in parts:
        own_squares.append(
            lax.dynamic_slice_in_dim(stats[part][0, 0], lax.axis_index("zq") * own_len, own_len, 0)
        )
        kept, sent = norm_sums[part]
        x, r, g = own[part], r0[part], added(kept, swap(sent, "zq"), F32)
        q0 = g * gain_in
        g_norm_gain = g_norm_gain + jnp.sum(g * x * r, axis=0)
        g_hidden.append(
            cotangent[part].astype(F32) + r * q0
            - x * (r * r * r) * jnp.mean(q0 * x, axis=-1, keepdims=True)
        )
    r1 = lax.rsqrt(jnp.stack(own_squares) / inner_full + EPS)[..., None]
    outputs = (own + r1 * branch_own).astype(BF16)

    g_taps, g_heads, g_skip = (sum(b[k] for b in heads_out) for k in range(3))
    g_gain = sum(g[2] for g in gates)
    skip_heads = jnp.sum(g_skip[0].reshape(heads, head_width), axis=1)
    small = jnp.concatenate(
        [g_taps[0:5, 0:inner].reshape(-1), g_gain[0], g_heads[0, 0:heads], g_heads[1, 0:heads], skip_heads]
    )
    size = small.shape[0]
    packed = jnp.concatenate([small, g_taps[0:5, inner:width].reshape(-1)])
    packed = hold(packed, norm_sums[-1][1])
    for axis in ("x", "y", "zp"):
        packed = sum_axis(packed, axis)
    small = packed[:size]
    bc_rows = sum_axis(sum_axis(packed[size:], "core"), "zq").reshape(5, states2)
    channel = own_of_slice(small[0 : 6 * inner].reshape(6, inner))
    per_head = own_of_slice(small[6 * inner :].reshape(3, heads))
    for axis in ("core", "zq", "x", "y", "zp"):
        g_norm_gain = sum_axis(g_norm_gain, axis)
    return (
        outputs,
        jnp.stack(g_hidden),
        g_norm_gain,
        g_second[:, 0:share],
        g_first[:, 0:share],
        g_bc,
        g_first[:, share + states2 : share + states2 + own_heads],
        channel[0:4],
        channel[4],
        bc_rows[0:4],
        bc_rows[4],
        per_head[0],
        per_head[1],
        per_head[2],
        channel[5],
        jnp.transpose(g_second[:, share : 2 * share]),
    )


def solution(mesh):
    dp, seq, tensor = (mesh.shape[name] for name in ("dp", "seq", "tensor"))
    fine = Mesh(
        mesh.devices.reshape(dp // 2, 2, seq, tensor // 2, 2), ("x", "core", "y", "zp", "zq")
    )
    data, tens = ("x", "core", "y"), ("zp", "zq")
    tokens = P(("x", "core"), ("y", "zp", "zq"), None)
    params = (
        P(),
        P(data, tens),
        P(data, tens),
        P(data, None),
        P(data, tens),
        P(None, tens),
        P(tens),
        P(),
        P(),
        P(tens),
        P(tens),
        P(tens),
        P(tens),
        P(tens, data),
    )
    return jax.shard_map(
        per_device,
        mesh=fine,
        in_specs=(tokens, tokens) + params,
        out_specs=(tokens, tokens) + params,
        check_vma=False,
    )
```

time: 1720 us -> 618 us (0.36)
  waiting for transfers between devices: 888 us -> 184 us
  matrix products: 272 us -> 89.3 us
  blocking collectives: 173 us -> 0 us
  other arithmetic: 199 us -> 77.4 us
  Pallas kernels: 0 us -> 115 us
  local copies, waits for them, and re-layouts: 146 us -> 47.8 us
  starting transfers between devices: 12.7 us -> 91.6 us
    reduce_scatter x8 -> x0, waiting for transfers between devices: 599 us -> none  [the longest x2 223 us: per_device(): lax.psum_scatter(jnp.einsum('tgf,fd->tgd', mixed, full_out, preferred_ele...]
    dot_general x66 -> x12, matrix products: 272 us -> 89.3 us  [matmul(): lax.dot_general(left, right, (contract, ((), ())), preferred_element_type...]
    ppermute x4 -> x71, waiting for transfers between devices: 2.38 us -> 184 us  [the longest x47 119 us: swap(): return lax.ppermute(value, axis, [(0, 1), (1, 0)])]
    all_gather x7 -> x0, waiting for transfers between devices: 157 us -> none  [the longest x2 74 us: per_device(): lax.all_gather(normed_own, 'tensor', axis=0, tiled=True)]
    psum x1 -> x0, waiting for transfers between devices: 126 us -> none  [per_device(): lax.psum((spread_part(acc_gain_out, inner_full, tensor_index), spread_par...]
    pallas_call x0 -> x10, Pallas kernels: none -> 115 us  [the longest x8 103 us: run(): pl.pallas_call(body, grid=grid, in_specs=[spec for _, spec in ins] + [pl....]
    psum x3 -> x0, blocking collectives: 86.1 us -> none  [the longest x1 65.5 us: per_device(): lax.psum(jnp.concatenate([grad_b, grad_c + grad_c_inject], axis=-1), 'ten...]
    ppermute x4 -> x71, starting transfers between devices: 11.2 us -> 91.6 us  [the longest x47 40.4 us: swap(): return lax.ppermute(value, axis, [(0, 1), (1, 0)])]
  transfers between devices with their start and end apart: 21 -> 71, of which waited for: 16 -> 24; matrix products, arithmetic and copies ran while one was open for 18% -> 30% of each run, Pallas kernels for 0% -> 16%
where the time goes in v1:
time: 618 us; the launch traced here: 608 us
  waiting for transfers between devices  184 us (30%)
  Pallas kernels  115 us (19%)
  starting transfers between devices  91.6 us (15%)
  matrix products  89.3 us (14%)
  other arithmetic  77.4 us (13%)
  local copies, waits for them, and re-layouts  47.8 us (8%)
    ppermute x47, waiting for transfers between devices, swap(): return lax.ppermute(value, axis, [(0, 1), (1, 0)])  119 us
    pallas_call x8, Pallas kernels, run(): pl.pallas_call(body, grid=grid, in_specs=[spec for _, spec in ins] + [pl....  103 us
    dot_general x12, matrix products, matmul(): lax.dot_general(left, right, (contract, ((), ())), preferred_element_type...  89.3 us
    ppermute x4, waiting for transfers between devices, within_row(): got = lax.ppermute(packed, 'zp', pairs).astype(F32)  41.4 us
    ppermute x47, starting transfers between devices, swap(): return lax.ppermute(value, axis, [(0, 1), (1, 0)])  40.4 us
    select_n x5, other arithmetic, ordered_pair(): jnp.where(low, jnp.concatenate([own, other]), jnp.concatenate([other, own]))  13.9 us
    ppermute x2, starting transfers between devices, fetch(): lax.ppermute(piece, ('core', 'zp'), NEAR)  12.9 us
  transfers between devices with their start and end apart: 71, of which 24 were waited for; matrix products, arithmetic and copies ran while one was open for 30% of the time, Pallas kernels for 16%

profile of v1, /device:TPU:0, one launch (start us, length us, event | category | flops | bytes accessed | tf_op | source)
XLA Modules:
  0.0 607.5 jit_solution(11808344978931273344)
XLA Ops:
  3.5 4.0 collective-permute-start.1
  18.2 2.6 fusion.74
  31.6 8.8 %collective-permute-start.15 = (bf16[192,1536]{1,0:T(8,128)(2,1)}, bf16[192,1536]{1,0:T(8,128)(2,1)S(1)}, u32[]{:S(2)}, u32[]{:S(2)}) collective-permute-start(bf16[192,1536]{1,0:T(8,128)(2,1)} %pad_maximum_fusion.21), channel_id=1, source_target_pairs={{0,2},{10,8},{2,10},{8,0},{1,3},{11,9},{3,11},{9,1},{4,6},{14,12},... | collective-permute-start | bytes 1769480 | tf_op jit(solution)/shard_map/ppermute | solution.py:708
  43.7 27.9 %collective-permute-done = bf16[256,1536]{1,0:T(8,128)(2,1)} collective-permute-done((bf16[256,1536]{1,0:T(8,128)(2,1)}, bf16[256,1536]{1,0:T(8,128)(2,1)}, u32[]{:S(2)}, u32[]{:S(2)}) %collective-permute-start) | collective-permute-done | bytes 786464 | tf_op jit(solution)/shard_map/ppermute | solution.py:605
  73.2 3.6 maximum_select_fusion.1
  78.3 3.4 maximum_select_fusion.3
  81.7 3.0 maximum_select_fusion.2
  84.7 3.0 maximum_select_fusion
  88.3 4.8 collective-permute-done.6.first_y
  93.1 4.9 collective-permute-done.7.second_x
  99.5 4.1 shard_map.279
  104.4 7.6 %collective-permute-done.17 = bf16[192,1536]{1,0:T(8,128)(2,1)S(1)} collective-permute-done((bf16[192,1536]{1,0:T(8,128)(2,1)S(1)}, bf16[192,1536]{1,0:T(8,128)(2,1)S(1)}, u32[]{:S(2)}, u32[]{:S(2)}) %collective-permute-start.17) | collective-permute-done | bytes 589856 | tf_op jit(solution)/shard_map/ppermute | solution.py:605
  112.0 5.4 collective-permute-done.18
  119.5 4.0 fusion.33
  123.5 5.7 convolution_convert_fusion.1.refs_0_.refs_2_.refs_7_.refs_8_.refs_10_
  129.2 6.5 %convolution_convert_fusion.2.refs_0_.refs_2_.refs_7_.refs_8_.refs_10_ = bf16[2,512,1152]{2,1,0:T(8,128)(2,1)S(1)} fusion(bf16[1536,1152,1]{1,0,2:T(8,128)(2,1)S(1)} %bitcast.239, bf16[1,512,1536]{2,1,0:T(8,128)(2,1)} %bitcast.6, bf16[1,512,1536]{2,1,0:T(8,128)(2,1)S(1)} %copy-done.42), kind=kOutput, calls=%fused_computation.25 | convolution fusion | flops 3626631168 | bytes 9043968 | tf_op jit(solution)/shard_map/dot_general | solution.py:803
  137.0 3.3 fusion.34
  140.4 6.5 %collective-permute-start.21 = (bf16[2,16,1024]{2,1,0:T(8,128)(2,1)S(1)}, bf16[2,16,1024]{2,1,0:T(8,128)(2,1)S(1)}, u32[]{:S(2)}, u32[]{:S(2)}) collective-permute-start(bf16[2,16,1024]{2,1,0:T(8,128)(2,1)S(1)} %slice.396), channel_id=1, source_target_pairs={{0,2},{2,4},{4,6},{1,3},{3,5},{5,7},{8,10},{10,12},{12,14},{9,11},... | collective-permute-start | bytes 196616 | tf_op jit(solution)/shard_map/ppermute | solution.py:637
  146.9 8.9 %shard_map.280 = (bf16[2,512,1024]{2,1,0:T(8,128)(2,1)S(1)}, f32[2,512,128]{2,1,0:T(8,128)S(1)}, f32[2,512,128]{2,1,0:T(8,128)S(1)}, f32[2,128,768]{2,1,0:T(8,128)S(1)}, f32[2,8,128]{2,1,0:T(8,128)S(1)}) custom-call(bf16[2,512,1152]{2,1,0:T(8,128)(2,1)} %copy-done.82, bf16[2,16,1024]{2,1,0:T(8,128)(2,1)S(1)} %collective-permute-done.8.refs_1_.refs_9_, ...), custom_call_target="tpu_custom_call" | custom-call | flops 6000000000 | bytes 8000000 | tf_op jit(solution)/shard_map/pallas_call | solution.py:391
  158.5 3.1 collective-permute-start.10
  161.6 8.9 %shard_map.281 = (bf16[2,512,1024]{2,1,0:T(8,128)(2,1)S(1)}, f32[2,512,128]{2,1,0:T(8,128)S(1)}, f32[2,512,128]{2,1,0:T(8,128)S(1)}, f32[2,128,768]{2,1,0:T(8,128)S(1)}, f32[2,8,128]{2,1,0:T(8,128)S(1)}) custom-call(bf16[2,512,1152]{2,1,0:T(8,128)(2,1)} %copy-done.81, bf16[2,16,1024]{2,1,0:T(8,128)(2,1)S(1)} %collective-permute-done.21.refs_1_.refs_9_, ...), custom_call_target="tpu_custom_call" | custom-call | flops 6000000000 | bytes 8000000 | tf_op jit(solution)/shard_map/pallas_call | solution.py:391
  176.3 3.0 fusion.71
  180.3 7.7 %shard_map.282 = bf16[2,2,2,192,1536]{4,3,2,1,0:T(8,128)(2,1)} custom-call(s32[3]{0:T(128)S(1)} %pad_add_fusion.at_ref, bf16[2,192,1536]{2,1,0:T(8,128)(2,1)S(1)} %pad_maximum_fusion.13.first, bf16[2,192,1536]{2,1,0:T(8,128)(2,1)} %collective-permute-done.19.first_y, bf16[2,192,1536]{2,1,0:T(8,128)(2,1)S(1)} %pad_maximum_fusion.14.second, ...), custom_call_target="tpu_custom_call" | custom-call | bytes 9437184 | tf_op jit(solution)/shard_map/pallas_call | solution.py:583
  188.0 8.2 %fusion.21.refs_4_.refs_2_ = bf16[2,2,512,768]{3,2,1,0:T(8,128)(2,1)} fusion(bf16[1,2,512,1536]{3,2,1,0:T(8,128)(2,1)S(1)} %copy-done.48, bf16[1,2,512,1536]{3,2,1,0:T(8,128)(2,1)S(1)} %copy-done.50, bf16[1536,1536]{1,0:T(8,128)(2,1)} %bitcast.233), kind=kOutput, calls=%fused_computation.46 | convolution fusion | flops 4836556800 | bytes 11796480 | tf_op jit(solution)/shard_map/dot_general | solution.py:803
  208.3 9.2 %fusion.9.refs_5_.refs_3_ = f32[2,2,512,768]{3,2,1,0:T(8,128)} fusion(bf16[1536,768]{1,0:T(8,128)(2,1)} %slice.398, bf16[2,1,512,1536]{3,2,0,1:T(8,128)(2,1)} %bitcast.34, bf16[2,1,512,1536]{3,2,0,1:T(8,128)(2,1)S(1)} %copy-done.54), kind=kOutput, calls=%fused_computation.16 | convolution fusion | flops 4834983936 | bytes 14942208 | tf_op jit(solution)/shard_map/dot_general | solution.py:803
  217.6 9.9 %shard_map.283 = (f32[2,512,768]{2,1,0:T(8,128)}, bf16[2,2,512,768]{3,2,1,0:T(8,128)(2,1)}, bf16[2,2,128,768]{3,2,1,0:T(8,128)(2,1)S(1)}, f32[2,8,512]{2,1,0:T(8,128)S(1)}) custom-call(bf16[2,512,1024]{2,1,0:T(8,128)(2,1)S(1)} %copy-done.13, f32[2,512,128]{2,1,0:T(8,128)S(1)} %copy-done.16, f32[2,512,128]{2,1,0:T(8,128)S(1)} %copy-done.24, ...), custom_call_target="tpu_custom_call" | custom-call | flops 10000000000 | bytes 16000000 | tf_op jit(solution)/shard_map/pallas_call | solution.py:391
  228.5 9.9 %shard_map.284 = (f32[2,512,768]{2,1,0:T(8,128)}, bf16[2,2,512,768]{3,2,1,0:T(8,128)(2,1)}, bf16[2,2,128,768]{3,2,1,0:T(8,128)(2,1)S(1)}, f32[2,8,512]{2,1,0:T(8,128)S(1)}) custom-call(bf16[2,512,1024]{2,1,0:T(8,128)(2,1)S(1)} %copy-done.3, f32[2,512,128]{2,1,0:T(8,128)S(1)} %copy-done.5, ...), custom_call_target="tpu_custom_call", output_to_operand_aliasing={{1}: (8, {})} | custom-call | flops 10000000000 | bytes 16000000 | tf_op jit(solution)/shard_map/pallas_call | solution.py:391
  238.3 7.5 %convolution_convert_fusion = bf16[2,2,512,1536]{3,2,0,1:T(8,128)(2,1)S(1)} fusion(bf16[2,2,512,768]{3,2,1,0:T(8,128)(2,1)} %get-tuple-element.119, bf16[1536,768]{1,0:T(8,128)(2,1)S(1)} %copy-done.56), kind=kOutput, calls=%fused_computation.18 | convolution fusion | flops 4834983936 | bytes 11796480 | tf_op jit(solution)/shard_map/dot_general | solution.py:803
  250.3 5.9 copy.51.refs_8_
  256.8 5.1 collective-permute-done.29
  261.9 7.6 %shard_map.285 = (bf16[2,512,768]{2,1,0:T(8,128)(2,1)S(1)}, bf16[2,2,512,768]{3,2,1,0:T(8,128)(2,1)}, bf16[2,2,512,768]{3,2,1,0:T(8,128)(2,1)}, f32[2,128,768]{2,1,0:T(8,128)S(1)}, f32[8,768]{1,0:T(8,128)S(1)}) custom-call(f32[2,512,768]{2,1,0:T(8,128)} %get-tuple-element.121.refs_0_.refs_4_, bf16[2,512,1024]{2,1,0:T(8,128)(2,1)S(1)} %copy-done.13, ...), custom_call_target="tpu_custom_call" | custom-call | flops 6000000000 | bytes 18000000 | tf_op jit(solution)/shard_map/pallas_call | solution.py:391
  272.1 7.7 %shard_map.286 = (bf16[2,512,768]{2,1,0:T(8,128)(2,1)S(1)}, bf16[2,2,512,768]{3,2,1,0:T(8,128)(2,1)}, bf16[2,2,512,768]{3,2,1,0:T(8,128)(2,1)}, f32[2,128,768]{2,1,0:T(8,128)S(1)}, f32[8,768]{1,0:T(8,128)S(1)}) custom-call(f32[2,512,768]{2,1,0:T(8,128)} %get-tuple-element.120.refs_0_.refs_4_, ...), custom_call_target="tpu_custom_call", output_to_operand_aliasing={{1}: (10, {}), {2}: (11, {})} | custom-call | flops 6000000000 | bytes 18000000 | tf_op jit(solution)/shard_map/pallas_call | solution.py:391
  281.5 7.9 %bitcast_convert_fusion.1 = bf16[1536,768]{0,1:T(8,128)(2,1)S(1)} fusion(bf16[2,2,512,768]{3,2,1,0:T(8,128)(2,1)} %get-tuple-element.132, bf16[2,1,512,1536]{3,2,0,1:T(8,128)(2,1)} %bitcast.34, bf16[2,1,512,1536]{3,2,0,1:T(8,128)(2,1)S(1)} %copy-done.55), kind=kOutput, calls=%fused_computation.21 | convolution fusion | flops 4836163584 | bytes 11796480 | tf_op jit(solution)/shard_map/dot_general | solution.py:803
  289.5 5.4 bitcast_convert_fusion
  294.9 2.5 pad_maximum_fusion.2
  297.5 41.4 %collective-permute-done.33 = bf16[2,144,768]{2,1,0:T(8,128)(2,1)S(1)} collective-permute-done((bf16[2,144,768]{2,1,0:T(8,128)(2,1)S(1)}, bf16[2,144,768]{2,1,0:T(8,128)(2,1)S(1)}, u32[]{:S(2)}, u32[]{:S(2)}) %collective-permute-start.33) | collective-permute-done | bytes 442400 | tf_op jit(solution)/shard_map/ppermute | solution.py:666
  344.1 8.2 %fusion.22.refs_16_ = f32[2,2,512,1536]{3,2,1,0:T(8,128)} fusion(bf16[2,2,512,768]{3,2,1,0:T(8,128)(2,1)S(1)} %copy-done.47, bf16[1536,1536]{1,0:T(8,128)(2,1)S(1)} %bitcast.237), kind=kOutput, calls=%fused_computation.47 | convolution fusion | flops 4831838208 | bytes 18087936 | tf_op jit(solution)/shard_map/dot_general | solution.py:803
  352.6 11.7 %collective-permute-done.37 = bf16[2,128,768]{2,1,0:T(8,128)(2,1)} collective-permute-done((bf16[2,128,768]{2,1,0:T(8,128)(2,1)S(1)}, bf16[2,128,768]{2,1,0:T(8,128)(2,1)}, u32[]{:S(2)}, u32[]{:S(2)}) %collective-permute-start.37) | collective-permute-done | bytes 393248 | tf_op jit(solution)/shard_map/ppermute | solution.py:688
  365.8 6.7 %copy.55 = bf16[1536,1536]{1,0:T(8,128)(2,1)} copy(bf16[1536,1536]{0,1:T(8,128)(2,1)} %pad_maximum_fusion.2) | data formatting | bytes 9437184 | tf_op jit(solution)/shard_map/optimization_barrier | solution.py:631
  378.1 3.7 fusion.6
  384.6 25.4 %shard_map.287 = (bf16[2,512,1152]{2,1,0:T(8,128)(2,1)}, f32[2,8,1024]{2,1,0:T(8,128)S(1)}, f32[8,1024]{1,0:T(8,128)S(1)}, f32[8,128]{1,0:T(8,128)S(1)}, f32[8,768]{1,0:T(8,128)S(1)}) custom-call(bf16[2,512,1024]{2,1,0:T(8,128)(2,1)} %copy-done.12, f32[2,512,128]{2,1,0:T(8,128)S(1)} %copy-done.17, f32[2,512,128]{2,1,0:T(8,128)S(1)} %copy-done.25, ...), custom_call_target="tpu_custom_call" | custom-call | flops 32000000000 | bytes 24000000 | tf_op jit(solution)/shard_map/pallas_call | solution.py:391
  411.9 2.2 fusion.18
  414.2 3.4 collective-permute-done.39
  417.7 6.4 %fusion.5 = bf16[2,512,1536]{2,1,0:T(8,128)(2,1)S(1)} fusion(f32[2,2,512,1536]{3,2,1,0:T(8,128)} %fusion.22.refs_16_, bf16[2,512,1152]{2,1,0:T(8,128)(2,1)S(1)} %fusion.43, bf16[1536,1152,1]{1,0,2:T(8,128)(2,1)S(1)} %bitcast.240), kind=kOutput, calls=%fused_computation.9 | convolution fusion | flops 3627024384 | bytes 15335424 | tf_op jit(solution)/shard_map/dot_general | solution.py:803
  427.1 8.6 %convolution_bitcast_fusion.1.refs_15_ = f32[1536,1152]{1,0:T(8,128)} fusion(bf16[2,512,1152]{2,1,0:T(8,128)(2,1)S(1)} %fusion.43, bf16[1,512,1536]{2,1,0:T(8,128)(2,1)} %bitcast.6, bf16[1,512,1536]{2,1,0:T(8,128)(2,1)S(1)} %copy-done.43), kind=kOutput, calls=%fused_computation.2 | convolution fusion | flops 3625451520 | bytes 12582912 | tf_op jit(solution)/shard_map/dot_general | solution.py:803
  435.7 4.8 collective-permute-done.43
  446.1 24.8 %shard_map.288 = (bf16[2,512,1152]{2,1,0:T(8,128)(2,1)}, f32[2,8,1024]{2,1,0:T(8,128)S(1)}, f32[8,1024]{1,0:T(8,128)S(1)}, f32[8,128]{1,0:T(8,128)S(1)}, f32[8,768]{1,0:T(8,128)S(1)}) custom-call(bf16[2,512,1024]{2,1,0:T(8,128)(2,1)} %copy-done.2, f32[2,512,128]{2,1,0:T(8,128)S(1)} %copy-done.6, f32[2,512,128]{2,1,0:T(8,128)S(1)} %copy-done.22, ...), custom_call_target="tpu_custom_call" | custom-call | flops 32000000000 | bytes 24000000 | tf_op jit(solution)/shard_map/pallas_call | solution.py:391
  472.7 7.9 %collective-permute-done.46 = f32[2,8,1024]{2,1,0:T(8,128)S(1)} collective-permute-done((f32[2,8,1024]{2,1,0:T(8,128)S(1)}, f32[2,8,1024]{2,1,0:T(8,128)S(1)}, u32[]{:S(2)}, u32[]{:S(2)}) %collective-permute-start.46) | collective-permute-done | bytes 65568 | tf_op jit(solution)/shard_map/ppermute | solution.py:637
  482.3 9.1 %fusion.1 = bf16[1536,1152]{1,0:T(8,128)(2,1)S(1)} fusion(f32[1536,1152]{1,0:T(8,128)} %convolution_bitcast_fusion.1.refs_15_, bf16[2,512,1152]{2,1,0:T(8,128)(2,1)} %fusion.44, bf16[1,512,1536]{2,1,0:T(8,128)(2,1)} %bitcast.22, bf16[1,512,1536]{2,1,0:T(8,128)(2,1)} %maximum_select_fusion.2), kind=kOutput, calls=%fused_computation.3 | convolution fusion | flops 3628990464 | bytes 16121856 | tf_op jit(solution)/shard_map/dot_general | solution.py:803
  493.4 6.5 %fusion.3 = bf16[2,512,1536]{2,1,0:T(8,128)(2,1)S(1)} fusion(f32[2,2,512,1536]{3,2,1,0:T(8,128)} %fusion.22.refs_16_, bf16[2,512,1152]{2,1,0:T(8,128)(2,1)S(1)} %copy-done.76, bf16[1536,1152,1]{1,0,2:T(8,128)(2,1)S(1)} %bitcast.241), kind=kOutput, calls=%fused_computation.6 | convolution fusion | flops 3627024384 | bytes 15335424 | tf_op jit(solution)/shard_map/dot_general | solution.py:803
  501.3 3.2 add_convert_fusion
  504.6 2.4 collective-permute-start.45
  507.0 6.3 %collective-permute-done.56 = bf16[2,192,1152]{2,1,0:T(8,128)(2,1)S(1)} collective-permute-done((bf16[2,192,1152]{2,1,0:T(8,128)(2,1)S(1)}, bf16[2,192,1152]{2,1,0:T(8,128)(2,1)S(1)}, u32[]{:S(2)}, u32[]{:S(2)}) %collective-permute-start.56) | collective-permute-done | bytes 884768 | tf_op jit(solution)/shard_map/ppermute | solution.py:605
  520.7 7.2 %collective-permute-done.64 = f32[5924]{0:T(1024)S(1)} collective-permute-done((f32[5924]{0:T(1024)S(1)}, f32[5924]{0:T(1024)S(1)}, u32[]{:S(2)}, u32[]{:S(2)}) %collective-permute-start.64) | collective-permute-done | bytes 23728 | tf_op jit(solution)/shard_map/ppermute | solution.py:605
  533.6 4.5 collective-permute-start.60
  538.1 3.2 collective-permute-start.48
  544.6 21.7 %collective-permute-done.69 = f32[1280]{0:T(1024)S(1)} collective-permute-done((f32[1280]{0:T(1024)S(1)}, f32[1280]{0:T(1024)S(1)}, u32[]{:S(2)}, u32[]{:S(2)}) %collective-permute-start.69) | collective-permute-done | bytes 5152 | tf_op jit(solution)/shard_map/ppermute | solution.py:605
  568.8 3.1 collective-permute-start.62
  571.9 9.8 %collective-permute-done.62 = f32[192,256]{1,0:T(8,128)S(1)} collective-permute-done((f32[192,256]{1,0:T(8,128)S(1)}, f32[192,256]{1,0:T(8,128)S(1)}, u32[]{:S(2)}, u32[]{:S(2)}) %collective-permute-start.62) | collective-permute-done | bytes 196640 | tf_op jit(solution)/shard_map/ppermute | solution.py:605
  582.6 3.1 multiply_reduce_fusion.2
  591.5 2.4 collective-permute-done.50
  594.5 3.1 collective-permute-done.51
  598.6 3.0 fusion.28
  601.6 3.2 collective-permute-start.53
  (480 shorter events, 129.9 us)
Async XLA Ops:
  3.5 17.4 %collective-permute-start.1 = (bf16[192,1152]{1,0:T(8,128)(2,1)}, bf16[192,1152]{1,0:T(8,128)(2,1)}, u32[]{:S(2)}, u32[]{:S(2)}) collective-permute-start(bf16[192,1152]{1,0:T(8,128)(2,1)} %concatenate.147), channel_id=1, source_target_pairs={{0,2},{10,8},{2,10},{8,0},{1,3},{11,9},{3,11},{9,1},{4,6},{14,12},... | collective-permute-start | bytes 1327112 | tf_op jit(solution)/shard_map/ppermute | solution.py:708
  7.5 13.4 %collective-permute-start.3 = (bf16[192,1152]{1,0:T(8,128)(2,1)}, bf16[192,1152]{1,0:T(8,128)(2,1)}, u32[]{:S(2)}, u32[]{:S(2)}) collective-permute-start(bf16[192,1152]{1,0:T(8,128)(2,1)} %concatenate.147), channel_id=1, source_target_pairs={{2,8},{8,2},{3,9},{9,3},{6,12},{12,6},{7,13},{13,7},{18,24},{24,18... | collective-permute-start | bytes 1327112 | tf_op jit(solution)/shard_map/ppermute | solution.py:708
  13.3 63.5 %collective-permute-start.13 = (bf16[256,1536]{1,0:T(8,128)(2,1)}, bf16[256,1536]{1,0:T(8,128)(2,1)}, u32[]{:S(2)}, u32[]{:S(2)}) collective-permute-start(bf16[256,1536]{1,0:T(8,128)(2,1)} %get-tuple-element.220), channel_id=1, source_target_pairs={{0,1},{1,0},{2,3},{3,2},{4,5},{5,4},{6,7},{7,6},{8,9},{9,8},{10,11... | collective-permute-start | bytes 2359304 | tf_op jit(solution)/shard_map/ppermute | solution.py:605
  14.9 56.7 %collective-permute-start = (bf16[256,1536]{1,0:T(8,128)(2,1)}, bf16[256,1536]{1,0:T(8,128)(2,1)}, u32[]{:S(2)}, u32[]{:S(2)}) collective-permute-start(bf16[256,1536]{1,0:T(8,128)(2,1)} %get-tuple-element.219), channel_id=1, source_target_pairs={{0,1},{1,0},{2,3},{3,2},{4,5},{5,4},{6,7},{7,6},{8,9},{9,8},{10,11... | collective-permute-start | bytes 2359304 | tf_op jit(solution)/shard_map/ppermute | solution.py:605
  15.7 88.0 %collective-permute-start.9 = (f32[8,768]{1,0:T(8,128)S(1)}, f32[8,768]{1,0:T(8,128)S(1)}, u32[]{:S(2)}, u32[]{:S(2)}) collective-permute-start(f32[8,768]{1,0:T(8,128)S(1)} %maximum_maximum_fusion), channel_id=1, source_target_pairs={{0,2},{2,0},{1,3},{3,1},{4,6},{6,4},{5,7},{7,5},{8,10},{10,8},{9,1... | collective-permute-start | bytes 73736 | tf_op jit(solution)/shard_map/ppermute | solution.py:605
  23.0 8.6 %collective-permute-start.2 = (bf16[192,1152]{1,0:T(8,128)(2,1)}, bf16[192,1152]{1,0:T(8,128)(2,1)}, u32[]{:S(2)}, u32[]{:S(2)}) collective-permute-start(bf16[192,1152]{1,0:T(8,128)(2,1)} %get-tuple-element.227), channel_id=1, source_target_pairs={{0,16},{16,0},{1,17},{17,1},{2,18},{18,2},{3,19},{19,3},{4,20},{20... | collective-permute-start | bytes 1327112 | tf_op jit(solution)/shard_map/ppermute | solution.py:605
  27.3 14.4 %collective-permute-start.4 = (bf16[192,1152]{1,0:T(8,128)(2,1)}, bf16[192,1152]{1,0:T(8,128)(2,1)S(1)}, u32[]{:S(2)}, u32[]{:S(2)}) collective-permute-start(bf16[192,1152]{1,0:T(8,128)(2,1)} %get-tuple-element.226), channel_id=1, source_target_pairs={{0,4},{4,0},{1,5},{5,1},{2,6},{6,2},{3,7},{7,3},{8,12},{12,8},{9,1... | collective-permute-start | bytes 1327112 | tf_op jit(solution)/shard_map/ppermute | solution.py:605
  31.6 56.1 %collective-permute-start.15 = (bf16[192,1536]{1,0:T(8,128)(2,1)}, bf16[192,1536]{1,0:T(8,128)(2,1)S(1)}, u32[]{:S(2)}, u32[]{:S(2)}) collective-permute-start(bf16[192,1536]{1,0:T(8,128)(2,1)} %pad_maximum_fusion.21), channel_id=1, source_target_pairs={{0,2},{10,8},{2,10},{8,0},{1,3},{11,9},{3,11},{9,1},{4,6},{14,12},... | collective-permute-start | bytes 1769480 | tf_op jit(solution)/shard_map/ppermute | solution.py:708
  41.7 46.0 %collective-permute-start.16 = (bf16[192,1536]{1,0:T(8,128)(2,1)}, bf16[192,1536]{1,0:T(8,128)(2,1)S(1)}, u32[]{:S(2)}, u32[]{:S(2)}) collective-permute-start(bf16[192,1536]{1,0:T(8,128)(2,1)} %pad_maximum_fusion.21), channel_id=1, source_target_pairs={{2,8},{8,2},{3,9},{9,3},{6,12},{12,6},{7,13},{13,7},{18,24},{24,18... | collective-permute-start | bytes 1769480 | tf_op jit(solution)/shard_map/ppermute | solution.py:708
  71.6 21.5 %collective-permute-start.6 = (bf16[2,192,1152]{2,1,0:T(8,128)(2,1)S(1)}, bf16[2,192,1152]{2,1,0:T(8,128)(2,1)S(1)}, u32[]{:S(2)}, u32[]{:S(2)}) collective-permute-start(bf16[2,192,1152]{2,1,0:T(8,128)(2,1)S(1)} %pad_maximum_fusion.19.first), channel_id=1, source_target_pairs={{0,4},{4,0},{1,5},{5,1},{2,6},{6,2},{3,7},{7,3},{8,12},{12,8},{9,1... | collective-permute-start | bytes 2654216 | tf_op jit(solution)/shard_map/ppermute | solution.py:605
  76.8 21.2 %collective-permute-start.7 = (bf16[2,192,1152]{2,1,0:T(8,128)(2,1)S(1)}, bf16[2,192,1152]{2,1,0:T(8,128)(2,1)S(1)}, u32[]{:S(2)}, u32[]{:S(2)}) collective-permute-start(bf16[2,192,1152]{2,1,0:T(8,128)(2,1)S(1)} %pad_maximum_fusion.20.second), channel_id=1, source_target_pairs={{0,16},{16,0},{1,17},{17,1},{2,18},{18,2},{3,19},{19,3},{4,20},{20... | collective-permute-start | bytes 2654216 | tf_op jit(solution)/shard_map/ppermute | solution.py:605
  87.7 31.7 %collective-permute-start.14 = (bf16[512,1536]{1,0:T(8,128)(2,1)}, bf16[512,1536]{1,0:T(8,128)(2,1)}, u32[]{:S(2)}, u32[]{:S(2)}) collective-permute-start(bf16[512,1536]{1,0:T(8,128)(2,1)} %maximum_select_fusion.3), channel_id=1, source_target_pairs={{0,8},{8,0},{1,9},{9,1},{2,10},{10,2},{3,11},{11,3},{4,12},{12,4},... | collective-permute-start | bytes 4718600 | tf_op jit(solution)/shard_map/ppermute | solution.py:605
  87.7 41.5 %collective-permute-start.5 = (bf16[512,1536]{1,0:T(8,128)(2,1)}, bf16[512,1536]{1,0:T(8,128)(2,1)}, u32[]{:S(2)}, u32[]{:S(2)}) collective-permute-start(bf16[512,1536]{1,0:T(8,128)(2,1)} %maximum_select_fusion.1), channel_id=1, source_target_pairs={{0,8},{8,0},{1,9},{9,1},{2,10},{10,2},{3,11},{11,3},{4,12},{12,4},... | collective-permute-start | bytes 4718600 | tf_op jit(solution)/shard_map/ppermute | solution.py:605
  93.1 80.7 %collective-permute-start.22 = (bf16[2,256,1536]{2,1,0:T(8,128)(2,1)}, bf16[2,256,1536]{2,1,0:T(8,128)(2,1)}, u32[]{:S(2)}, u32[]{:S(2)}) collective-permute-start(bf16[2,256,1536]{2,1,0:T(8,128)(2,1)} %param.17), channel_id=1, source_target_pairs={{0,1},{1,0},{2,3},{3,2},{4,5},{5,4},{6,7},{7,6},{8,9},{9,8},{10,11... | collective-permute-start | bytes 4718600 | tf_op jit(solution)/shard_map/ppermute | solution.py:605
  98.0 14.0 %collective-permute-start.17 = (bf16[192,1536]{1,0:T(8,128)(2,1)S(1)}, bf16[192,1536]{1,0:T(8,128)(2,1)S(1)}, u32[]{:S(2)}, u32[]{:S(2)}) collective-permute-start(bf16[192,1536]{1,0:T(8,128)(2,1)S(1)} %get-tuple-element.99), channel_id=1, source_target_pairs={{0,16},{16,0},{1,17},{17,1},{2,18},{18,2},{3,19},{19,3},{4,20},{20... | collective-permute-start | bytes 1769480 | tf_op jit(solution)/shard_map/ppermute | solution.py:605
  103.6 13.7 %collective-permute-start.18 = (bf16[192,1536]{1,0:T(8,128)(2,1)S(1)}, bf16[192,1536]{1,0:T(8,128)(2,1)S(1)}, u32[]{:S(2)}, u32[]{:S(2)}) collective-permute-start(bf16[192,1536]{1,0:T(8,128)(2,1)S(1)} %get-tuple-element.101), channel_id=1, source_target_pairs={{0,4},{4,0},{1,5},{5,1},{2,6},{6,2},{3,7},{7,3},{8,12},{12,8},{9,1... | collective-permute-start | bytes 1769480 | tf_op jit(solution)/shard_map/ppermute | solution.py:605
  117.5 62.8 %collective-permute-start.19 = (bf16[2,192,1536]{2,1,0:T(8,128)(2,1)S(1)}, bf16[2,192,1536]{2,1,0:T(8,128)(2,1)}, u32[]{:S(2)}, u32[]{:S(2)}) collective-permute-start(bf16[2,192,1536]{2,1,0:T(8,128)(2,1)S(1)} %pad_maximum_fusion.13.first), channel_id=1, source_target_pairs={{0,4},{4,0},{1,5},{5,1},{2,6},{6,2},{3,7},{7,3},{8,12},{12,8},{9,1... | collective-permute-start | bytes 3538952 | tf_op jit(solution)/shard_map/ppermute | solution.py:605
  118.1 62.1 %collective-permute-start.20 = (bf16[2,192,1536]{2,1,0:T(8,128)(2,1)S(1)}, bf16[2,192,1536]{2,1,0:T(8,128)(2,1)}, u32[]{:S(2)}, u32[]{:S(2)}) collective-permute-start(bf16[2,192,1536]{2,1,0:T(8,128)(2,1)S(1)} %pad_maximum_fusion.14.second), channel_id=1, source_target_pairs={{0,16},{16,0},{1,17},{17,1},{2,18},{18,2},{3,19},{19,3},{4,20},{20... | collective-permute-start | bytes 3538952 | tf_op jit(solution)/shard_map/ppermute | solution.py:605
  135.7 11.2 %collective-permute-start.8 = (bf16[2,16,1024]{2,1,0:T(8,128)(2,1)S(1)}, bf16[2,16,1024]{2,1,0:T(8,128)(2,1)S(1)}, u32[]{:S(2)}, u32[]{:S(2)}) collective-permute-start(bf16[2,16,1024]{2,1,0:T(8,128)(2,1)S(1)} %slice.389), channel_id=1, source_target_pairs={{0,2},{2,4},{4,6},{1,3},{3,5},{5,7},{8,10},{10,12},{12,14},{9,11},... | collective-permute-start | bytes 196616 | tf_op jit(solution)/shard_map/ppermute | solution.py:637
  140.4 21.2 %collective-permute-start.21 = (bf16[2,16,1024]{2,1,0:T(8,128)(2,1)S(1)}, bf16[2,16,1024]{2,1,0:T(8,128)(2,1)S(1)}, u32[]{:S(2)}, u32[]{:S(2)}) collective-permute-start(bf16[2,16,1024]{2,1,0:T(8,128)(2,1)S(1)} %slice.396), channel_id=1, source_target_pairs={{0,2},{2,4},{4,6},{1,3},{3,5},{5,7},{8,10},{10,12},{12,14},{9,11},... | collective-permute-start | bytes 196616 | tf_op jit(solution)/shard_map/ppermute | solution.py:637
  158.5 42.7 %collective-permute-start.10 = (bf16[2,144,768]{2,1,0:T(8,128)(2,1)}, bf16[2,144,768]{2,1,0:T(8,128)(2,1)}, u32[]{:S(2)}, u32[]{:S(2)}) collective-permute-start(bf16[2,144,768]{2,1,0:T(8,128)(2,1)} %pad_maximum_fusion.23.refs_6_), channel_id=1, source_target_pairs={{0,2},{1,3},{4,6},{5,7},{8,10},{9,11},{12,14},{13,15},{16,18},{17,... | collective-permute-start | bytes 1327112 | tf_op jit(solution)/shard_map/ppermute | solution.py:666
  171.6 26.3 %collective-permute-start.24 = (bf16[2,144,768]{2,1,0:T(8,128)(2,1)}, bf16[2,144,768]{2,1,0:T(8,128)(2,1)}, u32[]{:S(2)}, u32[]{:S(2)}) collective-permute-start(bf16[2,144,768]{2,1,0:T(8,128)(2,1)} %pad_maximum_fusion.25), channel_id=1, source_target_pairs={{0,2},{1,3},{4,6},{5,7},{8,10},{9,11},{12,14},{13,15},{16,18},{17,... | collective-permute-start | bytes 1327112 | tf_op jit(solution)/shard_map/ppermute | solution.py:666
  179.3 29.0 %collective-permute-start.23 = (bf16[2,512,1536]{2,1,0:T(8,128)(2,1)}, bf16[2,512,1536]{2,1,0:T(8,128)(2,1)}, u32[]{:S(2)}, u32[]{:S(2)}) collective-permute-start(bf16[2,512,1536]{2,1,0:T(8,128)(2,1)} %get-tuple-element.213), channel_id=1, source_target_pairs={{0,8},{8,0},{1,9},{9,1},{2,10},{10,2},{3,11},{11,3},{4,12},{12,4},... | collective-permute-start | bytes 9437192 | tf_op jit(solution)/shard_map/ppermute | solution.py:605
  199.1 6.5 %collective-permute-start.28 = (bf16[2,128,768]{2,1,0:T(8,128)(2,1)S(1)}, bf16[2,128,768]{2,1,0:T(8,128)(2,1)S(1)}, u32[]{:S(2)}, u32[]{:S(2)}) collective-permute-start(bf16[2,128,768]{2,1,0:T(8,128)(2,1)S(1)} %add_convert_fusion.4.refs_8_), channel_id=1, source_target_pairs={{2,6},{3,7},{10,14},{11,15},{18,22},{19,23},{26,30},{27,31}} | collective-permute-start | bytes 1179656 | tf_op jit(solution)/shard_map/ppermute | solution.py:688
  199.8 5.9 collective-permute-start.27
  202.4 4.6 collective-permute-start.12
  245.9 10.8 %collective-permute-start.25 = (f32[2,8,512]{2,1,0:T(8,128)S(1)}, f32[2,8,512]{2,1,0:T(8,128)S(1)}, u32[]{:S(2)}, u32[]{:S(2)}) collective-permute-start(f32[2,8,512]{2,1,0:T(8,128)S(1)} %get-tuple-element.113), channel_id=1, source_target_pairs={{0,8},{8,0},{1,9},{9,1},{2,10},{10,2},{3,11},{11,3},{4,12},{12,4},... | collective-permute-start | bytes 98312 | tf_op jit(solution)/shard_map/ppermute | solution.py:605
  256.2 121.9 %collective-permute-start.31 = (bf16[2,512,1536]{2,1,0:T(8,128)(2,1)}, bf16[2,512,1536]{2,1,0:T(8,128)(2,1)}, u32[]{:S(2)}, u32[]{:S(2)}) collective-permute-start(bf16[2,512,1536]{2,1,0:T(8,128)(2,1)} %slice_bitcast_fusion.2), channel_id=1, source_target_pairs={{0,8},{8,0},{1,9},{9,1},{2,10},{10,2},{3,11},{11,3},{4,12},{12,4},... | collective-permute-start | bytes 9437192 | tf_op jit(solution)/shard_map/ppermute | solution.py:605
  256.7 5.2 collective-permute-start.29
  256.7 5.2 collective-permute-start.26
  261.9 10.2 %collective-permute-start.30 = (f32[2,8,512]{2,1,0:T(8,128)S(1)}, f32[2,8,512]{2,1,0:T(8,128)S(1)}, u32[]{:S(2)}, u32[]{:S(2)}) collective-permute-start(f32[2,8,512]{2,1,0:T(8,128)S(1)} %reverse_add_fusion), channel_id=1, source_target_pairs={{0,1},{1,0},{2,3},{3,2},{4,5},{5,4},{6,7},{7,6},{8,9},{9,8},{10,11... | collective-permute-start | bytes 98312 | tf_op jit(solution)/shard_map/ppermute | solution.py:605
  270.8 70.3 %collective-permute-start.36 = (bf16[2,144,768]{2,1,0:T(8,128)(2,1)S(1)}, bf16[2,144,768]{2,1,0:T(8,128)(2,1)S(1)}, u32[]{:S(2)}, u32[]{:S(2)}) collective-permute-start(bf16[2,144,768]{2,1,0:T(8,128)(2,1)S(1)} %pad_maximum_fusion.22.refs_9_), channel_id=1, source_target_pairs={{2,0},{3,1},{6,4},{7,5},{10,8},{11,9},{14,12},{15,13},{18,16},{19,... | collective-permute-start | bytes 1327112 | tf_op jit(solution)/shard_map/ppermute | solution.py:666
  280.0 58.9 %collective-permute-start.33 = (bf16[2,144,768]{2,1,0:T(8,128)(2,1)S(1)}, bf16[2,144,768]{2,1,0:T(8,128)(2,1)S(1)}, u32[]{:S(2)}, u32[]{:S(2)}) collective-permute-start(bf16[2,144,768]{2,1,0:T(8,128)(2,1)S(1)} %pad_maximum_fusion.24), channel_id=1, source_target_pairs={{2,0},{3,1},{6,4},{7,5},{10,8},{11,9},{14,12},{15,13},{18,16},{19,... | collective-permute-start | bytes 1327112 | tf_op jit(solution)/shard_map/ppermute | solution.py:666
  339.1 37.8 %collective-permute-start.35 = (bf16[2,128,768]{2,1,0:T(8,128)(2,1)S(1)}, bf16[2,128,768]{2,1,0:T(8,128)(2,1)S(1)}, u32[]{:S(2)}, u32[]{:S(2)}) collective-permute-start(bf16[2,128,768]{2,1,0:T(8,128)(2,1)S(1)} %add_convert_fusion.3.refs_17_), channel_id=1, source_target_pairs={{4,2},{5,3},{12,10},{13,11},{20,18},{21,19},{28,26},{29,27}} | collective-permute-start | bytes 1179656 | tf_op jit(solution)/shard_map/ppermute | solution.py:688
  339.8 37.1 %collective-permute-start.34 = (bf16[2,128,768]{2,1,0:T(8,128)(2,1)S(1)}, bf16[2,128,768]{2,1,0:T(8,128)(2,1)}, u32[]{:S(2)}, u32[]{:S(2)}) collective-permute-start(bf16[2,128,768]{2,1,0:T(8,128)(2,1)S(1)} %add_convert_fusion.3.refs_17_), channel_id=1, source_target_pairs={{4,0},{5,1},{12,8},{13,9},{20,16},{21,17},{28,24},{29,25}} | collective-permute-start | bytes 1179656 | tf_op jit(solution)/shard_map/ppermute | solution.py:688
  341.3 11.3 %collective-permute-start.38 = (bf16[2,128,768]{2,1,0:T(8,128)(2,1)S(1)}, bf16[2,128,768]{2,1,0:T(8,128)(2,1)}, u32[]{:S(2)}, u32[]{:S(2)}) collective-permute-start(bf16[2,128,768]{2,1,0:T(8,128)(2,1)S(1)} %add_convert_fusion.2), channel_id=1, source_target_pairs={{4,2},{5,3},{12,10},{13,11},{20,18},{21,19},{28,26},{29,27}} | collective-permute-start | bytes 1179656 | tf_op jit(solution)/shard_map/ppermute | solution.py:688
  342.7 21.6 %collective-permute-start.37 = (bf16[2,128,768]{2,1,0:T(8,128)(2,1)S(1)}, bf16[2,128,768]{2,1,0:T(8,128)(2,1)}, u32[]{:S(2)}, u32[]{:S(2)}) collective-permute-start(bf16[2,128,768]{2,1,0:T(8,128)(2,1)S(1)} %add_convert_fusion.2), channel_id=1, source_target_pairs={{4,0},{5,1},{12,8},{13,9},{20,16},{21,17},{28,24},{29,25}} | collective-permute-start | bytes 1179656 | tf_op jit(solution)/shard_map/ppermute | solution.py:688
  373.9 36.2 %collective-permute-start.41 = (bf16[2,192,1536]{2,1,0:T(8,128)(2,1)S(1)}, bf16[2,192,1536]{2,1,0:T(8,128)(2,1)}, u32[]{:S(2)}, u32[]{:S(2)}) collective-permute-start(bf16[2,192,1536]{2,1,0:T(8,128)(2,1)S(1)} %dynamic-slice_bitcast_fusion.1.refs_18_), channel_id=1, source_target_pairs={{0,16},{16,0},{1,17},{17,1},{2,18},{18,2},{3,19},{19,3},{4,20},{20... | collective-permute-start | bytes 3538952 | tf_op jit(solution)/shard_map/ppermute | solution.py:605
  376.8 33.3 %collective-permute-start.42 = (bf16[2,192,1536]{2,1,0:T(8,128)(2,1)S(1)}, bf16[2,192,1536]{2,1,0:T(8,128)(2,1)}, u32[]{:S(2)}, u32[]{:S(2)}) collective-permute-start(bf16[2,192,1536]{2,1,0:T(8,128)(2,1)S(1)} %dynamic-slice_bitcast_fusion.refs_19_), channel_id=1, source_target_pairs={{0,4},{4,0},{1,5},{5,1},{2,6},{6,2},{3,7},{7,3},{8,12},{12,8},{9,1... | collective-permute-start | bytes 3538952 | tf_op jit(solution)/shard_map/ppermute | solution.py:605
  383.1 87.8 %collective-permute-start.32 = (bf16[2,256,1536]{2,1,0:T(8,128)(2,1)}, bf16[2,256,1536]{2,1,0:T(8,128)(2,1)}, u32[]{:S(2)}, u32[]{:S(2)}) collective-permute-start(bf16[2,256,1536]{2,1,0:T(8,128)(2,1)} %constant_dynamic-slice_fusion.2.refs_15_), channel_id=1, source_target_pairs={{0,1},{1,0},{2,3},{3,2},{4,5},{5,4},{6,7},{7,6},{8,9},{9,8},{10,11... | collective-permute-start | bytes 4718600 | tf_op jit(solution)/shard_map/ppermute | solution.py:605
  410.1 7.4 %collective-permute-start.39 = (f32[2,8,1024]{2,1,0:T(8,128)S(1)}, f32[2,8,1024]{2,1,0:T(8,128)S(1)}, u32[]{:S(2)}, u32[]{:S(2)}) collective-permute-start(f32[2,8,1024]{2,1,0:T(8,128)S(1)} %get-tuple-element.137), channel_id=1, source_target_pairs={{2,0},{4,2},{6,4},{3,1},{5,3},{7,5},{10,8},{12,10},{14,12},{11,9},... | collective-permute-start | bytes 196616 | tf_op jit(solution)/shard_map/ppermute | solution.py:637
  424.3 20.0 %collective-permute-start.40 = (bf16[512,1536]{1,0:T(8,128)(2,1)S(1)}, bf16[512,1536]{1,0:T(8,128)(2,1)S(1)}, u32[]{:S(2)}, u32[]{:S(2)}) collective-permute-start(bf16[512,1536]{1,0:T(8,128)(2,1)S(1)} %get-tuple-element.210), channel_id=1, source_target_pairs={{0,8},{8,0},{1,9},{9,1},{2,10},{10,2},{3,11},{11,3},{4,12},{12,4},... | collective-permute-start | bytes 4718600 | tf_op jit(solution)/shard_map/ppermute | solution.py:605
  424.4 16.0 %collective-permute-start.43 = (bf16[192,1536]{1,0:T(8,128)(2,1)S(1)}, bf16[192,1536]{1,0:T(8,128)(2,1)S(1)}, u32[]{:S(2)}, u32[]{:S(2)}) collective-permute-start(bf16[192,1536]{1,0:T(8,128)(2,1)S(1)} %dynamic-slice_bitcast_fusion.5), channel_id=1, source_target_pairs={{0,4},{4,0},{1,5},{5,1},{2,6},{6,2},{3,7},{7,3},{8,12},{12,8},{9,1... | collective-permute-start | bytes 1769480 | tf_op jit(solution)/shard_map/ppermute | solution.py:605
  426.6 15.5 %collective-permute-start.44 = (bf16[192,1536]{1,0:T(8,128)(2,1)S(1)}, bf16[192,1536]{1,0:T(8,128)(2,1)S(1)}, u32[]{:S(2)}, u32[]{:S(2)}) collective-permute-start(bf16[192,1536]{1,0:T(8,128)(2,1)S(1)} %dynamic-slice_bitcast_fusion.4), channel_id=1, source_target_pairs={{0,16},{16,0},{1,17},{17,1},{2,18},{18,2},{3,19},{19,3},{4,20},{20... | collective-permute-start | bytes 1769480 | tf_op jit(solution)/shard_map/ppermute | solution.py:605
  442.4 62.2 %collective-permute-start.54 = (bf16[192,1536]{1,0:T(8,128)(2,1)S(1)}, bf16[192,1536]{1,0:T(8,128)(2,1)}, u32[]{:S(2)}, u32[]{:S(2)}) collective-permute-start(bf16[192,1536]{1,0:T(8,128)(2,1)S(1)} %get-tuple-element.202.refs_17_), channel_id=1, source_target_pairs={{2,0},{8,10},{10,2},{0,8},{3,1},{9,11},{11,3},{1,9},{6,4},{12,14},... | collective-permute-start | bytes 1769480 | tf_op jit(solution)/shard_map/ppermute | solution.py:989
  442.5 64.5 %collective-permute-start.55 = (bf16[192,1536]{1,0:T(8,128)(2,1)S(1)}, bf16[192,1536]{1,0:T(8,128)(2,1)}, u32[]{:S(2)}, u32[]{:S(2)}) collective-permute-start(bf16[192,1536]{1,0:T(8,128)(2,1)S(1)} %get-tuple-element.203.refs_18_), channel_id=1, source_target_pairs={{2,8},{8,2},{3,9},{9,3},{6,12},{12,6},{7,13},{13,7},{18,24},{24,18... | collective-permute-start | bytes 1769480 | tf_op jit(solution)/shard_map/ppermute | solution.py:990
  470.9 9.7 %collective-permute-start.46 = (f32[2,8,1024]{2,1,0:T(8,128)S(1)}, f32[2,8,1024]{2,1,0:T(8,128)S(1)}, u32[]{:S(2)}, u32[]{:S(2)}) collective-permute-start(f32[2,8,1024]{2,1,0:T(8,128)S(1)} %get-tuple-element.147), channel_id=1, source_target_pairs={{2,0},{4,2},{6,4},{3,1},{5,3},{7,5},{10,8},{12,10},{14,12},{11,9},... | collective-permute-start | bytes 196616 | tf_op jit(solution)/shard_map/ppermute | solution.py:637
  491.6 21.7 %collective-permute-start.56 = (bf16[2,192,1152]{2,1,0:T(8,128)(2,1)S(1)}, bf16[2,192,1152]{2,1,0:T(8,128)(2,1)S(1)}, u32[]{:S(2)}, u32[]{:S(2)}) collective-permute-start(bf16[2,192,1152]{2,1,0:T(8,128)(2,1)S(1)} %dynamic-slice_bitcast_fusion.2), channel_id=1, source_target_pairs={{0,4},{4,0},{1,5},{5,1},{2,6},{6,2},{3,7},{7,3},{8,12},{12,8},{9,1... | collective-permute-start | bytes 2654216 | tf_op jit(solution)/shard_map/ppermute | solution.py:605
  492.3 22.2 %collective-permute-start.58 = (bf16[2,192,1152]{2,1,0:T(8,128)(2,1)S(1)}, bf16[2,192,1152]{2,1,0:T(8,128)(2,1)S(1)}, u32[]{:S(2)}, u32[]{:S(2)}) collective-permute-start(bf16[2,192,1152]{2,1,0:T(8,128)(2,1)S(1)} %dynamic-slice_bitcast_fusion.3), channel_id=1, source_target_pairs={{0,16},{16,0},{1,17},{17,1},{2,18},{18,2},{3,19},{19,3},{4,20},{20... | collective-permute-start | bytes 2654216 | tf_op jit(solution)/shard_map/ppermute | solution.py:605
  500.1 16.2 %collective-permute-start.47 = (bf16[512,1536]{1,0:T(8,128)(2,1)S(1)}, bf16[512,1536]{1,0:T(8,128)(2,1)S(1)}, u32[]{:S(2)}, u32[]{:S(2)}) collective-permute-start(bf16[512,1536]{1,0:T(8,128)(2,1)S(1)} %slice_bitcast_fusion.8), channel_id=1, source_target_pairs={{0,8},{8,0},{1,9},{9,1},{2,10},{10,2},{3,11},{11,3},{4,12},{12,4},... | collective-permute-start | bytes 4718600 | tf_op jit(solution)/shard_map/ppermute | solution.py:605
  504.6 78.0 %collective-permute-start.45 = (bf16[256,1536]{1,0:T(8,128)(2,1)S(1)}, bf16[256,1536]{1,0:T(8,128)(2,1)}, u32[]{:S(2)}, u32[]{:S(2)}) collective-permute-start(bf16[256,1536]{1,0:T(8,128)(2,1)S(1)} %constant_dynamic-slice_fusion.1.refs_16_), channel_id=1, source_target_pairs={{0,1},{1,0},{2,3},{3,2},{4,5},{5,4},{6,7},{7,6},{8,9},{9,8},{10,11... | collective-permute-start | bytes 2359304 | tf_op jit(solution)/shard_map/ppermute | solution.py:605
  515.0 16.8 %collective-permute-start.59 = (bf16[192,1152]{1,0:T(8,128)(2,1)S(1)}, bf16[192,1152]{1,0:T(8,128)(2,1)S(1)}, u32[]{:S(2)}, u32[]{:S(2)}) collective-permute-start(bf16[192,1152]{1,0:T(8,128)(2,1)S(1)} %dynamic-slice_bitcast_fusion.6), channel_id=1, source_target_pairs={{0,4},{4,0},{1,5},{5,1},{2,6},{6,2},{3,7},{7,3},{8,12},{12,8},{9,1... | collective-permute-start | bytes 1327112 | tf_op jit(solution)/shard_map/ppermute | solution.py:605
  515.7 16.1 %collective-permute-start.57 = (bf16[192,1152]{1,0:T(8,128)(2,1)S(1)}, bf16[192,1152]{1,0:T(8,128)(2,1)S(1)}, u32[]{:S(2)}, u32[]{:S(2)}) collective-permute-start(bf16[192,1152]{1,0:T(8,128)(2,1)S(1)} %dynamic-slice_bitcast_fusion.7), channel_id=1, source_target_pairs={{0,16},{16,0},{1,17},{17,1},{2,18},{18,2},{3,19},{19,3},{4,20},{20... | collective-permute-start | bytes 1327112 | tf_op jit(solution)/shard_map/ppermute | solution.py:605
  517.7 10.2 %collective-permute-start.64 = (f32[5924]{0:T(1024)S(1)}, f32[5924]{0:T(1024)S(1)}, u32[]{:S(2)}, u32[]{:S(2)}) collective-permute-start(f32[5924]{0:T(1024)S(1)} %concatenate.175), channel_id=1, source_target_pairs={{0,16},{16,0},{1,17},{17,1},{2,18},{18,2},{3,19},{19,3},{4,20},{20... | collective-permute-start | bytes 71096 | tf_op jit(solution)/shard_map/ppermute | solution.py:605
  531.7 9.6 %collective-permute-start.66 = (f32[5924]{0:T(1024)S(1)}, f32[5924]{0:T(1024)S(1)}, u32[]{:S(2)}, u32[]{:S(2)}) collective-permute-start(f32[5924]{0:T(1024)S(1)} %add.402), channel_id=1, source_target_pairs={{0,2},{2,0},{1,3},{3,1},{4,6},{6,4},{5,7},{7,5},{8,10},{10,8},{9,1... | collective-permute-start | bytes 71096 | tf_op jit(solution)/shard_map/ppermute | solution.py:605
  532.8 34.6 %collective-permute-start.61 = (bf16[192,1152]{1,0:T(8,128)(2,1)}, bf16[192,1152]{1,0:T(8,128)(2,1)S(1)}, u32[]{:S(2)}, u32[]{:S(2)}) collective-permute-start(bf16[192,1152]{1,0:T(8,128)(2,1)} %get-tuple-element.201), channel_id=1, source_target_pairs={{2,8},{8,2},{3,9},{9,3},{6,12},{12,6},{7,13},{13,7},{18,24},{24,18... | collective-permute-start | bytes 1327112 | tf_op jit(solution)/shard_map/ppermute | solution.py:1009
  533.6 33.8 %collective-permute-start.60 = (bf16[192,1152]{1,0:T(8,128)(2,1)S(1)}, bf16[192,1152]{1,0:T(8,128)(2,1)S(1)}, u32[]{:S(2)}, u32[]{:S(2)}) collective-permute-start(bf16[192,1152]{1,0:T(8,128)(2,1)S(1)} %get-tuple-element.200), channel_id=1, source_target_pairs={{2,0},{8,10},{10,2},{0,8},{3,1},{9,11},{11,3},{1,9},{6,4},{12,14},... | collective-permute-start | bytes 1327112 | tf_op jit(solution)/shard_map/ppermute | solution.py:1008
  538.1 44.4 %collective-permute-start.48 = (bf16[256,1536]{1,0:T(8,128)(2,1)}, bf16[256,1536]{1,0:T(8,128)(2,1)}, u32[]{:S(2)}, u32[]{:S(2)}) collective-permute-start(bf16[256,1536]{1,0:T(8,128)(2,1)} %constant_dynamic-slice_fusion), channel_id=1, source_target_pairs={{0,1},{1,0},{2,3},{3,2},{4,5},{5,4},{6,7},{7,6},{8,9},{9,8},{10,11... | collective-permute-start | bytes 2359304 | tf_op jit(solution)/shard_map/ppermute | solution.py:605
  543.9 22.3 %collective-permute-start.69 = (f32[1280]{0:T(1024)S(1)}, f32[1280]{0:T(1024)S(1)}, u32[]{:S(2)}, u32[]{:S(2)}) collective-permute-start(f32[1280]{0:T(1024)S(1)} %slice_add_fusion.2), channel_id=1, source_target_pairs={{0,1},{1,0},{2,3},{3,2},{4,5},{5,4},{6,7},{7,6},{8,9},{9,8},{10,11... | collective-permute-start | bytes 15368 | tf_op jit(solution)/shard_map/ppermute | solution.py:605
  566.2 5.7 collective-permute-start.67
  568.8 12.9 %collective-permute-start.62 = (f32[192,256]{1,0:T(8,128)S(1)}, f32[192,256]{1,0:T(8,128)S(1)}, u32[]{:S(2)}, u32[]{:S(2)}) collective-permute-start(f32[192,256]{1,0:T(8,128)S(1)} %slice.435), channel_id=1, source_target_pairs={{0,2},{2,0},{1,3},{3,1},{4,6},{6,4},{5,7},{7,5},{8,10},{10,8},{9,1... | collective-permute-start | bytes 589832 | tf_op jit(solution)/shard_map/ppermute | solution.py:605
  581.7 6.9 %collective-permute-start.63 = (f32[192,256]{1,0:T(8,128)S(1)}, f32[192,256]{1,0:T(8,128)}, u32[]{:S(2)}, u32[]{:S(2)}) collective-permute-start(f32[192,256]{1,0:T(8,128)S(1)} %slice_add_fusion.3), channel_id=1, source_target_pairs={{0,1},{1,0},{2,3},{3,2},{4,5},{5,4},{6,7},{7,6},{8,9},{9,8},{10,11... | collective-permute-start | bytes 589832 | tf_op jit(solution)/shard_map/ppermute | solution.py:605
  585.7 4.5 collective-permute-start.49
  601.6 5.1 collective-permute-start.53
  (98 other events, 849.6 us)

commit v2 on v1

v2 whole, which is shorter than its diff:
```python
import functools

import jax
import jax.numpy as jnp
from jax import lax
from jax.experimental import pallas as pl
from jax.experimental.pallas import tpu as pltpu
from jax.sharding import Mesh
from jax.sharding import PartitionSpec as P

CHUNK = 256
HALF = CHUNK // 2
LANES = 128
STRIP = 256
ROWS = 64
RIM = 16
EPS = 1e-05
F32 = jnp.float32
BF16 = jnp.bfloat16
VMEM_BYTES = 48 * 1024 * 1024


def dot(left, right):
    return lax.dot_general(left, right, (((1,), (0,)), ((), ())), preferred_element_type=F32)


def dot_nt(left, right):
    return lax.dot_general(left, right, (((1,), (1,)), ((), ())), preferred_element_type=F32)


def pieces(value, count):
    terms = []
    for _ in range(count):
        term = value.astype(BF16)
        terms.append(term)
        value = value - term.astype(F32)
    return terms


def doubled(value):
    return jnp.concatenate(pieces(value, 2), axis=1)


def spread_heads(pair, spread):
    return dot(pair, spread)


def gather_heads(value, spread, count=2):
    return sum(dot_nt(term, spread[0:LANES, :]) for term in pieces(value, count))


def running_sum(value, mask):
    return sum(dot(mask, term) for term in pieces(value, 3))


def iota2(rows, cols, dim):
    return lax.broadcasted_iota(jnp.int32, (rows, cols), dim)


def turned(value):
    return jnp.transpose(value.astype(F32)).astype(BF16)


def strips(width):
    return [slice(at, at + STRIP) for at in range(0, width, STRIP)]


def row_blocks():
    return [slice(at, at + ROWS) for at in range(0, CHUNK, ROWS)]


def conv_pre(ext, taps, rows, cols):
    total = taps[4:5, cols] + taps[0:1, cols] * ext[pl.ds(RIM - 3 + rows.start, ROWS), cols]
    for k in range(1, 4):
        total = total + taps[k : k + 1, cols] * ext[pl.ds(RIM - 3 + k + rows.start, ROWS), cols]
    return total


def softplus(value):
    return jnp.maximum(value, 0.0) + jnp.log1p(jnp.exp(-jnp.abs(value)))


def write_packed(packed_ref, end, total):
    packed_ref[0, 0:LANES, :] = end.astype(BF16)
    packed_ref[0, LANES:, :] = jnp.zeros((RIM, end.shape[1]), BF16)
    row = iota2(RIM, LANES, 0)
    logs = jnp.zeros((RIM, LANES), F32)
    for k, term in enumerate(pieces(total, 3)):
        logs = jnp.where(row == k, term.astype(F32), logs)
    packed_ref[0, LANES:, 0:LANES] = logs.astype(BF16)


def widened(log, spread):
    return spread_heads(doubled(jnp.broadcast_to(jnp.exp(log), (8, LANES))), spread)[0:1, :]


def entering_state(packed_ref, first_ref, second_ref, spread_ref):
    passed = jnp.sum(packed_ref[0, LANES:, 0:LANES].astype(F32), axis=0, keepdims=True)
    from_row = first_ref[0].astype(F32) + second_ref[0].astype(F32)
    return packed_ref[0, 0:LANES, :].astype(F32) + widened(passed, spread_ref[...]) * from_row


def leave_kernel(end_ref, total_ref, packed_ref, spread_ref, leaving_ref):
    kept = packed_ref[0, 0:LANES, :].astype(F32) * widened(total_ref[0, 0:1, :], spread_ref[...])
    leaving_ref[0] = (end_ref[0] + kept).astype(BF16)


def state_kernel(
    mix_ref, halo_ref, step_ref, taps_ref, heads_ref, spread_ref,
    xbc_ref, sum_ref, dt_ref, end_ref, total_ref, packed_ref, ext, weighted,
):
    inner = spread_ref.shape[1]
    place = pl.program_id(1)

    @pl.when(place == 0)
    def _():
        ext[0:RIM, :] = halo_ref[0].astype(F32)
        end_ref[...] = jnp.zeros_like(end_ref)
        total_ref[...] = jnp.zeros_like(total_ref)

    @pl.when(place > 0)
    def _():
        ext[0:RIM, :] = ext[CHUNK : CHUNK + RIM, :]

    dt = softplus(step_ref[0].astype(F32) + heads_ref[0:1, :])
    lower = (iota2(CHUNK, CHUNK, 0) >= iota2(CHUNK, CHUNK, 1)).astype(F32).astype(BF16)
    cumul = running_sum(dt * heads_ref[1:2, :], lower)
    sum_ref[0] = cumul
    dt_ref[0] = dt
    last = cumul[CHUNK - 1 : CHUNK, :]
    total_ref[0] += jnp.broadcast_to(last, total_ref.shape[1:])
    tail = doubled(jnp.exp(last - cumul) * dt)
    decay = doubled(jnp.broadcast_to(jnp.exp(last), (8, LANES)))
    b_turned = None
    for cols in reversed(strips(xbc_ref.shape[2])):
        held = spread_ref[:, cols] if cols.start < inner else None
        for rows in row_blocks():
            ext[RIM + rows.start : RIM + rows.stop, cols] = mix_ref[0, rows, cols].astype(F32)
            pre = conv_pre(ext, taps_ref, rows, cols)
            act = (pre * jax.nn.sigmoid(pre)).astype(BF16)
            xbc_ref[0, rows, cols] = act
            if held is not None:
                weighted[rows, :] = (act.astype(F32) * spread_heads(tail[rows], held)).astype(BF16)
        if held is None:
            b_turned = turned(xbc_ref[0, :, inner : inner + LANES])
        else:
            kept = end_ref[0, :, cols] * spread_heads(decay, held)[0:1, :]
            end_ref[0, :, cols] = kept + dot(b_turned, weighted[...])

    @pl.when(place == pl.num_programs(1) - 1)
    def _():
        write_packed(packed_ref, end_ref[0], total_ref[0, 0:1, :])


def scan_kernel(
    xbc_ref, sum_ref, dt_ref, packed_ref, first_ref, second_ref, gate_ref, gm_ref, rows_ref, spread_ref,
    y_ref, mixed_ref, enter_ref, stat_ref, state, stepped, weighted,
):
    inner = spread_ref.shape[1]

    @pl.when(pl.program_id(1) == 0)
    def _():
        state[...] = entering_state(packed_ref, first_ref, second_ref, spread_ref)

    cumul = sum_ref[0]
    dt = dt_ref[0]
    across = jnp.transpose(cumul)
    last = cumul[CHUNK - 1 : CHUNK, :]
    tail = doubled(jnp.exp(last - cumul) * dt)
    reach = doubled(jnp.exp(cumul))
    decay = doubled(jnp.broadcast_to(jnp.exp(last), (8, LANES)))
    dt = doubled(dt)
    b_low = xbc_ref[0, :, inner : inner + LANES]
    c_low = xbc_ref[0, :, inner + LANES :]
    b_turned = turned(b_low)
    score = dot_nt(c_low, b_low)
    causal = iota2(HALF, HALF, 0) >= iota2(HALF, HALF, 1)
    first = iota2(1, LANES, 1) < LANES // 2
    squares = [jnp.zeros((ROWS, STRIP), F32) for _ in row_blocks()]
    crossed = [jnp.zeros((ROWS, STRIP), F32) for _ in row_blocks()]
    for cols in strips(inner):
        held = spread_ref[:, cols]
        entering = state[:, cols].astype(BF16)
        enter_ref[0, 0, :, cols] = entering
        for rows in row_blocks():
            x = xbc_ref[0, rows, cols].astype(F32)
            stepped[rows, :] = x * spread_heads(dt[rows], held)
            weighted[rows, :] = (x * spread_heads(tail[rows], held)).astype(BF16)
            y_ref[0, rows, cols] = dot(c_low[rows], entering) * spread_heads(reach[rows], held)
        kept = state[:, cols] * spread_heads(decay, held)[0:1, :]
        state[:, cols] = kept + dot(b_turned, weighted[...])
        for pair in range(STRIP // LANES):
            lanes = slice(pair * LANES, (pair + 1) * LANES)
            into = slice(cols.start + pair * LANES, cols.start + (pair + 1) * LANES)
            top = y_ref[0, 0:HALF, into]
            bottom = y_ref[0, HALF:, into]
            u = stepped[:, lanes]
            for side in range(2):
                head = (cols.start + pair * LANES) // (LANES // 2) + side
                mine = jnp.where(first if side == 0 else ~first, u, 0.0).astype(BF16)
                column = cumul[:, head : head + 1]
                row = across[head : head + 1, :]
                corner = jnp.where(causal, jnp.exp(column[0:HALF] - row[:, 0:HALF]), 0.0)
                top = top + dot((score[0:HALF, 0:HALF] * corner).astype(BF16), mine[0:HALF])
                left = jnp.exp(column[HALF:] - row[:, 0:HALF])
                right = jnp.where(causal, jnp.exp(column[HALF:] - row[:, HALF:]), 0.0)
                below = jnp.concatenate([left, right], axis=1)
                bottom = bottom + dot((score[HALF:, :] * below).astype(BF16), mine)
            y_ref[0, 0:HALF, into] = top
            y_ref[0, HALF:, into] = bottom
        for k, rows in enumerate(row_blocks()):
            y = y_ref[0, rows, cols] + rows_ref[0:1, cols] * xbc_ref[0, rows, cols].astype(F32)
            gate = gate_ref[0, rows, cols].astype(F32)
            gated = y * gate * jax.nn.sigmoid(gate)
            gained = gated * rows_ref[1:2, cols]
            mixed_ref[0, rows, cols] = gained.astype(BF16)
            squares[k] = squares[k] + gated * gated
            crossed[k] = crossed[k] + gained * gm_ref[0, rows, cols]
    squares = jnp.concatenate(squares, axis=0)
    crossed = jnp.concatenate(crossed, axis=0)
    ones = jnp.ones((8, STRIP), BF16)
    square_row = sum(dot_nt(ones, term) for term in pieces(squares, 3))
    cross_row = sum(dot_nt(ones, term) for term in pieces(crossed, 3))
    stat_ref[0] = jnp.where(iota2(8, CHUNK, 0) == 0, square_row, cross_row)


def gate_kernel(
    inner_full, y_ref, xbc_ref, gate_ref, gm_ref, stat_ref, sum_ref, total_ref, rows_ref, spread_ref,
    gy_ref, gz_ref, mixed_ref, back_ref, gain_ref, packed_ref, reached,
):
    inner = spread_ref.shape[1]

    @pl.when(pl.program_id(1) == 0)
    def _():
        back_ref[...] = jnp.zeros_like(back_ref)

    @pl.when((pl.program_id(0) == 0) & (pl.program_id(1) == 0))
    def _():
        gain_ref[...] = jnp.zeros_like(gain_ref)

    stats = jnp.transpose(stat_ref[0])
    scale = lax.rsqrt(stats[:, 0:1] / inner_full + EPS)
    bent = scale * scale * scale * (stats[:, 1:2] / inner_full)
    cumul = sum_ref[0]
    reach = doubled(jnp.exp(cumul))
    decay = doubled(jnp.broadcast_to(jnp.exp(cumul[CHUNK - 1 : CHUNK, :]), (8, LANES)))
    c_turned = turned(xbc_ref[0, :, inner + LANES :])
    for cols in strips(inner):
        held = spread_ref[:, cols]
        gain = rows_ref[1:2, cols]
        gain_sum = jnp.zeros((1, STRIP), F32)
        for rows in row_blocks():
            x = xbc_ref[0, rows, cols].astype(F32)
            y = y_ref[0, rows, cols] + rows_ref[0:1, cols] * x
            gate = gate_ref[0, rows, cols].astype(F32)
            sigmoid = jax.nn.sigmoid(gate)
            silu = gate * sigmoid
            gated = y * silu
            scaled = gated * scale[rows]
            gm = gm_ref[0, rows, cols]
            gg = scale[rows] * gm * gain - gated * bent[rows]
            gy = (gg * silu).astype(BF16)
            gy_ref[0, rows, cols] = gy
            gz_ref[0, rows, cols] = (gg * y * sigmoid * (1.0 + gate * (1.0 - sigmoid))).astype(BF16)
            mixed_ref[0, rows, cols] = (scaled * gain).astype(BF16)
            gain_sum = gain_sum + jnp.sum(gm * scaled, axis=0, keepdims=True)
            reached[rows, :] = (gy.astype(F32) * spread_heads(reach[rows], held)).astype(BF16)
        gain_ref[:, cols] += jnp.broadcast_to(gain_sum, (8, STRIP))
        kept = back_ref[0, :, cols] * spread_heads(decay, held)[0:1, :]
        back_ref[0, :, cols] = kept + dot(c_turned, reached[...])

    @pl.when(pl.program_id(1) == pl.num_programs(1) - 1)
    def _():
        write_packed(packed_ref, back_ref[0], total_ref[0, 0:1, :])


def adjoint_kernel(
    xbc_ref, sum_ref, dt_ref, gy_ref, y_ref, enter_ref, packed_ref, first_ref, second_ref, mix_ref, before_ref, halo_ref,
    step_ref, taps_ref, heads_ref, rows_ref, spread_ref,
    gmix_ref, rim_ref, gtaps_ref, gheads_ref, gskip_ref, back, ext, gpre, pulled,
):
    inner = spread_ref.shape[1]
    chunks = pl.num_programs(1)
    order = pl.program_id(1)

    @pl.when((pl.program_id(0) == 0) & (order == 0))
    def _():
        gtaps_ref[...] = jnp.zeros_like(gtaps_ref)
        gheads_ref[...] = jnp.zeros_like(gheads_ref)
        gskip_ref[...] = jnp.zeros_like(gskip_ref)

    @pl.when(order == 0)
    def _():
        back[...] = entering_state(packed_ref, first_ref, second_ref, spread_ref)
        gpre[CHUNK:, :] = jnp.zeros((8, gpre.shape[1]), F32)

    @pl.when(order > 0)
    def _():
        gpre[CHUNK:, :] = gpre[0:8, :]

    @pl.when(order == chunks - 1)
    def _():
        ext[0:RIM, :] = halo_ref[0].astype(F32)

    @pl.when(order < chunks - 1)
    def _():
        ext[0:RIM, :] = before_ref[0].astype(F32)

    cumul = sum_ref[0]
    dt = dt_ref[0]
    across = jnp.transpose(cumul)
    last = cumul[CHUNK - 1 : CHUNK, :]
    fade_pair = doubled(jnp.exp(last - cumul))
    reach_pair = doubled(jnp.exp(cumul))
    dt_pair = doubled(dt)
    decay = jnp.broadcast_to(jnp.exp(last), (8, LANES))
    decay_pair = doubled(decay)
    b_low = xbc_ref[0, :, inner : inner + LANES]
    c_low = xbc_ref[0, :, inner + LANES :]
    c_turned = turned(c_low)
    score = dot_nt(b_low, c_low)
    causal = iota2(HALF, HALF, 0) <= iota2(HALF, HALF, 1)
    first = iota2(1, LANES, 1) < LANES // 2
    pulled[...] = jnp.zeros_like(pulled)
    gb = jnp.zeros((CHUNK, LANES), F32)
    gc = jnp.zeros((CHUNK, LANES), F32)
    between = jnp.zeros((CHUNK, LANES), F32)
    arrived = jnp.zeros((CHUNK, LANES), F32)
    direct = jnp.zeros((CHUNK, LANES), F32)
    joined = jnp.zeros((8, LANES), F32)

    def conv_part(cols, gact):
        sums = [jnp.zeros((1, STRIP), F32) for _ in range(5)]
        for rows in row_blocks():
            ext[RIM + rows.start : RIM + rows.stop, cols] = mix_ref[0, rows, cols].astype(F32)
        for rows in reversed(row_blocks()):
            pre = conv_pre(ext, taps_ref, rows, cols)
            sigmoid = jax.nn.sigmoid(pre)
            gp = gact[rows].astype(BF16).astype(F32) * sigmoid * (1.0 + pre * (1.0 - sigmoid))
            gpre[rows, cols] = gp
            total = taps_ref[3:4, cols] * gp
            for k in range(3):
                total = total + taps_ref[k : k + 1, cols] * gpre[pl.ds(3 - k + rows.start, ROWS), cols]
            for k in range(4):
                moved = ext[pl.ds(RIM - 3 + k + rows.start, ROWS), cols]
                sums[k] = sums[k] + jnp.sum(gp * moved, axis=0, keepdims=True)
            sums[4] = sums[4] + jnp.sum(gp, axis=0, keepdims=True)
            gmix_ref[0, rows, cols] = total.astype(BF16)
        rim_ref[0, :, cols] = gpre[0:8, cols]
        for k in range(5):
            gtaps_ref[k : k + 1, cols] += sums[k]

    for cols in strips(inner):
        held = spread_ref[:, cols]
        x = xbc_ref[0, :, cols].astype(F32)
        dt_wide = spread_heads(dt_pair, held)
        fade_wide = spread_heads(fade_pair, held)
        u = x * dt_wide
        u_low = u.astype(BF16)
        weighted = (u * fade_wide).astype(BF16)
        gy_low = gy_ref[0, :, cols]
        gy = gy_low.astype(F32)
        reached = (gy * spread_heads(reach_pair, held)).astype(BF16)
        later = back[:, cols]
        later_low = later.astype(BF16)
        entered = enter_ref[0, 0, :, cols]
        gb = gb + dot_nt(weighted, later_low)
        gc = gc + dot_nt(reached, entered)
        gu_carried = dot(b_low, later_low) * fade_wide
        sums = jnp.sum(later * entered.astype(F32), axis=0, keepdims=True)
        joined = joined + gather_heads(jnp.broadcast_to(sums, (8, STRIP)), held)
        back[:, cols] = later * spread_heads(decay_pair, held)[0:1, :] + dot(c_turned, reached)
        parts = []
        for pair in range(STRIP // LANES):
            lanes = slice(pair * LANES, (pair + 1) * LANES)
            top = gu_carried[0:HALF, lanes]
            bottom = gu_carried[HALF:, lanes]
            gy_pair = gy_low[:, lanes]
            for side in range(2):
                head = (cols.start + pair * LANES) // (LANES // 2) + side
                keep = first if side == 0 else ~first
                gy_mine = jnp.where(keep, gy[:, lanes], 0.0).astype(BF16)
                u_mine = jnp.where(keep, u[:, lanes], 0.0).astype(BF16)
                column = cumul[:, head : head + 1]
                row = across[head : head + 1, :]
                corner = jnp.where(causal, jnp.exp(row[:, 0:HALF] - column[0:HALF]), 0.0)
                side_right = jnp.exp(row[:, HALF:] - column[0:HALF])
                low_right = jnp.where(causal, jnp.exp(row[:, HALF:] - column[HALF:]), 0.0)
                above = jnp.concatenate([corner, side_right], axis=1)
                top = top + dot((score[0:HALF, :] * above).astype(BF16), gy_mine)
                bottom = bottom + dot((score[HALF:, HALF:] * low_right).astype(BF16), gy_mine[HALF:])
                pulled[0:HALF, :] += dot_nt(u_mine[0:HALF], gy_pair) * above
                pulled[HALF:, HALF:] += dot_nt(u_mine[HALF:], gy_pair[HALF:]) * low_right
            parts.append(jnp.concatenate([top, bottom], axis=0))
        gu = jnp.concatenate(parts, axis=1)
        u_kept = u_low.astype(F32)
        between = between + gather_heads(gy * y_ref[0, :, cols] - u_kept * gu, held)
        arrived = arrived + gather_heads(u_kept * gu_carried, held)
        direct = direct + gather_heads(x * gu, held)
        gskip_ref[:, cols] += jnp.broadcast_to(jnp.sum(gy * x, axis=0, keepdims=True), (8, STRIP))
        conv_part(cols, dt_wide * gu + rows_ref[0:1, cols] * gy)

    pulled_low = pulled[...].astype(BF16)
    gb = gb + dot(pulled_low, c_low)
    gc = gc + dot(jnp.transpose(pulled[...]).astype(BF16), b_low)
    conv_part(slice(inner, inner + 2 * LANES), jnp.concatenate([gb, gc], axis=1))

    upper = (iota2(CHUNK, CHUNK, 0) <= iota2(CHUNK, CHUNK, 1)).astype(F32).astype(BF16)
    whole = jnp.sum(arrived, axis=0, keepdims=True) + decay[0:1, :] * joined[0:1, :]
    glg = running_sum(between, upper) + whole
    rate = heads_ref[1:2, :]
    gdt = direct + rate * glg
    raw = step_ref[0].astype(F32) + heads_ref[0:1, :]
    gsi = gdt * jax.nn.sigmoid(raw) * heads_ref[2:3, :]
    gmix_ref[0, :, inner + 2 * LANES :] = gsi.astype(BF16)
    gheads_ref[0:1, :] += jnp.sum(gsi, axis=0, keepdims=True)
    gheads_ref[1:2, :] += jnp.sum(glg * dt * rate, axis=0, keepdims=True)


def flat(width, order=lambda i: i, column=0):
    return pl.BlockSpec((1, CHUNK, width), lambda g, i: (g, order(i), column))


def whole(*shape):
    return pl.BlockSpec((1,) + shape, lambda g, i: (g,) + (0,) * len(shape))


def fixed(shape):
    return pl.BlockSpec(shape, lambda g, i: (0,) * len(shape))


def shaped(shape, dtype=F32):
    return jax.ShapeDtypeStruct(shape, dtype)


def run(kernel, grid, ins, outs, scratch, flops, moved, after=()):
    count = len(ins)
    extra = list(after)

    def body(*refs):
        kernel(*refs[:count], *refs[count + len(extra) :])

    steps = grid[0] * grid[1]
    return pl.pallas_call(
        body,
        grid=grid,
        in_specs=[spec for _, spec in ins] + [pl.BlockSpec(memory_space=pl.ANY)] * len(extra),
        out_specs=[spec for _, spec in outs],
        out_shape=[shape for shape, _ in outs],
        scratch_shapes=scratch,
        compiler_params=pltpu.CompilerParams(
            dimension_semantics=("arbitrary", "arbitrary"), vmem_limit_bytes=VMEM_BYTES
        ),
        cost_estimate=pl.CostEstimate(
            flops=steps * flops, bytes_accessed=steps * moved, transcendentals=0
        ),
    )(*[array for array, _ in ins], *extra)


def local_states(xw, halo, taps, heads, spread, after):
    groups, length, _ = xw.shape
    inner = spread.shape[1]
    width = inner + 2 * LANES
    return run(
        state_kernel,
        (groups, length // CHUNK),
        [
            (xw, flat(width)),
            (halo, whole(RIM, width)),
            (xw, flat(LANES, column=width // LANES)),
            (taps, fixed(taps.shape)),
            (heads, fixed(heads.shape)),
            (spread, fixed(spread.shape)),
        ],
        [
            (shaped((groups, length, width), BF16), flat(width)),
            (shaped((groups, length, LANES)), flat(LANES)),
            (shaped((groups, length, LANES)), flat(LANES)),
            (shaped((groups, LANES, inner)), whole(LANES, inner)),
            (shaped((groups, 8, LANES)), whole(8, LANES)),
            (shaped((groups, LANES + RIM, inner), BF16), whole(LANES + RIM, inner)),
        ],
        [pltpu.VMEM((RIM + CHUNK, width), F32), pltpu.VMEM((CHUNK, STRIP), BF16)],
        1_500_000_000,
        2_000_000,
        after,
    )


def mixer(xbc, cumul, dt, start, gate, gm, rows, spread, after):
    groups, length, width = xbc.shape
    inner = spread.shape[1]
    chunks = length // CHUNK
    return run(
        scan_kernel,
        (groups, chunks),
        [
            (xbc, flat(width)),
            (cumul, flat(LANES)),
            (dt, flat(LANES)),
            (start[0], whole(LANES + RIM, inner)),
            (start[1], whole(LANES, inner)),
            (start[2], whole(LANES, inner)),
            (gate, flat(inner)),
            (gm, flat(inner)),
            (rows, fixed(rows.shape)),
            (spread, fixed(spread.shape)),
        ],
        [
            (shaped((groups, length, inner)), flat(inner)),
            (shaped(gate.shape, BF16), flat(inner)),
            (
                shaped((groups, chunks, LANES, inner), BF16),
                pl.BlockSpec((1, 1, LANES, inner), lambda g, i: (g, i, 0, 0)),
            ),
            (shaped((groups, 8, length)), pl.BlockSpec((1, 8, CHUNK), lambda g, i: (g, 0, i))),
        ],
        [
            pltpu.VMEM((LANES, inner), F32),
            pltpu.VMEM((CHUNK, STRIP), F32),
            pltpu.VMEM((CHUNK, STRIP), BF16),
        ],
        2_500_000_000,
        4_000_000,
        after,
    )


def gate_back(inner_full, y, xbc, gate, gm, stats, cumul, total, rows, spread, after):
    groups, length, width = xbc.shape
    inner = spread.shape[1]
    chunks = length // CHUNK
    back = lambda i: chunks - 1 - i
    return run(
        functools.partial(gate_kernel, float(inner_full)),
        (groups, chunks),
        [
            (y, flat(inner, back)),
            (xbc, flat(width, back)),
            (gate, flat(inner, back)),
            (gm, flat(inner, back)),
            (stats, pl.BlockSpec((1, 8, CHUNK), lambda g, i: (g, 0, back(i)))),
            (cumul, flat(LANES, back)),
            (total, whole(8, LANES)),
            (rows, fixed(rows.shape)),
            (spread, fixed(spread.shape)),
        ],
        [
            (shaped((groups, length, inner), BF16), flat(inner, back)),
            (shaped(gate.shape, BF16), flat(inner, back)),
            (shaped(gate.shape, BF16), flat(inner, back)),
            (shaped((groups, LANES, inner)), whole(LANES, inner)),
            (shaped((8, inner)), fixed((8, inner))),
            (shaped((groups, LANES + RIM, inner), BF16), whole(LANES + RIM, inner)),
        ],
        [pltpu.VMEM((CHUNK, STRIP), BF16)],
        1_500_000_000,
        4_500_000,
        after,
    )


def adjoint(xbc, cumul, dt, gy, y, enter, gin, xw, halo, taps, heads, rows, spread, after):
    groups, length, width = xbc.shape
    inner = spread.shape[1]
    chunks = length // CHUNK
    back = lambda i: chunks - 1 - i
    per = CHUNK // RIM
    return run(
        adjoint_kernel,
        (groups, chunks),
        [
            (xbc, flat(width, back)),
            (cumul, flat(LANES, back)),
            (dt, flat(LANES, back)),
            (gy, flat(inner, back)),
            (y, flat(inner, back)),
            (enter, pl.BlockSpec((1, 1, LANES, inner), lambda g, i: (g, back(i), 0, 0))),
            (gin[0], whole(LANES + RIM, inner)),
            (gin[1], whole(LANES, inner)),
            (gin[2], whole(LANES, inner)),
            (xw, flat(width, back)),
            (
                xw,
                pl.BlockSpec(
                    (1, RIM, width), lambda g, i: (g, jnp.maximum(back(i) * per - 1, 0), 0)
                ),
            ),
            (halo, whole(RIM, width)),
            (xw, flat(LANES, back, width // LANES)),
            (taps, fixed(taps.shape)),
            (heads, fixed(heads.shape)),
            (rows, fixed(rows.shape)),
            (spread, fixed(spread.shape)),
        ],
        [
            (shaped((groups, length, width + LANES), BF16), flat(width + LANES, back)),
            (shaped((groups, 8, width)), whole(8, width)),
            (shaped((8, width)), fixed((8, width))),
            (shaped((8, LANES)), fixed((8, LANES))),
            (shaped((8, inner)), fixed((8, inner))),
        ],
        [
            pltpu.VMEM((LANES, inner), F32),
            pltpu.VMEM((RIM + CHUNK, width), F32),
            pltpu.VMEM((CHUNK + 8, width), F32),
            pltpu.VMEM((CHUNK, CHUNK), F32),
        ],
        8_000_000_000,
        6_000_000,
        after,
    )


def leave(ends, totals, packed, spread):
    groups, states, inner = ends.shape

    def one(*shape):
        return pl.BlockSpec((1,) + shape, lambda g: (g,) + (0,) * len(shape))

    return pl.pallas_call(
        leave_kernel,
        grid=(groups,),
        in_specs=[
            one(states, inner), one(8, LANES), one(states + RIM, inner),
            pl.BlockSpec(spread.shape, lambda g: (0, 0)),
        ],
        out_specs=one(states, inner),
        out_shape=shaped(ends.shape, BF16),
        compiler_params=pltpu.CompilerParams(
            dimension_semantics=("arbitrary",), vmem_limit_bytes=VMEM_BYTES
        ),
        cost_estimate=pl.CostEstimate(
            flops=0, bytes_accessed=8 * groups * states * inner, transcendentals=0
        ),
    )(ends, totals, packed, spread)


def place_kernel(at_ref, first, first_y, second, second_x, full_ref):
    step = pl.program_id(0)
    for number, ref in enumerate((first, first_y, second, second_x)):

        @pl.when(step // 2 == number)
        def _(ref=ref):
            full_ref[0, 0, 0] = ref[0]


def place_row(number, step, at):
    x, core, y = at[0], at[1], at[2]
    later = number // 2
    side = number % 2
    row = x + jnp.where(later == 0, step, side)
    column = y + jnp.where(later == 0, side, step)
    return row % 2, jnp.where(later == 0, core, 1 - core), column % 2, 0, 0


def place(first, first_y, second, second_x):
    _, rows, columns = first.shape
    at = jnp.stack([lax.axis_index(name) for name in ("x", "core", "y")]).astype(jnp.int32)

    def piece(number):
        return pl.BlockSpec(
            (1, rows, columns), lambda i, at: (jnp.clip(i - 2 * number, 0, 1), 0, 0)
        )

    full = pl.pallas_call(
        place_kernel,
        grid_spec=pltpu.PrefetchScalarGridSpec(
            num_scalar_prefetch=1,
            grid=(8,),
            in_specs=[piece(number) for number in range(4)],
            out_specs=pl.BlockSpec(
                (1, 1, 1, rows, columns), lambda i, at: place_row(i // 2, i % 2, at)
            ),
        ),
        out_shape=shaped((2, 2, 2, rows, columns), first.dtype),
        compiler_params=pltpu.CompilerParams(
            dimension_semantics=("arbitrary",), vmem_limit_bytes=VMEM_BYTES
        ),
        cost_estimate=pl.CostEstimate(
            flops=0, bytes_accessed=rows * columns, transcendentals=0
        ),
    )(at, first, first_y, second, second_x)
    return full.reshape(8 * rows, columns)


def join_kernel(at_ref, own, got, far_own, far_got, full_ref):
    half_is_own = pl.program_id(1) == at_ref[0]
    for core, (mine, other) in enumerate(((own, got), (far_own, far_got))):
        for ref, wanted in ((mine, half_is_own), (other, ~half_is_own)):

            @pl.when(wanted & (pl.program_id(0) == core))
            def _(ref=ref):
                full_ref[0] = ref[...]


def joined(own, got, far_own, far_got, part=0):
    _, rows, columns = own.shape
    at = lax.axis_index("zq").astype(jnp.int32)[None]
    piece = pl.BlockSpec((None, rows, columns), lambda c, h, at: (part, 0, 0))
    return pl.pallas_call(
        join_kernel,
        grid_spec=pltpu.PrefetchScalarGridSpec(
            num_scalar_prefetch=1,
            grid=(2, 2),
            in_specs=[piece] * 4,
            out_specs=pl.BlockSpec((1, rows, columns), lambda c, h, at: (c, h, 0)),
        ),
        out_shape=shaped((2, 2 * rows, columns), own.dtype),
        compiler_params=pltpu.CompilerParams(
            dimension_semantics=("arbitrary", "arbitrary"), vmem_limit_bytes=VMEM_BYTES
        ),
        cost_estimate=pl.CostEstimate(
            flops=0, bytes_accessed=16 * rows * columns, transcendentals=0
        ),
    )(at, own, got, far_own, far_got)


def swap(value, axis):
    return lax.ppermute(value, axis, [(0, 1), (1, 0)])


def sum_axis(value, axis):
    if lax.axis_size(axis) == 2:
        return value + swap(value, axis)
    return lax.psum(value, axis)


def cut(value, axis, dim):
    size = value.shape[dim] // 2
    at = lax.axis_index(axis)
    kept = lax.dynamic_slice_in_dim(value, at * size, size, dim)
    return kept, lax.dynamic_slice_in_dim(value, (1 - at) * size, size, dim)


def added(kept, got, dtype=BF16):
    return (kept.astype(F32) + got.astype(F32)).astype(dtype)


def hold(value, *before):
    return lax.optimization_barrier((value,) + before)[0]


def shift(value, by):
    blocks = lax.axis_size(("y", "zp"))
    pairs = [(i, i + by) for i in range(blocks) if 0 <= i + by < blocks]
    return lax.ppermute(value, ("y", "zp"), pairs)


def row_hop(packed, way, *before):
    return hold(lax.ppermute(packed, "zp", [(0, 1)] if way == 1 else [(1, 0)]), *before)


def column_hops(leaving, way, *before):
    source = 1 if way == 1 else 2
    pairs = [[(source, source + way * (1 + to))] for to in range(2)]
    return [hold(lax.ppermute(leaving, ("y", "zp"), pair), *before) for pair in pairs]


def chained(packed, way):
    blocks = lax.axis_size(("y", "zp"))
    groups, _, inner = packed.shape
    heads = inner // (LANES // 2)
    entering = jnp.zeros((groups, LANES, inner), F32)
    passed = jnp.zeros((groups, 1, LANES), F32)
    for by in range(1, blocks):
        got = shift(packed, by * way).astype(F32)
        weight = jnp.repeat(jnp.exp(passed[:, :, 0:heads]), LANES // 2, axis=2)
        entering = entering + weight * got[:, 0:LANES]
        passed = passed + jnp.sum(got[:, LANES:, 0:LANES], axis=1, keepdims=True)
    none = jnp.zeros(entering.shape, BF16)
    return jnp.pad(entering.astype(BF16), ((0, 0), (0, RIM), (0, 0))), none, none


def all_pairs():
    return all(lax.axis_size(name) == 2 for name in ("x", "y", "zp"))


NEAR = [(0, 1), (3, 2), (1, 3), (2, 0)]
FAR = [(1, 2), (2, 1)]
HOME = [(to, source) for source, to in NEAR]


def fetched(piece, near, far):
    at_home = lax.axis_index("core") == lax.axis_index("zp")
    return jnp.where(at_home, piece, near), jnp.where(at_home, near, far)


def fetch(piece):
    return lax.ppermute(piece, ("core", "zp"), NEAR), lax.ppermute(piece, ("core", "zp"), FAR)


def gather_slice(piece):
    owners = lax.axis_size("zp")
    rows = lax.all_gather(piece, ("x", "core", "y"), axis=0, tiled=True)
    parts = lax.all_gather(rows, "zp")
    return lax.dynamic_slice_in_dim(parts, lax.axis_index("core") * (owners // 2), owners // 2, 0)


def reduce_slice(parts):
    owners = lax.axis_size("zp")
    full = jnp.zeros((owners,) + parts.shape[1:], parts.dtype)
    full = lax.dynamic_update_slice_in_dim(
        full, parts, lax.axis_index("core") * (owners // 2), axis=0
    )
    mine = lax.psum_scatter(full, "zp", scatter_dimension=0, tiled=True)[0]
    mine = lax.psum_scatter(mine, ("x", "core", "y"), scatter_dimension=0, tiled=True)
    return mine.astype(F32)


def cut_rows(fulls):
    core = lax.axis_index("core")
    same, cross = [], []
    for full in fulls:
        rows, columns = full.shape[0] // 8, full.shape[1]
        full = full.reshape(2, 2, 2, rows, columns)
        same.append(cut(lax.dynamic_index_in_dim(full, core, 1, False), "x", 0))
        cross.append(cut(lax.dynamic_index_in_dim(full, 1 - core, 1, False), "y", 1))
    return (
        [kept[0] for kept, _ in same],
        [kept[:, 0] for kept, _ in cross],
        jnp.stack([sent[0] for _, sent in same]),
        jnp.stack([sent[:, 0] for _, sent in cross]),
    )


def cut_again(sames, crosses):
    same = [cut(value, "y", 0) for value in sames]
    cross = [cut(value, "x", 0) for value in crosses]
    return (
        [kept[0] for kept, _ in same],
        [kept[0] for kept, _ in cross],
        jnp.stack([sent[0] for _, sent in same]),
        jnp.stack([sent[0] for _, sent in cross]),
    )


def both(kept, got):
    return [
        [added(mine, other[k]) for k, mine in enumerate(values)]
        for values, other in zip(kept[0:2], got)
    ]


def home_parts(sames, crosses):
    at_home = lax.axis_index("core") == lax.axis_index("zp")
    cross = jnp.stack(crosses)
    return jnp.where(at_home, cross, jnp.stack(sames)), cross


def at_owner(near, far, sames):
    at_home = lax.axis_index("core") == lax.axis_index("zp")
    return [
        near[k].astype(F32) + jnp.where(at_home, same.astype(F32), far[k].astype(F32))
        for k, same in enumerate(sames)
    ]


def go_home(sent):
    return (
        lax.ppermute(sent[0], ("core", "zp"), HOME),
        lax.ppermute(sent[1], ("core", "zp"), FAR),
    )


def own_of_slice(value):
    owners = lax.axis_size("zp")
    core, part = lax.axis_index("core"), lax.axis_index("zp")
    other = swap(value, "core")
    share = value.shape[-1] // (owners // 2)
    wanted = jnp.where(part // (owners // 2) == core, value, other)
    return lax.dynamic_slice_in_dim(wanted, (part % (owners // 2)) * share, share, value.ndim - 1)


def slice_of_own(value, after):
    owners = lax.axis_size("zp")
    core = lax.axis_index("core")
    if owners == 2:
        other = hold(swap(value, "zp"), after)
        return jnp.where(core == lax.axis_index("zp"), value, other)[None]
    parts = lax.all_gather(value, "zp")
    return lax.dynamic_slice_in_dim(parts, core * (owners // 2), owners // 2, 0)


def per_device(
    hidden,
    cotangent,
    norm_gain,
    w_z,
    w_x,
    w_bc,
    w_dt,
    conv_x,
    conv_x_bias,
    conv_bc,
    conv_bc_bias,
    dt_bias,
    a_log,
    d_skip,
    inner_gain,
    w_out,
):
    micro, own_len, model = hidden.shape
    owners = lax.axis_size("zp")
    share = w_x.shape[1]
    own_heads = w_dt.shape[1]
    inner_full = share * 2 * owners
    states2 = w_bc.shape[1]
    halves = owners // 2
    inner = share * halves
    heads = own_heads * halves
    head_width = inner // heads
    width = inner + states2

    def matmul(left, right, contract, dtype=F32):
        return lax.dot_general(
            left, right, (contract, ((), ())), preferred_element_type=F32
        ).astype(dtype)

    def spliced(parts, sizes):
        if halves == 1:
            return parts[0]
        columns, at = [], 0
        for size, copies in sizes:
            columns += [parts[k][:, at : at + size] for k in range(halves if copies else 1)]
            at += size
        return jnp.concatenate(columns, axis=1)

    parts = range(micro)

    own = hidden.astype(F32)
    gain_in = norm_gain.astype(F32)
    r0 = lax.rsqrt(jnp.mean(own * own, axis=-1, keepdims=True) + EPS)
    filler = LANES // halves - own_heads
    own_first = jnp.concatenate(
        [w_x, w_bc, w_dt, jnp.zeros((w_dt.shape[0], filler), BF16)], axis=1
    )
    own_second = jnp.concatenate([w_z, jnp.transpose(w_out)], axis=1)
    normed_own = [(own[part : part + 1] * r0[part : part + 1] * gain_in).astype(BF16) for part in parts]
    fast = all_pairs()

    if fast:
        got = fetch(own_first)
        start = swap(normed_own[0], "zq")
        same, cross = fetched(own_first, *got)
        first = jnp.stack([same, swap(same, "x")])
        second = jnp.stack([cross, swap(cross, "y")])
        rest = swap(first, "y"), swap(second, "x")
        own_second, after_first = hold((own_second, normed_own[1:]), first, second)
        got = fetch(own_second)
        started = [start] + [swap(value, "zq") for value in after_first]
        w_first = place(first, rest[0], second, rest[1])
        later = rest
        got = hold(got, w_first)
        same, cross = fetched(own_second, *got)
        moved = swap(same, "x"), swap(cross, "y")
    else:
        started = [swap(value, "zq") for value in normed_own]
        later = ()
        w_first = spliced(
            gather_slice(own_first), ((share, 1), (states2, 0), (own_heads, 1), (filler, 1))
        )
    per_head = jnp.concatenate([dt_bias, a_log, d_skip])
    per_head = jnp.pad(per_head, (0, share - 3 * own_heads))
    small = jnp.concatenate([conv_x, conv_x_bias[None], inner_gain[None]], axis=0).astype(F32)
    small = jnp.concatenate([small, per_head[None], jnp.zeros((1, share), F32)])
    small = slice_of_own(hold(small, w_first), w_first)
    channel_rows = jnp.concatenate([small[k, 0:6] for k in range(halves)], axis=1)
    head_rows = jnp.concatenate(
        [small[k, 6, 0 : 3 * own_heads].reshape(3, own_heads) for k in range(halves)], axis=1
    )
    conv_shared = jnp.concatenate([conv_bc, conv_bc_bias[None]], axis=0).astype(F32)
    taps = jnp.pad(jnp.concatenate([channel_rows[0:5], conv_shared], axis=1), ((0, 3), (0, 0)))
    head_in = jnp.stack([head_rows[0], -jnp.exp(head_rows[1]), jnp.ones((heads,), F32)])
    head_in = jnp.pad(head_in, ((0, 5), (0, LANES - heads)))
    rows = jnp.stack([jnp.repeat(head_rows[2], head_width), channel_rows[5]])
    rows = jnp.pad(rows, ((0, 6), (0, 0)))
    spread = (
        lax.broadcasted_iota(jnp.int32, (LANES, inner), 1) // head_width
        == lax.broadcasted_iota(jnp.int32, (LANES, inner), 0)
    ).astype(BF16)
    spread = jnp.concatenate([spread, spread])

    normed, scans = [], []
    for part in parts:
        value, got = normed_own[part], hold(started[part], *later)
        normed.append(joined(value, got, swap(value, "core"), swap(got, "core")))
        xw = matmul(normed[part], w_first, ((2,), (0,)), BF16)
        scans.append((xw, shift(xw[:, -RIM:, 0:width], 1)))
        later = (xw,)
    if fast:
        moved = hold(moved, scans[0][0])
        first, second = jnp.stack([same, moved[0]]), jnp.stack([cross, moved[1]])
        got_second = first, swap(first, "y"), second, swap(second, "x")
    local = []
    for part in parts:
        before = [k[5] for k in local[-1:]]
        local.append(local_states(*scans[part], taps, head_in, spread, before))
        if part == 0:
            cot_own = hold(cotangent, local[0][5], scans[-1][1])
            cot_own = [cot_own[k : k + 1] for k in parts]
            cot_got = [swap(value, "zq") for value in cot_own]
    totals = [local[part][4] for part in parts]
    packed = [local[part][5] for part in parts]
    if fast:
        w_second = place(*hold(got_second, packed[-1]))
    else:
        w_second = spliced(
            gather_slice(hold(own_second, packed[-1])), ((share, 1), (share, 1))
        )
    w_gate, w_down = w_second[:, 0:inner], w_second[:, inner:]
    def hop(part, packed, ends, way, *before):
        if not fast:
            return packed, packed
        got = row_hop(packed, way, *before)
        return got, leave(ends, totals[part], got, spread)

    def entering(found, way, *before):
        if not fast:
            return chained(found[0], way)
        return found[0], *column_hops(found[1], way, *before)

    found = [hop(0, packed[0], local[0][3], 1, w_second)]
    gate = [
        matmul(hold(normed[part], found[0][1]), w_gate, ((2,), (0,)), BF16) for part in parts
    ]
    cot_far = (
        swap(hold(cotangent, local[0][5]), "core"),
        [swap(hold(cot_got[k], gate[k]), "core") for k in parts],
    )

    def whole_cot(part, *before):
        far = hold((cot_far[0], cot_far[1][part]), *before)
        return joined(cot_own[part], cot_got[part], far[0][part : part + 1], far[1])

    cot = [whole_cot(0, gate[-1])]

    w_down_held = hold(w_down, found[0][1])
    gm = [matmul(cot[0], w_down_held, ((2,), (0,)))]
    mixes, stats, branches, gates = [], [], [], []
    g_gate = g_down = 0.0
    tokens = ((0, 1), (0, 1))
    for part in parts:
        xbc, cumul, dt = local[part][0:3]
        before = (gm[0],) if part == 0 else (gates[part - 1][5], gm[part])
        start = entering(found[part], 1, *before)
        y, gained, enter, stat = mixer(xbc, cumul, dt, start, gate[part], gm[part], rows, spread, before)
        mixes.append((y, enter))
        other = swap(stat, "core")
        if part + 1 < micro:
            following = hold(packed[part + 1], found[part][1])
            found.append(hop(part + 1, following, local[part + 1][3], 1, y))
            cot.append(whole_cot(part + 1, found[-1][1]))
            gm.append(matmul(cot[-1], w_down, ((2,), (0,))))
            other = hold(other, cot[-1])
        else:
            g_gate = matmul(normed[0], hold(gates[0][1], y), tokens)
            other = hold(other, g_gate)
        stat = stat + jnp.flip(other, 0)
        other = swap(stat, "zq")
        branch = matmul(hold(gained, stat, gm[-1]), w_down, ((2,), (1,)), BF16)
        stats.append(stat + hold(other, branch))
        branches.append((branch, swap(branch[1], "core")))
        gates.append(
            gate_back(
                inner_full, y, xbc, gate[part], gm[part], stats[part], cumul, totals[part],
                rows, spread, [branch],
            )
        )
    back_packed = [g[5] for g in gates]

    found = [hop(0, back_packed[0], gates[0][3], -1, back_packed[-1])]
    for part in parts:
        g_down = g_down + matmul(cot[part], hold(gates[part][2], found[0][1]), tokens)
        if part == 0:
            branch_cut = [
                cut(added(branch[0], hold(got, g_down)), "zq", 0) for branch, got in branches
            ]
            branch_sent = jnp.stack([sent for _, sent in branch_cut])
            branch_got = swap(branch_sent, "zq")
        else:
            g_gate = g_gate + matmul(normed[part], hold(gates[part][1], g_down), tokens)
    g_gate, g_down = g_gate.astype(BF16), g_down.astype(BF16)
    g_normed_gate = [matmul(hold(gates[0][1], g_gate), w_gate, ((2,), (1,)))]
    gin = entering(found[0], -1, g_normed_gate[0])
    for part in parts[1:]:
        following = hold(back_packed[part], found[part - 1][1])
        found.append(hop(part, following, gates[part][3], -1, g_normed_gate[0]))
        g_normed_gate.append(
            matmul(hold(gates[part][1], found[part][1]), w_gate, ((2,), (1,)))
        )
    wait_for = [g_normed_gate[-1], branch_sent]
    if fast:
        second = cut_rows(hold([g_gate, g_down], *gin))
        moved = swap(second[2], "x"), swap(second[3], "y")
        wait_for += second[2:]

    g_first, heads_out, g_hidden, g_norm_gain = 0.0, [], [], 0.0

    def token_grad(part, kept, got):
        x, r, g = own[part], r0[part], added(kept, got, F32)
        q0 = g * gain_in
        grad = (
            cotangent[part].astype(F32) + r * q0
            - x * (r * r * r) * jnp.mean(q0 * x, axis=-1, keepdims=True)
        )
        return grad, jnp.sum(g * x * r, axis=0)

    def whole_output(*before):
        outputs = []
        for part in parts:
            square = lax.dynamic_slice_in_dim(
                stats[part][0, 0], lax.axis_index("zq") * own_len, own_len, 0
            )
            r1 = lax.rsqrt(square / inner_full + EPS)[:, None]
            got = hold(branch_got, *before)[part]
            outputs.append((own[part] + r1 * added(branch_cut[part][0], got, F32)).astype(BF16))
        return jnp.stack(outputs)

    for part in parts:
        xbc, cumul, dt = local[part][0:3]
        gmix, rim, *sums = adjoint(
            xbc, cumul, dt, gates[part][0], mixes[part][0], mixes[part][1], gin,
            *scans[part], taps, head_in, rows, spread, wait_for,
        )
        if part == micro - 1 and fast and micro > 1:
            (gmix, rim, *sums), norm_cut, got_home = hold(
                ((gmix, rim, *sums), norm_cut, got_home)
            )
        if part < micro - 1:
            gin = entering(found[part + 1], -1)
            gmix, rim, *sums = hold(
                (gmix, rim, *sums), *gin, branch_got, *(moved if fast else ())
            )
        heads_out.append(sums)
        ahead = shift(rim, -1)
        last_part = part == micro - 1
        if last_part:
            if micro > 1:
                kept, got = norm_cut
                grad, gain = token_grad(part - 1, kept, hold(got, gmix))
                g_hidden.append(grad)
                g_norm_gain = g_norm_gain + gain
                ahead = hold(ahead, grad)
        else:
            if fast:
                moved = hold(moved, gmix)
                second = cut_again(*both(second, moved))
                moved = swap(second[2], "y"), swap(second[3], "x")
        fix = jnp.stack(
            [sum(taps[k, :] * ahead[:, r - k] for k in range(r + 1)) for r in range(3)], axis=1
        )
        length = gmix.shape[1]
        last = gmix[:, length - RIM :].astype(F32)
        last = last + jnp.pad(fix, ((0, 0), (RIM - 3, 0), (0, LANES)))
        gmix = lax.dynamic_update_slice_in_dim(gmix, last.astype(BF16), length - RIM, 1)

        def for_weights(gmix):
            return g_first + matmul(normed[part], gmix, tokens)

        def for_tokens(gmix):
            total = g_normed_gate[part] + matmul(gmix, w_first, ((2,), (1,)))
            return total.astype(BF16)

        if last_part:
            g_first = for_weights(gmix).astype(BF16)
            if fast:
                first = cut_rows([g_first])
                moved_first = swap(first[2], "x"), swap(first[3], "y")
            total = for_tokens(hold(gmix, g_first, *(first[2:] if fast else ())))
            other = swap(total[1], "core")
        else:
            total = for_tokens(gmix)
            other = swap(total[1], "core")
            g_first = for_weights(hold(gmix, total))
            kept, sent = cut(added(total[0], hold(other, g_first)), "zq", 0)
            norm_cut = kept, swap(sent, "zq")
            if part == micro - 2:
                outputs = whole_output(g_first, sent)
            gin = hold(gin, outputs)
            wait_for = [sent, outputs]
            if fast and part == micro - 2:
                moved = hold(moved, g_first)
                pair = both(second, moved)
                home = home_parts(*pair)
                wait_for += home
                got_home = go_home(home)

    kept, sent = cut(added(total[0], other), "zq", 0)
    got_norm = swap(sent, "zq")
    if fast:
        g_gate, g_down = at_owner(*got_home, pair[0])
        first = cut_again(*both(first, hold(moved_first, g_gate, g_down)))
        moved = swap(first[2], "y"), swap(first[3], "x")
        got_norm = hold(got_norm, *first[2:])
        pair = both(first, hold(moved, got_norm))
        home = home_parts(*pair)
        got_home = go_home(home)
        grad, gain = token_grad(micro - 1, kept, hold(got_norm, *home))
        g_first = at_owner(*hold(got_home, grad), pair[0])[0]
    else:
        g_gate, g_down = [
            reduce_slice(jnp.stack(jnp.split(value, halves, axis=1))) for value in (g_gate.astype(BF16), g_down.astype(BF16))
        ]
        grad, gain = token_grad(micro - 1, kept, got_norm)
        g_first = reduce_slice(
            jnp.concatenate(
                [
                    jnp.stack(jnp.split(g_first[:, 0:inner], halves, axis=1)),
                    jnp.concatenate(
                        [
                            g_first[None, :, inner:width],
                            jnp.zeros((halves - 1, model, states2), BF16),
                        ]
                    ),
                    jnp.stack(jnp.split(g_first[:, width : width + heads], halves, axis=1)),
                ],
                axis=2,
            )
        )
    g_hidden = jnp.stack(g_hidden + [grad])
    g_norm_gain = g_norm_gain + gain
    g_bc = g_first[:, share : share + states2]
    g_bc = sum_axis(sum_axis(g_bc, "zp"), "zq")

    g_taps, g_heads, g_skip = (sum(b[k] for b in heads_out) for k in range(3))
    g_gain = sum(g[4] for g in gates)
    skip_heads = jnp.sum(g_skip[0].reshape(heads, head_width), axis=1)
    small = jnp.concatenate(
        [g_taps[0:5, 0:inner].reshape(-1), g_gain[0], g_heads[0, 0:heads], g_heads[1, 0:heads], skip_heads]
    )
    size = small.shape[0]
    packed = jnp.concatenate([small, g_taps[0:5, inner:width].reshape(-1), g_norm_gain])
    for axis in ("x", "y", "zp"):
        packed = sum_axis(packed, axis)
    small = packed[:size]
    shared = sum_axis(sum_axis(packed[size:], "core"), "zq")
    bc_rows = shared[0 : 5 * states2].reshape(5, states2)
    channel = own_of_slice(small[0 : 6 * inner].reshape(6, inner))
    per_head = own_of_slice(small[6 * inner :].reshape(3, heads))
    return (
        outputs,
        g_hidden,
        shared[5 * states2 :],
        g_gate,
        g_first[:, 0:share],
        g_bc,
        g_first[:, share + states2 : share + states2 + own_heads],
        channel[0:4],
        channel[4],
        bc_rows[0:4],
        bc_rows[4],
        per_head[0],
        per_head[1],
        per_head[2],
        channel[5],
        jnp.transpose(g_down),
    )


def solution(mesh):
    dp, seq, tensor = (mesh.shape[name] for name in ("dp", "seq", "tensor"))
    fine = Mesh(
        mesh.devices.reshape(dp // 2, 2, seq, tensor // 2, 2), ("x", "core", "y", "zp", "zq")
    )
    data, tens = ("x", "core", "y"), ("zp", "zq")
    tokens = P(("x", "core"), ("y", "zp", "zq"), None)
    params = (
        P(),
        P(data, tens),
        P(data, tens),
        P(data, None),
        P(data, tens),
        P(None, tens),
        P(tens),
        P(),
        P(),
        P(tens),
        P(tens),
        P(tens),
        P(tens),
        P(tens, data),
    )
    return jax.shard_map(
        per_device,
        mesh=fine,
        in_specs=(tokens, tokens) + params,
        out_specs=(tokens, tokens) + params,
        check_vma=False,
    )
```

time: 618 us -> 579 us (0.937)
  waiting for transfers between devices: 184 us -> 138 us
  other arithmetic: 77.4 us -> 41 us
  starting transfers between devices: 91.6 us -> 113 us
  Pallas kernels: 115 us -> 132 us
  matrix products: 89.3 us -> 101 us
  local copies, waits for them, and re-layouts: 47.8 us -> 41.3 us
    ppermute x16, waiting for transfers between devices: 53.2 us -> 24.9 us  [the longest x8 24.9 us: column_hops(): lax.ppermute(leaving, ('y', 'zp'), pair)]
    ppermute x47 -> x48, starting transfers between devices: 40.4 us -> 62.7 us  [swap(): return lax.ppermute(value, axis, [(0, 1), (1, 0)])]
    ppermute x47 -> x48, waiting for transfers between devices: 119 us -> 103 us  [swap(): return lax.ppermute(value, axis, [(0, 1), (1, 0)])]
    pallas_call x0 -> x8, Pallas kernels: none -> 13.4 us  [the longest x4 11.7 us: joined(): pl.pallas_call(join_kernel, grid_spec=pltpu.PrefetchScalarGridSpec(num_sc...]
    select_n x7 -> x1, other arithmetic: 15.3 us -> 2.29 us  [home_parts(): return (jnp.where(at_home, cross, jnp.stack(sames)), cross)]
    dot_general x12 -> x18, matrix products: 89.3 us -> 101 us  [matmul(): lax.dot_general(left, right, (contract, ((), ())), preferred_element_type...]
    another operation x11, other arithmetic: 17.7 us -> 7 us  [the longest x2 3.23 us: whole_output(): return jnp.stack(outputs)]
    optimization_barrier x1 -> x0, local copies, waits for them, and re-layouts: 6.71 us -> none  [hold(): return lax.optimization_barrier((value,) + before)[0]]
  transfers between devices with their start and end apart: 71 -> 72, of which waited for: 24 -> 24; matrix products, arithmetic and copies ran while one was open for 30% -> 25% of each run, Pallas kernels for 16% -> 23%
where the time goes in v2:
time: 579 us; the launch traced here: 570 us
  waiting for transfers between devices  138 us (24%)
  Pallas kernels  132 us (23%)
  starting transfers between devices  113 us (20%)
  matrix products  101 us (17%)
  local copies, waits for them, and re-layouts  41.3 us (7%)
  other arithmetic  41 us (7%)
    pallas_call x8, Pallas kernels, run(): pl.pallas_call(body, grid=grid, in_specs=[spec for _, spec in ins] + [pl....  107 us
    ppermute x48, waiting for transfers between devices, swap(): return lax.ppermute(value, axis, [(0, 1), (1, 0)])  103 us
    dot_general x18, matrix products, matmul(): lax.dot_general(left, right, (contract, ((), ())), preferred_element_type...  101 us
    ppermute x48, starting transfers between devices, swap(): return lax.ppermute(value, axis, [(0, 1), (1, 0)])  62.7 us
    ppermute x8, waiting for transfers between devices, column_hops(): lax.ppermute(leaving, ('y', 'zp'), pair)  24.9 us
    ppermute x2, starting transfers between devices, fetch(): lax.ppermute(piece, ('core', 'zp'), NEAR)  17.1 us
    unnamed x220, local copies, waits for them, and re-layouts  15.6 us
    pallas_call x4, Pallas kernels, joined(): pl.pallas_call(join_kernel, grid_spec=pltpu.PrefetchScalarGridSpec(num_sc...  11.7 us
  transfers between devices with their start and end apart: 72, of which 24 were waited for; matrix products, arithmetic and copies ran while one was open for 25% of the time, Pallas kernels for 23%

profile of v2, /device:TPU:0, one launch (start us, length us, event | category | flops | bytes accessed | tf_op | source)
XLA Modules:
  0.0 570.3 jit_solution(6789392656498943825)
XLA Ops:
  2.6 4.1 collective-permute-start.1
  19.1 5.1 collective-permute-done.2
  27.7 13.0 %collective-permute-start.12 = (bf16[192,1536]{1,0:T(8,128)(2,1)S(1)}, bf16[192,1536]{1,0:T(8,128)(2,1)}, u32[]{:S(2)}, u32[]{:S(2)}) collective-permute-start(bf16[192,1536]{1,0:T(8,128)(2,1)S(1)} %pad_maximum_fusion.9), channel_id=1, source_target_pairs={{0,2},{10,8},{2,10},{8,0},{1,3},{11,9},{3,11},{9,1},{4,6},{14,12},... | collective-permute-start | bytes 1769480 | tf_op jit(solution)/shard_map/ppermute | solution.py:790
  45.0 6.7 %collective-permute-start.7 = (bf16[1,256,1536]{2,1,0:T(8,128)(2,1)}, bf16[1,256,1536]{2,1,0:T(8,128)(2,1)S(1)}, u32[]{:S(2)}, u32[]{:S(2)}) collective-permute-start(bf16[1,256,1536]{2,1,0:T(8,128)(2,1)} %get-tuple-element.336.own), channel_id=1, source_target_pairs={{0,8},{8,0},{1,9},{9,1},{2,10},{10,2},{3,11},{11,3},{4,12},{12,4},... | collective-permute-start | bytes 2359304 | tf_op jit(solution)/shard_map/ppermute | solution.py:720
  52.6 6.7 %shard_map.280 = bf16[2,2,2,192,1152]{4,3,2,1,0:T(8,128)(2,1)} custom-call(s32[3]{0:T(128)S(1)} %pad_add_fusion.at_ref, bf16[2,192,1152]{2,1,0:T(8,128)(2,1)S(1)} %pad_maximum_fusion.7.first, bf16[2,192,1152]{2,1,0:T(8,128)(2,1)} %collective-permute-done.3.first_y, bf16[2,192,1152]{2,1,0:T(8,128)(2,1)S(1)} %pad_maximum_fusion.8.second, ...), custom_call_target="tpu_custom_call" | custom-call | bytes 221184 | tf_op jit(solution)/shard_map/pallas_call | solution.py:666
  59.4 10.9 %collective-permute-start.18 = (bf16[1,256,1536]{2,1,0:T(8,128)(2,1)S(1)}, bf16[1,256,1536]{2,1,0:T(8,128)(2,1)S(1)}, u32[]{:S(2)}, u32[]{:S(2)}) collective-permute-start(bf16[1,256,1536]{2,1,0:T(8,128)(2,1)S(1)} %get-tuple-element.158.own), channel_id=1, source_target_pairs={{0,1},{1,0},{2,3},{3,2},{4,5},{5,4},{6,7},{7,6},{8,9},{9,8},{10,11... | collective-permute-start | bytes 2359304 | tf_op jit(solution)/shard_map/ppermute | solution.py:720
  73.8 14.5 %collective-permute-done.10 = f32[8,768]{1,0:T(8,128)S(1)} collective-permute-done((f32[8,768]{1,0:T(8,128)S(1)}, f32[8,768]{1,0:T(8,128)S(1)}, u32[]{:S(2)}, u32[]{:S(2)}) %collective-permute-start.10) | collective-permute-done | bytes 24608 | tf_op jit(solution)/shard_map/ppermute | solution.py:720
  90.8 3.7 shard_map.279
  94.5 6.1 %convolution_convert_fusion.3.refs_0_.refs_2_.refs_9_.refs_10_.refs_12_ = bf16[2,512,1152]{2,1,0:T(8,128)(2,1)S(1)} fusion(bf16[2,512,1536]{2,1,0:T(8,128)(2,1)} %shard_map.279, bf16[1536,1152,1]{1,0,2:T(8,128)(2,1)S(1)} %bitcast.274), kind=kOutput, calls=%fused_computation.12 | convolution fusion | flops 3625058304 | bytes 9043968 | tf_op jit(solution)/shard_map/dot_general | solution.py:916
  101.8 2.4 collective-permute-done.15
  106.6 5.3 collective-permute-start.9
  111.9 2.3 shard_map.282
  114.2 7.2 %convolution_convert_fusion.2.refs_0_.refs_2_.refs_9_.refs_10_.refs_12_ = bf16[2,512,1152]{2,1,0:T(8,128)(2,1)S(1)} fusion(bf16[2,512,1536]{2,1,0:T(8,128)(2,1)} %shard_map.282, bf16[1536,1152,1]{1,0,2:T(8,128)(2,1)} %bitcast.273), kind=kOutput, calls=%fused_computation.11 | convolution fusion | flops 3625058304 | bytes 9043968 | tf_op jit(solution)/shard_map/dot_general | solution.py:916
  122.8 2.6 collective-permute-start.21
  125.4 9.1 %shard_map.281 = (bf16[2,512,1024]{2,1,0:T(8,128)(2,1)S(1)}, f32[2,512,128]{2,1,0:T(8,128)S(1)}, f32[2,512,128]{2,1,0:T(8,128)S(1)}, f32[2,128,768]{2,1,0:T(8,12...) custom-call(bf16[2,512,1152]{2,1,0:T(8,128)(2,1)} %copy-done.92, ...), custom_call_target="tpu_custom_call" | custom-call | flops 6000000000 | bytes 8000000 | tf_op jit(solution)/shard_map/pallas_call | solution.py:444
  134.6 5.3 collective-permute-start.11
  141.7 9.1 %shard_map.283 = (bf16[2,512,1024]{2,1,0:T(8,128)(2,1)S(1)}, f32[2,512,128]{2,1,0:T(8,128)S(1)}, f32[2,512,128]{2,1,0:T(8,128)S(1)}, f32[2,128,768]{2,1,0:T(8,12...) custom-call(bf16[2,512,1152]{2,1,0:T(8,128)(2,1)} %copy-done.91, ...), custom_call_target="tpu_custom_call" | custom-call | flops 6000000000 | bytes 8000000 | tf_op jit(solution)/shard_map/pallas_call | solution.py:444
  153.7 4.4 shard_map.284
  158.6 6.5 %convolution_convert_fusion.5.refs_6_.refs_2_ = bf16[2,512,768]{2,1,0:T(8,128)(2,1)} fusion(bf16[2,512,1536]{2,1,0:T(8,128)(2,1)} %shard_map.279, bf16[1536,1536]{1,0:T(8,128)(2,1)} %bitcast.257), kind=kOutput, calls=%fused_computation.37 | convolution fusion | flops 2416705536 | bytes 7077888 | tf_op jit(solution)/shard_map/dot_general | solution.py:916
  165.1 2.2 collective-permute-done.23.got
  170.7 3.4 slice.387
  175.7 5.3 convolution_convert_fusion.4.refs_6_.refs_2_
  185.1 3.5 shard_map.286
  188.6 6.3 %fusion.11.refs_7_.refs_10_.refs_3_ = f32[2,512,768]{2,1,0:T(8,128)} fusion(bf16[2,512,1536]{2,1,0:T(8,128)(2,1)} %shard_map.286, bf16[1536,768]{1,0:T(8,128)(2,1)S(1)} %copy-done.63), kind=kOutput, calls=%fused_computation.30 | convolution fusion | flops 2415919104 | bytes 8650752 | tf_op jit(solution)/shard_map/dot_general | solution.py:916
  194.9 11.0 %shard_map.287 = (f32[2,512,768]{2,1,0:T(8,128)}, bf16[2,512,768]{2,1,0:T(8,128)(2,1)S(1)}, bf16[2,2,128,768]{3,2,1,0:T(8,128)(2,1)S(1)}, f32[2,8,512]{2,1,0:T(8,128)S(1)}) custom-call(bf16[2,512,1024]{2,1,0:T(8,128)(2,1)} %copy-done.19, f32[2,512,128]{2,1,0:T(8,128)S(1)} %copy-done.25, f32[2,512,128]{2,1,0:T(8,128)S(1)} %copy-done.29, ...), custom_call_target="tpu_custom_call" | custom-call | flops 10000000000 | bytes 16000000 | tf_op jit(solution)/shard_map/pallas_call | solution.py:444
  210.4 2.2 shard_map.289
  212.6 7.1 %fusion.9.refs_7_.refs_11_.refs_3_ = f32[2,512,768]{2,1,0:T(8,128)} fusion(bf16[2,512,1536]{2,1,0:T(8,128)(2,1)} %shard_map.289, bf16[1536,1536]{1,0:T(8,128)(2,1)} %bitcast.260), kind=kOutput, calls=%fused_computation.28 | convolution fusion | flops 2415919104 | bytes 8650752 | tf_op jit(solution)/shard_map/dot_general | solution.py:916
  219.7 2.5 collective-permute-start.31
  222.2 2.9 convolution_convert_fusion.1.refs_9_
  226.5 3.5 collective-permute-done.31
  230.0 8.3 %shard_map.290 = (bf16[2,512,768]{2,1,0:T(8,128)(2,1)S(1)}, bf16[2,512,768]{2,1,0:T(8,128)(2,1)S(1)}, bf16[2,512,768]{2,1,0:T(8,128)(2,1)}, f32[2,128,768]{2,1,0...) custom-call(f32[2,512,768]{2,1,0:T(8,128)} %get-tuple-element.183.refs_0_.refs_4_, ...), custom_call_target="tpu_custom_call" | custom-call | flops 6000000000 | bytes 18000000 | tf_op jit(solution)/shard_map/pallas_call | solution.py:444
  241.2 11.1 %shard_map.291 = (f32[2,512,768]{2,1,0:T(8,128)}, bf16[2,512,768]{2,1,0:T(8,128)(2,1)S(1)}, bf16[2,2,128,768]{3,2,1,0:T(8,128)(2,1)S(1)}, f32[2,8,512]{2,1,0:T(8,128)S(1)}) custom-call(bf16[2,512,1024]{2,1,0:T(8,128)(2,1)} %copy-done.18, f32[2,512,128]{2,1,0:T(8,128)S(1)} %copy-done.23, f32[2,512,128]{2,1,0:T(8,128)S(1)} %copy-done.27, ...), custom_call_target="tpu_custom_call" | custom-call | flops 10000000000 | bytes 16000000 | tf_op jit(solution)/shard_map/pallas_call | solution.py:444
  252.4 4.3 convolution_bitcast_fusion.3
  256.9 2.9 convolution_convert_fusion.refs_9_
  263.5 8.3 %shard_map.292 = (bf16[2,512,768]{2,1,0:T(8,128)(2,1)S(1)}, bf16[2,512,768]{2,1,0:T(8,128)(2,1)S(1)}, bf16[2,512,768]{2,1,0:T(8,128)(2,1)}, f32[2,128,768]{2,1,0...) custom-call(f32[2,512,768]{2,1,0:T(8,128)} %get-tuple-element.199.refs_0_.refs_4_, ...), custom_call_target="tpu_custom_call" | custom-call | flops 6000000000 | bytes 18000000 | tf_op jit(solution)/shard_map/pallas_call | solution.py:444
  276.0 7.3 %convolution_bitcast_fusion.2 = f32[1536,768]{1,0:T(8,128)} fusion(bf16[2,512,1536]{2,1,0:T(8,128)(2,1)} %shard_map.286, bf16[2,512,768]{2,1,0:T(8,128)(2,1)} %get-tuple-element.209), kind=kOutput, calls=%fused_computation.13 | convolution fusion | flops 2415919104 | bytes 9437184 | tf_op jit(solution)/shard_map/dot_general | solution.py:916
  283.4 4.8 bitcast_add_fusion.1
  288.2 2.9 fusion.2
  291.2 4.8 fusion.40
  296.2 4.0 collective-permute-start.46
  303.4 6.2 %fusion.39.refs_17_ = f32[2,512,1536]{2,1,0:T(8,128)} fusion(bf16[2,512,768]{2,1,0:T(8,128)(2,1)S(1)} %get-tuple-element.224, bf16[1536,1536]{1,0:T(8,128)(2,1)} %bitcast.261), kind=kOutput, calls=%fused_computation.104 | convolution fusion | flops 2415919104 | bytes 10223616 | tf_op jit(solution)/shard_map/dot_general | solution.py:916
  310.2 24.9 %collective-permute-done.44.refs_8_ = bf16[2,128,768]{2,1,0:T(8,128)(2,1)S(1)} collective-permute-done((bf16[2,128,768]{2,1,0:T(8,128)(2,1)S(1)}, bf16[2,128,768]{2,1,0:T(8,128)(2,1)S(1)}, u32[]{:S(2)}, u32[]{:S(2)}) %collective-permute-start.44) | collective-permute-done | bytes 393248 | tf_op jit(solution)/shard_map/ppermute | solution.py:757
  342.6 25.3 %shard_map.295 = (bf16[2,512,1152]{2,1,0:T(8,128)(2,1)}, f32[2,8,1024]{2,1,0:T(8,128)S(1)}, f32[8,1024]{1,0:T(8,128)S(1)}, f32[8,128]{1,0:T(8,128)S(1)}, f32[8,768]{1,0:T(8,128)S(1)}) custom-call(bf16[2,512,1024]{2,1,0:T(8,128)(2,1)} %copy-done.19, f32[2,512,128]{2,1,0:T(8,128)S(1)} %copy-done.25, f32[2,512,128]{2,1,0:T(8,128)S(1)} %copy-done.30, ...), custom_call_target="tpu_custom_call" | custom-call | flops 32000000000 | bytes 24000000 | tf_op jit(solution)/shard_map/pallas_call | solution.py:444
  367.9 9.3 %collective-permute-done.39 = bf16[2,256,1536]{2,1,0:T(8,128)(2,1)} collective-permute-done((bf16[2,256,1536]{2,1,0:T(8,128)(2,1)}, bf16[2,256,1536]{2,1,0:T(8,128)(2,1)}, u32[]{:S(2)}, u32[]{:S(2)}) %collective-permute-start.39) | collective-permute-done | bytes 1572896 | tf_op jit(solution)/shard_map/ppermute | solution.py:720
  377.3 2.3 fusion.33
  382.1 5.5 collective-permute-done.47
  387.7 7.2 %add_convert_fusion.1 = bf16[2,512,1536]{2,1,0:T(8,128)(2,1)S(1)} fusion(f32[2,512,1536]{2,1,0:T(8,128)} %fusion.40, bf16[2,512,1152]{2,1,0:T(8,128)(2,1)S(1)} %fusion.46, bf16[1536,1152,1]{1,0,2:T(8,128)(2,1)S(1)} %bitcast.275), kind=kOutput, calls=%fused_computation.5 | convolution fusion | flops 3627024384 | bytes 15335424 | tf_op jit(solution)/shard_map/dot_general | solution.py:916
  396.9 8.0 %convolution_bitcast_fusion.1 = f32[1536,1152]{1,0:T(8,128)} fusion(bf16[2,512,1536]{2,1,0:T(8,128)(2,1)S(1)} %copy-done.54, bf16[2,512,1152]{2,1,0:T(8,128)(2,1)} %copy-done.86), kind=kOutput, calls=%fused_computation.2 | convolution fusion | flops 3623878656 | bytes 12582912 | tf_op jit(solution)/shard_map/dot_general | solution.py:916
  404.9 6.1 %collective-permute-done.49 = bf16[2,192,768]{2,1,0:T(8,128)(2,1)S(1)} collective-permute-done((bf16[2,192,768]{2,1,0:T(8,128)(2,1)S(1)}, bf16[2,192,768]{2,1,0:T(8,128)(2,1)S(1)}, u32[]{:S(2)}, u32[]{:S(2)}) %collective-permute-start.49) | collective-permute-done | bytes 589856 | tf_op jit(solution)/shard_map/ppermute | solution.py:720
  418.1 25.2 %shard_map.296 = (bf16[2,512,1152]{2,1,0:T(8,128)(2,1)}, f32[2,8,1024]{2,1,0:T(8,128)S(1)}, f32[8,1024]{1,0:T(8,128)S(1)}, f32[8,128]{1,0:T(8,128)S(1)}, f32[8,768]{1,0:T(8,128)S(1)}) custom-call(bf16[2,512,1024]{2,1,0:T(8,128)(2,1)} %copy-done.18, f32[2,512,128]{2,1,0:T(8,128)S(1)} %copy-done.23, f32[2,512,128]{2,1,0:T(8,128)S(1)} %copy-done.27, ...), custom_call_target="tpu_custom_call" | custom-call | flops 32000000000 | bytes 24000000 | tf_op jit(solution)/shard_map/pallas_call | solution.py:444
  446.6 3.0 fusion.16
  449.6 3.1 collective-permute-done.54
  452.9 6.7 %fusion.1 = bf16[1536,1152]{1,0:T(8,128)(2,1)S(1)} fusion(f32[1536,1152]{1,0:T(8,128)} %convolution_bitcast_fusion.1, bf16[2,512,1536]{2,1,0:T(8,128)(2,1)S(1)} %copy-done.52, bf16[2,512,1152]{2,1,0:T(8,128)(2,1)S(1)} %fusion.47), kind=kOutput, calls=%fused_computation.3 | convolution fusion | flops 3627417600 | bytes 16121856 | tf_op jit(solution)/shard_map/dot_general | solution.py:916
  463.2 4.5 add_convert_fusion
  475.8 18.6 %collective-permute-done.58 = bf16[1,2,192,1152]{3,2,1,0:T(8,128)(2,1)} collective-permute-done((bf16[1,2,192,1152]{3,2,1,0:T(8,128)(2,1)}, bf16[1,2,192,1152]{3,2,1,0:T(8,128)(2,1)}, u32[]{:S(2)}, u32[]{:S(2)}) %collective-permute-start.58) | collective-permute-done | bytes 884768 | tf_op jit(solution)/shard_map/ppermute | solution.py:720
  495.1 2.5 fusion.13
  506.4 13.5 %collective-permute-done.56 = bf16[256,1536]{1,0:T(8,128)(2,1)S(1)} collective-permute-done((bf16[256,1536]{1,0:T(8,128)(2,1)}, bf16[256,1536]{1,0:T(8,128)(2,1)S(1)}, u32[]{:S(2)}, u32[]{:S(2)}) %collective-permute-start.56) | collective-permute-done | bytes 786464 | tf_op jit(solution)/shard_map/ppermute | solution.py:720
  520.9 2.3 broadcast_select_fusion.2
  524.7 2.2 fusion.26
  528.4 2.6 collective-permute-done.61
  535.0 4.1 collective-permute-start.63
  541.0 7.2 %collective-permute-done.63 = f32[7460]{0:T(1024)S(1)} collective-permute-done((f32[7460]{0:T(1024)S(1)}, f32[7460]{0:T(1024)S(1)}, u32[]{:S(2)}, u32[]{:S(2)}) %collective-permute-start.63) | collective-permute-done | bytes 29872 | tf_op jit(solution)/shard_map/ppermute | solution.py:720
  553.3 9.0 %collective-permute-done.68 = f32[192,256]{1,0:T(8,128)S(1)} collective-permute-done((f32[192,256]{1,0:T(8,128)S(1)}, f32[192,256]{1,0:T(8,128)S(1)}, u32[]{:S(2)}, u32[]{:S(2)}) %collective-permute-start.68) | collective-permute-done | bytes 196640 | tf_op jit(solution)/shard_map/ppermute | solution.py:720
  566.9 2.3 collective-permute-done.69
  (486 shorter events, 131.5 us)
Async XLA Ops:
  2.6 13.2 %collective-permute-start.1 = (bf16[192,1152]{1,0:T(8,128)(2,1)S(1)}, bf16[192,1152]{1,0:T(8,128)(2,1)S(1)}, u32[]{:S(2)}, u32[]{:S(2)}) collective-permute-start(bf16[192,1152]{1,0:T(8,128)(2,1)S(1)} %concatenate.29), channel_id=1, source_target_pairs={{0,2},{10,8},{2,10},{8,0},{1,3},{11,9},{3,11},{9,1},{4,6},{14,12},... | collective-permute-start | bytes 1327112 | tf_op jit(solution)/shard_map/ppermute | solution.py:790
  6.7 9.1 %collective-permute-start.4 = (bf16[192,1152]{1,0:T(8,128)(2,1)S(1)}, bf16[192,1152]{1,0:T(8,128)(2,1)S(1)}, u32[]{:S(2)}, u32[]{:S(2)}) collective-permute-start(bf16[192,1152]{1,0:T(8,128)(2,1)S(1)} %concatenate.29), channel_id=1, source_target_pairs={{2,8},{8,2},{3,9},{9,3},{6,12},{12,6},{7,13},{13,7},{18,24},{24,18... | collective-permute-start | bytes 1327112 | tf_op jit(solution)/shard_map/ppermute | solution.py:790
  12.0 61.0 %collective-permute-start = (bf16[1,256,1536]{2,1,0:T(8,128)(2,1)}, bf16[1,256,1536]{2,1,0:T(8,128)(2,1)}, u32[]{:S(2)}, u32[]{:S(2)}) collective-permute-start(bf16[1,256,1536]{2,1,0:T(8,128)(2,1)} %get-tuple-element.336.own), channel_id=1, source_target_pairs={{0,1},{1,0},{2,3},{3,2},{4,5},{5,4},{6,7},{7,6},{8,9},{9,8},{10,11... | collective-permute-start | bytes 2359304 | tf_op jit(solution)/shard_map/ppermute | solution.py:720
  15.9 8.4 %collective-permute-start.2 = (bf16[192,1152]{1,0:T(8,128)(2,1)S(1)}, bf16[192,1152]{1,0:T(8,128)(2,1)S(1)}, u32[]{:S(2)}, u32[]{:S(2)}) collective-permute-start(bf16[192,1152]{1,0:T(8,128)(2,1)S(1)} %get-tuple-element.359), channel_id=1, source_target_pairs={{0,16},{16,0},{1,17},{17,1},{2,18},{18,2},{3,19},{19,3},{4,20},{20... | collective-permute-start | bytes 1327112 | tf_op jit(solution)/shard_map/ppermute | solution.py:720
  17.5 8.5 %collective-permute-start.5 = (bf16[192,1152]{1,0:T(8,128)(2,1)S(1)}, bf16[192,1152]{1,0:T(8,128)(2,1)S(1)}, u32[]{:S(2)}, u32[]{:S(2)}) collective-permute-start(bf16[192,1152]{1,0:T(8,128)(2,1)S(1)} %get-tuple-element.358), channel_id=1, source_target_pairs={{0,4},{4,0},{1,5},{5,1},{2,6},{6,2},{3,7},{7,3},{8,12},{12,8},{9,1... | collective-permute-start | bytes 1327112 | tf_op jit(solution)/shard_map/ppermute | solution.py:720
  24.4 20.6 %collective-permute-start.3 = (bf16[2,192,1152]{2,1,0:T(8,128)(2,1)S(1)}, bf16[2,192,1152]{2,1,0:T(8,128)(2,1)}, u32[]{:S(2)}, u32[]{:S(2)}) collective-permute-start(bf16[2,192,1152]{2,1,0:T(8,128)(2,1)S(1)} %pad_maximum_fusion.7.first), channel_id=1, source_target_pairs={{0,4},{4,0},{1,5},{5,1},{2,6},{6,2},{3,7},{7,3},{8,12},{12,8},{9,1... | collective-permute-start | bytes 2654216 | tf_op jit(solution)/shard_map/ppermute | solution.py:720
  26.1 25.6 %collective-permute-start.6 = (bf16[2,192,1152]{2,1,0:T(8,128)(2,1)S(1)}, bf16[2,192,1152]{2,1,0:T(8,128)(2,1)}, u32[]{:S(2)}, u32[]{:S(2)}) collective-permute-start(bf16[2,192,1152]{2,1,0:T(8,128)(2,1)S(1)} %pad_maximum_fusion.8.second), channel_id=1, source_target_pairs={{0,16},{16,0},{1,17},{17,1},{2,18},{18,2},{3,19},{19,3},{4,20},{20... | collective-permute-start | bytes 2654216 | tf_op jit(solution)/shard_map/ppermute | solution.py:720
  27.7 31.7 %collective-permute-start.12 = (bf16[192,1536]{1,0:T(8,128)(2,1)S(1)}, bf16[192,1536]{1,0:T(8,128)(2,1)}, u32[]{:S(2)}, u32[]{:S(2)}) collective-permute-start(bf16[192,1536]{1,0:T(8,128)(2,1)S(1)} %pad_maximum_fusion.9), channel_id=1, source_target_pairs={{0,2},{10,8},{2,10},{8,0},{1,3},{11,9},{3,11},{9,1},{4,6},{14,12},... | collective-permute-start | bytes 1769480 | tf_op jit(solution)/shard_map/ppermute | solution.py:790
  40.6 29.6 %collective-permute-start.13 = (bf16[192,1536]{1,0:T(8,128)(2,1)S(1)}, bf16[192,1536]{1,0:T(8,128)(2,1)}, u32[]{:S(2)}, u32[]{:S(2)}) collective-permute-start(bf16[192,1536]{1,0:T(8,128)(2,1)S(1)} %pad_maximum_fusion.9), channel_id=1, source_target_pairs={{2,8},{8,2},{3,9},{9,3},{6,12},{12,6},{7,13},{13,7},{18,24},{24,18... | collective-permute-start | bytes 1769480 | tf_op jit(solution)/shard_map/ppermute | solution.py:790
  45.0 43.5 %collective-permute-start.7 = (bf16[1,256,1536]{2,1,0:T(8,128)(2,1)}, bf16[1,256,1536]{2,1,0:T(8,128)(2,1)S(1)}, u32[]{:S(2)}, u32[]{:S(2)}) collective-permute-start(bf16[1,256,1536]{2,1,0:T(8,128)(2,1)} %get-tuple-element.336.own), channel_id=1, source_target_pairs={{0,8},{8,0},{1,9},{9,1},{2,10},{10,2},{3,11},{11,3},{4,12},{12,4},... | collective-permute-start | bytes 2359304 | tf_op jit(solution)/shard_map/ppermute | solution.py:720
  51.6 60.3 %collective-permute-start.19 = (bf16[1,256,1536]{2,1,0:T(8,128)(2,1)S(1)}, bf16[1,256,1536]{2,1,0:T(8,128)(2,1)S(1)}, u32[]{:S(2)}, u32[]{:S(2)}) collective-permute-start(bf16[1,256,1536]{2,1,0:T(8,128)(2,1)S(1)} %get-tuple-element.158.own), channel_id=1, source_target_pairs={{0,8},{8,0},{1,9},{9,1},{2,10},{10,2},{3,11},{11,3},{4,12},{12,4},... | collective-permute-start | bytes 2359304 | tf_op jit(solution)/shard_map/ppermute | solution.py:720
  59.4 41.3 %collective-permute-start.18 = (bf16[1,256,1536]{2,1,0:T(8,128)(2,1)S(1)}, bf16[1,256,1536]{2,1,0:T(8,128)(2,1)S(1)}, u32[]{:S(2)}, u32[]{:S(2)}) collective-permute-start(bf16[1,256,1536]{2,1,0:T(8,128)(2,1)S(1)} %get-tuple-element.158.own), channel_id=1, source_target_pairs={{0,1},{1,0},{2,3},{3,2},{4,5},{5,4},{6,7},{7,6},{8,9},{9,8},{10,11... | collective-permute-start | bytes 2359304 | tf_op jit(solution)/shard_map/ppermute | solution.py:720
  70.3 18.0 %collective-permute-start.10 = (f32[8,768]{1,0:T(8,128)S(1)}, f32[8,768]{1,0:T(8,128)S(1)}, u32[]{:S(2)}, u32[]{:S(2)}) collective-permute-start(f32[8,768]{1,0:T(8,128)S(1)} %maximum_maximum_fusion), channel_id=1, source_target_pairs={{0,2},{2,0},{1,3},{3,1},{4,6},{6,4},{5,7},{7,5},{8,10},{10,8},{9,1... | collective-permute-start | bytes 73736 | tf_op jit(solution)/shard_map/ppermute | solution.py:720
  73.1 28.7 %collective-permute-start.14 = (bf16[192,1536]{1,0:T(8,128)(2,1)S(1)}, bf16[192,1536]{1,0:T(8,128)(2,1)S(1)}, u32[]{:S(2)}, u32[]{:S(2)}) collective-permute-start(bf16[192,1536]{1,0:T(8,128)(2,1)S(1)} %get-tuple-element.357), channel_id=1, source_target_pairs={{0,16},{16,0},{1,17},{17,1},{2,18},{18,2},{3,19},{19,3},{4,20},{20... | collective-permute-start | bytes 1769480 | tf_op jit(solution)/shard_map/ppermute | solution.py:720
  88.5 15.8 %collective-permute-start.15 = (bf16[192,1536]{1,0:T(8,128)(2,1)S(1)}, bf16[192,1536]{1,0:T(8,128)(2,1)S(1)}, u32[]{:S(2)}, u32[]{:S(2)}) collective-permute-start(bf16[192,1536]{1,0:T(8,128)(2,1)S(1)} %get-tuple-element.356), channel_id=1, source_target_pairs={{0,4},{4,0},{1,5},{5,1},{2,6},{6,2},{3,7},{7,3},{8,12},{12,8},{9,1... | collective-permute-start | bytes 1769480 | tf_op jit(solution)/shard_map/ppermute | solution.py:720
  100.7 11.2 %collective-permute-start.20 = (bf16[1,256,1536]{2,1,0:T(8,128)(2,1)S(1)}, bf16[1,256,1536]{2,1,0:T(8,128)(2,1)S(1)}, u32[]{:S(2)}, u32[]{:S(2)}) collective-permute-start(bf16[1,256,1536]{2,1,0:T(8,128)(2,1)S(1)} %collective-permute-done.18.got), channel_id=1, source_target_pairs={{0,8},{8,0},{1,9},{9,1},{2,10},{10,2},{3,11},{11,3},{4,12},{12,4},... | collective-permute-start | bytes 2359304 | tf_op jit(solution)/shard_map/ppermute | solution.py:720
  104.4 47.3 %collective-permute-start.17 = (bf16[2,192,1536]{2,1,0:T(8,128)(2,1)S(1)}, bf16[2,192,1536]{2,1,0:T(8,128)(2,1)S(1)}, u32[]{:S(2)}, u32[]{:S(2)}) collective-permute-start(bf16[2,192,1536]{2,1,0:T(8,128)(2,1)S(1)} %pad_maximum_fusion.4.second), channel_id=1, source_target_pairs={{0,16},{16,0},{1,17},{17,1},{2,18},{18,2},{3,19},{19,3},{4,20},{20... | collective-permute-start | bytes 3538952 | tf_op jit(solution)/shard_map/ppermute | solution.py:720
  106.0 47.7 %collective-permute-start.16 = (bf16[2,192,1536]{2,1,0:T(8,128)(2,1)S(1)}, bf16[2,192,1536]{2,1,0:T(8,128)(2,1)S(1)}, u32[]{:S(2)}, u32[]{:S(2)}) collective-permute-start(bf16[2,192,1536]{2,1,0:T(8,128)(2,1)S(1)} %pad_maximum_fusion.3.first), channel_id=1, source_target_pairs={{0,4},{4,0},{1,5},{5,1},{2,6},{6,2},{3,7},{7,3},{8,12},{12,8},{9,1... | collective-permute-start | bytes 3538952 | tf_op jit(solution)/shard_map/ppermute | solution.py:720
  106.6 18.8 %collective-permute-start.9 = (bf16[2,16,1024]{2,1,0:T(8,128)(2,1)S(1)}, bf16[2,16,1024]{2,1,0:T(8,128)(2,1)S(1)}, u32[]{:S(2)}, u32[]{:S(2)}) collective-permute-start(bf16[2,16,1024]{2,1,0:T(8,128)(2,1)S(1)} %slice.379), channel_id=1, source_target_pairs={{0,2},{2,4},{4,6},{1,3},{3,5},{5,7},{8,10},{10,12},{12,14},{9,11},... | collective-permute-start | bytes 196616 | tf_op jit(solution)/shard_map/ppermute | solution.py:747
  122.8 17.2 %collective-permute-start.21 = (bf16[2,16,1024]{2,1,0:T(8,128)(2,1)S(1)}, bf16[2,16,1024]{2,1,0:T(8,128)(2,1)S(1)}, u32[]{:S(2)}, u32[]{:S(2)}) collective-permute-start(bf16[2,16,1024]{2,1,0:T(8,128)(2,1)S(1)} %slice.385), channel_id=1, source_target_pairs={{0,2},{2,4},{4,6},{1,3},{3,5},{5,7},{8,10},{10,12},{12,14},{9,11},... | collective-permute-start | bytes 196616 | tf_op jit(solution)/shard_map/ppermute | solution.py:747
  134.6 23.5 %collective-permute-start.11 = (bf16[2,144,768]{2,1,0:T(8,128)(2,1)S(1)}, bf16[2,144,768]{2,1,0:T(8,128)(2,1)S(1)}, u32[]{:S(2)}, u32[]{:S(2)}) collective-permute-start(bf16[2,144,768]{2,1,0:T(8,128)(2,1)S(1)} %get-tuple-element.152.refs_6_), channel_id=1, source_target_pairs={{0,2},{1,3},{4,6},{5,7},{8,10},{9,11},{12,14},{13,15},{16,18},{17,... | collective-permute-start | bytes 1327112 | tf_op jit(solution)/shard_map/ppermute | solution.py:751
  139.9 43.9 %collective-permute-start.24 = (bf16[2,256,1536]{2,1,0:T(8,128)(2,1)}, bf16[2,256,1536]{2,1,0:T(8,128)(2,1)}, u32[]{:S(2)}, u32[]{:S(2)}) collective-permute-start(bf16[2,256,1536]{2,1,0:T(8,128)(2,1)} %param.17), channel_id=1, source_target_pairs={{0,8},{8,0},{1,9},{9,1},{2,10},{10,2},{3,11},{11,3},{4,12},{12,4},... | collective-permute-start | bytes 4718600 | tf_op jit(solution)/shard_map/ppermute | solution.py:720
  141.6 25.8 %collective-permute-start.23 = (bf16[1,256,1536]{2,1,0:T(8,128)(2,1)S(1)}, bf16[1,256,1536]{2,1,0:T(8,128)(2,1)S(1)}, u32[]{:S(2)}, u32[]{:S(2)}) collective-permute-start(bf16[1,256,1536]{2,1,0:T(8,128)(2,1)S(1)} %get-tuple-element.347.own), channel_id=1, source_target_pairs={{0,1},{1,0},{2,3},{3,2},{4,5},{5,4},{6,7},{7,6},{8,9},{9,8},{10,11... | collective-permute-start | bytes 2359304 | tf_op jit(solution)/shard_map/ppermute | solution.py:720
  151.7 30.2 %collective-permute-start.28 = (bf16[1,256,1536]{2,1,0:T(8,128)(2,1)S(1)}, bf16[1,256,1536]{2,1,0:T(8,128)(2,1)S(1)}, u32[]{:S(2)}, u32[]{:S(2)}) collective-permute-start(bf16[1,256,1536]{2,1,0:T(8,128)(2,1)S(1)} %get-tuple-element.346.own), channel_id=1, source_target_pairs={{0,1},{1,0},{2,3},{3,2},{4,5},{5,4},{6,7},{7,6},{8,9},{9,8},{10,11... | collective-permute-start | bytes 2359304 | tf_op jit(solution)/shard_map/ppermute | solution.py:720
  167.4 16.5 %collective-permute-start.25 = (bf16[1,256,1536]{2,1,0:T(8,128)(2,1)S(1)}, bf16[1,256,1536]{2,1,0:T(8,128)(2,1)}, u32[]{:S(2)}, u32[]{:S(2)}) collective-permute-start(bf16[1,256,1536]{2,1,0:T(8,128)(2,1)S(1)} %collective-permute-done.23.got), channel_id=1, source_target_pairs={{0,8},{8,0},{1,9},{9,1},{2,10},{10,2},{3,11},{11,3},{4,12},{12,4},... | collective-permute-start | bytes 2359304 | tf_op jit(solution)/shard_map/ppermute | solution.py:720
  174.1 20.7 %collective-permute-start.26 = (bf16[2,128,768]{2,1,0:T(8,128)(2,1)S(1)}, bf16[2,128,768]{2,1,0:T(8,128)(2,1)S(1)}, u32[]{:S(2)}, u32[]{:S(2)}) collective-permute-start(bf16[2,128,768]{2,1,0:T(8,128)(2,1)S(1)} %copy-done.5), channel_id=1, source_target_pairs={{2,6},{3,7},{10,14},{11,15},{18,22},{19,23},{26,30},{27,31}} | collective-permute-start | bytes 1179656 | tf_op jit(solution)/shard_map/ppermute | solution.py:757
  175.0 19.9 %collective-permute-start.22 = (bf16[2,128,768]{2,1,0:T(8,128)(2,1)S(1)}, bf16[2,128,768]{2,1,0:T(8,128)(2,1)S(1)}, u32[]{:S(2)}, u32[]{:S(2)}) collective-permute-start(bf16[2,128,768]{2,1,0:T(8,128)(2,1)S(1)} %copy-done.5), channel_id=1, source_target_pairs={{2,4},{3,5},{10,12},{11,13},{18,20},{19,21},{26,28},{27,29}} | collective-permute-start | bytes 1179656 | tf_op jit(solution)/shard_map/ppermute | solution.py:757
  181.8 25.0 %collective-permute-start.30 = (bf16[2,144,768]{2,1,0:T(8,128)(2,1)S(1)}, bf16[2,144,768]{2,1,0:T(8,128)(2,1)S(1)}, u32[]{:S(2)}, u32[]{:S(2)}) collective-permute-start(bf16[2,144,768]{2,1,0:T(8,128)(2,1)S(1)} %copy-done.13), channel_id=1, source_target_pairs={{0,2},{1,3},{4,6},{5,7},{8,10},{9,11},{12,14},{13,15},{16,18},{17,... | collective-permute-start | bytes 1327112 | tf_op jit(solution)/shard_map/ppermute | solution.py:751
  183.8 24.8 %collective-permute-start.29 = (bf16[1,256,1536]{2,1,0:T(8,128)(2,1)S(1)}, bf16[1,256,1536]{2,1,0:T(8,128)(2,1)S(1)}, u32[]{:S(2)}, u32[]{:S(2)}) collective-permute-start(bf16[1,256,1536]{2,1,0:T(8,128)(2,1)S(1)} %collective-permute-done.28.got), channel_id=1, source_target_pairs={{0,8},{8,0},{1,9},{9,1},{2,10},{10,2},{3,11},{11,3},{4,12},{12,4},... | collective-permute-start | bytes 2359304 | tf_op jit(solution)/shard_map/ppermute | solution.py:720
  207.2 33.9 %collective-permute-start.35 = (bf16[2,128,768]{2,1,0:T(8,128)(2,1)S(1)}, bf16[2,128,768]{2,1,0:T(8,128)(2,1)S(1)}, u32[]{:S(2)}, u32[]{:S(2)}) collective-permute-start(bf16[2,128,768]{2,1,0:T(8,128)(2,1)S(1)} %shard_map.288), channel_id=1, source_target_pairs={{2,6},{3,7},{10,14},{11,15},{18,22},{19,23},{26,30},{27,31}} | collective-permute-start | bytes 1179656 | tf_op jit(solution)/shard_map/ppermute | solution.py:757
  207.9 33.2 %collective-permute-start.34 = (bf16[2,128,768]{2,1,0:T(8,128)(2,1)S(1)}, bf16[2,128,768]{2,1,0:T(8,128)(2,1)S(1)}, u32[]{:S(2)}, u32[]{:S(2)}) collective-permute-start(bf16[2,128,768]{2,1,0:T(8,128)(2,1)S(1)} %shard_map.288), channel_id=1, source_target_pairs={{2,4},{3,5},{10,12},{11,13},{18,20},{19,21},{26,28},{27,29}} | collective-permute-start | bytes 1179656 | tf_op jit(solution)/shard_map/ppermute | solution.py:757
  209.8 9.9 %collective-permute-start.27 = (f32[2,8,512]{2,1,0:T(8,128)S(1)}, f32[2,8,512]{2,1,0:T(8,128)S(1)}, u32[]{:S(2)}, u32[]{:S(2)}) collective-permute-start(f32[2,8,512]{2,1,0:T(8,128)S(1)} %get-tuple-element.178), channel_id=1, source_target_pairs={{0,8},{8,0},{1,9},{9,1},{2,10},{10,2},{3,11},{11,3},{4,12},{12,4},... | collective-permute-start | bytes 98312 | tf_op jit(solution)/shard_map/ppermute | solution.py:720
  219.7 10.3 %collective-permute-start.31 = (f32[2,8,512]{2,1,0:T(8,128)S(1)}, f32[2,8,512]{2,1,0:T(8,128)S(1)}, u32[]{:S(2)}, u32[]{:S(2)}) collective-permute-start(f32[2,8,512]{2,1,0:T(8,128)S(1)} %reverse_add_fusion.1), channel_id=1, source_target_pairs={{0,1},{1,0},{2,3},{3,2},{4,5},{5,4},{6,7},{7,6},{8,9},{9,8},{10,11... | collective-permute-start | bytes 98312 | tf_op jit(solution)/shard_map/ppermute | solution.py:720
  226.5 108.6 %collective-permute-start.32 = (bf16[512,1536]{1,0:T(8,128)(2,1)}, bf16[512,1536]{1,0:T(8,128)(2,1)}, u32[]{:S(2)}, u32[]{:S(2)}) collective-permute-start(bf16[512,1536]{1,0:T(8,128)(2,1)} %slice_bitcast_fusion.7), channel_id=1, source_target_pairs={{0,8},{8,0},{1,9},{9,1},{2,10},{10,2},{3,11},{11,3},{4,12},{12,4},... | collective-permute-start | bytes 4718600 | tf_op jit(solution)/shard_map/ppermute | solution.py:720
  239.6 32.2 %collective-permute-start.33 = (bf16[2,144,768]{2,1,0:T(8,128)(2,1)S(1)}, bf16[2,144,768]{2,1,0:T(8,128)(2,1)S(1)}, u32[]{:S(2)}, u32[]{:S(2)}) collective-permute-start(bf16[2,144,768]{2,1,0:T(8,128)(2,1)S(1)} %get-tuple-element.193.refs_10_), channel_id=1, source_target_pairs={{2,0},{3,1},{6,4},{7,5},{10,8},{11,9},{14,12},{15,13},{18,16},{19,... | collective-permute-start | bytes 1327112 | tf_op jit(solution)/shard_map/ppermute | solution.py:751
  261.1 76.0 %collective-permute-start.38 = (bf16[512,1536]{1,0:T(8,128)(2,1)}, bf16[512,1536]{1,0:T(8,128)(2,1)}, u32[]{:S(2)}, u32[]{:S(2)}) collective-permute-start(bf16[512,1536]{1,0:T(8,128)(2,1)} %slice_bitcast_fusion.5), channel_id=1, source_target_pairs={{0,8},{8,0},{1,9},{9,1},{2,10},{10,2},{3,11},{11,3},{4,12},{12,4},... | collective-permute-start | bytes 4718600 | tf_op jit(solution)/shard_map/ppermute | solution.py:720
  272.3 23.8 %collective-permute-start.41 = (bf16[2,128,768]{2,1,0:T(8,128)(2,1)S(1)}, bf16[2,128,768]{2,1,0:T(8,128)(2,1)S(1)}, u32[]{:S(2)}, u32[]{:S(2)}) collective-permute-start(bf16[2,128,768]{2,1,0:T(8,128)(2,1)S(1)} %shard_map.293), channel_id=1, source_target_pairs={{4,0},{5,1},{12,8},{13,9},{20,16},{21,17},{28,24},{29,25}} | collective-permute-start | bytes 1179656 | tf_op jit(solution)/shard_map/ppermute | solution.py:757
  273.6 22.5 %collective-permute-start.40 = (bf16[2,128,768]{2,1,0:T(8,128)(2,1)S(1)}, bf16[2,128,768]{2,1,0:T(8,128)(2,1)S(1)}, u32[]{:S(2)}, u32[]{:S(2)}) collective-permute-start(bf16[2,128,768]{2,1,0:T(8,128)(2,1)S(1)} %shard_map.293), channel_id=1, source_target_pairs={{4,2},{5,3},{12,10},{13,11},{20,18},{21,19},{28,26},{29,27}} | collective-permute-start | bytes 1179656 | tf_op jit(solution)/shard_map/ppermute | solution.py:757
  274.2 26.3 %collective-permute-start.42 = (bf16[2,144,768]{2,1,0:T(8,128)(2,1)S(1)}, bf16[2,144,768]{2,1,0:T(8,128)(2,1)S(1)}, u32[]{:S(2)}, u32[]{:S(2)}) collective-permute-start(bf16[2,144,768]{2,1,0:T(8,128)(2,1)S(1)} %get-tuple-element.222), channel_id=1, source_target_pairs={{2,0},{3,1},{6,4},{7,5},{10,8},{11,9},{14,12},{15,13},{18,16},{19,... | collective-permute-start | bytes 1327112 | tf_op jit(solution)/shard_map/ppermute | solution.py:751
  296.2 71.7 %collective-permute-start.46 = (bf16[2,2,192,768]{3,2,1,0:T(8,128)(2,1)S(1)}, bf16[2,2,192,768]{3,2,1,0:T(8,128)(2,1)S(1)}, u32[]{:S(2)}, u32[]{:S(2)}) collective-permute-start(bf16[2,2,192,768]{3,2,1,0:T(8,128)(2,1)S(1)} %pad_maximum_fusion.6.refs_20_), channel_id=1, source_target_pairs={{0,4},{4,0},{1,5},{5,1},{2,6},{6,2},{3,7},{7,3},{8,12},{12,8},{9,1... | collective-permute-start | bytes 3538952 | tf_op jit(solution)/shard_map/ppermute | solution.py:720
  301.0 8.6 %collective-permute-start.43 = (bf16[2,128,768]{2,1,0:T(8,128)(2,1)S(1)}, bf16[2,128,768]{2,1,0:T(8,128)(2,1)S(1)}, u32[]{:S(2)}, u32[]{:S(2)}) collective-permute-start(bf16[2,128,768]{2,1,0:T(8,128)(2,1)S(1)} %shard_map.294), channel_id=1, source_target_pairs={{4,2},{5,3},{12,10},{13,11},{20,18},{21,19},{28,26},{29,27}} | collective-permute-start | bytes 1179656 | tf_op jit(solution)/shard_map/ppermute | solution.py:757
  301.8 33.2 %collective-permute-start.44 = (bf16[2,128,768]{2,1,0:T(8,128)(2,1)S(1)}, bf16[2,128,768]{2,1,0:T(8,128)(2,1)S(1)}, u32[]{:S(2)}, u32[]{:S(2)}) collective-permute-start(bf16[2,128,768]{2,1,0:T(8,128)(2,1)S(1)} %shard_map.294), channel_id=1, source_target_pairs={{4,0},{5,1},{12,8},{13,9},{20,16},{21,17},{28,24},{29,25}} | collective-permute-start | bytes 1179656 | tf_op jit(solution)/shard_map/ppermute | solution.py:757
  309.6 58.3 %collective-permute-start.45 = (bf16[2,2,192,768]{3,2,1,0:T(8,128)(2,1)S(1)}, bf16[2,2,192,768]{3,2,1,0:T(8,128)(2,1)}, u32[]{:S(2)}, u32[]{:S(2)}) collective-permute-start(bf16[2,2,192,768]{3,2,1,0:T(8,128)(2,1)S(1)} %pad_maximum_fusion.5.refs_19_), channel_id=1, source_target_pairs={{0,16},{16,0},{1,17},{17,1},{2,18},{18,2},{3,19},{19,3},{4,20},{20... | collective-permute-start | bytes 3538952 | tf_op jit(solution)/shard_map/ppermute | solution.py:720
  340.9 36.4 %collective-permute-start.39 = (bf16[2,256,1536]{2,1,0:T(8,128)(2,1)}, bf16[2,256,1536]{2,1,0:T(8,128)(2,1)}, u32[]{:S(2)}, u32[]{:S(2)}) collective-permute-start(bf16[2,256,1536]{2,1,0:T(8,128)(2,1)} %pad_maximum_fusion.1.refs_18_), channel_id=1, source_target_pairs={{0,1},{1,0},{2,3},{3,2},{4,5},{5,4},{6,7},{7,6},{8,9},{9,8},{10,11... | collective-permute-start | bytes 4718600 | tf_op jit(solution)/shard_map/ppermute | solution.py:720
  379.8 25.1 %collective-permute-start.50 = (bf16[2,192,768]{2,1,0:T(8,128)(2,1)S(1)}, bf16[2,192,768]{2,1,0:T(8,128)(2,1)S(1)}, u32[]{:S(2)}, u32[]{:S(2)}) collective-permute-start(bf16[2,192,768]{2,1,0:T(8,128)(2,1)S(1)} %pad_maximum_fusion.11), channel_id=1, source_target_pairs={{0,16},{16,0},{1,17},{17,1},{2,18},{18,2},{3,19},{19,3},{4,20},{20... | collective-permute-start | bytes 1769480 | tf_op jit(solution)/shard_map/ppermute | solution.py:720
  380.4 7.2 %collective-permute-start.47 = (f32[2,8,1024]{2,1,0:T(8,128)S(1)}, f32[2,8,1024]{2,1,0:T(8,128)S(1)}, u32[]{:S(2)}, u32[]{:S(2)}) collective-permute-start(f32[2,8,1024]{2,1,0:T(8,128)S(1)} %get-tuple-element.233), channel_id=1, source_target_pairs={{2,0},{4,2},{6,4},{3,1},{5,3},{7,5},{10,8},{12,10},{14,12},{11,9},... | collective-permute-start | bytes 196616 | tf_op jit(solution)/shard_map/ppermute | solution.py:747
  395.1 17.2 %collective-permute-start.48 = (bf16[512,1536]{1,0:T(8,128)(2,1)S(1)}, bf16[512,1536]{1,0:T(8,128)(2,1)S(1)}, u32[]{:S(2)}, u32[]{:S(2)}) collective-permute-start(bf16[512,1536]{1,0:T(8,128)(2,1)S(1)} %slice_bitcast_fusion.3), channel_id=1, source_target_pairs={{0,8},{8,0},{1,9},{9,1},{2,10},{10,2},{3,11},{11,3},{4,12},{12,4},... | collective-permute-start | bytes 4718600 | tf_op jit(solution)/shard_map/ppermute | solution.py:720
  395.3 15.8 %collective-permute-start.49 = (bf16[2,192,768]{2,1,0:T(8,128)(2,1)S(1)}, bf16[2,192,768]{2,1,0:T(8,128)(2,1)S(1)}, u32[]{:S(2)}, u32[]{:S(2)}) collective-permute-start(bf16[2,192,768]{2,1,0:T(8,128)(2,1)S(1)} %pad_maximum_fusion.10), channel_id=1, source_target_pairs={{0,4},{4,0},{1,5},{5,1},{2,6},{6,2},{3,7},{7,3},{8,12},{12,8},{9,1... | collective-permute-start | bytes 1769480 | tf_op jit(solution)/shard_map/ppermute | solution.py:720
  411.5 31.8 %collective-permute-start.52 = (bf16[2,192,768]{2,1,0:T(8,128)(2,1)S(1)}, bf16[2,192,768]{2,1,0:T(8,128)(2,1)S(1)}, u32[]{:S(2)}, u32[]{:S(2)}) collective-permute-start(bf16[2,192,768]{2,1,0:T(8,128)(2,1)S(1)} %get-tuple-element.351.refs_19_), channel_id=1, source_target_pairs={{2,0},{8,10},{10,2},{0,8},{3,1},{9,11},{11,3},{1,9},{6,4},{12,14},... | collective-permute-start | bytes 1769480 | tf_op jit(solution)/shard_map/ppermute | solution.py:861
  411.6 31.7 %collective-permute-start.53 = (bf16[2,192,768]{2,1,0:T(8,128)(2,1)S(1)}, bf16[2,192,768]{2,1,0:T(8,128)(2,1)S(1)}, u32[]{:S(2)}, u32[]{:S(2)}) collective-permute-start(bf16[2,192,768]{2,1,0:T(8,128)(2,1)S(1)} %get-tuple-element.350.refs_20_), channel_id=1, source_target_pairs={{2,8},{8,2},{3,9},{9,3},{6,12},{12,6},{7,13},{13,7},{18,24},{24,18... | collective-permute-start | bytes 1769480 | tf_op jit(solution)/shard_map/ppermute | solution.py:862
  412.8 31.2 %collective-permute-start.51 = (bf16[256,1536]{1,0:T(8,128)(2,1)S(1)}, bf16[256,1536]{1,0:T(8,128)(2,1)S(1)}, u32[]{:S(2)}, u32[]{:S(2)}) collective-permute-start(bf16[256,1536]{1,0:T(8,128)(2,1)S(1)} %get-tuple-element.345.refs_17_), channel_id=1, source_target_pairs={{0,1},{1,0},{2,3},{3,2},{4,5},{5,4},{6,7},{7,6},{8,9},{9,8},{10,11... | collective-permute-start | bytes 2359304 | tf_op jit(solution)/shard_map/ppermute | solution.py:720
  444.8 8.0 %collective-permute-start.54 = (f32[2,8,1024]{2,1,0:T(8,128)S(1)}, f32[2,8,1024]{2,1,0:T(8,128)S(1)}, u32[]{:S(2)}, u32[]{:S(2)}) collective-permute-start(f32[2,8,1024]{2,1,0:T(8,128)S(1)} %get-tuple-element.255), channel_id=1, source_target_pairs={{2,0},{4,2},{6,4},{3,1},{5,3},{7,5},{10,8},{12,10},{14,12},{11,9},... | collective-permute-start | bytes 196616 | tf_op jit(solution)/shard_map/ppermute | solution.py:747
  470.8 26.8 %collective-permute-start.55 = (bf16[512,1536]{1,0:T(8,128)(2,1)}, bf16[512,1536]{1,0:T(8,128)(2,1)}, u32[]{:S(2)}, u32[]{:S(2)}) collective-permute-start(bf16[512,1536]{1,0:T(8,128)(2,1)} %slice_bitcast_fusion.1), channel_id=1, source_target_pairs={{0,8},{8,0},{1,9},{9,1},{2,10},{10,2},{3,11},{11,3},{4,12},{12,4},... | collective-permute-start | bytes 4718600 | tf_op jit(solution)/shard_map/ppermute | solution.py:720
  472.5 21.9 %collective-permute-start.58 = (bf16[1,2,192,1152]{3,2,1,0:T(8,128)(2,1)}, bf16[1,2,192,1152]{3,2,1,0:T(8,128)(2,1)}, u32[]{:S(2)}, u32[]{:S(2)}) collective-permute-start(bf16[1,2,192,1152]{3,2,1,0:T(8,128)(2,1)} %dynamic-slice_bitcast_fusion), channel_id=1, source_target_pairs={{0,4},{4,0},{1,5},{5,1},{2,6},{6,2},{3,7},{7,3},{8,12},{12,8},{9,1... | collective-permute-start | bytes 2654216 | tf_op jit(solution)/shard_map/ppermute | solution.py:720
  473.2 21.9 %collective-permute-start.57 = (bf16[1,2,192,1152]{3,2,1,0:T(8,128)(2,1)S(1)}, bf16[1,2,192,1152]{3,2,1,0:T(8,128)(2,1)}, u32[]{:S(2)}, u32[]{:S(2)}) collective-permute-start(bf16[1,2,192,1152]{3,2,1,0:T(8,128)(2,1)S(1)} %dynamic-slice_bitcast_fusion.1), channel_id=1, source_target_pairs={{0,16},{16,0},{1,17},{17,1},{2,18},{18,2},{3,19},{19,3},{4,20},{20... | collective-permute-start | bytes 2654216 | tf_op jit(solution)/shard_map/ppermute | solution.py:720
  500.9 19.1 %collective-permute-start.56 = (bf16[256,1536]{1,0:T(8,128)(2,1)}, bf16[256,1536]{1,0:T(8,128)(2,1)S(1)}, u32[]{:S(2)}, u32[]{:S(2)}) collective-permute-start(bf16[256,1536]{1,0:T(8,128)(2,1)} %constant_dynamic-slice_fusion.2), channel_id=1, source_target_pairs={{0,1},{1,0},{2,3},{3,2},{4,5},{5,4},{6,7},{7,6},{8,9},{9,8},{10,11... | collective-permute-start | bytes 2359304 | tf_op jit(solution)/shard_map/ppermute | solution.py:720
  503.1 16.9 %collective-permute-start.60 = (bf16[1,192,1152]{2,1,0:T(8,128)(2,1)}, bf16[1,192,1152]{2,1,0:T(8,128)(2,1)}, u32[]{:S(2)}, u32[]{:S(2)}) collective-permute-start(bf16[1,192,1152]{2,1,0:T(8,128)(2,1)} %constant_dynamic-slice_fusion), channel_id=1, source_target_pairs={{0,16},{16,0},{1,17},{17,1},{2,18},{18,2},{3,19},{19,3},{4,20},{20... | collective-permute-start | bytes 1327112 | tf_op jit(solution)/shard_map/ppermute | solution.py:720
  505.2 14.7 %collective-permute-start.59 = (bf16[1,192,1152]{2,1,0:T(8,128)(2,1)}, bf16[1,192,1152]{2,1,0:T(8,128)(2,1)}, u32[]{:S(2)}, u32[]{:S(2)}) collective-permute-start(bf16[1,192,1152]{2,1,0:T(8,128)(2,1)} %constant_dynamic-slice_fusion.1), channel_id=1, source_target_pairs={{0,4},{4,0},{1,5},{5,1},{2,6},{6,2},{3,7},{7,3},{8,12},{12,8},{9,1... | collective-permute-start | bytes 1327112 | tf_op jit(solution)/shard_map/ppermute | solution.py:720
  523.1 26.9 %collective-permute-start.66 = (bf16[1,192,1152]{2,1,0:T(8,128)(2,1)}, bf16[1,192,1152]{2,1,0:T(8,128)(2,1)}, u32[]{:S(2)}, u32[]{:S(2)}) collective-permute-start(bf16[1,192,1152]{2,1,0:T(8,128)(2,1)} %get-tuple-element.330), channel_id=1, source_target_pairs={{2,0},{8,10},{10,2},{0,8},{3,1},{9,11},{11,3},{1,9},{6,4},{12,14},... | collective-permute-start | bytes 1327112 | tf_op jit(solution)/shard_map/ppermute | solution.py:861
  523.1 26.9 %collective-permute-start.67 = (bf16[1,192,1152]{2,1,0:T(8,128)(2,1)}, bf16[1,192,1152]{2,1,0:T(8,128)(2,1)}, u32[]{:S(2)}, u32[]{:S(2)}) collective-permute-start(bf16[1,192,1152]{2,1,0:T(8,128)(2,1)} %get-tuple-element.331), channel_id=1, source_target_pairs={{2,8},{8,2},{3,9},{9,3},{6,12},{12,6},{7,13},{13,7},{18,24},{24,18... | collective-permute-start | bytes 1327112 | tf_op jit(solution)/shard_map/ppermute | solution.py:862
  535.0 13.2 %collective-permute-start.63 = (f32[7460]{0:T(1024)S(1)}, f32[7460]{0:T(1024)S(1)}, u32[]{:S(2)}, u32[]{:S(2)}) collective-permute-start(f32[7460]{0:T(1024)S(1)} %add.417), channel_id=1, source_target_pairs={{0,2},{2,0},{1,3},{3,1},{4,6},{6,4},{5,7},{7,5},{8,10},{10,8},{9,1... | collective-permute-start | bytes 89528 | tf_op jit(solution)/shard_map/ppermute | solution.py:720
  548.4 14.0 %collective-permute-start.70 = (f32[6,768]{1,0:T(8,128)S(1)}, f32[6,768]{1,0:T(8,128)S(1)}, u32[]{:S(2)}, u32[]{:S(2)}) collective-permute-start(f32[6,768]{1,0:T(8,128)S(1)} %reshape.363), channel_id=1, source_target_pairs={{0,8},{8,0},{1,9},{9,1},{2,10},{10,2},{3,11},{11,3},{4,12},{12,4},... | collective-permute-start | bytes 55304 | tf_op jit(solution)/shard_map/ppermute | solution.py:720
  551.6 10.7 %collective-permute-start.68 = (f32[192,256]{1,0:T(8,128)S(1)}, f32[192,256]{1,0:T(8,128)S(1)}, u32[]{:S(2)}, u32[]{:S(2)}) collective-permute-start(f32[192,256]{1,0:T(8,128)S(1)} %slice.418), channel_id=1, source_target_pairs={{0,2},{2,0},{1,3},{3,1},{4,6},{6,4},{5,7},{7,5},{8,10},{10,8},{9,1... | collective-permute-start | bytes 589832 | tf_op jit(solution)/shard_map/ppermute | solution.py:720
  551.7 11.9 %collective-permute-start.65 = (f32[2816]{0:T(1024)S(1)}, f32[2816]{0:T(1024)S(1)}, u32[]{:S(2)}, u32[]{:S(2)}) collective-permute-start(f32[2816]{0:T(1024)S(1)} %slice_add_fusion.2), channel_id=1, source_target_pairs={{0,1},{1,0},{2,3},{3,2},{4,5},{5,4},{6,7},{7,6},{8,9},{9,8},{10,11... | collective-permute-start | bytes 33800 | tf_op jit(solution)/shard_map/ppermute | solution.py:720
  (117 other events, 1058.9 us)

commit v3 on v2

--- a/solution.py
+++ b/solution.py
@@ -12,7 +12,6 @@
 HALF = CHUNK // 2
 LANES = 128
 STRIP = 256
-ROWS = 64
 RIM = 16
 EPS = 1e-05
 F32 = jnp.float32
@@ -37,16 +36,12 @@
     return terms
 
 
-def doubled(value):
-    return jnp.concatenate(pieces(value, 2), axis=1)
-
-
-def spread_heads(pair, spread):
-    return dot(pair, spread)
-
-
-def gather_heads(value, spread, count=2):
-    return sum(dot_nt(term, spread[0:LANES, :]) for term in pieces(value, count))
+def spread_heads(value, spread):
+    return sum(dot(term, spread) for term in pieces(value, 2))
+
+
+def gather_heads(value, spread):
+    return sum(dot_nt(term, spread) for term in pieces(value, 2))
 
 
 def running_sum(value, mask):
@@ -65,14 +60,10 @@
     return [slice(at, at + STRIP) for at in range(0, width, STRIP)]
 
 
-def row_blocks():
-    return [slice(at, at + ROWS) for at in range(0, CHUNK, ROWS)]
-
-
-def conv_pre(ext, taps, rows, cols):
-    total = taps[4:5, cols] + taps[0:1, cols] * ext[pl.ds(RIM - 3 + rows.start, ROWS), cols]
+def conv_pre(ext, taps, cols):
+    total = taps[4:5, cols] + taps[0:1, cols] * ext[pl.ds(RIM - 3, CHUNK), cols]
     for k in range(1, 4):
-        total = total + taps[k : k + 1, cols] * ext[pl.ds(RIM - 3 + k + rows.start, ROWS), cols]
+        total = total + taps[k : k + 1, cols] * ext[pl.ds(RIM - 3 + k, CHUNK), cols]
     return total
 
 
@@ -91,7 +82,7 @@
 
 
 def widened(log, spread):
-    return spread_heads(doubled(jnp.broadcast_to(jnp.exp(log), (8, LANES))), spread)[0:1, :]
+    return spread_heads(jnp.broadcast_to(jnp.exp(log), (8, LANES)), spread)[0:1, :]
 
 
 def entering_state(packed_ref, first_ref, second_ref, spread_ref):
@@ -107,7 +98,7 @@
 
 def state_kernel(
     mix_ref, halo_ref, step_ref, taps_ref, heads_ref, spread_ref,
-    xbc_ref, sum_ref, dt_ref, end_ref, total_ref, packed_ref, ext, weighted,
+    xbc_ref, sum_ref, dt_ref, end_ref, total_ref, packed_ref, ext,
 ):
     inner = spread_ref.shape[1]
     place = pl.program_id(1)
@@ -129,23 +120,21 @@
     dt_ref[0] = dt
     last = cumul[CHUNK - 1 : CHUNK, :]
     total_ref[0] += jnp.broadcast_to(last, total_ref.shape[1:])
-    tail = doubled(jnp.exp(last - cumul) * dt)
-    decay = doubled(jnp.broadcast_to(jnp.exp(last), (8, LANES)))
+    tail = jnp.exp(last - cumul) * dt
+    decay = jnp.broadcast_to(jnp.exp(last), (8, LANES))
     b_turned = None
     for cols in reversed(strips(xbc_ref.shape[2])):
-        held = spread_ref[:, cols] if cols.start < inner else None
-        for rows in row_blocks():
-            ext[RIM + rows.start : RIM + rows.stop, cols] = mix_ref[0, rows, cols].astype(F32)
-            pre = conv_pre(ext, taps_ref, rows, cols)
-            act = (pre * jax.nn.sigmoid(pre)).astype(BF16)
-            xbc_ref[0, rows, cols] = act
-            if held is not None:
-                weighted[rows, :] = (act.astype(F32) * spread_heads(tail[rows], held)).astype(BF16)
-        if held is None:
-            b_turned = turned(xbc_ref[0, :, inner : inner + LANES])
+        ext[RIM:, cols] = mix_ref[0, :, cols].astype(F32)
+        pre = conv_pre(ext, taps_ref, cols)
+        act = (pre * jax.nn.sigmoid(pre)).astype(BF16)
+        xbc_ref[0, :, cols] = act
+        if cols.start >= inner:
+            b_turned = turned(act[:, 0:LANES])
         else:
+            held = spread_ref[:, cols]
+            weighted = (act.astype(F32) * spread_heads(tail, held)).astype(BF16)
             kept = end_ref[0, :, cols] * spread_heads(decay, held)[0:1, :]
-            end_ref[0, :, cols] = kept + dot(b_turned, weighted[...])
+            end_ref[0, :, cols] = kept + dot(b_turned, weighted)
 
     @pl.when(place == pl.num_programs(1) - 1)
     def _():
@@ -154,7 +143,7 @@
 
 def scan_kernel(
     xbc_ref, sum_ref, dt_ref, packed_ref, first_ref, second_ref, gate_ref, gm_ref, rows_ref, spread_ref,
-    y_ref, mixed_ref, enter_ref, stat_ref, state, stepped, weighted,
+    y_ref, mixed_ref, enter_ref, stat_ref, state,
 ):
     inner = spread_ref.shape[1]
 
@@ -166,58 +155,51 @@
     dt = dt_ref[0]
     across = jnp.transpose(cumul)
     last = cumul[CHUNK - 1 : CHUNK, :]
-    tail = doubled(jnp.exp(last - cumul) * dt)
-    reach = doubled(jnp.exp(cumul))
-    decay = doubled(jnp.broadcast_to(jnp.exp(last), (8, LANES)))
-    dt = doubled(dt)
+    tail = jnp.exp(last - cumul) * dt
+    reach = jnp.exp(cumul)
+    decay = jnp.broadcast_to(jnp.exp(last), (8, LANES))
     b_low = xbc_ref[0, :, inner : inner + LANES]
     c_low = xbc_ref[0, :, inner + LANES :]
     b_turned = turned(b_low)
     score = dot_nt(c_low, b_low)
     causal = iota2(HALF, HALF, 0) >= iota2(HALF, HALF, 1)
     first = iota2(1, LANES, 1) < LANES // 2
-    squares = [jnp.zeros((ROWS, STRIP), F32) for _ in row_blocks()]
-    crossed = [jnp.zeros((ROWS, STRIP), F32) for _ in row_blocks()]
+    squares = jnp.zeros((CHUNK, STRIP), F32)
+    crossed = jnp.zeros((CHUNK, STRIP), F32)
     for cols in strips(inner):
         held = spread_ref[:, cols]
+        x = xbc_ref[0, :, cols].astype(F32)
+        u = x * spread_heads(dt, held)
+        weighted = (x * spread_heads(tail, held)).astype(BF16)
         entering = state[:, cols].astype(BF16)
         enter_ref[0, 0, :, cols] = entering
-        for rows in row_blocks():
-            x = xbc_ref[0, rows, cols].astype(F32)
-            stepped[rows, :] = x * spread_heads(dt[rows], held)
-            weighted[rows, :] = (x * spread_heads(tail[rows], held)).astype(BF16)
-            y_ref[0, rows, cols] = dot(c_low[rows], entering) * spread_heads(reach[rows], held)
-        kept = state[:, cols] * spread_heads(decay, held)[0:1, :]
-        state[:, cols] = kept + dot(b_turned, weighted[...])
+        carried = dot(c_low, entering) * spread_heads(reach, held)
+        state[:, cols] = state[:, cols] * spread_heads(decay, held)[0:1, :] + dot(b_turned, weighted)
         for pair in range(STRIP // LANES):
             lanes = slice(pair * LANES, (pair + 1) * LANES)
-            into = slice(cols.start + pair * LANES, cols.start + (pair + 1) * LANES)
-            top = y_ref[0, 0:HALF, into]
-            bottom = y_ref[0, HALF:, into]
-            u = stepped[:, lanes]
+            top = carried[0:HALF, lanes]
+            bottom = carried[HALF:, lanes]
             for side in range(2):
                 head = (cols.start + pair * LANES) // (LANES // 2) + side
-                mine = jnp.where(first if side == 0 else ~first, u, 0.0).astype(BF16)
+                mine = jnp.where(first if side == 0 else ~first, u[:, lanes], 0.0).astype(BF16)
                 column = cumul[:, head : head + 1]
                 row = across[head : head + 1, :]
                 corner = jnp.where(causal, jnp.exp(column[0:HALF] - row[:, 0:HALF]), 0.0)
                 top = top + dot((score[0:HALF, 0:HALF] * corner).astype(BF16), mine[0:HALF])
                 left = jnp.exp(column[HALF:] - row[:, 0:HALF])
                 right = jnp.where(causal, jnp.exp(column[HALF:] - row[:, HALF:]), 0.0)
-                below = jnp.concatenate([left, right], axis=1)
-                bottom = bottom + dot((score[HALF:, :] * below).astype(BF16), mine)
+                bottom = bottom + dot((score[HALF:, 0:HALF] * left).astype(BF16), mine[0:HALF])
+                bottom = bottom + dot((score[HALF:, HALF:] * right).astype(BF16), mine[HALF:])
+            into = slice(cols.start + pair * LANES, cols.start + (pair + 1) * LANES)
             y_ref[0, 0:HALF, into] = top
             y_ref[0, HALF:, into] = bottom
-        for k, rows in enumerate(row_blocks()):
-            y = y_ref[0, rows, cols] + rows_ref[0:1, cols] * xbc_ref[0, rows, cols].astype(F32)
-            gate = gate_ref[0, rows, cols].astype(F32)
-            gated = y * gate * jax.nn.sigmoid(gate)
-            gained = gated * rows_ref[1:2, cols]
-            mixed_ref[0, rows, cols] = gained.astype(BF16)
-            squares[k] = squares[k] + gated * gated
-            crossed[k] = crossed[k] + gained * gm_ref[0, rows, cols]
-    squares = jnp.concatenate(squares, axis=0)
-    crossed = jnp.concatenate(crossed, axis=0)
+        y = y_ref[0, :, cols] + rows_ref[0:1, cols] * x
+        gate = gate_ref[0, :, cols].astype(F32)
+        gated = y * gate * jax.nn.sigmoid(gate)
+        gained = gated * rows_ref[1:2, cols]
+        mixed_ref[0, :, cols] = gained.astype(BF16)
+        squares = squares + gated * gated
+        crossed = crossed + gained * gm_ref[0, :, cols]
     ones = jnp.ones((8, STRIP), BF16)
     square_row = sum(dot_nt(ones, term) for term in pieces(squares, 3))
     cross_row = sum(dot_nt(ones, term) for term in pieces(crossed, 3))
@@ -226,7 +208,7 @@
 
 def gate_kernel(
     inner_full, y_ref, xbc_ref, gate_ref, gm_ref, stat_ref, sum_ref, total_ref, rows_ref, spread_ref,
-    gy_ref, gz_ref, mixed_ref, back_ref, gain_ref, packed_ref, reached,
+    gy_ref, gz_ref, mixed_ref, back_ref, gain_ref, packed_ref,
 ):
     inner = spread_ref.shape[1]
 
@@ -242,32 +224,29 @@
     scale = lax.rsqrt(stats[:, 0:1] / inner_full + EPS)
     bent = scale * scale * scale * (stats[:, 1:2] / inner_full)
     cumul = sum_ref[0]
-    reach = doubled(jnp.exp(cumul))
-    decay = doubled(jnp.broadcast_to(jnp.exp(cumul[CHUNK - 1 : CHUNK, :]), (8, LANES)))
+    reach = jnp.exp(cumul)
+    decay = jnp.broadcast_to(jnp.exp(cumul[CHUNK - 1 : CHUNK, :]), (8, LANES))
     c_turned = turned(xbc_ref[0, :, inner + LANES :])
     for cols in strips(inner):
         held = spread_ref[:, cols]
+        x = xbc_ref[0, :, cols].astype(F32)
+        y = y_ref[0, :, cols] + rows_ref[0:1, cols] * x
+        gate = gate_ref[0, :, cols].astype(F32)
+        sigmoid = jax.nn.sigmoid(gate)
+        silu = gate * sigmoid
+        gated = y * silu
+        scaled = gated * scale
+        gm = gm_ref[0, :, cols]
         gain = rows_ref[1:2, cols]
-        gain_sum = jnp.zeros((1, STRIP), F32)
-        for rows in row_blocks():
-            x = xbc_ref[0, rows, cols].astype(F32)
-            y = y_ref[0, rows, cols] + rows_ref[0:1, cols] * x
-            gate = gate_ref[0, rows, cols].astype(F32)
-            sigmoid = jax.nn.sigmoid(gate)
-            silu = gate * sigmoid
-            gated = y * silu
-            scaled = gated * scale[rows]
-            gm = gm_ref[0, rows, cols]
-            gg = scale[rows] * gm * gain - gated * bent[rows]
-            gy = (gg * silu).astype(BF16)
-            gy_ref[0, rows, cols] = gy
-            gz_ref[0, rows, cols] = (gg * y * sigmoid * (1.0 + gate * (1.0 - sigmoid))).astype(BF16)
-            mixed_ref[0, rows, cols] = (scaled * gain).astype(BF16)
-            gain_sum = gain_sum + jnp.sum(gm * scaled, axis=0, keepdims=True)
-            reached[rows, :] = (gy.astype(F32) * spread_heads(reach[rows], held)).astype(BF16)
-        gain_ref[:, cols] += jnp.broadcast_to(gain_sum, (8, STRIP))
+        gg = scale * gm * gain - gated * bent
+        gy = (gg * silu).astype(BF16)
+        gy_ref[0, :, cols] = gy
+        gz_ref[0, :, cols] = (gg * y * sigmoid * (1.0 + gate * (1.0 - sigmoid))).astype(BF16)
+        mixed_ref[0, :, cols] = (scaled * gain).astype(BF16)
+        gain_ref[:, cols] += jnp.broadcast_to(jnp.sum(gm * scaled, axis=0, keepdims=True), (8, STRIP))
+        reached = (gy.astype(F32) * spread_heads(reach, held)).astype(BF16)
         kept = back_ref[0, :, cols] * spread_heads(decay, held)[0:1, :]
-        back_ref[0, :, cols] = kept + dot(c_turned, reached[...])
+        back_ref[0, :, cols] = kept + dot(c_turned, reached)
 
     @pl.when(pl.program_id(1) == pl.num_programs(1) - 1)
     def _():
@@ -310,11 +289,9 @@
     dt = dt_ref[0]
     across = jnp.transpose(cumul)
     last = cumul[CHUNK - 1 : CHUNK, :]
-    fade_pair = doubled(jnp.exp(last - cumul))
-    reach_pair = doubled(jnp.exp(cumul))
-    dt_pair = doubled(dt)
+    fade = jnp.exp(last - cumul)
+    reach = jnp.exp(cumul)
     decay = jnp.broadcast_to(jnp.exp(last), (8, LANES))
-    decay_pair = doubled(decay)
     b_low = xbc_ref[0, :, inner : inner + LANES]
     c_low = xbc_ref[0, :, inner + LANES :]
     c_turned = turned(c_low)
@@ -330,37 +307,33 @@
     joined = jnp.zeros((8, LANES), F32)
 
     def conv_part(cols, gact):
-        sums = [jnp.zeros((1, STRIP), F32) for _ in range(5)]
-        for rows in row_blocks():
-            ext[RIM + rows.start : RIM + rows.stop, cols] = mix_ref[0, rows, cols].astype(F32)
-        for rows in reversed(row_blocks()):
-            pre = conv_pre(ext, taps_ref, rows, cols)
-            sigmoid = jax.nn.sigmoid(pre)
-            gp = gact[rows].astype(BF16).astype(F32) * sigmoid * (1.0 + pre * (1.0 - sigmoid))
-            gpre[rows, cols] = gp
-            total = taps_ref[3:4, cols] * gp
-            for k in range(3):
-                total = total + taps_ref[k : k + 1, cols] * gpre[pl.ds(3 - k + rows.start, ROWS), cols]
-            for k in range(4):
-                moved = ext[pl.ds(RIM - 3 + k + rows.start, ROWS), cols]
-                sums[k] = sums[k] + jnp.sum(gp * moved, axis=0, keepdims=True)
-            sums[4] = sums[4] + jnp.sum(gp, axis=0, keepdims=True)
-            gmix_ref[0, rows, cols] = total.astype(BF16)
-        rim_ref[0, :, cols] = gpre[0:8, cols]
-        for k in range(5):
-            gtaps_ref[k : k + 1, cols] += sums[k]
+        ext[RIM:, cols] = mix_ref[0, :, cols].astype(F32)
+        pre = conv_pre(ext, taps_ref, cols)
+        sigmoid = jax.nn.sigmoid(pre)
+        gp = gact.astype(BF16).astype(F32) * sigmoid * (1.0 + pre * (1.0 - sigmoid))
+        gpre[0:CHUNK, cols] = gp
+        rim_ref[0, :, cols] = gp[0:8, :]
+        total = taps_ref[3:4, cols] * gp
+        for k in range(3):
+            total = total + taps_ref[k : k + 1, cols] * gpre[pl.ds(3 - k, CHUNK), cols]
+            gtaps_ref[k : k + 1, cols] += jnp.sum(
+                gp * ext[pl.ds(RIM - 3 + k, CHUNK), cols], axis=0, keepdims=True
+            )
+        gtaps_ref[3:4, cols] += jnp.sum(gp * ext[RIM:, cols], axis=0, keepdims=True)
+        gtaps_ref[4:5, cols] += jnp.sum(gp, axis=0, keepdims=True)
+        gmix_ref[0, :, cols] = total.astype(BF16)
 
     for cols in strips(inner):
         held = spread_ref[:, cols]
         x = xbc_ref[0, :, cols].astype(F32)
-        dt_wide = spread_heads(dt_pair, held)
-        fade_wide = spread_heads(fade_pair, held)
+        dt_wide = spread_heads(dt, held)
+        fade_wide = spread_heads(fade, held)
         u = x * dt_wide
         u_low = u.astype(BF16)
         weighted = (u * fade_wide).astype(BF16)
         gy_low = gy_ref[0, :, cols]
         gy = gy_low.astype(F32)
-        reached = (gy * spread_heads(reach_pair, held)).astype(BF16)
+        reached = (gy * spread_heads(reach, held)).astype(BF16)
         later = back[:, cols]
         later_low = later.astype(BF16)
         entered = enter_ref[0, 0, :, cols]
@@ -369,7 +342,7 @@
         gu_carried = dot(b_low, later_low) * fade_wide
         sums = jnp.sum(later * entered.astype(F32), axis=0, keepdims=True)
         joined = joined + gather_heads(jnp.broadcast_to(sums, (8, STRIP)), held)
-        back[:, cols] = later * spread_heads(decay_pair, held)[0:1, :] + dot(c_turned, reached)
+        back[:, cols] = later * spread_heads(decay, held)[0:1, :] + dot(c_turned, reached)
         parts = []
         for pair in range(STRIP // LANES):
             lanes = slice(pair * LANES, (pair + 1) * LANES)
@@ -386,10 +359,12 @@
                 corner = jnp.where(causal, jnp.exp(row[:, 0:HALF] - column[0:HALF]), 0.0)
                 side_right = jnp.exp(row[:, HALF:] - column[0:HALF])
                 low_right = jnp.where(causal, jnp.exp(row[:, HALF:] - column[HALF:]), 0.0)
-                above = jnp.concatenate([corner, side_right], axis=1)
-                top = top + dot((score[0:HALF, :] * above).astype(BF16), gy_mine)
+                top = top + dot((score[0:HALF, 0:HALF] * corner).astype(BF16), gy_mine[0:HALF])
+                top = top + dot((score[0:HALF, HALF:] * side_right).astype(BF16), gy_mine[HALF:])
                 bottom = bottom + dot((score[HALF:, HALF:] * low_right).astype(BF16), gy_mine[HALF:])
-                pulled[0:HALF, :] += dot_nt(u_mine[0:HALF], gy_pair) * above
+                upper = dot_nt(u_mine[0:HALF], gy_pair)
+                pulled[0:HALF, 0:HALF] += upper[:, 0:HALF] * corner
+                pulled[0:HALF, HALF:] += upper[:, HALF:] * side_right
                 pulled[HALF:, HALF:] += dot_nt(u_mine[HALF:], gy_pair[HALF:]) * low_right
             parts.append(jnp.concatenate([top, bottom], axis=0))
         gu = jnp.concatenate(parts, axis=1)
@@ -480,7 +455,7 @@
             (shaped((groups, 8, LANES)), whole(8, LANES)),
             (shaped((groups, LANES + RIM, inner), BF16), whole(LANES + RIM, inner)),
         ],
-        [pltpu.VMEM((RIM + CHUNK, width), F32), pltpu.VMEM((CHUNK, STRIP), BF16)],
+        [pltpu.VMEM((RIM + CHUNK, width), F32)],
         1_500_000_000,
         2_000_000,
         after,
@@ -515,11 +490,7 @@
             ),
             (shaped((groups, 8, length)), pl.BlockSpec((1, 8, CHUNK), lambda g, i: (g, 0, i))),
         ],
-        [
-            pltpu.VMEM((LANES, inner), F32),
-            pltpu.VMEM((CHUNK, STRIP), F32),
-            pltpu.VMEM((CHUNK, STRIP), BF16),
-        ],
+        [pltpu.VMEM((LANES, inner), F32)],
         2_500_000_000,
         4_000_000,
         after,
@@ -553,7 +524,7 @@
             (shaped((8, inner)), fixed((8, inner))),
             (shaped((groups, LANES + RIM, inner), BF16), whole(LANES + RIM, inner)),
         ],
-        [pltpu.VMEM((CHUNK, STRIP), BF16)],
+        [],
         1_500_000_000,
         4_500_000,
         after,
@@ -738,6 +709,8 @@
 
 
 def hold(value, *before):
+    if not before:
+        return value
     return lax.optimization_barrier((value,) + before)[0]
 
 
@@ -939,32 +912,41 @@
     normed_own = [(own[part : part + 1] * r0[part : part + 1] * gain_in).astype(BF16) for part in parts]
     fast = all_pairs()
 
+    def tokens_of(value, *before):
+        got = hold(swap(value, "zq"), *before)
+        return value, got, swap(value, "core"), swap(got, "core")
+
     if fast:
         got = fetch(own_first)
-        start = swap(normed_own[0], "zq")
+    fours = [tokens_of(normed_own[0])]
+    if fast:
         same, cross = fetched(own_first, *got)
-        first = jnp.stack([same, swap(same, "x")])
-        second = jnp.stack([cross, swap(cross, "y")])
+        moved = hold((swap(same, "x"), swap(cross, "y")), fours[0][1])
+        first, second = jnp.stack([same, moved[0]]), jnp.stack([cross, moved[1]])
+        own_second = hold(own_second, fours[0][1], *moved)
+        got = fetch(own_second)
         rest = swap(first, "y"), swap(second, "x")
-        own_second, after_first = hold((own_second, normed_own[1:]), first, second)
-        got = fetch(own_second)
-        started = [start] + [swap(value, "zq") for value in after_first]
+        later = first, second
+    else:
+        later = (fours[0][1],)
+    for part in parts[1:]:
+        fours.append(tokens_of(hold(normed_own[part], fours[0][1]), *later))
+        later = (fours[-1][1],)
+    if fast:
         w_first = place(first, rest[0], second, rest[1])
-        later = rest
         got = hold(got, w_first)
         same, cross = fetched(own_second, *got)
         moved = swap(same, "x"), swap(cross, "y")
     else:
-        started = [swap(value, "zq") for value in normed_own]
-        later = ()
         w_first = spliced(
             gather_slice(own_first), ((share, 1), (states2, 0), (own_heads, 1), (filler, 1))
         )
+    normed = [joined(*four) for four in fours]
     per_head = jnp.concatenate([dt_bias, a_log, d_skip])
     per_head = jnp.pad(per_head, (0, share - 3 * own_heads))
     small = jnp.concatenate([conv_x, conv_x_bias[None], inner_gain[None]], axis=0).astype(F32)
     small = jnp.concatenate([small, per_head[None], jnp.zeros((1, share), F32)])
-    small = slice_of_own(hold(small, w_first), w_first)
+    small = slice_of_own(small, w_first)
     channel_rows = jnp.concatenate([small[k, 0:6] for k in range(halves)], axis=1)
     head_rows = jnp.concatenate(
         [small[k, 6, 0 : 3 * own_heads].reshape(3, own_heads) for k in range(halves)], axis=1
@@ -979,15 +961,13 @@
         lax.broadcasted_iota(jnp.int32, (LANES, inner), 1) // head_width
         == lax.broadcasted_iota(jnp.int32, (LANES, inner), 0)
     ).astype(BF16)
-    spread = jnp.concatenate([spread, spread])
-
-    normed, scans = [], []
+
+    scans = []
     for part in parts:
-        value, got = normed_own[part], hold(started[part], *later)
-        normed.append(joined(value, got, swap(value, "core"), swap(got, "core")))
         xw = matmul(normed[part], w_first, ((2,), (0,)), BF16)
         scans.append((xw, shift(xw[:, -RIM:, 0:width], 1)))
-        later = (xw,)
+        if part == 0:
+            normed[-1] = hold(normed[-1], xw)
     if fast:
         moved = hold(moved, scans[0][0])
         first, second = jnp.stack([same, moved[0]]), jnp.stack([cross, moved[1]])
@@ -1086,10 +1066,7 @@
     for part in parts[1:]:
         following = hold(back_packed[part], found[part - 1][1])
         found.append(hop(part, following, gates[part][3], -1, g_normed_gate[0]))
-        g_normed_gate.append(
-            matmul(hold(gates[part][1], found[part][1]), w_gate, ((2,), (1,)))
-        )
-    wait_for = [g_normed_gate[-1], branch_sent]
+    wait_for = [found[-1][1], branch_sent]
     if fast:
         second = cut_rows(hold([g_gate, g_down], *gin))
         moved = swap(second[2], "x"), swap(second[3], "y")
@@ -1124,9 +1101,9 @@
             *scans[part], taps, head_in, rows, spread, wait_for,
         )
         if part == micro - 1 and fast and micro > 1:
-            (gmix, rim, *sums), norm_cut, got_home = hold(
-                ((gmix, rim, *sums), norm_cut, got_home)
-            )
+            got_home = hold(got_home, gmix)
+            g_gate, g_down = at_owner(*got_home, pair[0])
+            rim = hold(rim, g_gate, g_down)
         if part < micro - 1:
             gin = entering(found[part + 1], -1)
             gmix, rim, *sums = hold(
@@ -1162,35 +1139,35 @@
             total = g_normed_gate[part] + matmul(gmix, w_first, ((2,), (1,)))
             return total.astype(BF16)
 
+        total = for_tokens(gmix)
+        other = swap(total[1], "core")
+        g_first = for_weights(hold(gmix, total))
         if last_part:
-            g_first = for_weights(gmix).astype(BF16)
+            g_first = g_first.astype(BF16)
             if fast:
                 first = cut_rows([g_first])
                 moved_first = swap(first[2], "x"), swap(first[3], "y")
-            total = for_tokens(hold(gmix, g_first, *(first[2:] if fast else ())))
-            other = swap(total[1], "core")
         else:
-            total = for_tokens(gmix)
-            other = swap(total[1], "core")
-            g_first = for_weights(hold(gmix, total))
+            g_normed_gate.append(
+                matmul(hold(gates[part + 1][1], g_first), w_gate, ((2,), (1,)))
+            )
             kept, sent = cut(added(total[0], hold(other, g_first)), "zq", 0)
             norm_cut = kept, swap(sent, "zq")
             if part == micro - 2:
-                outputs = whole_output(g_first, sent)
+                outputs = whole_output(g_normed_gate[-1], sent)
             gin = hold(gin, outputs)
             wait_for = [sent, outputs]
             if fast and part == micro - 2:
-                moved = hold(moved, g_first)
+                moved = hold(moved, g_normed_gate[-1])
                 pair = both(second, moved)
                 home = home_parts(*pair)
                 wait_for += home
                 got_home = go_home(home)
 
-    kept, sent = cut(added(total[0], other), "zq", 0)
+    kept, sent = cut(added(total[0], hold(other, g_first, *(first[2:] if fast else ()))), "zq", 0)
     got_norm = swap(sent, "zq")
     if fast:
-        g_gate, g_down = at_owner(*got_home, pair[0])
-        first = cut_again(*both(first, hold(moved_first, g_gate, g_down)))
+        first = cut_again(*both(first, hold(moved_first, sent)))
         moved = swap(first[2], "y"), swap(first[3], "x")
         got_norm = hold(got_norm, *first[2:])
         pair = both(first, hold(moved, got_norm))
@@ -1221,7 +1198,11 @@
     g_hidden = jnp.stack(g_hidden + [grad])
     g_norm_gain = g_norm_gain + gain
     g_bc = g_first[:, share : share + states2]
-    g_bc = sum_axis(sum_axis(g_bc, "zp"), "zq")
+    if fast:
+        across = lax.ppermute(g_bc, ("zp", "zq"), [(0, 3), (3, 0), (1, 2), (2, 1)])
+        g_bc = (g_bc + swap(g_bc, "zq")) + (swap(g_bc, "zp") + across)
+    else:
+        g_bc = sum_axis(sum_axis(g_bc, "zp"), "zq")
 
     g_taps, g_heads, g_skip = (sum(b[k] for b in heads_out) for k in range(3))
     g_gain = sum(g[4] for g in gates)
@@ -1231,8 +1212,8 @@
     )
     size = small.shape[0]
     packed = jnp.concatenate([small, g_taps[0:5, inner:width].reshape(-1), g_norm_gain])
-    for axis in ("x", "y", "zp"):
-        packed = sum_axis(packed, axis)
+    packed = sum_axis(sum_axis(packed, "x"), "y")
+    packed = sum_axis(hold(packed, g_first), "zp")
     small = packed[:size]
     shared = sum_axis(sum_axis(packed[size:], "core"), "zq")
     bc_rows = shared[0 : 5 * states2].reshape(5, states2)

time: 579 us -> 536 us (0.926)
  waiting for transfers between devices: 138 us -> 112 us
  starting transfers between devices: 113 us -> 96.7 us
  local copies, waits for them, and re-layouts: 41.3 us -> 32.8 us
  other arithmetic: 41 us -> 48.4 us
    ppermute x8, waiting for transfers between devices: 24.9 us -> 0.02 us  [column_hops(): lax.ppermute(leaving, ('y', 'zp'), pair)]
    ppermute x2, starting transfers between devices: 17.1 us -> 5.98 us  [fetch(): lax.ppermute(piece, ('core', 'zp'), NEAR)]
    ppermute x2, waiting for transfers between devices: 0.01 us -> 7.81 us  [go_home(): lax.ppermute(sent[0], ('core', 'zp'), HOME)]
    ppermute x48, waiting for transfers between devices: 103 us -> 96.9 us  [swap(): return lax.ppermute(value, axis, [(0, 1), (1, 0)])]
    unnamed x220 -> x172, local copies, waits for them, and re-layouts: 15.6 us -> 9.45 us
  transfers between devices with their start and end apart: 72 -> 73, of which waited for: 24 -> 21; matrix products, arithmetic and copies ran while one was open for 25% -> 30% of each run, Pallas kernels for 23% -> 25%
where the time goes in v3:
time: 536 us; the launch traced here: 526 us
  Pallas kernels  132 us (25%)
  waiting for transfers between devices  112 us (21%)
  matrix products  102 us (19%)
  starting transfers between devices  96.7 us (18%)
  other arithmetic  48.4 us (9%)
  local copies, waits for them, and re-layouts  32.8 us (6%)
    pallas_call x8, Pallas kernels, run(): pl.pallas_call(body, grid=grid, in_specs=[spec for _, spec in ins] + [pl....  106 us
    dot_general x18, matrix products, matmul(): lax.dot_general(left, right, (contract, ((), ())), preferred_element_type...  102 us
    ppermute x48, waiting for transfers between devices, swap(): return lax.ppermute(value, axis, [(0, 1), (1, 0)])  96.9 us
    ppermute x48, starting transfers between devices, swap(): return lax.ppermute(value, axis, [(0, 1), (1, 0)])  58.5 us
    pallas_call x4, Pallas kernels, joined(): pl.pallas_call(join_kernel, grid_spec=pltpu.PrefetchScalarGridSpec(num_sc...  13.1 us
    convert_element_type x8, other arithmetic, added(): return (kept.astype(F32) + got.astype(F32)).astype(dtype)  12.1 us
    pallas_call x2, Pallas kernels, place(): pl.pallas_call(place_kernel, grid_spec=pltpu.PrefetchScalarGridSpec(num_s...  11.5 us
  transfers between devices with their start and end apart: 73, of which 21 were waited for; matrix products, arithmetic and copies ran while one was open for 30% of the time, Pallas kernels for 25%

profile of v3, /device:TPU:0, one launch (start us, length us, event | category | flops | bytes accessed | tf_op | source)
XLA Modules:
  0.0 526.3 jit_solution(7676929019022815166)
XLA Ops:
  2.6 4.1 collective-permute-start.3
  21.5 18.8 %collective-permute-done.got = bf16[1,256,1536]{2,1,0:T(8,128)(2,1)} collective-permute-done((bf16[1,256,1536]{2,1,0:T(8,128)(2,1)S(1)}, bf16[1,256,1536]{2,1,0:T(8,128)(2,1)}, u32[]{:S(2)}, u32[]{:S(2)}) %collective-permute-start) | collective-permute-done | bytes 786464 | tf_op jit(solution)/shard_map/ppermute | solution.py:691
  49.2 16.9 %collective-permute-done.18.got = bf16[1,256,1536]{2,1,0:T(8,128)(2,1)} collective-permute-done((bf16[1,256,1536]{2,1,0:T(8,128)(2,1)S(1)}, bf16[1,256,1536]{2,1,0:T(8,128)(2,1)}, u32[]{:S(2)}, u32[]{:S(2)}) %collective-permute-start.18) | collective-permute-done | bytes 786464 | tf_op jit(solution)/shard_map/ppermute | solution.py:691
  71.4 3.8 shard_map.279
  75.7 7.1 %shard_map.280 = bf16[2,2,2,192,1152]{4,3,2,1,0:T(8,128)(2,1)} custom-call(s32[3]{0:T(128)S(1)} %pad_add_fusion.at_ref, bf16[2,192,1152]{2,1,0:T(8,128)(2,1)S(1)} %pad_maximum_fusion.7.first, bf16[2,192,1152]{2,1,0:T(8,128)(2,1)} %collective-permute-done.7.first_y, bf16[2,192,1152]{2,1,0:T(8,128)(2,1)S(1)} %pad_maximum_fusion.8.second, ...), custom_call_target="tpu_custom_call" | custom-call | bytes 221184 | tf_op jit(solution)/shard_map/pallas_call | solution.py:637
  87.4 6.5 %convolution_convert_fusion.3.refs_0_.refs_2_.refs_9_.refs_10_.refs_12_ = bf16[2,512,1152]{2,1,0:T(8,128)(2,1)S(1)} fusion(bf16[2,512,1536]{2,1,0:T(8,128)(2,1)S(1)} %copy-done.37, bf16[1536,1152,1]{1,0,2:T(8,128)(2,1)} %bitcast.273), kind=kOutput, calls=%fused_computation.12 | convolution fusion | flops 3625058304 | bytes 9043968 | tf_op jit(solution)/shard_map/dot_general | solution.py:889
  94.1 2.7 collective-permute-start.9
  96.8 3.3 collective-permute-done.14
  102.8 2.5 collective-permute-start.16
  105.4 3.4 shard_map.282
  108.8 7.2 %convolution_convert_fusion.2.refs_0_.refs_2_.refs_9_.refs_10_.refs_12_ = bf16[2,512,1152]{2,1,0:T(8,128)(2,1)S(1)} fusion(bf16[2,512,1536]{2,1,0:T(8,128)(2,1)} %shard_map.282, bf16[1536,1152,1]{1,0,2:T(8,128)(2,1)} %bitcast.274), kind=kOutput, calls=%fused_computation.11 | convolution fusion | flops 3625058304 | bytes 9043968 | tf_op jit(solution)/shard_map/dot_general | solution.py:889
  117.3 8.9 %shard_map.281 = (bf16[2,512,1024]{2,1,0:T(8,128)(2,1)S(1)}, f32[2,512,128]{2,1,0:T(8,128)S(1)}, f32[2,512,128]{2,1,0:T(8,128)S(1)}, f32[2,128,768]{2,1,0:T(8,12...) custom-call(bf16[2,512,1152]{2,1,0:T(8,128)(2,1)} %copy-done.68, ...), custom_call_target="tpu_custom_call" | custom-call | flops 6000000000 | bytes 8000000 | tf_op jit(solution)/shard_map/pallas_call | solution.py:419
  126.3 5.1 collective-permute-start.11
  133.1 8.9 %shard_map.283 = (bf16[2,512,1024]{2,1,0:T(8,128)(2,1)S(1)}, f32[2,512,128]{2,1,0:T(8,128)S(1)}, f32[2,512,128]{2,1,0:T(8,128)S(1)}, f32[2,128,768]{2,1,0:T(8,12...) custom-call(bf16[2,512,1152]{2,1,0:T(8,128)(2,1)} %copy-done.67, ...), custom_call_target="tpu_custom_call" | custom-call | flops 6000000000 | bytes 8000000 | tf_op jit(solution)/shard_map/pallas_call | solution.py:419
  144.8 4.4 shard_map.284
  149.7 6.5 %convolution_convert_fusion.5.refs_6_.refs_2_ = bf16[2,512,768]{2,1,0:T(8,128)(2,1)} fusion(bf16[2,512,1536]{2,1,0:T(8,128)(2,1)} %shard_map.279, bf16[1536,1536]{1,0:T(8,128)(2,1)} %bitcast.257), kind=kOutput, calls=%fused_computation.37 | convolution fusion | flops 2416705536 | bytes 7077888 | tf_op jit(solution)/shard_map/dot_general | solution.py:889
  156.3 2.4 collective-permute-done.23.got
  158.9 3.3 slice.387
  163.8 5.3 %convolution_convert_fusion.4.refs_6_.refs_2_ = bf16[2,512,768]{2,1,0:T(8,128)(2,1)} fusion(bf16[2,512,1536]{2,1,0:T(8,128)(2,1)S(1)} %copy-done.34, bf16[1536,1536]{1,0:T(8,128)(2,1)} %bitcast.259), kind=kOutput, calls=%fused_computation.36 | convolution fusion | flops 2416705536 | bytes 7077888 | tf_op jit(solution)/shard_map/dot_general | solution.py:889
  169.1 4.7 collective-permute-done.28.got
  176.4 3.7 shard_map.286
  180.1 6.3 %fusion.11.refs_7_.refs_10_.refs_3_ = f32[2,512,768]{2,1,0:T(8,128)} fusion(bf16[2,512,1536]{2,1,0:T(8,128)(2,1)} %shard_map.286, bf16[1536,768]{1,0:T(8,128)(2,1)S(1)} %copy-done.45), kind=kOutput, calls=%fused_computation.30 | convolution fusion | flops 2415919104 | bytes 8650752 | tf_op jit(solution)/shard_map/dot_general | solution.py:889
  186.4 10.3 %shard_map.287 = (f32[2,512,768]{2,1,0:T(8,128)}, bf16[2,512,768]{2,1,0:T(8,128)(2,1)S(1)}, bf16[2,2,128,768]{3,2,1,0:T(8,128)(2,1)S(1)}, f32[2,8,512]{2,1,0:T(8,128)S(1)}) custom-call(bf16[2,512,1024]{2,1,0:T(8,128)(2,1)} %copy-done.7, f32[2,512,128]{2,1,0:T(8,128)S(1)} %copy-done.13, f32[2,512,128]{2,1,0:T(8,128)S(1)} %copy-done.17, ...), custom_call_target="tpu_custom_call" | custom-call | flops 10000000000 | bytes 16000000 | tf_op jit(solution)/shard_map/pallas_call | solution.py:419
  202.7 6.9 %fusion.9.refs_7_.refs_11_.refs_3_ = f32[2,512,768]{2,1,0:T(8,128)} fusion(bf16[2,512,1536]{2,1,0:T(8,128)(2,1)} %shard_map.289, bf16[1536,1536]{1,0:T(8,128)(2,1)} %bitcast.260), kind=kOutput, calls=%fused_computation.28 | convolution fusion | flops 2415919104 | bytes 8650752 | tf_op jit(solution)/shard_map/dot_general | solution.py:889
  209.6 2.5 collective-permute-start.31
  212.1 4.5 convolution_convert_fusion.1.refs_9_
  218.9 8.3 %shard_map.290 = (bf16[2,512,768]{2,1,0:T(8,128)(2,1)S(1)}, bf16[2,512,768]{2,1,0:T(8,128)(2,1)S(1)}, bf16[2,512,768]{2,1,0:T(8,128)(2,1)}, f32[2,128,768]{2,1,0...) custom-call(f32[2,512,768]{2,1,0:T(8,128)} %get-tuple-element.181.refs_0_.refs_4_, ...), custom_call_target="tpu_custom_call" | custom-call | flops 6000000000 | bytes 18000000 | tf_op jit(solution)/shard_map/pallas_call | solution.py:419
  229.8 10.5 %shard_map.291 = (f32[2,512,768]{2,1,0:T(8,128)}, bf16[2,512,768]{2,1,0:T(8,128)(2,1)S(1)}, bf16[2,2,128,768]{3,2,1,0:T(8,128)(2,1)S(1)}, f32[2,8,512]{2,1,0:T(8,128)S(1)}) custom-call(bf16[2,512,1024]{2,1,0:T(8,128)(2,1)} %copy-done.6, f32[2,512,128]{2,1,0:T(8,128)S(1)} %copy-done.11, f32[2,512,128]{2,1,0:T(8,128)S(1)} %copy-done.15, ...), custom_call_target="tpu_custom_call" | custom-call | flops 10000000000 | bytes 16000000 | tf_op jit(solution)/shard_map/pallas_call | solution.py:419
  240.2 4.4 convolution_bitcast_fusion.3
  244.8 2.9 convolution_convert_fusion.refs_9_
  249.5 3.5 collective-permute-done.37
  253.0 8.2 %shard_map.292 = (bf16[2,512,768]{2,1,0:T(8,128)(2,1)S(1)}, bf16[2,512,768]{2,1,0:T(8,128)(2,1)S(1)}, bf16[2,512,768]{2,1,0:T(8,128)(2,1)}, f32[2,128,768]{2,1,0...) custom-call(f32[2,512,768]{2,1,0:T(8,128)} %get-tuple-element.197.refs_0_.refs_4_, ...), custom_call_target="tpu_custom_call" | custom-call | flops 6000000000 | bytes 18000000 | tf_op jit(solution)/shard_map/pallas_call | solution.py:419
  265.4 7.3 %convolution_bitcast_fusion.2 = f32[1536,768]{1,0:T(8,128)} fusion(bf16[2,512,1536]{2,1,0:T(8,128)(2,1)} %shard_map.286, bf16[2,512,768]{2,1,0:T(8,128)(2,1)} %get-tuple-element.207), kind=kOutput, calls=%fused_computation.13 | convolution fusion | flops 2415919104 | bytes 9437184 | tf_op jit(solution)/shard_map/dot_general | solution.py:889
  272.7 4.8 bitcast_add_fusion.1
  277.5 3.0 fusion.2
  280.6 4.7 fusion.40
  286.6 3.3 collective-permute-start.46
  294.2 2.4 fusion.6
  301.7 25.3 %shard_map.295 = (bf16[2,512,1152]{2,1,0:T(8,128)(2,1)}, f32[2,8,1024]{2,1,0:T(8,128)S(1)}, f32[8,1024]{1,0:T(8,128)S(1)}, f32[8,128]{1,0:T(8,128)S(1)}, f32[8,768]{1,0:T(8,128)S(1)}) custom-call(bf16[2,512,1024]{2,1,0:T(8,128)(2,1)} %copy-done.7, f32[2,512,128]{2,1,0:T(8,128)S(1)} %copy-done.13, f32[2,512,128]{2,1,0:T(8,128)S(1)} %copy-done.17, ...), custom_call_target="tpu_custom_call" | custom-call | flops 32000000000 | bytes 24000000 | tf_op jit(solution)/shard_map/pallas_call | solution.py:419
  327.0 9.4 %collective-permute-done.39 = bf16[2,256,1536]{2,1,0:T(8,128)(2,1)} collective-permute-done((bf16[2,256,1536]{2,1,0:T(8,128)(2,1)}, bf16[2,256,1536]{2,1,0:T(8,128)(2,1)}, u32[]{:S(2)}, u32[]{:S(2)}) %collective-permute-start.39) | collective-permute-done | bytes 1572896 | tf_op jit(solution)/shard_map/ppermute | solution.py:691
  336.3 2.9 fusion.33
  341.8 6.4 %collective-permute-start.50 = (bf16[2,192,768]{2,1,0:T(8,128)(2,1)S(1)}, bf16[2,192,768]{2,1,0:T(8,128)(2,1)S(1)}, u32[]{:S(2)}, u32[]{:S(2)}) collective-permute-start(bf16[2,192,768]{2,1,0:T(8,128)(2,1)S(1)} %pad_maximum_fusion.10), channel_id=1, source_target_pairs={{0,4},{4,0},{1,5},{5,1},{2,6},{6,2},{3,7},{7,3},{8,12},{12,8},{9,1... | collective-permute-start | bytes 1769480 | tf_op jit(solution)/shard_map/ppermute | solution.py:691
  349.8 7.3 %add_convert_fusion.1 = bf16[2,512,1536]{2,1,0:T(8,128)(2,1)S(1)} fusion(f32[2,512,1536]{2,1,0:T(8,128)} %fusion.40, bf16[2,512,1152]{2,1,0:T(8,128)(2,1)} %fusion.47, bf16[1536,1152,1]{1,0,2:T(8,128)(2,1)S(1)} %bitcast.275), kind=kOutput, calls=%fused_computation.5 | convolution fusion | flops 3627024384 | bytes 15335424 | tf_op jit(solution)/shard_map/dot_general | solution.py:889
  357.3 8.2 %convolution_bitcast_fusion.1 = f32[1536,1152]{1,0:T(8,128)} fusion(bf16[2,512,1536]{2,1,0:T(8,128)(2,1)S(1)} %copy-done.39, bf16[2,512,1152]{2,1,0:T(8,128)(2,1)} %fusion.47), kind=kOutput, calls=%fused_computation.2 | convolution fusion | flops 3623878656 | bytes 12582912 | tf_op jit(solution)/shard_map/dot_general | solution.py:889
  365.5 4.6 fusion.39
  377.6 25.3 %shard_map.296 = (bf16[2,512,1152]{2,1,0:T(8,128)(2,1)}, f32[2,8,1024]{2,1,0:T(8,128)S(1)}, f32[8,1024]{1,0:T(8,128)S(1)}, f32[8,128]{1,0:T(8,128)S(1)}, f32[8,768]{1,0:T(8,128)S(1)}) custom-call(bf16[2,512,1024]{2,1,0:T(8,128)(2,1)} %copy-done.6, f32[2,512,128]{2,1,0:T(8,128)S(1)} %copy-done.11, f32[2,512,128]{2,1,0:T(8,128)S(1)} %copy-done.15, ...), custom_call_target="tpu_custom_call" | custom-call | flops 32000000000 | bytes 24000000 | tf_op jit(solution)/shard_map/pallas_call | solution.py:419
  408.0 3.0 fusion.16
  411.1 5.5 %collective-permute-done.54 = f32[2,8,1024]{2,1,0:T(8,128)S(1)} collective-permute-done((f32[2,8,1024]{2,1,0:T(8,128)S(1)}, f32[2,8,1024]{2,1,0:T(8,128)S(1)}, u32[]{:S(2)}, u32[]{:S(2)}) %collective-permute-start.54) | collective-permute-done | bytes 65568 | tf_op jit(solution)/shard_map/ppermute | solution.py:720
  416.7 6.6 %add_convert_fusion = bf16[2,512,1536]{2,1,0:T(8,128)(2,1)S(1)} fusion(f32[2,512,1536]{2,1,0:T(8,128)} %fusion.39, bf16[2,512,1152]{2,1,0:T(8,128)(2,1)S(1)} %fusion.48, bf16[1536,1152,1]{1,0,2:T(8,128)(2,1)S(1)} %bitcast.276), kind=kOutput, calls=%fused_computation.4 | convolution fusion | flops 3627024384 | bytes 15335424 | tf_op jit(solution)/shard_map/dot_general | solution.py:889
  424.6 2.3 copy-done.36
  427.0 4.7 fusion.1
  432.9 4.4 collective-permute-start.58
  439.8 2.4 fusion.3
  445.1 12.7 %collective-permute-done.58 = bf16[1,2,192,1152]{3,2,1,0:T(8,128)(2,1)} collective-permute-done((bf16[1,2,192,1152]{3,2,1,0:T(8,128)(2,1)}, bf16[1,2,192,1152]{3,2,1,0:T(8,128)(2,1)}, u32[]{:S(2)}, u32[]{:S(2)}) %collective-permute-start.58) | collective-permute-done | bytes 884768 | tf_op jit(solution)/shard_map/ppermute | solution.py:691
  457.8 2.5 collective-permute-done.57
  466.2 8.6 %collective-permute-done.60 = bf16[1,192,1152]{2,1,0:T(8,128)(2,1)} collective-permute-done((bf16[1,192,1152]{2,1,0:T(8,128)(2,1)}, bf16[1,192,1152]{2,1,0:T(8,128)(2,1)}, u32[]{:S(2)}, u32[]{:S(2)}) %collective-permute-start.60) | collective-permute-done | bytes 442400 | tf_op jit(solution)/shard_map/ppermute | solution.py:691
  476.6 2.6 broadcast_select_fusion.2
  483.2 3.2 collective-permute-done.61
  487.3 2.2 fusion.15
  490.4 7.8 %collective-permute-done.63 = bf16[1,192,1152]{2,1,0:T(8,128)(2,1)} collective-permute-done((bf16[1,192,1152]{2,1,0:T(8,128)(2,1)}, bf16[1,192,1152]{2,1,0:T(8,128)(2,1)}, u32[]{:S(2)}, u32[]{:S(2)}) %collective-permute-start.63) | collective-permute-done | bytes 442400 | tf_op jit(solution)/shard_map/ppermute | solution.py:834
  499.7 4.3 collective-permute-start.65
  505.9 3.5 collective-permute-start.68
  509.5 2.4 collective-permute-start.70
  518.3 4.9 collective-permute-done.67
  (438 shorter events, 126.8 us)
Async XLA Ops:
  2.6 13.2 %collective-permute-start.3 = (bf16[192,1152]{1,0:T(8,128)(2,1)S(1)}, bf16[192,1152]{1,0:T(8,128)(2,1)S(1)}, u32[]{:S(2)}, u32[]{:S(2)}) collective-permute-start(bf16[192,1152]{1,0:T(8,128)(2,1)S(1)} %concatenate.24), channel_id=1, source_target_pairs={{0,2},{10,8},{2,10},{8,0},{1,3},{11,9},{3,11},{9,1},{4,6},{14,12},... | collective-permute-start | bytes 1327112 | tf_op jit(solution)/shard_map/ppermute | solution.py:763
  6.7 9.1 %collective-permute-start.5 = (bf16[192,1152]{1,0:T(8,128)(2,1)S(1)}, bf16[192,1152]{1,0:T(8,128)(2,1)}, u32[]{:S(2)}, u32[]{:S(2)}) collective-permute-start(bf16[192,1152]{1,0:T(8,128)(2,1)S(1)} %concatenate.24), channel_id=1, source_target_pairs={{2,8},{8,2},{3,9},{9,3},{6,12},{12,6},{7,13},{13,7},{18,24},{24,18... | collective-permute-start | bytes 1327112 | tf_op jit(solution)/shard_map/ppermute | solution.py:763
  11.6 28.6 %collective-permute-start = (bf16[1,256,1536]{2,1,0:T(8,128)(2,1)S(1)}, bf16[1,256,1536]{2,1,0:T(8,128)(2,1)}, u32[]{:S(2)}, u32[]{:S(2)}) collective-permute-start(bf16[1,256,1536]{2,1,0:T(8,128)(2,1)S(1)} %get-tuple-element.330.own), channel_id=1, source_target_pairs={{0,1},{1,0},{2,3},{3,2},{4,5},{5,4},{6,7},{7,6},{8,9},{9,8},{10,11... | collective-permute-start | bytes 2359304 | tf_op jit(solution)/shard_map/ppermute | solution.py:691
  13.2 34.1 %collective-permute-start.1 = (bf16[1,256,1536]{2,1,0:T(8,128)(2,1)S(1)}, bf16[1,256,1536]{2,1,0:T(8,128)(2,1)}, u32[]{:S(2)}, u32[]{:S(2)}) collective-permute-start(bf16[1,256,1536]{2,1,0:T(8,128)(2,1)S(1)} %get-tuple-element.330.own), channel_id=1, source_target_pairs={{0,8},{8,0},{1,9},{9,1},{2,10},{10,2},{3,11},{11,3},{4,12},{12,4},... | collective-permute-start | bytes 2359304 | tf_op jit(solution)/shard_map/ppermute | solution.py:691
  15.9 24.4 %collective-permute-start.4 = (bf16[192,1152]{1,0:T(8,128)(2,1)S(1)}, bf16[192,1152]{1,0:T(8,128)(2,1)S(1)}, u32[]{:S(2)}, u32[]{:S(2)}) collective-permute-start(bf16[192,1152]{1,0:T(8,128)(2,1)S(1)} %get-tuple-element.351), channel_id=1, source_target_pairs={{0,16},{16,0},{1,17},{17,1},{2,18},{18,2},{3,19},{19,3},{4,20},{20... | collective-permute-start | bytes 1327112 | tf_op jit(solution)/shard_map/ppermute | solution.py:691
  17.4 22.8 %collective-permute-start.6 = (bf16[192,1152]{1,0:T(8,128)(2,1)S(1)}, bf16[192,1152]{1,0:T(8,128)(2,1)S(1)}, u32[]{:S(2)}, u32[]{:S(2)}) collective-permute-start(bf16[192,1152]{1,0:T(8,128)(2,1)S(1)} %get-tuple-element.350), channel_id=1, source_target_pairs={{0,4},{4,0},{1,5},{5,1},{2,6},{6,2},{3,7},{7,3},{8,12},{12,8},{9,1... | collective-permute-start | bytes 1327112 | tf_op jit(solution)/shard_map/ppermute | solution.py:691
  40.2 25.9 %collective-permute-start.18 = (bf16[1,256,1536]{2,1,0:T(8,128)(2,1)S(1)}, bf16[1,256,1536]{2,1,0:T(8,128)(2,1)}, u32[]{:S(2)}, u32[]{:S(2)}) collective-permute-start(bf16[1,256,1536]{2,1,0:T(8,128)(2,1)S(1)} %get-tuple-element.155.own), channel_id=1, source_target_pairs={{0,1},{1,0},{2,3},{3,2},{4,5},{5,4},{6,7},{7,6},{8,9},{9,8},{10,11... | collective-permute-start | bytes 2359304 | tf_op jit(solution)/shard_map/ppermute | solution.py:691
  42.4 32.8 %collective-permute-start.8 = (bf16[2,192,1152]{2,1,0:T(8,128)(2,1)S(1)}, bf16[2,192,1152]{2,1,0:T(8,128)(2,1)}, u32[]{:S(2)}, u32[]{:S(2)}) collective-permute-start(bf16[2,192,1152]{2,1,0:T(8,128)(2,1)S(1)} %pad_maximum_fusion.8.second), channel_id=1, source_target_pairs={{0,16},{16,0},{1,17},{17,1},{2,18},{18,2},{3,19},{19,3},{4,20},{20... | collective-permute-start | bytes 2654216 | tf_op jit(solution)/shard_map/ppermute | solution.py:691
  45.1 30.1 %collective-permute-start.7 = (bf16[2,192,1152]{2,1,0:T(8,128)(2,1)S(1)}, bf16[2,192,1152]{2,1,0:T(8,128)(2,1)}, u32[]{:S(2)}, u32[]{:S(2)}) collective-permute-start(bf16[2,192,1152]{2,1,0:T(8,128)(2,1)S(1)} %pad_maximum_fusion.7.first), channel_id=1, source_target_pairs={{0,4},{4,0},{1,5},{5,1},{2,6},{6,2},{3,7},{7,3},{8,12},{12,8},{9,1... | collective-permute-start | bytes 2654216 | tf_op jit(solution)/shard_map/ppermute | solution.py:691
  46.8 22.5 %collective-permute-start.2 = (bf16[1,256,1536]{2,1,0:T(8,128)(2,1)}, bf16[1,256,1536]{2,1,0:T(8,128)(2,1)}, u32[]{:S(2)}, u32[]{:S(2)}) collective-permute-start(bf16[1,256,1536]{2,1,0:T(8,128)(2,1)} %collective-permute-done.got), channel_id=1, source_target_pairs={{0,8},{8,0},{1,9},{9,1},{2,10},{10,2},{3,11},{11,3},{4,12},{12,4},... | collective-permute-start | bytes 2359304 | tf_op jit(solution)/shard_map/ppermute | solution.py:691
  47.4 35.4 %collective-permute-start.12 = (bf16[192,1536]{1,0:T(8,128)(2,1)}, bf16[192,1536]{1,0:T(8,128)(2,1)}, u32[]{:S(2)}, u32[]{:S(2)}) collective-permute-start(bf16[192,1536]{1,0:T(8,128)(2,1)} %pad_maximum_fusion.9), channel_id=1, source_target_pairs={{0,2},{10,8},{2,10},{8,0},{1,3},{11,9},{3,11},{9,1},{4,6},{14,12},... | collective-permute-start | bytes 1769480 | tf_op jit(solution)/shard_map/ppermute | solution.py:763
  66.1 16.7 %collective-permute-start.13 = (bf16[192,1536]{1,0:T(8,128)(2,1)}, bf16[192,1536]{1,0:T(8,128)(2,1)}, u32[]{:S(2)}, u32[]{:S(2)}) collective-permute-start(bf16[192,1536]{1,0:T(8,128)(2,1)} %pad_maximum_fusion.9), channel_id=1, source_target_pairs={{2,8},{8,2},{3,9},{9,3},{6,12},{12,6},{7,13},{13,7},{18,24},{24,18... | collective-permute-start | bytes 1769480 | tf_op jit(solution)/shard_map/ppermute | solution.py:763
  69.2 18.0 %collective-permute-start.10 = (f32[8,768]{1,0:T(8,128)S(1)}, f32[8,768]{1,0:T(8,128)S(1)}, u32[]{:S(2)}, u32[]{:S(2)}) collective-permute-start(f32[8,768]{1,0:T(8,128)S(1)} %maximum_maximum_fusion), channel_id=1, source_target_pairs={{0,2},{2,0},{1,3},{3,1},{4,6},{6,4},{5,7},{7,5},{8,10},{10,8},{9,1... | collective-permute-start | bytes 73736 | tf_op jit(solution)/shard_map/ppermute | solution.py:691
  75.2 30.2 %collective-permute-start.19 = (bf16[1,256,1536]{2,1,0:T(8,128)(2,1)S(1)}, bf16[1,256,1536]{2,1,0:T(8,128)(2,1)S(1)}, u32[]{:S(2)}, u32[]{:S(2)}) collective-permute-start(bf16[1,256,1536]{2,1,0:T(8,128)(2,1)S(1)} %get-tuple-element.155.own), channel_id=1, source_target_pairs={{0,8},{8,0},{1,9},{9,1},{2,10},{10,2},{3,11},{11,3},{4,12},{12,4},... | collective-permute-start | bytes 2359304 | tf_op jit(solution)/shard_map/ppermute | solution.py:691
  75.2 30.2 %collective-permute-start.20 = (bf16[1,256,1536]{2,1,0:T(8,128)(2,1)}, bf16[1,256,1536]{2,1,0:T(8,128)(2,1)S(1)}, u32[]{:S(2)}, u32[]{:S(2)}) collective-permute-start(bf16[1,256,1536]{2,1,0:T(8,128)(2,1)} %collective-permute-done.18.got), channel_id=1, source_target_pairs={{0,8},{8,0},{1,9},{9,1},{2,10},{10,2},{3,11},{11,3},{4,12},{12,4},... | collective-permute-start | bytes 2359304 | tf_op jit(solution)/shard_map/ppermute | solution.py:691
  84.1 16.0 %collective-permute-start.14 = (bf16[192,1536]{1,0:T(8,128)(2,1)S(1)}, bf16[192,1536]{1,0:T(8,128)(2,1)S(1)}, u32[]{:S(2)}, u32[]{:S(2)}) collective-permute-start(bf16[192,1536]{1,0:T(8,128)(2,1)S(1)} %get-tuple-element.349), channel_id=1, source_target_pairs={{0,16},{16,0},{1,17},{17,1},{2,18},{18,2},{3,19},{19,3},{4,20},{20... | collective-permute-start | bytes 1769480 | tf_op jit(solution)/shard_map/ppermute | solution.py:691
  85.7 16.3 %collective-permute-start.15 = (bf16[192,1536]{1,0:T(8,128)(2,1)S(1)}, bf16[192,1536]{1,0:T(8,128)(2,1)S(1)}, u32[]{:S(2)}, u32[]{:S(2)}) collective-permute-start(bf16[192,1536]{1,0:T(8,128)(2,1)S(1)} %get-tuple-element.348), channel_id=1, source_target_pairs={{0,4},{4,0},{1,5},{5,1},{2,6},{6,2},{3,7},{7,3},{8,12},{12,8},{9,1... | collective-permute-start | bytes 1769480 | tf_op jit(solution)/shard_map/ppermute | solution.py:691
  94.1 23.3 %collective-permute-start.9 = (bf16[2,16,1024]{2,1,0:T(8,128)(2,1)S(1)}, bf16[2,16,1024]{2,1,0:T(8,128)(2,1)S(1)}, u32[]{:S(2)}, u32[]{:S(2)}) collective-permute-start(bf16[2,16,1024]{2,1,0:T(8,128)(2,1)S(1)} %slice.379), channel_id=1, source_target_pairs={{0,2},{2,4},{4,6},{1,3},{3,5},{5,7},{8,10},{10,12},{12,14},{9,11},... | collective-permute-start | bytes 196616 | tf_op jit(solution)/shard_map/ppermute | solution.py:720
  102.1 40.7 %collective-permute-start.17 = (bf16[2,192,1536]{2,1,0:T(8,128)(2,1)S(1)}, bf16[2,192,1536]{2,1,0:T(8,128)(2,1)S(1)}, u32[]{:S(2)}, u32[]{:S(2)}) collective-permute-start(bf16[2,192,1536]{2,1,0:T(8,128)(2,1)S(1)} %pad_maximum_fusion.4.second), channel_id=1, source_target_pairs={{0,16},{16,0},{1,17},{17,1},{2,18},{18,2},{3,19},{19,3},{4,20},{20... | collective-permute-start | bytes 3538952 | tf_op jit(solution)/shard_map/ppermute | solution.py:691
  102.8 42.0 %collective-permute-start.16 = (bf16[2,192,1536]{2,1,0:T(8,128)(2,1)S(1)}, bf16[2,192,1536]{2,1,0:T(8,128)(2,1)S(1)}, u32[]{:S(2)}, u32[]{:S(2)}) collective-permute-start(bf16[2,192,1536]{2,1,0:T(8,128)(2,1)S(1)} %pad_maximum_fusion.3.first), channel_id=1, source_target_pairs={{0,4},{4,0},{1,5},{5,1},{2,6},{6,2},{3,7},{7,3},{8,12},{12,8},{9,1... | collective-permute-start | bytes 3538952 | tf_op jit(solution)/shard_map/ppermute | solution.py:691
  116.0 15.5 %collective-permute-start.21 = (bf16[2,16,1024]{2,1,0:T(8,128)(2,1)S(1)}, bf16[2,16,1024]{2,1,0:T(8,128)(2,1)S(1)}, u32[]{:S(2)}, u32[]{:S(2)}) collective-permute-start(bf16[2,16,1024]{2,1,0:T(8,128)(2,1)S(1)} %slice.385), channel_id=1, source_target_pairs={{0,2},{2,4},{4,6},{1,3},{3,5},{5,7},{8,10},{10,12},{12,14},{9,11},... | collective-permute-start | bytes 196616 | tf_op jit(solution)/shard_map/ppermute | solution.py:720
  126.3 23.0 %collective-permute-start.11 = (bf16[2,144,768]{2,1,0:T(8,128)(2,1)S(1)}, bf16[2,144,768]{2,1,0:T(8,128)(2,1)S(1)}, u32[]{:S(2)}, u32[]{:S(2)}) collective-permute-start(bf16[2,144,768]{2,1,0:T(8,128)(2,1)S(1)} %get-tuple-element.149.refs_6_), channel_id=1, source_target_pairs={{0,2},{1,3},{4,6},{5,7},{8,10},{9,11},{12,14},{13,15},{16,18},{17,... | collective-permute-start | bytes 1327112 | tf_op jit(solution)/shard_map/ppermute | solution.py:724
  131.4 42.4 %collective-permute-start.24 = (bf16[2,256,1536]{2,1,0:T(8,128)(2,1)}, bf16[2,256,1536]{2,1,0:T(8,128)(2,1)}, u32[]{:S(2)}, u32[]{:S(2)}) collective-permute-start(bf16[2,256,1536]{2,1,0:T(8,128)(2,1)} %param.17), channel_id=1, source_target_pairs={{0,8},{8,0},{1,9},{9,1},{2,10},{10,2},{3,11},{11,3},{4,12},{12,4},... | collective-permute-start | bytes 4718600 | tf_op jit(solution)/shard_map/ppermute | solution.py:691
  133.0 25.7 %collective-permute-start.23 = (bf16[1,256,1536]{2,1,0:T(8,128)(2,1)S(1)}, bf16[1,256,1536]{2,1,0:T(8,128)(2,1)}, u32[]{:S(2)}, u32[]{:S(2)}) collective-permute-start(bf16[1,256,1536]{2,1,0:T(8,128)(2,1)S(1)} %get-tuple-element.339.own), channel_id=1, source_target_pairs={{0,1},{1,0},{2,3},{3,2},{4,5},{5,4},{6,7},{7,6},{8,9},{9,8},{10,11... | collective-permute-start | bytes 2359304 | tf_op jit(solution)/shard_map/ppermute | solution.py:691
  142.8 31.0 %collective-permute-start.28 = (bf16[1,256,1536]{2,1,0:T(8,128)(2,1)S(1)}, bf16[1,256,1536]{2,1,0:T(8,128)(2,1)S(1)}, u32[]{:S(2)}, u32[]{:S(2)}) collective-permute-start(bf16[1,256,1536]{2,1,0:T(8,128)(2,1)S(1)} %get-tuple-element.338.own), channel_id=1, source_target_pairs={{0,1},{1,0},{2,3},{3,2},{4,5},{5,4},{6,7},{7,6},{8,9},{9,8},{10,11... | collective-permute-start | bytes 2359304 | tf_op jit(solution)/shard_map/ppermute | solution.py:691
  158.7 16.5 %collective-permute-start.25 = (bf16[1,256,1536]{2,1,0:T(8,128)(2,1)}, bf16[1,256,1536]{2,1,0:T(8,128)(2,1)}, u32[]{:S(2)}, u32[]{:S(2)}) collective-permute-start(bf16[1,256,1536]{2,1,0:T(8,128)(2,1)} %collective-permute-done.23.got), channel_id=1, source_target_pairs={{0,8},{8,0},{1,9},{9,1},{2,10},{10,2},{3,11},{11,3},{4,12},{12,4},... | collective-permute-start | bytes 2359304 | tf_op jit(solution)/shard_map/ppermute | solution.py:691
  162.2 24.2 %collective-permute-start.26 = (bf16[2,128,768]{2,1,0:T(8,128)(2,1)S(1)}, bf16[2,128,768]{2,1,0:T(8,128)(2,1)S(1)}, u32[]{:S(2)}, u32[]{:S(2)}) collective-permute-start(bf16[2,128,768]{2,1,0:T(8,128)(2,1)S(1)} %copy-done.3), channel_id=1, source_target_pairs={{2,6},{3,7},{10,14},{11,15},{18,22},{19,23},{26,30},{27,31}} | collective-permute-start | bytes 1179656 | tf_op jit(solution)/shard_map/ppermute | solution.py:730
  163.1 23.4 %collective-permute-start.22 = (bf16[2,128,768]{2,1,0:T(8,128)(2,1)S(1)}, bf16[2,128,768]{2,1,0:T(8,128)(2,1)S(1)}, u32[]{:S(2)}, u32[]{:S(2)}) collective-permute-start(bf16[2,128,768]{2,1,0:T(8,128)(2,1)S(1)} %copy-done.3), channel_id=1, source_target_pairs={{2,4},{3,5},{10,12},{11,13},{18,20},{19,21},{26,28},{27,29}} | collective-permute-start | bytes 1179656 | tf_op jit(solution)/shard_map/ppermute | solution.py:730
  173.8 25.0 %collective-permute-start.29 = (bf16[1,256,1536]{2,1,0:T(8,128)(2,1)S(1)}, bf16[1,256,1536]{2,1,0:T(8,128)(2,1)S(1)}, u32[]{:S(2)}, u32[]{:S(2)}) collective-permute-start(bf16[1,256,1536]{2,1,0:T(8,128)(2,1)S(1)} %collective-permute-done.28.got), channel_id=1, source_target_pairs={{0,8},{8,0},{1,9},{9,1},{2,10},{10,2},{3,11},{11,3},{4,12},{12,4},... | collective-permute-start | bytes 2359304 | tf_op jit(solution)/shard_map/ppermute | solution.py:691
  173.8 22.9 %collective-permute-start.30 = (bf16[2,144,768]{2,1,0:T(8,128)(2,1)S(1)}, bf16[2,144,768]{2,1,0:T(8,128)(2,1)S(1)}, u32[]{:S(2)}, u32[]{:S(2)}) collective-permute-start(bf16[2,144,768]{2,1,0:T(8,128)(2,1)S(1)} %copy-done.5), channel_id=1, source_target_pairs={{0,2},{1,3},{4,6},{5,7},{8,10},{9,11},{12,14},{13,15},{16,18},{17,... | collective-permute-start | bytes 1327112 | tf_op jit(solution)/shard_map/ppermute | solution.py:724
  197.2 32.5 %collective-permute-start.35 = (bf16[2,128,768]{2,1,0:T(8,128)(2,1)S(1)}, bf16[2,128,768]{2,1,0:T(8,128)(2,1)S(1)}, u32[]{:S(2)}, u32[]{:S(2)}) collective-permute-start(bf16[2,128,768]{2,1,0:T(8,128)(2,1)S(1)} %shard_map.288), channel_id=1, source_target_pairs={{2,6},{3,7},{10,14},{11,15},{18,22},{19,23},{26,30},{27,31}} | collective-permute-start | bytes 1179656 | tf_op jit(solution)/shard_map/ppermute | solution.py:730
  197.9 31.8 %collective-permute-start.34 = (bf16[2,128,768]{2,1,0:T(8,128)(2,1)S(1)}, bf16[2,128,768]{2,1,0:T(8,128)(2,1)S(1)}, u32[]{:S(2)}, u32[]{:S(2)}) collective-permute-start(bf16[2,128,768]{2,1,0:T(8,128)(2,1)S(1)} %shard_map.288), channel_id=1, source_target_pairs={{2,4},{3,5},{10,12},{11,13},{18,20},{19,21},{26,28},{27,29}} | collective-permute-start | bytes 1179656 | tf_op jit(solution)/shard_map/ppermute | solution.py:730
  200.0 9.6 %collective-permute-start.27 = (f32[2,8,512]{2,1,0:T(8,128)S(1)}, f32[2,8,512]{2,1,0:T(8,128)S(1)}, u32[]{:S(2)}, u32[]{:S(2)}) collective-permute-start(f32[2,8,512]{2,1,0:T(8,128)S(1)} %get-tuple-element.176), channel_id=1, source_target_pairs={{0,8},{8,0},{1,9},{9,1},{2,10},{10,2},{3,11},{11,3},{4,12},{12,4},... | collective-permute-start | bytes 98312 | tf_op jit(solution)/shard_map/ppermute | solution.py:691
  209.6 8.8 %collective-permute-start.31 = (f32[2,8,512]{2,1,0:T(8,128)S(1)}, f32[2,8,512]{2,1,0:T(8,128)S(1)}, u32[]{:S(2)}, u32[]{:S(2)}) collective-permute-start(f32[2,8,512]{2,1,0:T(8,128)S(1)} %reverse_add_fusion.1), channel_id=1, source_target_pairs={{0,1},{1,0},{2,3},{3,2},{4,5},{5,4},{6,7},{7,6},{8,9},{9,8},{10,11... | collective-permute-start | bytes 98312 | tf_op jit(solution)/shard_map/ppermute | solution.py:691
  218.0 74.7 %collective-permute-start.32 = (bf16[512,1536]{1,0:T(8,128)(2,1)}, bf16[512,1536]{1,0:T(8,128)(2,1)}, u32[]{:S(2)}, u32[]{:S(2)}) collective-permute-start(bf16[512,1536]{1,0:T(8,128)(2,1)} %slice_bitcast_fusion.7), channel_id=1, source_target_pairs={{0,8},{8,0},{1,9},{9,1},{2,10},{10,2},{3,11},{11,3},{4,12},{12,4},... | collective-permute-start | bytes 4718600 | tf_op jit(solution)/shard_map/ppermute | solution.py:691
  228.4 32.8 %collective-permute-start.33 = (bf16[2,144,768]{2,1,0:T(8,128)(2,1)S(1)}, bf16[2,144,768]{2,1,0:T(8,128)(2,1)S(1)}, u32[]{:S(2)}, u32[]{:S(2)}) collective-permute-start(bf16[2,144,768]{2,1,0:T(8,128)(2,1)S(1)} %get-tuple-element.191.refs_10_), channel_id=1, source_target_pairs={{2,0},{3,1},{6,4},{7,5},{10,8},{11,9},{14,12},{15,13},{18,16},{19,... | collective-permute-start | bytes 1327112 | tf_op jit(solution)/shard_map/ppermute | solution.py:724
  249.0 47.7 %collective-permute-start.38 = (bf16[512,1536]{1,0:T(8,128)(2,1)}, bf16[512,1536]{1,0:T(8,128)(2,1)}, u32[]{:S(2)}, u32[]{:S(2)}) collective-permute-start(bf16[512,1536]{1,0:T(8,128)(2,1)} %slice_bitcast_fusion.5), channel_id=1, source_target_pairs={{0,8},{8,0},{1,9},{9,1},{2,10},{10,2},{3,11},{11,3},{4,12},{12,4},... | collective-permute-start | bytes 4718600 | tf_op jit(solution)/shard_map/ppermute | solution.py:691
  261.7 23.6 %collective-permute-start.41 = (bf16[2,128,768]{2,1,0:T(8,128)(2,1)S(1)}, bf16[2,128,768]{2,1,0:T(8,128)(2,1)S(1)}, u32[]{:S(2)}, u32[]{:S(2)}) collective-permute-start(bf16[2,128,768]{2,1,0:T(8,128)(2,1)S(1)} %shard_map.293), channel_id=1, source_target_pairs={{4,0},{5,1},{12,8},{13,9},{20,16},{21,17},{28,24},{29,25}} | collective-permute-start | bytes 1179656 | tf_op jit(solution)/shard_map/ppermute | solution.py:730
  263.0 22.3 %collective-permute-start.40 = (bf16[2,128,768]{2,1,0:T(8,128)(2,1)S(1)}, bf16[2,128,768]{2,1,0:T(8,128)(2,1)S(1)}, u32[]{:S(2)}, u32[]{:S(2)}) collective-permute-start(bf16[2,128,768]{2,1,0:T(8,128)(2,1)S(1)} %shard_map.293), channel_id=1, source_target_pairs={{4,2},{5,3},{12,10},{13,11},{20,18},{21,19},{28,26},{29,27}} | collective-permute-start | bytes 1179656 | tf_op jit(solution)/shard_map/ppermute | solution.py:730
  263.7 28.0 %collective-permute-start.42 = (bf16[2,144,768]{2,1,0:T(8,128)(2,1)S(1)}, bf16[2,144,768]{2,1,0:T(8,128)(2,1)S(1)}, u32[]{:S(2)}, u32[]{:S(2)}) collective-permute-start(bf16[2,144,768]{2,1,0:T(8,128)(2,1)S(1)} %get-tuple-element.220), channel_id=1, source_target_pairs={{2,0},{3,1},{6,4},{7,5},{10,8},{11,9},{14,12},{15,13},{18,16},{19,... | collective-permute-start | bytes 1327112 | tf_op jit(solution)/shard_map/ppermute | solution.py:724
  286.6 40.4 %collective-permute-start.46 = (bf16[2,2,192,768]{3,2,1,0:T(8,128)(2,1)}, bf16[2,2,192,768]{3,2,1,0:T(8,128)(2,1)}, u32[]{:S(2)}, u32[]{:S(2)}) collective-permute-start(bf16[2,2,192,768]{3,2,1,0:T(8,128)(2,1)} %pad_maximum_fusion.6.refs_20_), channel_id=1, source_target_pairs={{0,4},{4,0},{1,5},{5,1},{2,6},{6,2},{3,7},{7,3},{8,12},{12,8},{9,1... | collective-permute-start | bytes 3538952 | tf_op jit(solution)/shard_map/ppermute | solution.py:691
  290.1 36.9 %collective-permute-start.45 = (bf16[2,2,192,768]{3,2,1,0:T(8,128)(2,1)S(1)}, bf16[2,2,192,768]{3,2,1,0:T(8,128)(2,1)}, u32[]{:S(2)}, u32[]{:S(2)}) collective-permute-start(bf16[2,2,192,768]{3,2,1,0:T(8,128)(2,1)S(1)} %pad_maximum_fusion.5.refs_19_), channel_id=1, source_target_pairs={{0,16},{16,0},{1,17},{17,1},{2,18},{18,2},{3,19},{19,3},{4,20},{20... | collective-permute-start | bytes 3538952 | tf_op jit(solution)/shard_map/ppermute | solution.py:691
  292.0 34.9 %collective-permute-start.43 = (bf16[2,128,768]{2,1,0:T(8,128)(2,1)S(1)}, bf16[2,128,768]{2,1,0:T(8,128)(2,1)S(1)}, u32[]{:S(2)}, u32[]{:S(2)}) collective-permute-start(bf16[2,128,768]{2,1,0:T(8,128)(2,1)S(1)} %shard_map.294.refs_17_), channel_id=1, source_target_pairs={{4,2},{5,3},{12,10},{13,11},{20,18},{21,19},{28,26},{29,27}} | collective-permute-start | bytes 1179656 | tf_op jit(solution)/shard_map/ppermute | solution.py:730
  292.7 34.2 %collective-permute-start.44 = (bf16[2,128,768]{2,1,0:T(8,128)(2,1)S(1)}, bf16[2,128,768]{2,1,0:T(8,128)(2,1)S(1)}, u32[]{:S(2)}, u32[]{:S(2)}) collective-permute-start(bf16[2,128,768]{2,1,0:T(8,128)(2,1)S(1)} %shard_map.294.refs_17_), channel_id=1, source_target_pairs={{4,0},{5,1},{12,8},{13,9},{20,16},{21,17},{28,24},{29,25}} | collective-permute-start | bytes 1179656 | tf_op jit(solution)/shard_map/ppermute | solution.py:730
  300.5 35.8 %collective-permute-start.39 = (bf16[2,256,1536]{2,1,0:T(8,128)(2,1)}, bf16[2,256,1536]{2,1,0:T(8,128)(2,1)}, u32[]{:S(2)}, u32[]{:S(2)}) collective-permute-start(bf16[2,256,1536]{2,1,0:T(8,128)(2,1)} %pad_maximum_fusion.1.refs_18_), channel_id=1, source_target_pairs={{0,1},{1,0},{2,3},{3,2},{4,5},{5,4},{6,7},{7,6},{8,9},{9,8},{10,11... | collective-permute-start | bytes 4718600 | tf_op jit(solution)/shard_map/ppermute | solution.py:691
  339.4 30.8 %collective-permute-start.51 = (bf16[2,192,768]{2,1,0:T(8,128)(2,1)S(1)}, bf16[2,192,768]{2,1,0:T(8,128)(2,1)S(1)}, u32[]{:S(2)}, u32[]{:S(2)}) collective-permute-start(bf16[2,192,768]{2,1,0:T(8,128)(2,1)S(1)} %pad_maximum_fusion.11), channel_id=1, source_target_pairs={{0,16},{16,0},{1,17},{17,1},{2,18},{18,2},{3,19},{19,3},{4,20},{20... | collective-permute-start | bytes 1769480 | tf_op jit(solution)/shard_map/ppermute | solution.py:691
  341.8 28.4 %collective-permute-start.50 = (bf16[2,192,768]{2,1,0:T(8,128)(2,1)S(1)}, bf16[2,192,768]{2,1,0:T(8,128)(2,1)S(1)}, u32[]{:S(2)}, u32[]{:S(2)}) collective-permute-start(bf16[2,192,768]{2,1,0:T(8,128)(2,1)S(1)} %pad_maximum_fusion.10), channel_id=1, source_target_pairs={{0,4},{4,0},{1,5},{5,1},{2,6},{6,2},{3,7},{7,3},{8,12},{12,8},{9,1... | collective-permute-start | bytes 1769480 | tf_op jit(solution)/shard_map/ppermute | solution.py:691
  357.2 14.7 %collective-permute-start.48 = (bf16[512,1536]{1,0:T(8,128)(2,1)S(1)}, bf16[512,1536]{1,0:T(8,128)(2,1)S(1)}, u32[]{:S(2)}, u32[]{:S(2)}) collective-permute-start(bf16[512,1536]{1,0:T(8,128)(2,1)S(1)} %slice_bitcast_fusion.3), channel_id=1, source_target_pairs={{0,8},{8,0},{1,9},{9,1},{2,10},{10,2},{3,11},{11,3},{4,12},{12,4},... | collective-permute-start | bytes 4718600 | tf_op jit(solution)/shard_map/ppermute | solution.py:691
  370.6 32.3 %collective-permute-start.52 = (bf16[2,192,768]{2,1,0:T(8,128)(2,1)S(1)}, bf16[2,192,768]{2,1,0:T(8,128)(2,1)S(1)}, u32[]{:S(2)}, u32[]{:S(2)}) collective-permute-start(bf16[2,192,768]{2,1,0:T(8,128)(2,1)S(1)} %get-tuple-element.343.refs_19_), channel_id=1, source_target_pairs={{2,0},{8,10},{10,2},{0,8},{3,1},{9,11},{11,3},{1,9},{6,4},{12,14},... | collective-permute-start | bytes 1769480 | tf_op jit(solution)/shard_map/ppermute | solution.py:834
  371.0 31.9 %collective-permute-start.53 = (bf16[2,192,768]{2,1,0:T(8,128)(2,1)S(1)}, bf16[2,192,768]{2,1,0:T(8,128)(2,1)S(1)}, u32[]{:S(2)}, u32[]{:S(2)}) collective-permute-start(bf16[2,192,768]{2,1,0:T(8,128)(2,1)S(1)} %get-tuple-element.342.refs_20_), channel_id=1, source_target_pairs={{2,8},{8,2},{3,9},{9,3},{6,12},{12,6},{7,13},{13,7},{18,24},{24,18... | collective-permute-start | bytes 1769480 | tf_op jit(solution)/shard_map/ppermute | solution.py:835
  372.4 33.6 %collective-permute-start.49 = (bf16[256,1536]{1,0:T(8,128)(2,1)S(1)}, bf16[256,1536]{1,0:T(8,128)(2,1)S(1)}, u32[]{:S(2)}, u32[]{:S(2)}) collective-permute-start(bf16[256,1536]{1,0:T(8,128)(2,1)S(1)} %constant_dynamic-slice_fusion.8.refs_17_), channel_id=1, source_target_pairs={{0,1},{1,0},{2,3},{3,2},{4,5},{5,4},{6,7},{7,6},{8,9},{9,8},{10,11... | collective-permute-start | bytes 2359304 | tf_op jit(solution)/shard_map/ppermute | solution.py:691
  404.1 12.5 %collective-permute-start.54 = (f32[2,8,1024]{2,1,0:T(8,128)S(1)}, f32[2,8,1024]{2,1,0:T(8,128)S(1)}, u32[]{:S(2)}, u32[]{:S(2)}) collective-permute-start(f32[2,8,1024]{2,1,0:T(8,128)S(1)} %get-tuple-element.249), channel_id=1, source_target_pairs={{2,0},{4,2},{6,4},{3,1},{5,3},{7,5},{10,8},{12,10},{14,12},{11,9},... | collective-permute-start | bytes 196616 | tf_op jit(solution)/shard_map/ppermute | solution.py:720
  424.6 15.2 %collective-permute-start.55 = (bf16[512,1536]{1,0:T(8,128)(2,1)}, bf16[512,1536]{1,0:T(8,128)(2,1)}, u32[]{:S(2)}, u32[]{:S(2)}) collective-permute-start(bf16[512,1536]{1,0:T(8,128)(2,1)} %slice_bitcast_fusion.1), channel_id=1, source_target_pairs={{0,8},{8,0},{1,9},{9,1},{2,10},{10,2},{3,11},{11,3},{4,12},{12,4},... | collective-permute-start | bytes 4718600 | tf_op jit(solution)/shard_map/ppermute | solution.py:691
  432.9 24.9 %collective-permute-start.58 = (bf16[1,2,192,1152]{3,2,1,0:T(8,128)(2,1)}, bf16[1,2,192,1152]{3,2,1,0:T(8,128)(2,1)}, u32[]{:S(2)}, u32[]{:S(2)}) collective-permute-start(bf16[1,2,192,1152]{3,2,1,0:T(8,128)(2,1)} %dynamic-slice_bitcast_fusion), channel_id=1, source_target_pairs={{0,4},{4,0},{1,5},{5,1},{2,6},{6,2},{3,7},{7,3},{8,12},{12,8},{9,1... | collective-permute-start | bytes 2654216 | tf_op jit(solution)/shard_map/ppermute | solution.py:691
  438.4 21.9 %collective-permute-start.57 = (bf16[1,2,192,1152]{3,2,1,0:T(8,128)(2,1)}, bf16[1,2,192,1152]{3,2,1,0:T(8,128)(2,1)}, u32[]{:S(2)}, u32[]{:S(2)}) collective-permute-start(bf16[1,2,192,1152]{3,2,1,0:T(8,128)(2,1)} %dynamic-slice_bitcast_fusion.1), channel_id=1, source_target_pairs={{0,16},{16,0},{1,17},{17,1},{2,18},{18,2},{3,19},{19,3},{4,20},{20... | collective-permute-start | bytes 2654216 | tf_op jit(solution)/shard_map/ppermute | solution.py:691
  443.3 23.0 %collective-permute-start.56 = (bf16[256,1536]{1,0:T(8,128)(2,1)}, bf16[256,1536]{1,0:T(8,128)(2,1)}, u32[]{:S(2)}, u32[]{:S(2)}) collective-permute-start(bf16[256,1536]{1,0:T(8,128)(2,1)} %constant_dynamic-slice_fusion.2), channel_id=1, source_target_pairs={{0,1},{1,0},{2,3},{3,2},{4,5},{5,4},{6,7},{7,6},{8,9},{9,8},{10,11... | collective-permute-start | bytes 2359304 | tf_op jit(solution)/shard_map/ppermute | solution.py:691
  463.2 11.6 %collective-permute-start.60 = (bf16[1,192,1152]{2,1,0:T(8,128)(2,1)}, bf16[1,192,1152]{2,1,0:T(8,128)(2,1)}, u32[]{:S(2)}, u32[]{:S(2)}) collective-permute-start(bf16[1,192,1152]{2,1,0:T(8,128)(2,1)} %constant_dynamic-slice_fusion), channel_id=1, source_target_pairs={{0,16},{16,0},{1,17},{17,1},{2,18},{18,2},{3,19},{19,3},{4,20},{20... | collective-permute-start | bytes 1327112 | tf_op jit(solution)/shard_map/ppermute | solution.py:691
  465.3 11.3 %collective-permute-start.59 = (bf16[1,192,1152]{2,1,0:T(8,128)(2,1)}, bf16[1,192,1152]{2,1,0:T(8,128)(2,1)}, u32[]{:S(2)}, u32[]{:S(2)}) collective-permute-start(bf16[1,192,1152]{2,1,0:T(8,128)(2,1)} %constant_dynamic-slice_fusion.1), channel_id=1, source_target_pairs={{0,4},{4,0},{1,5},{5,1},{2,6},{6,2},{3,7},{7,3},{8,12},{12,8},{9,1... | collective-permute-start | bytes 1327112 | tf_op jit(solution)/shard_map/ppermute | solution.py:691
  479.2 19.0 %collective-permute-start.63 = (bf16[1,192,1152]{2,1,0:T(8,128)(2,1)}, bf16[1,192,1152]{2,1,0:T(8,128)(2,1)}, u32[]{:S(2)}, u32[]{:S(2)}) collective-permute-start(bf16[1,192,1152]{2,1,0:T(8,128)(2,1)} %get-tuple-element.324), channel_id=1, source_target_pairs={{2,0},{8,10},{10,2},{0,8},{3,1},{9,11},{11,3},{1,9},{6,4},{12,14},... | collective-permute-start | bytes 1327112 | tf_op jit(solution)/shard_map/ppermute | solution.py:834
  479.2 19.0 %collective-permute-start.64 = (bf16[1,192,1152]{2,1,0:T(8,128)(2,1)}, bf16[1,192,1152]{2,1,0:T(8,128)(2,1)}, u32[]{:S(2)}, u32[]{:S(2)}) collective-permute-start(bf16[1,192,1152]{2,1,0:T(8,128)(2,1)} %get-tuple-element.325), channel_id=1, source_target_pairs={{2,8},{8,2},{3,9},{9,3},{6,12},{12,6},{7,13},{13,7},{18,24},{24,18... | collective-permute-start | bytes 1327112 | tf_op jit(solution)/shard_map/ppermute | solution.py:835
  499.7 13.8 %collective-permute-start.65 = (f32[7460]{0:T(1024)S(1)}, f32[7460]{0:T(1024)S(1)}, u32[]{:S(2)}, u32[]{:S(2)}) collective-permute-start(f32[7460]{0:T(1024)S(1)} %add.420), channel_id=1, source_target_pairs={{0,2},{2,0},{1,3},{3,1},{4,6},{6,4},{5,7},{7,5},{8,10},{10,8},{9,1... | collective-permute-start | bytes 89528 | tf_op jit(solution)/shard_map/ppermute | solution.py:691
  505.9 19.1 %collective-permute-start.68 = (f32[192,256]{1,0:T(8,128)S(1)}, f32[192,256]{1,0:T(8,128)S(1)}, u32[]{:S(2)}, u32[]{:S(2)}) collective-permute-start(f32[192,256]{1,0:T(8,128)S(1)} %slice.418), channel_id=1, source_target_pairs={{0,1},{1,0},{2,3},{3,2},{4,5},{5,4},{6,7},{7,6},{8,9},{9,8},{10,11... | collective-permute-start | bytes 589832 | tf_op jit(solution)/shard_map/ppermute | solution.py:691
  509.5 15.6 %collective-permute-start.69 = (f32[192,256]{1,0:T(8,128)S(1)}, f32[192,256]{1,0:T(8,128)S(1)}, u32[]{:S(2)}, u32[]{:S(2)}) collective-permute-start(f32[192,256]{1,0:T(8,128)S(1)} %slice.418), channel_id=1, source_target_pairs={{0,2},{2,0},{1,3},{3,1},{4,6},{6,4},{5,7},{7,5},{8,10},{10,8},{9,1... | collective-permute-start | bytes 589832 | tf_op jit(solution)/shard_map/ppermute | solution.py:691
  509.5 15.6 %collective-permute-start.70 = (f32[192,256]{1,0:T(8,128)S(1)}, f32[192,256]{1,0:T(8,128)S(1)}, u32[]{:S(2)}, u32[]{:S(2)}) collective-permute-start(f32[192,256]{1,0:T(8,128)S(1)} %slice.418), channel_id=1, source_target_pairs={{0,3},{3,0},{1,2},{2,1},{4,7},{7,4},{5,6},{6,5},{8,11},{11,8},{9,1... | collective-permute-start | bytes 589832 | tf_op jit(solution)/shard_map/ppermute | solution.py:1202
  (94 other events, 726.7 us)

commit v4 on v3

--- a/solution.py
+++ b/solution.py
@@ -40,8 +40,13 @@
     return sum(dot(term, spread) for term in pieces(value, 2))
 
 
-def gather_heads(value, spread):
-    return sum(dot_nt(term, spread) for term in pieces(value, 2))
+def gather_heads(value, collect):
+    return sum(dot(term, collect) for term in pieces(value, 2))
+
+
+def lane_sums(value):
+    folded = sum(value[:, at : at + LANES] for at in range(0, value.shape[1], LANES))
+    return jnp.sum(jnp.transpose(folded), axis=0, keepdims=True)
 
 
 def running_sum(value, mask):
@@ -161,7 +166,7 @@
     b_low = xbc_ref[0, :, inner : inner + LANES]
     c_low = xbc_ref[0, :, inner + LANES :]
     b_turned = turned(b_low)
-    score = dot_nt(c_low, b_low)
+    score = dot(c_low, b_turned)
     causal = iota2(HALF, HALF, 0) >= iota2(HALF, HALF, 1)
     first = iota2(1, LANES, 1) < LANES // 2
     squares = jnp.zeros((CHUNK, STRIP), F32)
@@ -200,10 +205,7 @@
         mixed_ref[0, :, cols] = gained.astype(BF16)
         squares = squares + gated * gated
         crossed = crossed + gained * gm_ref[0, :, cols]
-    ones = jnp.ones((8, STRIP), BF16)
-    square_row = sum(dot_nt(ones, term) for term in pieces(squares, 3))
-    cross_row = sum(dot_nt(ones, term) for term in pieces(crossed, 3))
-    stat_ref[0] = jnp.where(iota2(8, CHUNK, 0) == 0, square_row, cross_row)
+    stat_ref[0] = jnp.where(iota2(8, CHUNK, 0) == 0, lane_sums(squares), lane_sums(crossed))
 
 
 def gate_kernel(
@@ -255,7 +257,7 @@
 
 def adjoint_kernel(
     xbc_ref, sum_ref, dt_ref, gy_ref, y_ref, enter_ref, packed_ref, first_ref, second_ref, mix_ref, before_ref, halo_ref,
-    step_ref, taps_ref, heads_ref, rows_ref, spread_ref,
+    step_ref, taps_ref, heads_ref, rows_ref, spread_ref, collect_ref,
     gmix_ref, rim_ref, gtaps_ref, gheads_ref, gskip_ref, back, ext, gpre, pulled,
 ):
     inner = spread_ref.shape[1]
@@ -295,7 +297,7 @@
     b_low = xbc_ref[0, :, inner : inner + LANES]
     c_low = xbc_ref[0, :, inner + LANES :]
     c_turned = turned(c_low)
-    score = dot_nt(b_low, c_low)
+    score = dot(b_low, c_turned)
     causal = iota2(HALF, HALF, 0) <= iota2(HALF, HALF, 1)
     first = iota2(1, LANES, 1) < LANES // 2
     pulled[...] = jnp.zeros_like(pulled)
@@ -325,6 +327,7 @@
 
     for cols in strips(inner):
         held = spread_ref[:, cols]
+        collect = collect_ref[cols, :]
         x = xbc_ref[0, :, cols].astype(F32)
         dt_wide = spread_heads(dt, held)
         fade_wide = spread_heads(fade, held)
@@ -333,6 +336,7 @@
         weighted = (u * fade_wide).astype(BF16)
         gy_low = gy_ref[0, :, cols]
         gy = gy_low.astype(F32)
+        gy_turned = jnp.transpose(gy).astype(BF16)
         reached = (gy * spread_heads(reach, held)).astype(BF16)
         later = back[:, cols]
         later_low = later.astype(BF16)
@@ -341,14 +345,14 @@
         gc = gc + dot_nt(reached, entered)
         gu_carried = dot(b_low, later_low) * fade_wide
         sums = jnp.sum(later * entered.astype(F32), axis=0, keepdims=True)
-        joined = joined + gather_heads(jnp.broadcast_to(sums, (8, STRIP)), held)
+        joined = joined + gather_heads(jnp.broadcast_to(sums, (8, STRIP)), collect)
         back[:, cols] = later * spread_heads(decay, held)[0:1, :] + dot(c_turned, reached)
         parts = []
         for pair in range(STRIP // LANES):
             lanes = slice(pair * LANES, (pair + 1) * LANES)
             top = gu_carried[0:HALF, lanes]
             bottom = gu_carried[HALF:, lanes]
-            gy_pair = gy_low[:, lanes]
+            gy_pair = gy_turned[lanes, :]
             for side in range(2):
                 head = (cols.start + pair * LANES) // (LANES // 2) + side
                 keep = first if side == 0 else ~first
@@ -362,16 +366,16 @@
                 top = top + dot((score[0:HALF, 0:HALF] * corner).astype(BF16), gy_mine[0:HALF])
                 top = top + dot((score[0:HALF, HALF:] * side_right).astype(BF16), gy_mine[HALF:])
                 bottom = bottom + dot((score[HALF:, HALF:] * low_right).astype(BF16), gy_mine[HALF:])
-                upper = dot_nt(u_mine[0:HALF], gy_pair)
+                upper = dot(u_mine[0:HALF], gy_pair)
                 pulled[0:HALF, 0:HALF] += upper[:, 0:HALF] * corner
                 pulled[0:HALF, HALF:] += upper[:, HALF:] * side_right
-                pulled[HALF:, HALF:] += dot_nt(u_mine[HALF:], gy_pair[HALF:]) * low_right
+                pulled[HALF:, HALF:] += dot(u_mine[HALF:], gy_pair[:, HALF:]) * low_right
             parts.append(jnp.concatenate([top, bottom], axis=0))
         gu = jnp.concatenate(parts, axis=1)
         u_kept = u_low.astype(F32)
-        between = between + gather_heads(gy * y_ref[0, :, cols] - u_kept * gu, held)
-        arrived = arrived + gather_heads(u_kept * gu_carried, held)
-        direct = direct + gather_heads(x * gu, held)
+        between = between + gather_heads(gy * y_ref[0, :, cols] - u_kept * gu, collect)
+        arrived = arrived + gather_heads(u_kept * gu_carried, collect)
+        direct = direct + gather_heads(x * gu, collect)
         gskip_ref[:, cols] += jnp.broadcast_to(jnp.sum(gy * x, axis=0, keepdims=True), (8, STRIP))
         conv_part(cols, dt_wide * gu + rows_ref[0:1, cols] * gy)
 
@@ -531,7 +535,7 @@
     )
 
 
-def adjoint(xbc, cumul, dt, gy, y, enter, gin, xw, halo, taps, heads, rows, spread, after):
+def adjoint(xbc, cumul, dt, gy, y, enter, gin, xw, halo, taps, heads, rows, spread, collect, after):
     groups, length, width = xbc.shape
     inner = spread.shape[1]
     chunks = length // CHUNK
@@ -563,6 +567,7 @@
             (heads, fixed(heads.shape)),
             (rows, fixed(rows.shape)),
             (spread, fixed(spread.shape)),
+            (collect, fixed(collect.shape)),
         ],
         [
             (shaped((groups, length, width + LANES), BF16), flat(width + LANES, back)),
@@ -1098,7 +1103,7 @@
         xbc, cumul, dt = local[part][0:3]
         gmix, rim, *sums = adjoint(
             xbc, cumul, dt, gates[part][0], mixes[part][0], mixes[part][1], gin,
-            *scans[part], taps, head_in, rows, spread, wait_for,
+            *scans[part], taps, head_in, rows, spread, jnp.transpose(spread), wait_for,
         )
         if part == micro - 1 and fast and micro > 1:
             got_home = hold(got_home, gmix)

time: 536 us -> 541 us (level)
  no operation moved by 1% of the time
where the time goes in v4:
time: 541 us; the launch traced here: 531 us
  Pallas kernels  131 us (24%)
  waiting for transfers between devices  111 us (21%)
  matrix products  104 us (19%)
  starting transfers between devices  99.9 us (18%)
  other arithmetic  49.9 us (9%)
  local copies, waits for them, and re-layouts  32.2 us (6%)
    pallas_call x8, Pallas kernels, run(): pl.pallas_call(body, grid=grid, in_specs=[spec for _, spec in ins] + [pl....  105 us
    dot_general x18, matrix products, matmul(): lax.dot_general(left, right, (contract, ((), ())), preferred_element_type...  104 us
    ppermute x48, waiting for transfers between devices, swap(): return lax.ppermute(value, axis, [(0, 1), (1, 0)])  97.5 us
    ppermute x48, starting transfers between devices, swap(): return lax.ppermute(value, axis, [(0, 1), (1, 0)])  58.8 us
    pallas_call x4, Pallas kernels, joined(): pl.pallas_call(join_kernel, grid_spec=pltpu.PrefetchScalarGridSpec(num_sc...  13 us
    ppermute x4, starting transfers between devices, row_hop(): lax.ppermute(packed, 'zp', [(0, 1)] if way == 1 else [(1, 0)])  12.6 us
    convert_element_type x8, other arithmetic, added(): return (kept.astype(F32) + got.astype(F32)).astype(dtype)  11.8 us
    pallas_call x2, Pallas kernels, place(): pl.pallas_call(place_kernel, grid_spec=pltpu.PrefetchScalarGridSpec(num_s...  11.5 us
  transfers between devices with their start and end apart: 73, of which 21 were waited for; matrix products, arithmetic and copies ran while one was open for 30% of the time, Pallas kernels for 25%

profile of v4, /device:TPU:0, one launch (start us, length us, event | category | flops | bytes accessed | tf_op | source)
XLA Modules:
  0.0 531.3 jit_solution(14478217423751743836)
XLA Ops:
  2.6 4.1 collective-permute-start.3
  19.6 20.6 %collective-permute-done.got = bf16[1,256,1536]{2,1,0:T(8,128)(2,1)} collective-permute-done((bf16[1,256,1536]{2,1,0:T(8,128)(2,1)S(1)}, bf16[1,256,1536]{2,1,0:T(8,128)(2,1)}, u32[]{:S(2)}, u32[]{:S(2)}) %collective-permute-start) | collective-permute-done | bytes 786464 | tf_op jit(solution)/shard_map/ppermute | solution.py:696
  49.6 16.5 %collective-permute-done.18.got = bf16[1,256,1536]{2,1,0:T(8,128)(2,1)} collective-permute-done((bf16[1,256,1536]{2,1,0:T(8,128)(2,1)S(1)}, bf16[1,256,1536]{2,1,0:T(8,128)(2,1)}, u32[]{:S(2)}, u32[]{:S(2)}) %collective-permute-start.18) | collective-permute-done | bytes 786464 | tf_op jit(solution)/shard_map/ppermute | solution.py:696
  73.3 3.7 shard_map.279
  77.5 7.1 %shard_map.280 = bf16[2,2,2,192,1152]{4,3,2,1,0:T(8,128)(2,1)} custom-call(s32[3]{0:T(128)S(1)} %pad_add_fusion.at_ref, bf16[2,192,1152]{2,1,0:T(8,128)(2,1)S(1)} %pad_maximum_fusion.7.first, bf16[2,192,1152]{2,1,0:T(8,128)(2,1)} %collective-permute-done.7.first_y, bf16[2,192,1152]{2,1,0:T(8,128)(2,1)S(1)} %pad_maximum_fusion.8.second, ...), custom_call_target="tpu_custom_call" | custom-call | bytes 221184 | tf_op jit(solution)/shard_map/pallas_call | solution.py:642
  89.3 6.5 %convolution_convert_fusion.3.refs_0_.refs_2_.refs_9_.refs_10_.refs_12_ = bf16[2,512,1152]{2,1,0:T(8,128)(2,1)S(1)} fusion(bf16[2,512,1536]{2,1,0:T(8,128)(2,1)S(1)} %copy-done.39, bf16[1536,1152,1]{1,0,2:T(8,128)(2,1)} %bitcast.273), kind=kOutput, calls=%fused_computation.12 | convolution fusion | flops 3625058304 | bytes 9043968 | tf_op jit(solution)/shard_map/dot_general | solution.py:894
  95.9 2.7 collective-permute-start.9
  98.7 2.7 collective-permute-done.14
  103.9 2.5 collective-permute-start.16
  106.4 3.4 shard_map.282
  109.8 7.2 %convolution_convert_fusion.2.refs_0_.refs_2_.refs_9_.refs_10_.refs_12_ = bf16[2,512,1152]{2,1,0:T(8,128)(2,1)S(1)} fusion(bf16[2,512,1536]{2,1,0:T(8,128)(2,1)} %shard_map.282, bf16[1536,1152,1]{1,0,2:T(8,128)(2,1)} %bitcast.274), kind=kOutput, calls=%fused_computation.11 | convolution fusion | flops 3625058304 | bytes 9043968 | tf_op jit(solution)/shard_map/dot_general | solution.py:894
  118.4 8.9 %shard_map.281 = (bf16[2,512,1024]{2,1,0:T(8,128)(2,1)S(1)}, f32[2,512,128]{2,1,0:T(8,128)S(1)}, f32[2,512,128]{2,1,0:T(8,128)S(1)}, f32[2,128,768]{2,1,0:T(8,12...) custom-call(bf16[2,512,1152]{2,1,0:T(8,128)(2,1)} %copy-done.72, ...), custom_call_target="tpu_custom_call" | custom-call | flops 6000000000 | bytes 8000000 | tf_op jit(solution)/shard_map/pallas_call | solution.py:423
  127.3 5.1 collective-permute-start.11
  134.1 8.9 %shard_map.283 = (bf16[2,512,1024]{2,1,0:T(8,128)(2,1)S(1)}, f32[2,512,128]{2,1,0:T(8,128)S(1)}, f32[2,512,128]{2,1,0:T(8,128)S(1)}, f32[2,128,768]{2,1,0:T(8,12...) custom-call(bf16[2,512,1152]{2,1,0:T(8,128)(2,1)} %copy-done.71, ...), custom_call_target="tpu_custom_call" | custom-call | flops 6000000000 | bytes 8000000 | tf_op jit(solution)/shard_map/pallas_call | solution.py:423
  145.9 4.4 shard_map.284
  150.8 6.5 %convolution_convert_fusion.5.refs_6_.refs_2_ = bf16[2,512,768]{2,1,0:T(8,128)(2,1)} fusion(bf16[2,512,1536]{2,1,0:T(8,128)(2,1)} %shard_map.279, bf16[1536,1536]{1,0:T(8,128)(2,1)} %bitcast.257), kind=kOutput, calls=%fused_computation.37 | convolution fusion | flops 2416705536 | bytes 7077888 | tf_op jit(solution)/shard_map/dot_general | solution.py:894
  157.4 2.3 collective-permute-done.23.got
  159.9 3.3 slice.387
  164.8 5.3 %convolution_convert_fusion.4.refs_6_.refs_2_ = bf16[2,512,768]{2,1,0:T(8,128)(2,1)} fusion(bf16[2,512,1536]{2,1,0:T(8,128)(2,1)S(1)} %copy-done.36, bf16[1536,1536]{1,0:T(8,128)(2,1)} %bitcast.259), kind=kOutput, calls=%fused_computation.36 | convolution fusion | flops 2416705536 | bytes 7077888 | tf_op jit(solution)/shard_map/dot_general | solution.py:894
  170.1 3.4 collective-permute-done.28.got
  173.5 4.5 collective-permute-start.30
  179.3 3.7 shard_map.286
  183.0 6.3 %fusion.11.refs_7_.refs_10_.refs_3_ = f32[2,512,768]{2,1,0:T(8,128)} fusion(bf16[2,512,1536]{2,1,0:T(8,128)(2,1)} %shard_map.286, bf16[1536,768]{1,0:T(8,128)(2,1)S(1)} %copy-done.45), kind=kOutput, calls=%fused_computation.30 | convolution fusion | flops 2415919104 | bytes 8650752 | tf_op jit(solution)/shard_map/dot_general | solution.py:894
  189.3 10.2 %shard_map.287 = (f32[2,512,768]{2,1,0:T(8,128)}, bf16[2,512,768]{2,1,0:T(8,128)(2,1)S(1)}, bf16[2,2,128,768]{3,2,1,0:T(8,128)(2,1)S(1)}, f32[2,8,512]{2,1,0:T(8,128)S(1)}) custom-call(bf16[2,512,1024]{2,1,0:T(8,128)(2,1)} %copy-done.8, f32[2,512,128]{2,1,0:T(8,128)S(1)} %copy-done.14, f32[2,512,128]{2,1,0:T(8,128)S(1)} %copy-done.18, ...), custom_call_target="tpu_custom_call" | custom-call | flops 10000000000 | bytes 16000000 | tf_op jit(solution)/shard_map/pallas_call | solution.py:423
  205.2 6.8 %fusion.9.refs_7_.refs_11_.refs_3_ = f32[2,512,768]{2,1,0:T(8,128)} fusion(bf16[2,512,1536]{2,1,0:T(8,128)(2,1)} %shard_map.289, bf16[1536,1536]{1,0:T(8,128)(2,1)} %bitcast.260), kind=kOutput, calls=%fused_computation.28 | convolution fusion | flops 2415919104 | bytes 8650752 | tf_op jit(solution)/shard_map/dot_general | solution.py:894
  212.0 2.5 collective-permute-start.31
  214.6 4.5 convolution_convert_fusion.1.refs_9_
  221.4 8.3 %shard_map.290 = (bf16[2,512,768]{2,1,0:T(8,128)(2,1)S(1)}, bf16[2,512,768]{2,1,0:T(8,128)(2,1)S(1)}, bf16[2,512,768]{2,1,0:T(8,128)(2,1)}, f32[2,128,768]{2,1,0...) custom-call(f32[2,512,768]{2,1,0:T(8,128)} %get-tuple-element.181.refs_0_.refs_4_, ...), custom_call_target="tpu_custom_call" | custom-call | flops 6000000000 | bytes 18000000 | tf_op jit(solution)/shard_map/pallas_call | solution.py:423
  232.2 10.2 %shard_map.291 = (f32[2,512,768]{2,1,0:T(8,128)}, bf16[2,512,768]{2,1,0:T(8,128)(2,1)S(1)}, bf16[2,2,128,768]{3,2,1,0:T(8,128)(2,1)S(1)}, f32[2,8,512]{2,1,0:T(8,128)S(1)}) custom-call(bf16[2,512,1024]{2,1,0:T(8,128)(2,1)} %copy-done.7, f32[2,512,128]{2,1,0:T(8,128)S(1)} %copy-done.12, f32[2,512,128]{2,1,0:T(8,128)S(1)} %copy-done.16, ...), custom_call_target="tpu_custom_call" | custom-call | flops 10000000000 | bytes 16000000 | tf_op jit(solution)/shard_map/pallas_call | solution.py:423
  242.5 6.9 %convolution_bitcast_fusion.3 = f32[1536,768]{1,0:T(8,128)} fusion(bf16[2,512,1536]{2,1,0:T(8,128)(2,1)} %shard_map.279, bf16[2,512,768]{2,1,0:T(8,128)(2,1)S(1)} %get-tuple-element.216), kind=kOutput, calls=%fused_computation.14 | convolution fusion | flops 2415919104 | bytes 9437184 | tf_op jit(solution)/shard_map/dot_general | solution.py:894
  249.8 2.9 convolution_convert_fusion.refs_9_
  255.7 8.2 %shard_map.292 = (bf16[2,512,768]{2,1,0:T(8,128)(2,1)S(1)}, bf16[2,512,768]{2,1,0:T(8,128)(2,1)S(1)}, bf16[2,512,768]{2,1,0:T(8,128)(2,1)}, f32[2,128,768]{2,1,0...) custom-call(f32[2,512,768]{2,1,0:T(8,128)} %get-tuple-element.197.refs_0_.refs_4_, ...), custom_call_target="tpu_custom_call" | custom-call | flops 6000000000 | bytes 18000000 | tf_op jit(solution)/shard_map/pallas_call | solution.py:423
  268.1 7.3 %convolution_bitcast_fusion.2 = f32[1536,768]{1,0:T(8,128)} fusion(bf16[2,512,1536]{2,1,0:T(8,128)(2,1)} %shard_map.286, bf16[2,512,768]{2,1,0:T(8,128)(2,1)} %get-tuple-element.207), kind=kOutput, calls=%fused_computation.13 | convolution fusion | flops 2415919104 | bytes 9437184 | tf_op jit(solution)/shard_map/dot_general | solution.py:894
  275.4 4.8 bitcast_add_fusion.1
  280.3 3.0 fusion.2
  283.3 4.7 fusion.40
  289.3 4.5 collective-permute-start.46
  297.7 2.4 fusion.6
  306.2 25.2 %shard_map.295 = (bf16[2,512,1152]{2,1,0:T(8,128)(2,1)}, f32[2,8,1024]{2,1,0:T(8,128)S(1)}, f32[8,1024]{1,0:T(8,128)S(1)}, f32[8,128]{1,0:T(8,128)S(1)}, f32[8,768]{1,0:T(8,128)S(1)}) custom-call(bf16[2,512,1024]{2,1,0:T(8,128)(2,1)} %copy-done.8, f32[2,512,128]{2,1,0:T(8,128)S(1)} %copy-done.14, f32[2,512,128]{2,1,0:T(8,128)S(1)} %copy-done.18, ...), custom_call_target="tpu_custom_call" | custom-call | flops 32000000000 | bytes 24000000 | tf_op jit(solution)/shard_map/pallas_call | solution.py:423
  331.5 9.3 %collective-permute-done.39 = bf16[2,256,1536]{2,1,0:T(8,128)(2,1)} collective-permute-done((bf16[2,256,1536]{2,1,0:T(8,128)(2,1)}, bf16[2,256,1536]{2,1,0:T(8,128)(2,1)}, u32[]{:S(2)}, u32[]{:S(2)}) %collective-permute-start.39) | collective-permute-done | bytes 1572896 | tf_op jit(solution)/shard_map/ppermute | solution.py:696
  340.7 2.9 fusion.33
  346.4 6.4 %collective-permute-start.50 = (bf16[2,192,768]{2,1,0:T(8,128)(2,1)S(1)}, bf16[2,192,768]{2,1,0:T(8,128)(2,1)S(1)}, u32[]{:S(2)}, u32[]{:S(2)}) collective-permute-start(bf16[2,192,768]{2,1,0:T(8,128)(2,1)S(1)} %pad_maximum_fusion.10), channel_id=1, source_target_pairs={{0,4},{4,0},{1,5},{5,1},{2,6},{6,2},{3,7},{7,3},{8,12},{12,8},{9,1... | collective-permute-start | bytes 1769480 | tf_op jit(solution)/shard_map/ppermute | solution.py:696
  354.5 7.3 %add_convert_fusion.1 = bf16[2,512,1536]{2,1,0:T(8,128)(2,1)S(1)} fusion(f32[2,512,1536]{2,1,0:T(8,128)} %fusion.40, bf16[2,512,1152]{2,1,0:T(8,128)(2,1)} %fusion.48, bf16[1536,1152,1]{1,0,2:T(8,128)(2,1)S(1)} %bitcast.275), kind=kOutput, calls=%fused_computation.5 | convolution fusion | flops 3627024384 | bytes 15335424 | tf_op jit(solution)/shard_map/dot_general | solution.py:894
  361.9 8.2 %convolution_bitcast_fusion.1 = f32[1536,1152]{1,0:T(8,128)} fusion(bf16[2,512,1536]{2,1,0:T(8,128)(2,1)S(1)} %copy-done.40, bf16[2,512,1152]{2,1,0:T(8,128)(2,1)} %fusion.48), kind=kOutput, calls=%fused_computation.2 | convolution fusion | flops 3623878656 | bytes 12582912 | tf_op jit(solution)/shard_map/dot_general | solution.py:894
  370.1 4.6 fusion.39
  382.8 25.2 %shard_map.296 = (bf16[2,512,1152]{2,1,0:T(8,128)(2,1)}, f32[2,8,1024]{2,1,0:T(8,128)S(1)}, f32[8,1024]{1,0:T(8,128)S(1)}, f32[8,128]{1,0:T(8,128)S(1)}, f32[8,768]{1,0:T(8,128)S(1)}) custom-call(bf16[2,512,1024]{2,1,0:T(8,128)(2,1)} %copy-done.7, f32[2,512,128]{2,1,0:T(8,128)S(1)} %copy-done.12, f32[2,512,128]{2,1,0:T(8,128)S(1)} %copy-done.16, ...), custom_call_target="tpu_custom_call" | custom-call | flops 32000000000 | bytes 24000000 | tf_op jit(solution)/shard_map/pallas_call | solution.py:423
  412.9 3.3 fusion.16
  416.2 5.3 %collective-permute-done.54 = f32[2,8,1024]{2,1,0:T(8,128)S(1)} collective-permute-done((f32[2,8,1024]{2,1,0:T(8,128)S(1)}, f32[2,8,1024]{2,1,0:T(8,128)S(1)}, u32[]{:S(2)}, u32[]{:S(2)}) %collective-permute-start.54) | collective-permute-done | bytes 65568 | tf_op jit(solution)/shard_map/ppermute | solution.py:725
  421.6 6.5 %add_convert_fusion = bf16[2,512,1536]{2,1,0:T(8,128)(2,1)S(1)} fusion(f32[2,512,1536]{2,1,0:T(8,128)} %fusion.39, bf16[2,512,1152]{2,1,0:T(8,128)(2,1)S(1)} %fusion.49, bf16[1536,1152,1]{1,0,2:T(8,128)(2,1)S(1)} %bitcast.276), kind=kOutput, calls=%fused_computation.4 | convolution fusion | flops 3627024384 | bytes 15335424 | tf_op jit(solution)/shard_map/dot_general | solution.py:894
  430.6 4.7 fusion.1
  436.5 4.5 collective-permute-start.58
  446.2 2.2 collective-permute-start.56
  448.5 13.0 %collective-permute-done.58 = bf16[1,2,192,1152]{3,2,1,0:T(8,128)(2,1)} collective-permute-done((bf16[1,2,192,1152]{3,2,1,0:T(8,128)(2,1)}, bf16[1,2,192,1152]{3,2,1,0:T(8,128)(2,1)}, u32[]{:S(2)}, u32[]{:S(2)}) %collective-permute-start.58) | collective-permute-done | bytes 884768 | tf_op jit(solution)/shard_map/ppermute | solution.py:696
  461.5 3.4 collective-permute-done.57
  469.9 10.1 %collective-permute-done.60 = bf16[1,192,1152]{2,1,0:T(8,128)(2,1)} collective-permute-done((bf16[1,192,1152]{2,1,0:T(8,128)(2,1)}, bf16[1,192,1152]{2,1,0:T(8,128)(2,1)}, u32[]{:S(2)}, u32[]{:S(2)}) %collective-permute-start.60) | collective-permute-done | bytes 442400 | tf_op jit(solution)/shard_map/ppermute | solution.py:696
  481.7 2.6 broadcast_select_fusion.2
  488.7 3.0 collective-permute-done.61
  492.1 2.2 fusion.15
  495.7 7.5 %collective-permute-done.63 = bf16[1,192,1152]{2,1,0:T(8,128)(2,1)} collective-permute-done((bf16[1,192,1152]{2,1,0:T(8,128)(2,1)}, bf16[1,192,1152]{2,1,0:T(8,128)(2,1)}, u32[]{:S(2)}, u32[]{:S(2)}) %collective-permute-start.63) | collective-permute-done | bytes 442400 | tf_op jit(solution)/shard_map/ppermute | solution.py:839
  504.8 4.3 collective-permute-start.65
  511.0 2.5 collective-permute-start.68
  513.5 2.4 collective-permute-start.70
  522.4 2.6 collective-permute-done.67
  526.8 3.4 collective-permute-done.69
  (447 shorter events, 128.7 us)
Async XLA Ops:
  2.6 13.2 %collective-permute-start.3 = (bf16[192,1152]{1,0:T(8,128)(2,1)S(1)}, bf16[192,1152]{1,0:T(8,128)(2,1)S(1)}, u32[]{:S(2)}, u32[]{:S(2)}) collective-permute-start(bf16[192,1152]{1,0:T(8,128)(2,1)S(1)} %concatenate.24), channel_id=1, source_target_pairs={{0,2},{10,8},{2,10},{8,0},{1,3},{11,9},{3,11},{9,1},{4,6},{14,12},... | collective-permute-start | bytes 1327112 | tf_op jit(solution)/shard_map/ppermute | solution.py:768
  6.7 9.1 %collective-permute-start.5 = (bf16[192,1152]{1,0:T(8,128)(2,1)S(1)}, bf16[192,1152]{1,0:T(8,128)(2,1)}, u32[]{:S(2)}, u32[]{:S(2)}) collective-permute-start(bf16[192,1152]{1,0:T(8,128)(2,1)S(1)} %concatenate.24), channel_id=1, source_target_pairs={{2,8},{8,2},{3,9},{9,3},{6,12},{12,6},{7,13},{13,7},{18,24},{24,18... | collective-permute-start | bytes 1327112 | tf_op jit(solution)/shard_map/ppermute | solution.py:768
  11.6 28.6 %collective-permute-start = (bf16[1,256,1536]{2,1,0:T(8,128)(2,1)S(1)}, bf16[1,256,1536]{2,1,0:T(8,128)(2,1)}, u32[]{:S(2)}, u32[]{:S(2)}) collective-permute-start(bf16[1,256,1536]{2,1,0:T(8,128)(2,1)S(1)} %get-tuple-element.330.own), channel_id=1, source_target_pairs={{0,1},{1,0},{2,3},{3,2},{4,5},{5,4},{6,7},{7,6},{8,9},{9,8},{10,11... | collective-permute-start | bytes 2359304 | tf_op jit(solution)/shard_map/ppermute | solution.py:696
  13.2 34.6 %collective-permute-start.1 = (bf16[1,256,1536]{2,1,0:T(8,128)(2,1)S(1)}, bf16[1,256,1536]{2,1,0:T(8,128)(2,1)}, u32[]{:S(2)}, u32[]{:S(2)}) collective-permute-start(bf16[1,256,1536]{2,1,0:T(8,128)(2,1)S(1)} %get-tuple-element.330.own), channel_id=1, source_target_pairs={{0,8},{8,0},{1,9},{9,1},{2,10},{10,2},{3,11},{11,3},{4,12},{12,4},... | collective-permute-start | bytes 2359304 | tf_op jit(solution)/shard_map/ppermute | solution.py:696
  15.9 24.9 %collective-permute-start.4 = (bf16[192,1152]{1,0:T(8,128)(2,1)S(1)}, bf16[192,1152]{1,0:T(8,128)(2,1)S(1)}, u32[]{:S(2)}, u32[]{:S(2)}) collective-permute-start(bf16[192,1152]{1,0:T(8,128)(2,1)S(1)} %get-tuple-element.351), channel_id=1, source_target_pairs={{0,16},{16,0},{1,17},{17,1},{2,18},{18,2},{3,19},{19,3},{4,20},{20... | collective-permute-start | bytes 1327112 | tf_op jit(solution)/shard_map/ppermute | solution.py:696
  17.4 23.4 %collective-permute-start.6 = (bf16[192,1152]{1,0:T(8,128)(2,1)S(1)}, bf16[192,1152]{1,0:T(8,128)(2,1)S(1)}, u32[]{:S(2)}, u32[]{:S(2)}) collective-permute-start(bf16[192,1152]{1,0:T(8,128)(2,1)S(1)} %get-tuple-element.350), channel_id=1, source_target_pairs={{0,4},{4,0},{1,5},{5,1},{2,6},{6,2},{3,7},{7,3},{8,12},{12,8},{9,1... | collective-permute-start | bytes 1327112 | tf_op jit(solution)/shard_map/ppermute | solution.py:696
  40.2 25.9 %collective-permute-start.18 = (bf16[1,256,1536]{2,1,0:T(8,128)(2,1)S(1)}, bf16[1,256,1536]{2,1,0:T(8,128)(2,1)}, u32[]{:S(2)}, u32[]{:S(2)}) collective-permute-start(bf16[1,256,1536]{2,1,0:T(8,128)(2,1)S(1)} %get-tuple-element.155.own), channel_id=1, source_target_pairs={{0,1},{1,0},{2,3},{3,2},{4,5},{5,4},{6,7},{7,6},{8,9},{9,8},{10,11... | collective-permute-start | bytes 2359304 | tf_op jit(solution)/shard_map/ppermute | solution.py:696
  42.9 34.1 %collective-permute-start.8 = (bf16[2,192,1152]{2,1,0:T(8,128)(2,1)S(1)}, bf16[2,192,1152]{2,1,0:T(8,128)(2,1)}, u32[]{:S(2)}, u32[]{:S(2)}) collective-permute-start(bf16[2,192,1152]{2,1,0:T(8,128)(2,1)S(1)} %pad_maximum_fusion.8.second), channel_id=1, source_target_pairs={{0,16},{16,0},{1,17},{17,1},{2,18},{18,2},{3,19},{19,3},{4,20},{20... | collective-permute-start | bytes 2654216 | tf_op jit(solution)/shard_map/ppermute | solution.py:696
  45.6 31.4 %collective-permute-start.7 = (bf16[2,192,1152]{2,1,0:T(8,128)(2,1)S(1)}, bf16[2,192,1152]{2,1,0:T(8,128)(2,1)}, u32[]{:S(2)}, u32[]{:S(2)}) collective-permute-start(bf16[2,192,1152]{2,1,0:T(8,128)(2,1)S(1)} %pad_maximum_fusion.7.first), channel_id=1, source_target_pairs={{0,4},{4,0},{1,5},{5,1},{2,6},{6,2},{3,7},{7,3},{8,12},{12,8},{9,1... | collective-permute-start | bytes 2654216 | tf_op jit(solution)/shard_map/ppermute | solution.py:696
  47.2 24.0 %collective-permute-start.2 = (bf16[1,256,1536]{2,1,0:T(8,128)(2,1)}, bf16[1,256,1536]{2,1,0:T(8,128)(2,1)}, u32[]{:S(2)}, u32[]{:S(2)}) collective-permute-start(bf16[1,256,1536]{2,1,0:T(8,128)(2,1)} %collective-permute-done.got), channel_id=1, source_target_pairs={{0,8},{8,0},{1,9},{9,1},{2,10},{10,2},{3,11},{11,3},{4,12},{12,4},... | collective-permute-start | bytes 2359304 | tf_op jit(solution)/shard_map/ppermute | solution.py:696
  47.8 36.9 %collective-permute-start.12 = (bf16[192,1536]{1,0:T(8,128)(2,1)}, bf16[192,1536]{1,0:T(8,128)(2,1)}, u32[]{:S(2)}, u32[]{:S(2)}) collective-permute-start(bf16[192,1536]{1,0:T(8,128)(2,1)} %pad_maximum_fusion.9), channel_id=1, source_target_pairs={{0,2},{10,8},{2,10},{8,0},{1,3},{11,9},{3,11},{9,1},{4,6},{14,12},... | collective-permute-start | bytes 1769480 | tf_op jit(solution)/shard_map/ppermute | solution.py:768
  66.1 18.5 %collective-permute-start.13 = (bf16[192,1536]{1,0:T(8,128)(2,1)}, bf16[192,1536]{1,0:T(8,128)(2,1)}, u32[]{:S(2)}, u32[]{:S(2)}) collective-permute-start(bf16[192,1536]{1,0:T(8,128)(2,1)} %pad_maximum_fusion.9), channel_id=1, source_target_pairs={{2,8},{8,2},{3,9},{9,3},{6,12},{12,6},{7,13},{13,7},{18,24},{24,18... | collective-permute-start | bytes 1769480 | tf_op jit(solution)/shard_map/ppermute | solution.py:768
  71.2 18.0 %collective-permute-start.10 = (f32[8,768]{1,0:T(8,128)}, f32[8,768]{1,0:T(8,128)S(1)}, u32[]{:S(2)}, u32[]{:S(2)}) collective-permute-start(f32[8,768]{1,0:T(8,128)} %maximum_maximum_fusion), channel_id=1, source_target_pairs={{0,2},{2,0},{1,3},{3,1},{4,6},{6,4},{5,7},{7,5},{8,10},{10,8},{9,1... | collective-permute-start | bytes 73736 | tf_op jit(solution)/shard_map/ppermute | solution.py:696
  77.0 29.4 %collective-permute-start.19 = (bf16[1,256,1536]{2,1,0:T(8,128)(2,1)S(1)}, bf16[1,256,1536]{2,1,0:T(8,128)(2,1)S(1)}, u32[]{:S(2)}, u32[]{:S(2)}) collective-permute-start(bf16[1,256,1536]{2,1,0:T(8,128)(2,1)S(1)} %get-tuple-element.155.own), channel_id=1, source_target_pairs={{0,8},{8,0},{1,9},{9,1},{2,10},{10,2},{3,11},{11,3},{4,12},{12,4},... | collective-permute-start | bytes 2359304 | tf_op jit(solution)/shard_map/ppermute | solution.py:696
  77.0 29.4 %collective-permute-start.20 = (bf16[1,256,1536]{2,1,0:T(8,128)(2,1)}, bf16[1,256,1536]{2,1,0:T(8,128)(2,1)S(1)}, u32[]{:S(2)}, u32[]{:S(2)}) collective-permute-start(bf16[1,256,1536]{2,1,0:T(8,128)(2,1)} %collective-permute-done.18.got), channel_id=1, source_target_pairs={{0,8},{8,0},{1,9},{9,1},{2,10},{10,2},{3,11},{11,3},{4,12},{12,4},... | collective-permute-start | bytes 2359304 | tf_op jit(solution)/shard_map/ppermute | solution.py:696
  86.0 15.4 %collective-permute-start.14 = (bf16[192,1536]{1,0:T(8,128)(2,1)S(1)}, bf16[192,1536]{1,0:T(8,128)(2,1)S(1)}, u32[]{:S(2)}, u32[]{:S(2)}) collective-permute-start(bf16[192,1536]{1,0:T(8,128)(2,1)S(1)} %get-tuple-element.349), channel_id=1, source_target_pairs={{0,16},{16,0},{1,17},{17,1},{2,18},{18,2},{3,19},{19,3},{4,20},{20... | collective-permute-start | bytes 1769480 | tf_op jit(solution)/shard_map/ppermute | solution.py:696
  87.6 15.5 %collective-permute-start.15 = (bf16[192,1536]{1,0:T(8,128)(2,1)S(1)}, bf16[192,1536]{1,0:T(8,128)(2,1)S(1)}, u32[]{:S(2)}, u32[]{:S(2)}) collective-permute-start(bf16[192,1536]{1,0:T(8,128)(2,1)S(1)} %get-tuple-element.348), channel_id=1, source_target_pairs={{0,4},{4,0},{1,5},{5,1},{2,6},{6,2},{3,7},{7,3},{8,12},{12,8},{9,1... | collective-permute-start | bytes 1769480 | tf_op jit(solution)/shard_map/ppermute | solution.py:696
  95.9 22.5 %collective-permute-start.9 = (bf16[2,16,1024]{2,1,0:T(8,128)(2,1)S(1)}, bf16[2,16,1024]{2,1,0:T(8,128)(2,1)S(1)}, u32[]{:S(2)}, u32[]{:S(2)}) collective-permute-start(bf16[2,16,1024]{2,1,0:T(8,128)(2,1)S(1)} %slice.379), channel_id=1, source_target_pairs={{0,2},{2,4},{4,6},{1,3},{3,5},{5,7},{8,10},{10,12},{12,14},{9,11},... | collective-permute-start | bytes 196616 | tf_op jit(solution)/shard_map/ppermute | solution.py:725
  103.2 40.7 %collective-permute-start.17 = (bf16[2,192,1536]{2,1,0:T(8,128)(2,1)S(1)}, bf16[2,192,1536]{2,1,0:T(8,128)(2,1)S(1)}, u32[]{:S(2)}, u32[]{:S(2)}) collective-permute-start(bf16[2,192,1536]{2,1,0:T(8,128)(2,1)S(1)} %pad_maximum_fusion.4.second), channel_id=1, source_target_pairs={{0,16},{16,0},{1,17},{17,1},{2,18},{18,2},{3,19},{19,3},{4,20},{20... | collective-permute-start | bytes 3538952 | tf_op jit(solution)/shard_map/ppermute | solution.py:696
  103.9 42.0 %collective-permute-start.16 = (bf16[2,192,1536]{2,1,0:T(8,128)(2,1)S(1)}, bf16[2,192,1536]{2,1,0:T(8,128)(2,1)S(1)}, u32[]{:S(2)}, u32[]{:S(2)}) collective-permute-start(bf16[2,192,1536]{2,1,0:T(8,128)(2,1)S(1)} %pad_maximum_fusion.3.first), channel_id=1, source_target_pairs={{0,4},{4,0},{1,5},{5,1},{2,6},{6,2},{3,7},{7,3},{8,12},{12,8},{9,1... | collective-permute-start | bytes 3538952 | tf_op jit(solution)/shard_map/ppermute | solution.py:696
  117.0 15.5 %collective-permute-start.21 = (bf16[2,16,1024]{2,1,0:T(8,128)(2,1)S(1)}, bf16[2,16,1024]{2,1,0:T(8,128)(2,1)S(1)}, u32[]{:S(2)}, u32[]{:S(2)}) collective-permute-start(bf16[2,16,1024]{2,1,0:T(8,128)(2,1)S(1)} %slice.385), channel_id=1, source_target_pairs={{0,2},{2,4},{4,6},{1,3},{3,5},{5,7},{8,10},{10,12},{12,14},{9,11},... | collective-permute-start | bytes 196616 | tf_op jit(solution)/shard_map/ppermute | solution.py:725
  127.3 23.0 %collective-permute-start.11 = (bf16[2,144,768]{2,1,0:T(8,128)(2,1)S(1)}, bf16[2,144,768]{2,1,0:T(8,128)(2,1)S(1)}, u32[]{:S(2)}, u32[]{:S(2)}) collective-permute-start(bf16[2,144,768]{2,1,0:T(8,128)(2,1)S(1)} %get-tuple-element.149.refs_6_), channel_id=1, source_target_pairs={{0,2},{1,3},{4,6},{5,7},{8,10},{9,11},{12,14},{13,15},{16,18},{17,... | collective-permute-start | bytes 1327112 | tf_op jit(solution)/shard_map/ppermute | solution.py:729
  132.4 41.1 %collective-permute-start.24 = (bf16[2,256,1536]{2,1,0:T(8,128)(2,1)}, bf16[2,256,1536]{2,1,0:T(8,128)(2,1)}, u32[]{:S(2)}, u32[]{:S(2)}) collective-permute-start(bf16[2,256,1536]{2,1,0:T(8,128)(2,1)} %param.17), channel_id=1, source_target_pairs={{0,8},{8,0},{1,9},{9,1},{2,10},{10,2},{3,11},{11,3},{4,12},{12,4},... | collective-permute-start | bytes 4718600 | tf_op jit(solution)/shard_map/ppermute | solution.py:696
  134.0 25.7 %collective-permute-start.23 = (bf16[1,256,1536]{2,1,0:T(8,128)(2,1)S(1)}, bf16[1,256,1536]{2,1,0:T(8,128)(2,1)}, u32[]{:S(2)}, u32[]{:S(2)}) collective-permute-start(bf16[1,256,1536]{2,1,0:T(8,128)(2,1)S(1)} %get-tuple-element.339.own), channel_id=1, source_target_pairs={{0,1},{1,0},{2,3},{3,2},{4,5},{5,4},{6,7},{7,6},{8,9},{9,8},{10,11... | collective-permute-start | bytes 2359304 | tf_op jit(solution)/shard_map/ppermute | solution.py:696
  143.9 29.7 %collective-permute-start.28 = (bf16[1,256,1536]{2,1,0:T(8,128)(2,1)S(1)}, bf16[1,256,1536]{2,1,0:T(8,128)(2,1)S(1)}, u32[]{:S(2)}, u32[]{:S(2)}) collective-permute-start(bf16[1,256,1536]{2,1,0:T(8,128)(2,1)S(1)} %get-tuple-element.338.own), channel_id=1, source_target_pairs={{0,1},{1,0},{2,3},{3,2},{4,5},{5,4},{6,7},{7,6},{8,9},{9,8},{10,11... | collective-permute-start | bytes 2359304 | tf_op jit(solution)/shard_map/ppermute | solution.py:696
  159.7 18.3 %collective-permute-start.25 = (bf16[1,256,1536]{2,1,0:T(8,128)(2,1)}, bf16[1,256,1536]{2,1,0:T(8,128)(2,1)}, u32[]{:S(2)}, u32[]{:S(2)}) collective-permute-start(bf16[1,256,1536]{2,1,0:T(8,128)(2,1)} %collective-permute-done.23.got), channel_id=1, source_target_pairs={{0,8},{8,0},{1,9},{9,1},{2,10},{10,2},{3,11},{11,3},{4,12},{12,4},... | collective-permute-start | bytes 2359304 | tf_op jit(solution)/shard_map/ppermute | solution.py:696
  163.3 26.0 %collective-permute-start.26 = (bf16[2,128,768]{2,1,0:T(8,128)(2,1)S(1)}, bf16[2,128,768]{2,1,0:T(8,128)(2,1)S(1)}, u32[]{:S(2)}, u32[]{:S(2)}) collective-permute-start(bf16[2,128,768]{2,1,0:T(8,128)(2,1)S(1)} %copy-done.3), channel_id=1, source_target_pairs={{2,6},{3,7},{10,14},{11,15},{18,22},{19,23},{26,30},{27,31}} | collective-permute-start | bytes 1179656 | tf_op jit(solution)/shard_map/ppermute | solution.py:735
  164.1 25.2 %collective-permute-start.22 = (bf16[2,128,768]{2,1,0:T(8,128)(2,1)S(1)}, bf16[2,128,768]{2,1,0:T(8,128)(2,1)S(1)}, u32[]{:S(2)}, u32[]{:S(2)}) collective-permute-start(bf16[2,128,768]{2,1,0:T(8,128)(2,1)S(1)} %copy-done.3), channel_id=1, source_target_pairs={{2,4},{3,5},{10,12},{11,13},{18,20},{19,21},{26,28},{27,29}} | collective-permute-start | bytes 1179656 | tf_op jit(solution)/shard_map/ppermute | solution.py:735
  173.5 28.0 %collective-permute-start.29 = (bf16[1,256,1536]{2,1,0:T(8,128)(2,1)S(1)}, bf16[1,256,1536]{2,1,0:T(8,128)(2,1)S(1)}, u32[]{:S(2)}, u32[]{:S(2)}) collective-permute-start(bf16[1,256,1536]{2,1,0:T(8,128)(2,1)S(1)} %collective-permute-done.28.got), channel_id=1, source_target_pairs={{0,8},{8,0},{1,9},{9,1},{2,10},{10,2},{3,11},{11,3},{4,12},{12,4},... | collective-permute-start | bytes 2359304 | tf_op jit(solution)/shard_map/ppermute | solution.py:696
  173.5 26.0 %collective-permute-start.30 = (bf16[2,144,768]{2,1,0:T(8,128)(2,1)S(1)}, bf16[2,144,768]{2,1,0:T(8,128)(2,1)S(1)}, u32[]{:S(2)}, u32[]{:S(2)}) collective-permute-start(bf16[2,144,768]{2,1,0:T(8,128)(2,1)S(1)} %copy-done.6), channel_id=1, source_target_pairs={{0,2},{1,3},{4,6},{5,7},{8,10},{9,11},{12,14},{13,15},{16,18},{17,... | collective-permute-start | bytes 1327112 | tf_op jit(solution)/shard_map/ppermute | solution.py:729
  199.9 32.3 %collective-permute-start.35 = (bf16[2,128,768]{2,1,0:T(8,128)(2,1)S(1)}, bf16[2,128,768]{2,1,0:T(8,128)(2,1)S(1)}, u32[]{:S(2)}, u32[]{:S(2)}) collective-permute-start(bf16[2,128,768]{2,1,0:T(8,128)(2,1)S(1)} %shard_map.288), channel_id=1, source_target_pairs={{2,6},{3,7},{10,14},{11,15},{18,22},{19,23},{26,30},{27,31}} | collective-permute-start | bytes 1179656 | tf_op jit(solution)/shard_map/ppermute | solution.py:735
  200.6 31.6 %collective-permute-start.34 = (bf16[2,128,768]{2,1,0:T(8,128)(2,1)S(1)}, bf16[2,128,768]{2,1,0:T(8,128)(2,1)S(1)}, u32[]{:S(2)}, u32[]{:S(2)}) collective-permute-start(bf16[2,128,768]{2,1,0:T(8,128)(2,1)S(1)} %shard_map.288), channel_id=1, source_target_pairs={{2,4},{3,5},{10,12},{11,13},{18,20},{19,21},{26,28},{27,29}} | collective-permute-start | bytes 1179656 | tf_op jit(solution)/shard_map/ppermute | solution.py:735
  202.7 9.3 %collective-permute-start.27 = (f32[2,8,512]{2,1,0:T(8,128)S(1)}, f32[2,8,512]{2,1,0:T(8,128)S(1)}, u32[]{:S(2)}, u32[]{:S(2)}) collective-permute-start(f32[2,8,512]{2,1,0:T(8,128)S(1)} %get-tuple-element.176), channel_id=1, source_target_pairs={{0,8},{8,0},{1,9},{9,1},{2,10},{10,2},{3,11},{11,3},{4,12},{12,4},... | collective-permute-start | bytes 98312 | tf_op jit(solution)/shard_map/ppermute | solution.py:696
  212.0 9.3 %collective-permute-start.31 = (f32[2,8,512]{2,1,0:T(8,128)S(1)}, f32[2,8,512]{2,1,0:T(8,128)S(1)}, u32[]{:S(2)}, u32[]{:S(2)}) collective-permute-start(f32[2,8,512]{2,1,0:T(8,128)S(1)} %reverse_add_fusion.1), channel_id=1, source_target_pairs={{0,1},{1,0},{2,3},{3,2},{4,5},{5,4},{6,7},{7,6},{8,9},{9,8},{10,11... | collective-permute-start | bytes 98312 | tf_op jit(solution)/shard_map/ppermute | solution.py:696
  220.4 75.8 %collective-permute-start.32 = (bf16[512,1536]{1,0:T(8,128)(2,1)}, bf16[512,1536]{1,0:T(8,128)(2,1)}, u32[]{:S(2)}, u32[]{:S(2)}) collective-permute-start(bf16[512,1536]{1,0:T(8,128)(2,1)} %slice_bitcast_fusion.7), channel_id=1, source_target_pairs={{0,8},{8,0},{1,9},{9,1},{2,10},{10,2},{3,11},{11,3},{4,12},{12,4},... | collective-permute-start | bytes 4718600 | tf_op jit(solution)/shard_map/ppermute | solution.py:696
  230.9 33.0 %collective-permute-start.33 = (bf16[2,144,768]{2,1,0:T(8,128)(2,1)S(1)}, bf16[2,144,768]{2,1,0:T(8,128)(2,1)S(1)}, u32[]{:S(2)}, u32[]{:S(2)}) collective-permute-start(bf16[2,144,768]{2,1,0:T(8,128)(2,1)S(1)} %get-tuple-element.191.refs_10_), channel_id=1, source_target_pairs={{2,0},{3,1},{6,4},{7,5},{10,8},{11,9},{14,12},{15,13},{18,16},{19,... | collective-permute-start | bytes 1327112 | tf_op jit(solution)/shard_map/ppermute | solution.py:729
  254.0 46.3 %collective-permute-start.38 = (bf16[512,1536]{1,0:T(8,128)(2,1)}, bf16[512,1536]{1,0:T(8,128)(2,1)}, u32[]{:S(2)}, u32[]{:S(2)}) collective-permute-start(bf16[512,1536]{1,0:T(8,128)(2,1)} %slice_bitcast_fusion.5), channel_id=1, source_target_pairs={{0,8},{8,0},{1,9},{9,1},{2,10},{10,2},{3,11},{11,3},{4,12},{12,4},... | collective-permute-start | bytes 4718600 | tf_op jit(solution)/shard_map/ppermute | solution.py:696
  264.4 23.6 %collective-permute-start.41 = (bf16[2,128,768]{2,1,0:T(8,128)(2,1)S(1)}, bf16[2,128,768]{2,1,0:T(8,128)(2,1)S(1)}, u32[]{:S(2)}, u32[]{:S(2)}) collective-permute-start(bf16[2,128,768]{2,1,0:T(8,128)(2,1)S(1)} %shard_map.293), channel_id=1, source_target_pairs={{4,0},{5,1},{12,8},{13,9},{20,16},{21,17},{28,24},{29,25}} | collective-permute-start | bytes 1179656 | tf_op jit(solution)/shard_map/ppermute | solution.py:735
  265.7 22.3 %collective-permute-start.40 = (bf16[2,128,768]{2,1,0:T(8,128)(2,1)S(1)}, bf16[2,128,768]{2,1,0:T(8,128)(2,1)S(1)}, u32[]{:S(2)}, u32[]{:S(2)}) collective-permute-start(bf16[2,128,768]{2,1,0:T(8,128)(2,1)S(1)} %shard_map.293), channel_id=1, source_target_pairs={{4,2},{5,3},{12,10},{13,11},{20,18},{21,19},{28,26},{29,27}} | collective-permute-start | bytes 1179656 | tf_op jit(solution)/shard_map/ppermute | solution.py:735
  266.4 28.7 %collective-permute-start.42 = (bf16[2,144,768]{2,1,0:T(8,128)(2,1)S(1)}, bf16[2,144,768]{2,1,0:T(8,128)(2,1)S(1)}, u32[]{:S(2)}, u32[]{:S(2)}) collective-permute-start(bf16[2,144,768]{2,1,0:T(8,128)(2,1)S(1)} %get-tuple-element.220), channel_id=1, source_target_pairs={{2,0},{3,1},{6,4},{7,5},{10,8},{11,9},{14,12},{15,13},{18,16},{19,... | collective-permute-start | bytes 1327112 | tf_op jit(solution)/shard_map/ppermute | solution.py:729
  289.3 42.2 %collective-permute-start.46 = (bf16[2,2,192,768]{3,2,1,0:T(8,128)(2,1)}, bf16[2,2,192,768]{3,2,1,0:T(8,128)(2,1)}, u32[]{:S(2)}, u32[]{:S(2)}) collective-permute-start(bf16[2,2,192,768]{3,2,1,0:T(8,128)(2,1)} %pad_maximum_fusion.6.refs_21_), channel_id=1, source_target_pairs={{0,4},{4,0},{1,5},{5,1},{2,6},{6,2},{3,7},{7,3},{8,12},{12,8},{9,1... | collective-permute-start | bytes 3538952 | tf_op jit(solution)/shard_map/ppermute | solution.py:696
  294.0 37.5 %collective-permute-start.45 = (bf16[2,2,192,768]{3,2,1,0:T(8,128)(2,1)S(1)}, bf16[2,2,192,768]{3,2,1,0:T(8,128)(2,1)}, u32[]{:S(2)}, u32[]{:S(2)}) collective-permute-start(bf16[2,2,192,768]{3,2,1,0:T(8,128)(2,1)S(1)} %pad_maximum_fusion.5.refs_20_), channel_id=1, source_target_pairs={{0,16},{16,0},{1,17},{17,1},{2,18},{18,2},{3,19},{19,3},{4,20},{20... | collective-permute-start | bytes 3538952 | tf_op jit(solution)/shard_map/ppermute | solution.py:696
  295.5 35.9 %collective-permute-start.43 = (bf16[2,128,768]{2,1,0:T(8,128)(2,1)S(1)}, bf16[2,128,768]{2,1,0:T(8,128)(2,1)S(1)}, u32[]{:S(2)}, u32[]{:S(2)}) collective-permute-start(bf16[2,128,768]{2,1,0:T(8,128)(2,1)S(1)} %shard_map.294.refs_18_), channel_id=1, source_target_pairs={{4,2},{5,3},{12,10},{13,11},{20,18},{21,19},{28,26},{29,27}} | collective-permute-start | bytes 1179656 | tf_op jit(solution)/shard_map/ppermute | solution.py:735
  296.3 35.2 %collective-permute-start.44 = (bf16[2,128,768]{2,1,0:T(8,128)(2,1)S(1)}, bf16[2,128,768]{2,1,0:T(8,128)(2,1)S(1)}, u32[]{:S(2)}, u32[]{:S(2)}) collective-permute-start(bf16[2,128,768]{2,1,0:T(8,128)(2,1)S(1)} %shard_map.294.refs_18_), channel_id=1, source_target_pairs={{4,0},{5,1},{12,8},{13,9},{20,16},{21,17},{28,24},{29,25}} | collective-permute-start | bytes 1179656 | tf_op jit(solution)/shard_map/ppermute | solution.py:735
  304.2 36.5 %collective-permute-start.39 = (bf16[2,256,1536]{2,1,0:T(8,128)(2,1)}, bf16[2,256,1536]{2,1,0:T(8,128)(2,1)}, u32[]{:S(2)}, u32[]{:S(2)}) collective-permute-start(bf16[2,256,1536]{2,1,0:T(8,128)(2,1)} %pad_maximum_fusion.1.refs_19_), channel_id=1, source_target_pairs={{0,1},{1,0},{2,3},{3,2},{4,5},{5,4},{6,7},{7,6},{8,9},{9,8},{10,11... | collective-permute-start | bytes 4718600 | tf_op jit(solution)/shard_map/ppermute | solution.py:696
  343.8 31.0 %collective-permute-start.51 = (bf16[2,192,768]{2,1,0:T(8,128)(2,1)S(1)}, bf16[2,192,768]{2,1,0:T(8,128)(2,1)S(1)}, u32[]{:S(2)}, u32[]{:S(2)}) collective-permute-start(bf16[2,192,768]{2,1,0:T(8,128)(2,1)S(1)} %pad_maximum_fusion.11), channel_id=1, source_target_pairs={{0,16},{16,0},{1,17},{17,1},{2,18},{18,2},{3,19},{19,3},{4,20},{20... | collective-permute-start | bytes 1769480 | tf_op jit(solution)/shard_map/ppermute | solution.py:696
  346.4 28.3 %collective-permute-start.50 = (bf16[2,192,768]{2,1,0:T(8,128)(2,1)S(1)}, bf16[2,192,768]{2,1,0:T(8,128)(2,1)S(1)}, u32[]{:S(2)}, u32[]{:S(2)}) collective-permute-start(bf16[2,192,768]{2,1,0:T(8,128)(2,1)S(1)} %pad_maximum_fusion.10), channel_id=1, source_target_pairs={{0,4},{4,0},{1,5},{5,1},{2,6},{6,2},{3,7},{7,3},{8,12},{12,8},{9,1... | collective-permute-start | bytes 1769480 | tf_op jit(solution)/shard_map/ppermute | solution.py:696
  361.9 14.7 %collective-permute-start.48 = (bf16[512,1536]{1,0:T(8,128)(2,1)S(1)}, bf16[512,1536]{1,0:T(8,128)(2,1)S(1)}, u32[]{:S(2)}, u32[]{:S(2)}) collective-permute-start(bf16[512,1536]{1,0:T(8,128)(2,1)S(1)} %slice_bitcast_fusion.3), channel_id=1, source_target_pairs={{0,8},{8,0},{1,9},{9,1},{2,10},{10,2},{3,11},{11,3},{4,12},{12,4},... | collective-permute-start | bytes 4718600 | tf_op jit(solution)/shard_map/ppermute | solution.py:696
  375.2 32.8 %collective-permute-start.52 = (bf16[2,192,768]{2,1,0:T(8,128)(2,1)S(1)}, bf16[2,192,768]{2,1,0:T(8,128)(2,1)S(1)}, u32[]{:S(2)}, u32[]{:S(2)}) collective-permute-start(bf16[2,192,768]{2,1,0:T(8,128)(2,1)S(1)} %get-tuple-element.343.refs_20_), channel_id=1, source_target_pairs={{2,0},{8,10},{10,2},{0,8},{3,1},{9,11},{11,3},{1,9},{6,4},{12,14},... | collective-permute-start | bytes 1769480 | tf_op jit(solution)/shard_map/ppermute | solution.py:839
  375.6 32.4 %collective-permute-start.53 = (bf16[2,192,768]{2,1,0:T(8,128)(2,1)S(1)}, bf16[2,192,768]{2,1,0:T(8,128)(2,1)S(1)}, u32[]{:S(2)}, u32[]{:S(2)}) collective-permute-start(bf16[2,192,768]{2,1,0:T(8,128)(2,1)S(1)} %get-tuple-element.342.refs_21_), channel_id=1, source_target_pairs={{2,8},{8,2},{3,9},{9,3},{6,12},{12,6},{7,13},{13,7},{18,24},{24,18... | collective-permute-start | bytes 1769480 | tf_op jit(solution)/shard_map/ppermute | solution.py:840
  377.1 33.9 %collective-permute-start.49 = (bf16[256,1536]{1,0:T(8,128)(2,1)S(1)}, bf16[256,1536]{1,0:T(8,128)(2,1)}, u32[]{:S(2)}, u32[]{:S(2)}) collective-permute-start(bf16[256,1536]{1,0:T(8,128)(2,1)S(1)} %constant_dynamic-slice_fusion.8.refs_18_), channel_id=1, source_target_pairs={{0,1},{1,0},{2,3},{3,2},{4,5},{5,4},{6,7},{7,6},{8,9},{9,8},{10,11... | collective-permute-start | bytes 2359304 | tf_op jit(solution)/shard_map/ppermute | solution.py:696
  409.3 12.2 %collective-permute-start.54 = (f32[2,8,1024]{2,1,0:T(8,128)S(1)}, f32[2,8,1024]{2,1,0:T(8,128)S(1)}, u32[]{:S(2)}, u32[]{:S(2)}) collective-permute-start(f32[2,8,1024]{2,1,0:T(8,128)S(1)} %get-tuple-element.249), channel_id=1, source_target_pairs={{2,0},{4,2},{6,4},{3,1},{5,3},{7,5},{10,8},{12,10},{14,12},{11,9},... | collective-permute-start | bytes 196616 | tf_op jit(solution)/shard_map/ppermute | solution.py:725
  429.4 13.8 %collective-permute-start.55 = (bf16[512,1536]{1,0:T(8,128)(2,1)}, bf16[512,1536]{1,0:T(8,128)(2,1)}, u32[]{:S(2)}, u32[]{:S(2)}) collective-permute-start(bf16[512,1536]{1,0:T(8,128)(2,1)} %slice_bitcast_fusion.1), channel_id=1, source_target_pairs={{0,8},{8,0},{1,9},{9,1},{2,10},{10,2},{3,11},{11,3},{4,12},{12,4},... | collective-permute-start | bytes 4718600 | tf_op jit(solution)/shard_map/ppermute | solution.py:696
  436.5 24.9 %collective-permute-start.58 = (bf16[1,2,192,1152]{3,2,1,0:T(8,128)(2,1)}, bf16[1,2,192,1152]{3,2,1,0:T(8,128)(2,1)}, u32[]{:S(2)}, u32[]{:S(2)}) collective-permute-start(bf16[1,2,192,1152]{3,2,1,0:T(8,128)(2,1)} %dynamic-slice_bitcast_fusion), channel_id=1, source_target_pairs={{0,4},{4,0},{1,5},{5,1},{2,6},{6,2},{3,7},{7,3},{8,12},{12,8},{9,1... | collective-permute-start | bytes 2654216 | tf_op jit(solution)/shard_map/ppermute | solution.py:696
  442.1 22.8 %collective-permute-start.57 = (bf16[1,2,192,1152]{3,2,1,0:T(8,128)(2,1)}, bf16[1,2,192,1152]{3,2,1,0:T(8,128)(2,1)}, u32[]{:S(2)}, u32[]{:S(2)}) collective-permute-start(bf16[1,2,192,1152]{3,2,1,0:T(8,128)(2,1)} %dynamic-slice_bitcast_fusion.1), channel_id=1, source_target_pairs={{0,16},{16,0},{1,17},{17,1},{2,18},{18,2},{3,19},{19,3},{4,20},{20... | collective-permute-start | bytes 2654216 | tf_op jit(solution)/shard_map/ppermute | solution.py:696
  446.2 23.7 %collective-permute-start.56 = (bf16[256,1536]{1,0:T(8,128)(2,1)}, bf16[256,1536]{1,0:T(8,128)(2,1)}, u32[]{:S(2)}, u32[]{:S(2)}) collective-permute-start(bf16[256,1536]{1,0:T(8,128)(2,1)} %constant_dynamic-slice_fusion.2), channel_id=1, source_target_pairs={{0,1},{1,0},{2,3},{3,2},{4,5},{5,4},{6,7},{7,6},{8,9},{9,8},{10,11... | collective-permute-start | bytes 2359304 | tf_op jit(solution)/shard_map/ppermute | solution.py:696
  467.6 12.4 %collective-permute-start.60 = (bf16[1,192,1152]{2,1,0:T(8,128)(2,1)}, bf16[1,192,1152]{2,1,0:T(8,128)(2,1)}, u32[]{:S(2)}, u32[]{:S(2)}) collective-permute-start(bf16[1,192,1152]{2,1,0:T(8,128)(2,1)} %constant_dynamic-slice_fusion), channel_id=1, source_target_pairs={{0,16},{16,0},{1,17},{17,1},{2,18},{18,2},{3,19},{19,3},{4,20},{20... | collective-permute-start | bytes 1327112 | tf_op jit(solution)/shard_map/ppermute | solution.py:696
  469.6 12.2 %collective-permute-start.59 = (bf16[1,192,1152]{2,1,0:T(8,128)(2,1)}, bf16[1,192,1152]{2,1,0:T(8,128)(2,1)}, u32[]{:S(2)}, u32[]{:S(2)}) collective-permute-start(bf16[1,192,1152]{2,1,0:T(8,128)(2,1)} %constant_dynamic-slice_fusion.1), channel_id=1, source_target_pairs={{0,4},{4,0},{1,5},{5,1},{2,6},{6,2},{3,7},{7,3},{8,12},{12,8},{9,1... | collective-permute-start | bytes 1327112 | tf_op jit(solution)/shard_map/ppermute | solution.py:696
  484.3 19.0 %collective-permute-start.63 = (bf16[1,192,1152]{2,1,0:T(8,128)(2,1)}, bf16[1,192,1152]{2,1,0:T(8,128)(2,1)}, u32[]{:S(2)}, u32[]{:S(2)}) collective-permute-start(bf16[1,192,1152]{2,1,0:T(8,128)(2,1)} %get-tuple-element.324), channel_id=1, source_target_pairs={{2,0},{8,10},{10,2},{0,8},{3,1},{9,11},{11,3},{1,9},{6,4},{12,14},... | collective-permute-start | bytes 1327112 | tf_op jit(solution)/shard_map/ppermute | solution.py:839
  484.3 19.0 %collective-permute-start.64 = (bf16[1,192,1152]{2,1,0:T(8,128)(2,1)}, bf16[1,192,1152]{2,1,0:T(8,128)(2,1)}, u32[]{:S(2)}, u32[]{:S(2)}) collective-permute-start(bf16[1,192,1152]{2,1,0:T(8,128)(2,1)} %get-tuple-element.325), channel_id=1, source_target_pairs={{2,8},{8,2},{3,9},{9,3},{6,12},{12,6},{7,13},{13,7},{18,24},{24,18... | collective-permute-start | bytes 1327112 | tf_op jit(solution)/shard_map/ppermute | solution.py:840
  504.8 12.7 %collective-permute-start.65 = (f32[7460]{0:T(1024)S(1)}, f32[7460]{0:T(1024)S(1)}, u32[]{:S(2)}, u32[]{:S(2)}) collective-permute-start(f32[7460]{0:T(1024)S(1)} %add.420), channel_id=1, source_target_pairs={{0,2},{2,0},{1,3},{3,1},{4,6},{6,4},{5,7},{7,5},{8,10},{10,8},{9,1... | collective-permute-start | bytes 89528 | tf_op jit(solution)/shard_map/ppermute | solution.py:696
  511.0 15.8 %collective-permute-start.68 = (f32[192,256]{1,0:T(8,128)S(1)}, f32[192,256]{1,0:T(8,128)S(1)}, u32[]{:S(2)}, u32[]{:S(2)}) collective-permute-start(f32[192,256]{1,0:T(8,128)S(1)} %slice.418), channel_id=1, source_target_pairs={{0,1},{1,0},{2,3},{3,2},{4,5},{5,4},{6,7},{7,6},{8,9},{9,8},{10,11... | collective-permute-start | bytes 589832 | tf_op jit(solution)/shard_map/ppermute | solution.py:696
  513.5 16.6 %collective-permute-start.69 = (f32[192,256]{1,0:T(8,128)S(1)}, f32[192,256]{1,0:T(8,128)S(1)}, u32[]{:S(2)}, u32[]{:S(2)}) collective-permute-start(f32[192,256]{1,0:T(8,128)S(1)} %slice.418), channel_id=1, source_target_pairs={{0,2},{2,0},{1,3},{3,1},{4,6},{6,4},{5,7},{7,5},{8,10},{10,8},{9,1... | collective-permute-start | bytes 589832 | tf_op jit(solution)/shard_map/ppermute | solution.py:696
  513.5 16.6 %collective-permute-start.70 = (f32[192,256]{1,0:T(8,128)S(1)}, f32[192,256]{1,0:T(8,128)S(1)}, u32[]{:S(2)}, u32[]{:S(2)}) collective-permute-start(f32[192,256]{1,0:T(8,128)S(1)} %slice.418), channel_id=1, source_target_pairs={{0,3},{3,0},{1,2},{2,1},{4,7},{7,4},{5,6},{6,5},{8,11},{11,8},{9,1... | collective-permute-start | bytes 589832 | tf_op jit(solution)/shard_map/ppermute | solution.py:1207
  (98 other events, 721.6 us)

commit v5 on v3

--- a/solution.py
+++ b/solution.py
@@ -912,41 +912,47 @@
     normed_own = [(own[part : part + 1] * r0[part : part + 1] * gain_in).astype(BF16) for part in parts]
     fast = all_pairs()
 
-    def tokens_of(value, *before):
-        got = hold(swap(value, "zq"), *before)
-        return value, got, swap(value, "core"), swap(got, "core")
-
     if fast:
         got = fetch(own_first)
-    fours = [tokens_of(normed_own[0])]
-    if fast:
+        start = swap(normed_own[0], "zq")
         same, cross = fetched(own_first, *got)
-        moved = hold((swap(same, "x"), swap(cross, "y")), fours[0][1])
-        first, second = jnp.stack([same, moved[0]]), jnp.stack([cross, moved[1]])
-        own_second = hold(own_second, fours[0][1], *moved)
+        first = jnp.stack([same, swap(same, "x")])
+        second = jnp.stack([cross, swap(cross, "y")])
+        rest = swap(first, "y"), swap(second, "x")
+        following = hold(normed_own[1:], first, second)
+        started = [start] + [swap(value, "zq") for value in following]
+        w_first = place(first, rest[0], second, rest[1])
+        own_second = hold(own_second, w_first)
         got = fetch(own_second)
-        rest = swap(first, "y"), swap(second, "x")
-        later = first, second
+        later = [rest] + [(w_first,)] * (micro - 1)
     else:
-        later = (fours[0][1],)
-    for part in parts[1:]:
-        fours.append(tokens_of(hold(normed_own[part], fours[0][1]), *later))
-        later = (fours[-1][1],)
-    if fast:
-        w_first = place(first, rest[0], second, rest[1])
-        got = hold(got, w_first)
-        same, cross = fetched(own_second, *got)
-        moved = swap(same, "x"), swap(cross, "y")
-    else:
+        started = [swap(value, "zq") for value in normed_own]
+        later = [()] * micro
         w_first = spliced(
             gather_slice(own_first), ((share, 1), (states2, 0), (own_heads, 1), (filler, 1))
         )
+    fours = []
+    for part in parts:
+        value, got_tokens = normed_own[part], hold(started[part], *later[part])
+        fours.append((value, got_tokens, swap(value, "core"), swap(got_tokens, "core")))
     normed = [joined(*four) for four in fours]
+
+    scans = []
+    for part in parts:
+        xw = matmul(normed[part], w_first, ((2,), (0,)), BF16)
+        scans.append((xw, shift(xw[:, -RIM:, 0:width], 1)))
+        if part == 0:
+            normed[-1] = hold(normed[-1], xw)
+    if fast:
+        same, cross = fetched(own_second, *hold(got, scans[-1][0]))
+        moved = swap(same, "x"), swap(cross, "y")
+        first, second = jnp.stack([same, moved[0]]), jnp.stack([cross, moved[1]])
+        got_second = first, swap(first, "y"), second, swap(second, "x")
     per_head = jnp.concatenate([dt_bias, a_log, d_skip])
     per_head = jnp.pad(per_head, (0, share - 3 * own_heads))
     small = jnp.concatenate([conv_x, conv_x_bias[None], inner_gain[None]], axis=0).astype(F32)
     small = jnp.concatenate([small, per_head[None], jnp.zeros((1, share), F32)])
-    small = slice_of_own(small, w_first)
+    small = slice_of_own(hold(small, scans[0][0]), scans[0][0])
     channel_rows = jnp.concatenate([small[k, 0:6] for k in range(halves)], axis=1)
     head_rows = jnp.concatenate(
         [small[k, 6, 0 : 3 * own_heads].reshape(3, own_heads) for k in range(halves)], axis=1
@@ -962,16 +968,6 @@
         == lax.broadcasted_iota(jnp.int32, (LANES, inner), 0)
     ).astype(BF16)
 
-    scans = []
-    for part in parts:
-        xw = matmul(normed[part], w_first, ((2,), (0,)), BF16)
-        scans.append((xw, shift(xw[:, -RIM:, 0:width], 1)))
-        if part == 0:
-            normed[-1] = hold(normed[-1], xw)
-    if fast:
-        moved = hold(moved, scans[0][0])
-        first, second = jnp.stack([same, moved[0]]), jnp.stack([cross, moved[1]])
-        got_second = first, swap(first, "y"), second, swap(second, "x")
     local = []
     for part in parts:
         before = [k[5] for k in local[-1:]]

time: 536 us -> 538 us (level)
  starting transfers between devices: 96.7 us -> 104 us
    ppermute x48, starting transfers between devices: 58.5 us -> 68.8 us  [swap(): return lax.ppermute(value, axis, [(0, 1), (1, 0)])]
  transfers between devices with their start and end apart: 73 -> 73, of which waited for: 21 -> 24; matrix products, arithmetic and copies ran while one was open for 30% -> 28% of each run, Pallas kernels for 25% -> 25%
where the time goes in v5:
time: 538 us; the launch traced here: 529 us
  Pallas kernels  132 us (25%)
  waiting for transfers between devices  114 us (21%)
  starting transfers between devices  104 us (19%)
  matrix products  99.2 us (18%)
  other arithmetic  43.2 us (8%)
  local copies, waits for them, and re-layouts  33.6 us (6%)
    pallas_call x8, Pallas kernels, run(): pl.pallas_call(body, grid=grid, in_specs=[spec for _, spec in ins] + [pl....  106 us
    dot_general x18, matrix products, matmul(): lax.dot_general(left, right, (contract, ((), ())), preferred_element_type...  99.2 us
    ppermute x48, waiting for transfers between devices, swap(): return lax.ppermute(value, axis, [(0, 1), (1, 0)])  92.6 us
    ppermute x48, starting transfers between devices, swap(): return lax.ppermute(value, axis, [(0, 1), (1, 0)])  68.8 us
    pallas_call x4, Pallas kernels, joined(): pl.pallas_call(join_kernel, grid_spec=pltpu.PrefetchScalarGridSpec(num_sc...  13 us
    convert_element_type x8, other arithmetic, added(): return (kept.astype(F32) + got.astype(F32)).astype(dtype)  12.2 us
    pallas_call x2, Pallas kernels, place(): pl.pallas_call(place_kernel, grid_spec=pltpu.PrefetchScalarGridSpec(num_s...  11.2 us
  transfers between devices with their start and end apart: 73, of which 24 were waited for; matrix products, arithmetic and copies ran while one was open for 28% of the time, Pallas kernels for 25%

profile of v5, /device:TPU:0, one launch (start us, length us, event | category | flops | bytes accessed | tf_op | source)
XLA Modules:
  0.0 529.0 jit_solution(5903180241067719745)
XLA Ops:
  2.6 4.1 collective-permute-start.1
  7.4 3.6 convert_element_type.423
  11.4 4.5 collective-permute-done.1
  19.1 5.3 collective-permute-done.2
  28.1 16.3 %collective-permute-start = (bf16[1,256,1536]{2,1,0:T(8,128)(2,1)S(1)}, bf16[1,256,1536]{2,1,0:T(8,128)(2,1)}, u32[]{:S(2)}, u32[]{:S(2)}) collective-permute-start(bf16[1,256,1536]{2,1,0:T(8,128)(2,1)S(1)} %get-tuple-element.326.own), channel_id=1, source_target_pairs={{0,1},{1,0},{2,3},{3,2},{4,5},{5,4},{6,7},{7,6},{8,9},{9,8},{10,11... | collective-permute-start | bytes 2359304 | tf_op jit(solution)/shard_map/ppermute | solution.py:691
  45.9 15.5 %collective-permute-done.got = bf16[1,256,1536]{2,1,0:T(8,128)(2,1)} collective-permute-done((bf16[1,256,1536]{2,1,0:T(8,128)(2,1)S(1)}, bf16[1,256,1536]{2,1,0:T(8,128)(2,1)}, u32[]{:S(2)}, u32[]{:S(2)}) %collective-permute-start) | collective-permute-done | bytes 786464 | tf_op jit(solution)/shard_map/ppermute | solution.py:691
  64.3 6.8 %shard_map.280 = bf16[2,2,2,192,1152]{4,3,2,1,0:T(8,128)(2,1)} custom-call(s32[3]{0:T(128)S(1)} %pad_add_fusion.at_ref, bf16[2,192,1152]{2,1,0:T(8,128)(2,1)S(1)} %pad_maximum_fusion.7.first, bf16[2,192,1152]{2,1,0:T(8,128)(2,1)} %collective-permute-done.3.first_y, bf16[2,192,1152]{2,1,0:T(8,128)(2,1)S(1)} %pad_maximum_fusion.8.second, ...), custom_call_target="tpu_custom_call" | custom-call | bytes 221184 | tf_op jit(solution)/shard_map/pallas_call | solution.py:637
  71.0 8.5 %collective-permute-done.14.got = bf16[1,256,1536]{2,1,0:T(8,128)(2,1)S(1)} collective-permute-done((bf16[1,256,1536]{2,1,0:T(8,128)(2,1)S(1)}, bf16[1,256,1536]{2,1,0:T(8,128)(2,1)S(1)}, u32[]{:S(2)}, u32[]{:S(2)}) %collective-permute-start.14) | collective-permute-done | bytes 786464 | tf_op jit(solution)/shard_map/ppermute | solution.py:691
  80.4 3.7 shard_map.279
  84.1 7.5 %convolution_convert_fusion.3.refs_0_.refs_2_.refs_9_.refs_10_.refs_12_ = bf16[2,512,1152]{2,1,0:T(8,128)(2,1)} fusion(bf16[2,512,1536]{2,1,0:T(8,128)(2,1)} %shard_map.279, bf16[1536,1152,1]{1,0,2:T(8,128)(2,1)S(1)} %bitcast.275), kind=kOutput, calls=%fused_computation.12 | convolution fusion | flops 3625058304 | bytes 9043968 | tf_op jit(solution)/shard_map/dot_general | solution.py:889
  91.7 3.4 shard_map.282
  95.1 6.1 %convolution_convert_fusion.2.refs_0_.refs_2_.refs_9_.refs_10_.refs_12_ = bf16[2,512,1152]{2,1,0:T(8,128)(2,1)S(1)} fusion(bf16[2,512,1536]{2,1,0:T(8,128)(2,1)} %shard_map.282, bf16[1536,1152,1]{1,0,2:T(8,128)(2,1)S(1)} %bitcast.276), kind=kOutput, calls=%fused_computation.11 | convolution fusion | flops 3625058304 | bytes 9043968 | tf_op jit(solution)/shard_map/dot_general | solution.py:889
  104.2 2.8 collective-permute-start.17
  106.9 2.9 collective-permute-start.9
  109.8 3.5 collective-permute-start.21
  113.6 6.3 %collective-permute-done.19 = bf16[192,1536]{1,0:T(8,128)(2,1)S(1)} collective-permute-done((bf16[192,1536]{1,0:T(8,128)(2,1)S(1)}, bf16[192,1536]{1,0:T(8,128)(2,1)S(1)}, u32[]{:S(2)}, u32[]{:S(2)}) %collective-permute-start.19) | collective-permute-done | bytes 589856 | tf_op jit(solution)/shard_map/ppermute | solution.py:691
  120.0 2.8 collective-permute-start.20
  123.0 2.5 collective-permute-start.18
  125.5 8.9 %shard_map.281 = (bf16[2,512,1024]{2,1,0:T(8,128)(2,1)S(1)}, f32[2,512,128]{2,1,0:T(8,128)S(1)}, f32[2,512,128]{2,1,0:T(8,128)S(1)}, f32[2,128,768]{2,1,0:T(8,12...) custom-call(bf16[2,512,1152]{2,1,0:T(8,128)(2,1)} %convolution_convert_fusion.3.refs_0_.refs_2_.refs_9_.refs_10_.refs_12_, ...), custom_call_target="tpu_custom_call" | custom-call | flops 6000000000 | bytes 8000000 | tf_op jit(solution)/shard_map/pallas_call | solution.py:419
  137.5 8.9 %shard_map.283 = (bf16[2,512,1024]{2,1,0:T(8,128)(2,1)S(1)}, f32[2,512,128]{2,1,0:T(8,128)S(1)}, f32[2,512,128]{2,1,0:T(8,128)S(1)}, f32[2,128,768]{2,1,0:T(8,12...) custom-call(bf16[2,512,1152]{2,1,0:T(8,128)(2,1)} %copy-done.65, ...), custom_call_target="tpu_custom_call" | custom-call | flops 6000000000 | bytes 8000000 | tf_op jit(solution)/shard_map/pallas_call | solution.py:419
  150.7 4.4 shard_map.284
  155.6 6.5 %convolution_convert_fusion.5.refs_6_.refs_2_ = bf16[2,512,768]{2,1,0:T(8,128)(2,1)} fusion(bf16[2,512,1536]{2,1,0:T(8,128)(2,1)} %shard_map.279, bf16[1536,1536]{1,0:T(8,128)(2,1)} %bitcast.257), kind=kOutput, calls=%fused_computation.37 | convolution fusion | flops 2416705536 | bytes 7077888 | tf_op jit(solution)/shard_map/dot_general | solution.py:889
  164.0 3.4 slice.387
  169.0 5.3 %convolution_convert_fusion.4.refs_6_.refs_2_ = bf16[2,512,768]{2,1,0:T(8,128)(2,1)} fusion(bf16[2,512,1536]{2,1,0:T(8,128)(2,1)S(1)} %copy-done.36, bf16[1536,1536]{1,0:T(8,128)(2,1)} %bitcast.259), kind=kOutput, calls=%fused_computation.36 | convolution fusion | flops 2416705536 | bytes 7077888 | tf_op jit(solution)/shard_map/dot_general | solution.py:889
  174.3 3.8 collective-permute-done.28.got
  178.2 2.9 collective-permute-start.30
  182.2 3.6 shard_map.286
  185.9 7.0 %fusion.11.refs_7_.refs_10_.refs_3_ = f32[2,512,768]{2,1,0:T(8,128)} fusion(bf16[2,512,1536]{2,1,0:T(8,128)(2,1)} %shard_map.286, bf16[1536,768]{1,0:T(8,128)(2,1)} %slice.387), kind=kOutput, calls=%fused_computation.30 | convolution fusion | flops 2415919104 | bytes 8650752 | tf_op jit(solution)/shard_map/dot_general | solution.py:889
  192.9 10.4 %shard_map.287 = (f32[2,512,768]{2,1,0:T(8,128)}, bf16[2,512,768]{2,1,0:T(8,128)(2,1)S(1)}, bf16[2,2,128,768]{3,2,1,0:T(8,128)(2,1)S(1)}, f32[2,8,512]{2,1,0:T(8,128)S(1)}) custom-call(bf16[2,512,1024]{2,1,0:T(8,128)(2,1)} %copy-done.9, f32[2,512,128]{2,1,0:T(8,128)S(1)} %copy-done.15, f32[2,512,128]{2,1,0:T(8,128)S(1)} %copy-done.19, ...), custom_call_target="tpu_custom_call" | custom-call | flops 10000000000 | bytes 16000000 | tf_op jit(solution)/shard_map/pallas_call | solution.py:419
  208.6 6.3 %fusion.9.refs_7_.refs_11_.refs_3_ = f32[2,512,768]{2,1,0:T(8,128)} fusion(bf16[2,512,1536]{2,1,0:T(8,128)(2,1)} %shard_map.289, bf16[1536,1536]{1,0:T(8,128)(2,1)S(1)} %bitcast.262), kind=kOutput, calls=%fused_computation.28 | convolution fusion | flops 2415919104 | bytes 8650752 | tf_op jit(solution)/shard_map/dot_general | solution.py:889
  217.1 2.9 convolution_convert_fusion.1.refs_9_
  222.0 8.3 %shard_map.290 = (bf16[2,512,768]{2,1,0:T(8,128)(2,1)S(1)}, bf16[2,512,768]{2,1,0:T(8,128)(2,1)S(1)}, bf16[2,512,768]{2,1,0:T(8,128)(2,1)}, f32[2,128,768]{2,1,0...) custom-call(f32[2,512,768]{2,1,0:T(8,128)} %get-tuple-element.177.refs_0_.refs_4_, ...), custom_call_target="tpu_custom_call" | custom-call | flops 6000000000 | bytes 18000000 | tf_op jit(solution)/shard_map/pallas_call | solution.py:419
  233.1 10.5 %shard_map.291 = (f32[2,512,768]{2,1,0:T(8,128)}, bf16[2,512,768]{2,1,0:T(8,128)(2,1)S(1)}, bf16[2,2,128,768]{3,2,1,0:T(8,128)(2,1)S(1)}, f32[2,8,512]{2,1,0:T(8,128)S(1)}) custom-call(bf16[2,512,1024]{2,1,0:T(8,128)(2,1)} %copy-done.8, f32[2,512,128]{2,1,0:T(8,128)S(1)} %copy-done.13, f32[2,512,128]{2,1,0:T(8,128)S(1)} %copy-done.17, ...), custom_call_target="tpu_custom_call" | custom-call | flops 10000000000 | bytes 16000000 | tf_op jit(solution)/shard_map/pallas_call | solution.py:419
  243.6 4.4 convolution_bitcast_fusion.3
  248.4 2.9 convolution_convert_fusion.refs_9_
  252.9 4.3 collective-permute-done.37
  257.3 8.2 %shard_map.292 = (bf16[2,512,768]{2,1,0:T(8,128)(2,1)S(1)}, bf16[2,512,768]{2,1,0:T(8,128)(2,1)S(1)}, bf16[2,512,768]{2,1,0:T(8,128)(2,1)}, f32[2,128,768]{2,1,0...) custom-call(f32[2,512,768]{2,1,0:T(8,128)} %get-tuple-element.193.refs_0_.refs_4_, ...), custom_call_target="tpu_custom_call" | custom-call | flops 6000000000 | bytes 18000000 | tf_op jit(solution)/shard_map/pallas_call | solution.py:419
  269.8 7.3 %convolution_bitcast_fusion.2 = f32[1536,768]{1,0:T(8,128)} fusion(bf16[2,512,1536]{2,1,0:T(8,128)(2,1)} %shard_map.286, bf16[2,512,768]{2,1,0:T(8,128)(2,1)} %get-tuple-element.203), kind=kOutput, calls=%fused_computation.13 | convolution fusion | flops 2415919104 | bytes 9437184 | tf_op jit(solution)/shard_map/dot_general | solution.py:889
  277.1 4.8 bitcast_add_fusion.1
  281.9 3.0 fusion.2
  284.9 4.7 fusion.40
  290.9 3.3 collective-permute-start.46
  305.1 25.4 %shard_map.295 = (bf16[2,512,1152]{2,1,0:T(8,128)(2,1)}, f32[2,8,1024]{2,1,0:T(8,128)S(1)}, f32[8,1024]{1,0:T(8,128)S(1)}, f32[8,128]{1,0:T(8,128)S(1)}, f32[8,768]{1,0:T(8,128)S(1)}) custom-call(bf16[2,512,1024]{2,1,0:T(8,128)(2,1)} %copy-done.9, f32[2,512,128]{2,1,0:T(8,128)S(1)} %copy-done.15, f32[2,512,128]{2,1,0:T(8,128)S(1)} %copy-done.19, ...), custom_call_target="tpu_custom_call" | custom-call | flops 32000000000 | bytes 24000000 | tf_op jit(solution)/shard_map/pallas_call | solution.py:419
  330.5 9.6 %collective-permute-done.39 = bf16[2,256,1536]{2,1,0:T(8,128)(2,1)} collective-permute-done((bf16[2,256,1536]{2,1,0:T(8,128)(2,1)}, bf16[2,256,1536]{2,1,0:T(8,128)(2,1)}, u32[]{:S(2)}, u32[]{:S(2)}) %collective-permute-start.39) | collective-permute-done | bytes 1572896 | tf_op jit(solution)/shard_map/ppermute | solution.py:691
  340.1 3.0 fusion.33
  346.2 6.4 %collective-permute-start.50 = (bf16[2,192,768]{2,1,0:T(8,128)(2,1)S(1)}, bf16[2,192,768]{2,1,0:T(8,128)(2,1)S(1)}, u32[]{:S(2)}, u32[]{:S(2)}) collective-permute-start(bf16[2,192,768]{2,1,0:T(8,128)(2,1)S(1)} %pad_maximum_fusion.10), channel_id=1, source_target_pairs={{0,4},{4,0},{1,5},{5,1},{2,6},{6,2},{3,7},{7,3},{8,12},{12,8},{9,1... | collective-permute-start | bytes 1769480 | tf_op jit(solution)/shard_map/ppermute | solution.py:691
  354.2 6.4 %add_convert_fusion.1 = bf16[2,512,1536]{2,1,0:T(8,128)(2,1)S(1)} fusion(f32[2,512,1536]{2,1,0:T(8,128)} %fusion.40, bf16[2,512,1152]{2,1,0:T(8,128)(2,1)S(1)} %fusion.47, bf16[1536,1152,1]{1,0,2:T(8,128)(2,1)S(1)} %bitcast.277), kind=kOutput, calls=%fused_computation.5 | convolution fusion | flops 3627024384 | bytes 15335424 | tf_op jit(solution)/shard_map/dot_general | solution.py:889
  360.9 8.2 %convolution_bitcast_fusion.1 = f32[1536,1152]{1,0:T(8,128)} fusion(bf16[2,512,1536]{2,1,0:T(8,128)(2,1)S(1)} %copy-done.39, bf16[2,512,1152]{2,1,0:T(8,128)(2,1)} %copy-done.60), kind=kOutput, calls=%fused_computation.2 | convolution fusion | flops 3623878656 | bytes 12582912 | tf_op jit(solution)/shard_map/dot_general | solution.py:889
  369.1 4.6 fusion.39
  382.0 25.4 %shard_map.296 = (bf16[2,512,1152]{2,1,0:T(8,128)(2,1)}, f32[2,8,1024]{2,1,0:T(8,128)S(1)}, f32[8,1024]{1,0:T(8,128)S(1)}, f32[8,128]{1,0:T(8,128)S(1)}, f32[8,768]{1,0:T(8,128)S(1)}) custom-call(bf16[2,512,1024]{2,1,0:T(8,128)(2,1)} %copy-done.8, f32[2,512,128]{2,1,0:T(8,128)S(1)} %copy-done.13, f32[2,512,128]{2,1,0:T(8,128)S(1)} %copy-done.17, ...), custom_call_target="tpu_custom_call" | custom-call | flops 32000000000 | bytes 24000000 | tf_op jit(solution)/shard_map/pallas_call | solution.py:419
  407.4 2.5 add_bitcast_fusion.1
  412.3 3.0 fusion.16
  415.3 7.4 %collective-permute-done.54 = f32[2,8,1024]{2,1,0:T(8,128)S(1)} collective-permute-done((f32[2,8,1024]{2,1,0:T(8,128)S(1)}, f32[2,8,1024]{2,1,0:T(8,128)S(1)}, u32[]{:S(2)}, u32[]{:S(2)}) %collective-permute-start.54) | collective-permute-done | bytes 65568 | tf_op jit(solution)/shard_map/ppermute | solution.py:720
  422.8 6.6 %add_convert_fusion = bf16[2,512,1536]{2,1,0:T(8,128)(2,1)S(1)} fusion(f32[2,512,1536]{2,1,0:T(8,128)} %fusion.39, bf16[2,512,1152]{2,1,0:T(8,128)(2,1)S(1)} %fusion.48, bf16[1536,1152,1]{1,0,2:T(8,128)(2,1)S(1)} %bitcast.278), kind=kOutput, calls=%fused_computation.4 | convolution fusion | flops 3627024384 | bytes 15335424 | tf_op jit(solution)/shard_map/dot_general | solution.py:889
  433.0 4.7 fusion.1
  447.6 13.1 %collective-permute-done.58 = bf16[1,2,192,1152]{3,2,1,0:T(8,128)(2,1)} collective-permute-done((bf16[1,2,192,1152]{3,2,1,0:T(8,128)(2,1)}, bf16[1,2,192,1152]{3,2,1,0:T(8,128)(2,1)}, u32[]{:S(2)}, u32[]{:S(2)}) %collective-permute-start.58) | collective-permute-done | bytes 884768 | tf_op jit(solution)/shard_map/ppermute | solution.py:691
  468.4 8.1 %collective-permute-done.60 = bf16[1,192,1152]{2,1,0:T(8,128)(2,1)} collective-permute-done((bf16[1,192,1152]{2,1,0:T(8,128)(2,1)}, bf16[1,192,1152]{2,1,0:T(8,128)(2,1)}, u32[]{:S(2)}, u32[]{:S(2)}) %collective-permute-start.60) | collective-permute-done | bytes 442400 | tf_op jit(solution)/shard_map/ppermute | solution.py:691
  478.1 2.6 broadcast_select_fusion.2
  484.9 2.9 collective-permute-done.61
  491.8 9.1 %collective-permute-done.63 = bf16[1,192,1152]{2,1,0:T(8,128)(2,1)} collective-permute-done((bf16[1,192,1152]{2,1,0:T(8,128)(2,1)}, bf16[1,192,1152]{2,1,0:T(8,128)(2,1)}, u32[]{:S(2)}, u32[]{:S(2)}) %collective-permute-start.63) | collective-permute-done | bytes 442400 | tf_op jit(solution)/shard_map/ppermute | solution.py:834
  502.4 4.3 collective-permute-start.65
  508.6 2.9 collective-permute-start.68
  511.5 2.4 collective-permute-start.70
  524.4 3.4 collective-permute-done.69
  (435 shorter events, 121.7 us)
Async XLA Ops:
  2.6 13.3 %collective-permute-start.1 = (bf16[192,1152]{1,0:T(8,128)(2,1)S(1)}, bf16[192,1152]{1,0:T(8,128)(2,1)S(1)}, u32[]{:S(2)}, u32[]{:S(2)}) collective-permute-start(bf16[192,1152]{1,0:T(8,128)(2,1)S(1)} %concatenate.24), channel_id=1, source_target_pairs={{0,2},{10,8},{2,10},{8,0},{1,3},{11,9},{3,11},{9,1},{4,6},{14,12},... | collective-permute-start | bytes 1327112 | tf_op jit(solution)/shard_map/ppermute | solution.py:763
  6.7 9.2 %collective-permute-start.4 = (bf16[192,1152]{1,0:T(8,128)(2,1)S(1)}, bf16[192,1152]{1,0:T(8,128)(2,1)S(1)}, u32[]{:S(2)}, u32[]{:S(2)}) collective-permute-start(bf16[192,1152]{1,0:T(8,128)(2,1)S(1)} %concatenate.24), channel_id=1, source_target_pairs={{2,8},{8,2},{3,9},{9,3},{6,12},{12,6},{7,13},{13,7},{18,24},{24,18... | collective-permute-start | bytes 1327112 | tf_op jit(solution)/shard_map/ppermute | solution.py:763
  16.0 8.4 %collective-permute-start.2 = (bf16[192,1152]{1,0:T(8,128)(2,1)S(1)}, bf16[192,1152]{1,0:T(8,128)(2,1)S(1)}, u32[]{:S(2)}, u32[]{:S(2)}) collective-permute-start(bf16[192,1152]{1,0:T(8,128)(2,1)S(1)} %get-tuple-element.347), channel_id=1, source_target_pairs={{0,16},{16,0},{1,17},{17,1},{2,18},{18,2},{3,19},{19,3},{4,20},{20... | collective-permute-start | bytes 1327112 | tf_op jit(solution)/shard_map/ppermute | solution.py:691
  17.6 8.5 %collective-permute-start.5 = (bf16[192,1152]{1,0:T(8,128)(2,1)S(1)}, bf16[192,1152]{1,0:T(8,128)(2,1)S(1)}, u32[]{:S(2)}, u32[]{:S(2)}) collective-permute-start(bf16[192,1152]{1,0:T(8,128)(2,1)S(1)} %get-tuple-element.346), channel_id=1, source_target_pairs={{0,4},{4,0},{1,5},{5,1},{2,6},{6,2},{3,7},{7,3},{8,12},{12,8},{9,1... | collective-permute-start | bytes 1327112 | tf_op jit(solution)/shard_map/ppermute | solution.py:691
  24.5 38.5 %collective-permute-start.3 = (bf16[2,192,1152]{2,1,0:T(8,128)(2,1)S(1)}, bf16[2,192,1152]{2,1,0:T(8,128)(2,1)}, u32[]{:S(2)}, u32[]{:S(2)}) collective-permute-start(bf16[2,192,1152]{2,1,0:T(8,128)(2,1)S(1)} %pad_maximum_fusion.7.first), channel_id=1, source_target_pairs={{0,4},{4,0},{1,5},{5,1},{2,6},{6,2},{3,7},{7,3},{8,12},{12,8},{9,1... | collective-permute-start | bytes 2654216 | tf_op jit(solution)/shard_map/ppermute | solution.py:691
  26.1 36.8 %collective-permute-start.6 = (bf16[2,192,1152]{2,1,0:T(8,128)(2,1)S(1)}, bf16[2,192,1152]{2,1,0:T(8,128)(2,1)}, u32[]{:S(2)}, u32[]{:S(2)}) collective-permute-start(bf16[2,192,1152]{2,1,0:T(8,128)(2,1)S(1)} %pad_maximum_fusion.8.second), channel_id=1, source_target_pairs={{0,16},{16,0},{1,17},{17,1},{2,18},{18,2},{3,19},{19,3},{4,20},{20... | collective-permute-start | bytes 2654216 | tf_op jit(solution)/shard_map/ppermute | solution.py:691
  28.1 33.3 %collective-permute-start = (bf16[1,256,1536]{2,1,0:T(8,128)(2,1)S(1)}, bf16[1,256,1536]{2,1,0:T(8,128)(2,1)}, u32[]{:S(2)}, u32[]{:S(2)}) collective-permute-start(bf16[1,256,1536]{2,1,0:T(8,128)(2,1)S(1)} %get-tuple-element.326.own), channel_id=1, source_target_pairs={{0,1},{1,0},{2,3},{3,2},{4,5},{5,4},{6,7},{7,6},{8,9},{9,8},{10,11... | collective-permute-start | bytes 2359304 | tf_op jit(solution)/shard_map/ppermute | solution.py:691
  44.5 35.8 %collective-permute-start.7 = (bf16[1,256,1536]{2,1,0:T(8,128)(2,1)S(1)}, bf16[1,256,1536]{2,1,0:T(8,128)(2,1)}, u32[]{:S(2)}, u32[]{:S(2)}) collective-permute-start(bf16[1,256,1536]{2,1,0:T(8,128)(2,1)S(1)} %get-tuple-element.326.own), channel_id=1, source_target_pairs={{0,8},{8,0},{1,9},{9,1},{2,10},{10,2},{3,11},{11,3},{4,12},{12,4},... | collective-permute-start | bytes 2359304 | tf_op jit(solution)/shard_map/ppermute | solution.py:691
  44.5 47.2 %collective-permute-start.15 = (bf16[1,256,1536]{2,1,0:T(8,128)(2,1)S(1)}, bf16[1,256,1536]{2,1,0:T(8,128)(2,1)}, u32[]{:S(2)}, u32[]{:S(2)}) collective-permute-start(bf16[1,256,1536]{2,1,0:T(8,128)(2,1)S(1)} %get-tuple-element.149.own), channel_id=1, source_target_pairs={{0,8},{8,0},{1,9},{9,1},{2,10},{10,2},{3,11},{11,3},{4,12},{12,4},... | collective-permute-start | bytes 2359304 | tf_op jit(solution)/shard_map/ppermute | solution.py:691
  61.5 18.1 %collective-permute-start.14 = (bf16[1,256,1536]{2,1,0:T(8,128)(2,1)S(1)}, bf16[1,256,1536]{2,1,0:T(8,128)(2,1)S(1)}, u32[]{:S(2)}, u32[]{:S(2)}) collective-permute-start(bf16[1,256,1536]{2,1,0:T(8,128)(2,1)S(1)} %get-tuple-element.149.own), channel_id=1, source_target_pairs={{0,1},{1,0},{2,3},{3,2},{4,5},{5,4},{6,7},{7,6},{8,9},{9,8},{10,11... | collective-permute-start | bytes 2359304 | tf_op jit(solution)/shard_map/ppermute | solution.py:691
  63.0 17.4 %collective-permute-start.8 = (bf16[1,256,1536]{2,1,0:T(8,128)(2,1)}, bf16[1,256,1536]{2,1,0:T(8,128)(2,1)S(1)}, u32[]{:S(2)}, u32[]{:S(2)}) collective-permute-start(bf16[1,256,1536]{2,1,0:T(8,128)(2,1)} %collective-permute-done.got), channel_id=1, source_target_pairs={{0,8},{8,0},{1,9},{9,1},{2,10},{10,2},{3,11},{11,3},{4,12},{12,4},... | collective-permute-start | bytes 2359304 | tf_op jit(solution)/shard_map/ppermute | solution.py:691
  71.0 30.2 %collective-permute-start.12 = (bf16[192,1536]{1,0:T(8,128)(2,1)S(1)}, bf16[192,1536]{1,0:T(8,128)(2,1)S(1)}, u32[]{:S(2)}, u32[]{:S(2)}) collective-permute-start(bf16[192,1536]{1,0:T(8,128)(2,1)S(1)} %pad_maximum_fusion.9), channel_id=1, source_target_pairs={{0,2},{10,8},{2,10},{8,0},{1,3},{11,9},{3,11},{9,1},{4,6},{14,12},... | collective-permute-start | bytes 1769480 | tf_op jit(solution)/shard_map/ppermute | solution.py:763
  79.6 21.7 %collective-permute-start.13 = (bf16[192,1536]{1,0:T(8,128)(2,1)S(1)}, bf16[192,1536]{1,0:T(8,128)(2,1)S(1)}, u32[]{:S(2)}, u32[]{:S(2)}) collective-permute-start(bf16[192,1536]{1,0:T(8,128)(2,1)S(1)} %pad_maximum_fusion.9), channel_id=1, source_target_pairs={{2,8},{8,2},{3,9},{9,3},{6,12},{12,6},{7,13},{13,7},{18,24},{24,18... | collective-permute-start | bytes 1769480 | tf_op jit(solution)/shard_map/ppermute | solution.py:763
  80.3 11.4 %collective-permute-start.16 = (bf16[1,256,1536]{2,1,0:T(8,128)(2,1)S(1)}, bf16[1,256,1536]{2,1,0:T(8,128)(2,1)S(1)}, u32[]{:S(2)}, u32[]{:S(2)}) collective-permute-start(bf16[1,256,1536]{2,1,0:T(8,128)(2,1)S(1)} %collective-permute-done.14.got), channel_id=1, source_target_pairs={{0,8},{8,0},{1,9},{9,1},{2,10},{10,2},{3,11},{11,3},{4,12},{12,4},... | collective-permute-start | bytes 2359304 | tf_op jit(solution)/shard_map/ppermute | solution.py:691
  101.3 12.1 %collective-permute-start.10 = (f32[8,768]{1,0:T(8,128)S(1)}, f32[8,768]{1,0:T(8,128)S(1)}, u32[]{:S(2)}, u32[]{:S(2)}) collective-permute-start(f32[8,768]{1,0:T(8,128)S(1)} %maximum_maximum_fusion), channel_id=1, source_target_pairs={{0,2},{2,0},{1,3},{3,1},{4,6},{6,4},{5,7},{7,5},{8,10},{10,8},{9,1... | collective-permute-start | bytes 73736 | tf_op jit(solution)/shard_map/ppermute | solution.py:691
  103.7 16.2 %collective-permute-start.19 = (bf16[192,1536]{1,0:T(8,128)(2,1)S(1)}, bf16[192,1536]{1,0:T(8,128)(2,1)S(1)}, u32[]{:S(2)}, u32[]{:S(2)}) collective-permute-start(bf16[192,1536]{1,0:T(8,128)(2,1)S(1)} %get-tuple-element.344), channel_id=1, source_target_pairs={{0,4},{4,0},{1,5},{5,1},{2,6},{6,2},{3,7},{7,3},{8,12},{12,8},{9,1... | collective-permute-start | bytes 1769480 | tf_op jit(solution)/shard_map/ppermute | solution.py:691
  104.2 18.7 %collective-permute-start.17 = (bf16[192,1536]{1,0:T(8,128)(2,1)S(1)}, bf16[192,1536]{1,0:T(8,128)(2,1)S(1)}, u32[]{:S(2)}, u32[]{:S(2)}) collective-permute-start(bf16[192,1536]{1,0:T(8,128)(2,1)S(1)} %get-tuple-element.345), channel_id=1, source_target_pairs={{0,16},{16,0},{1,17},{17,1},{2,18},{18,2},{3,19},{19,3},{4,20},{20... | collective-permute-start | bytes 1769480 | tf_op jit(solution)/shard_map/ppermute | solution.py:691
  106.9 18.6 %collective-permute-start.9 = (bf16[2,16,1024]{2,1,0:T(8,128)(2,1)S(1)}, bf16[2,16,1024]{2,1,0:T(8,128)(2,1)S(1)}, u32[]{:S(2)}, u32[]{:S(2)}) collective-permute-start(bf16[2,16,1024]{2,1,0:T(8,128)(2,1)S(1)} %slice.379), channel_id=1, source_target_pairs={{0,2},{2,4},{4,6},{1,3},{3,5},{5,7},{8,10},{10,12},{12,14},{9,11},... | collective-permute-start | bytes 196616 | tf_op jit(solution)/shard_map/ppermute | solution.py:720
  109.8 26.0 %collective-permute-start.21 = (bf16[2,16,1024]{2,1,0:T(8,128)(2,1)S(1)}, bf16[2,16,1024]{2,1,0:T(8,128)(2,1)S(1)}, u32[]{:S(2)}, u32[]{:S(2)}) collective-permute-start(bf16[2,16,1024]{2,1,0:T(8,128)(2,1)S(1)} %slice.385), channel_id=1, source_target_pairs={{0,2},{2,4},{4,6},{1,3},{3,5},{5,7},{8,10},{10,12},{12,14},{9,11},... | collective-permute-start | bytes 196616 | tf_op jit(solution)/shard_map/ppermute | solution.py:720
  120.0 28.3 %collective-permute-start.20 = (bf16[2,192,1536]{2,1,0:T(8,128)(2,1)S(1)}, bf16[2,192,1536]{2,1,0:T(8,128)(2,1)S(1)}, u32[]{:S(2)}, u32[]{:S(2)}) collective-permute-start(bf16[2,192,1536]{2,1,0:T(8,128)(2,1)S(1)} %pad_maximum_fusion.4.second), channel_id=1, source_target_pairs={{0,16},{16,0},{1,17},{17,1},{2,18},{18,2},{3,19},{19,3},{4,20},{20... | collective-permute-start | bytes 3538952 | tf_op jit(solution)/shard_map/ppermute | solution.py:691
  123.0 27.7 %collective-permute-start.18 = (bf16[2,192,1536]{2,1,0:T(8,128)(2,1)S(1)}, bf16[2,192,1536]{2,1,0:T(8,128)(2,1)S(1)}, u32[]{:S(2)}, u32[]{:S(2)}) collective-permute-start(bf16[2,192,1536]{2,1,0:T(8,128)(2,1)S(1)} %pad_maximum_fusion.3.first), channel_id=1, source_target_pairs={{0,4},{4,0},{1,5},{5,1},{2,6},{6,2},{3,7},{7,3},{8,12},{12,8},{9,1... | collective-permute-start | bytes 3538952 | tf_op jit(solution)/shard_map/ppermute | solution.py:691
  134.5 20.6 %collective-permute-start.11 = (bf16[2,144,768]{2,1,0:T(8,128)(2,1)S(1)}, bf16[2,144,768]{2,1,0:T(8,128)(2,1)S(1)}, u32[]{:S(2)}, u32[]{:S(2)}) collective-permute-start(bf16[2,144,768]{2,1,0:T(8,128)(2,1)S(1)} %get-tuple-element.147.refs_6_), channel_id=1, source_target_pairs={{0,2},{1,3},{4,6},{5,7},{8,10},{9,11},{12,14},{13,15},{16,18},{17,... | collective-permute-start | bytes 1327112 | tf_op jit(solution)/shard_map/ppermute | solution.py:724
  137.3 25.9 %collective-permute-start.23 = (bf16[1,256,1536]{2,1,0:T(8,128)(2,1)S(1)}, bf16[1,256,1536]{2,1,0:T(8,128)(2,1)}, u32[]{:S(2)}, u32[]{:S(2)}) collective-permute-start(bf16[1,256,1536]{2,1,0:T(8,128)(2,1)S(1)} %get-tuple-element.335.own), channel_id=1, source_target_pairs={{0,1},{1,0},{2,3},{3,2},{4,5},{5,4},{6,7},{7,6},{8,9},{9,8},{10,11... | collective-permute-start | bytes 2359304 | tf_op jit(solution)/shard_map/ppermute | solution.py:691
  137.5 40.6 %collective-permute-start.24 = (bf16[2,256,1536]{2,1,0:T(8,128)(2,1)}, bf16[2,256,1536]{2,1,0:T(8,128)(2,1)}, u32[]{:S(2)}, u32[]{:S(2)}) collective-permute-start(bf16[2,256,1536]{2,1,0:T(8,128)(2,1)} %param.17), channel_id=1, source_target_pairs={{0,8},{8,0},{1,9},{9,1},{2,10},{10,2},{3,11},{11,3},{4,12},{12,4},... | collective-permute-start | bytes 4718600 | tf_op jit(solution)/shard_map/ppermute | solution.py:691
  148.3 29.8 %collective-permute-start.28 = (bf16[1,256,1536]{2,1,0:T(8,128)(2,1)S(1)}, bf16[1,256,1536]{2,1,0:T(8,128)(2,1)S(1)}, u32[]{:S(2)}, u32[]{:S(2)}) collective-permute-start(bf16[1,256,1536]{2,1,0:T(8,128)(2,1)S(1)} %get-tuple-element.334.own), channel_id=1, source_target_pairs={{0,1},{1,0},{2,3},{3,2},{4,5},{5,4},{6,7},{7,6},{8,9},{9,8},{10,11... | collective-permute-start | bytes 2359304 | tf_op jit(solution)/shard_map/ppermute | solution.py:691
  163.2 17.8 %collective-permute-start.25 = (bf16[1,256,1536]{2,1,0:T(8,128)(2,1)}, bf16[1,256,1536]{2,1,0:T(8,128)(2,1)}, u32[]{:S(2)}, u32[]{:S(2)}) collective-permute-start(bf16[1,256,1536]{2,1,0:T(8,128)(2,1)} %collective-permute-done.23.got), channel_id=1, source_target_pairs={{0,8},{8,0},{1,9},{9,1},{2,10},{10,2},{3,11},{11,3},{4,12},{12,4},... | collective-permute-start | bytes 2359304 | tf_op jit(solution)/shard_map/ppermute | solution.py:691
  167.5 25.4 %collective-permute-start.26 = (bf16[2,128,768]{2,1,0:T(8,128)(2,1)S(1)}, bf16[2,128,768]{2,1,0:T(8,128)(2,1)S(1)}, u32[]{:S(2)}, u32[]{:S(2)}) collective-permute-start(bf16[2,128,768]{2,1,0:T(8,128)(2,1)S(1)} %copy-done.3), channel_id=1, source_target_pairs={{2,6},{3,7},{10,14},{11,15},{18,22},{19,23},{26,30},{27,31}} | collective-permute-start | bytes 1179656 | tf_op jit(solution)/shard_map/ppermute | solution.py:730
  168.3 24.6 %collective-permute-start.22 = (bf16[2,128,768]{2,1,0:T(8,128)(2,1)S(1)}, bf16[2,128,768]{2,1,0:T(8,128)(2,1)S(1)}, u32[]{:S(2)}, u32[]{:S(2)}) collective-permute-start(bf16[2,128,768]{2,1,0:T(8,128)(2,1)S(1)} %copy-done.3), channel_id=1, source_target_pairs={{2,4},{3,5},{10,12},{11,13},{18,20},{19,21},{26,28},{27,29}} | collective-permute-start | bytes 1179656 | tf_op jit(solution)/shard_map/ppermute | solution.py:730
  178.2 26.9 %collective-permute-start.29 = (bf16[1,256,1536]{2,1,0:T(8,128)(2,1)S(1)}, bf16[1,256,1536]{2,1,0:T(8,128)(2,1)S(1)}, u32[]{:S(2)}, u32[]{:S(2)}) collective-permute-start(bf16[1,256,1536]{2,1,0:T(8,128)(2,1)S(1)} %collective-permute-done.28.got), channel_id=1, source_target_pairs={{0,8},{8,0},{1,9},{9,1},{2,10},{10,2},{3,11},{11,3},{4,12},{12,4},... | collective-permute-start | bytes 2359304 | tf_op jit(solution)/shard_map/ppermute | solution.py:691
  178.2 25.1 %collective-permute-start.30 = (bf16[2,144,768]{2,1,0:T(8,128)(2,1)S(1)}, bf16[2,144,768]{2,1,0:T(8,128)(2,1)S(1)}, u32[]{:S(2)}, u32[]{:S(2)}) collective-permute-start(bf16[2,144,768]{2,1,0:T(8,128)(2,1)S(1)} %copy-done.5), channel_id=1, source_target_pairs={{0,2},{1,3},{4,6},{5,7},{8,10},{9,11},{12,14},{13,15},{16,18},{17,... | collective-permute-start | bytes 1327112 | tf_op jit(solution)/shard_map/ppermute | solution.py:724
  203.7 29.4 %collective-permute-start.35 = (bf16[2,128,768]{2,1,0:T(8,128)(2,1)S(1)}, bf16[2,128,768]{2,1,0:T(8,128)(2,1)S(1)}, u32[]{:S(2)}, u32[]{:S(2)}) collective-permute-start(bf16[2,128,768]{2,1,0:T(8,128)(2,1)S(1)} %shard_map.288), channel_id=1, source_target_pairs={{2,6},{3,7},{10,14},{11,15},{18,22},{19,23},{26,30},{27,31}} | collective-permute-start | bytes 1179656 | tf_op jit(solution)/shard_map/ppermute | solution.py:730
  204.4 28.7 %collective-permute-start.34 = (bf16[2,128,768]{2,1,0:T(8,128)(2,1)S(1)}, bf16[2,128,768]{2,1,0:T(8,128)(2,1)S(1)}, u32[]{:S(2)}, u32[]{:S(2)}) collective-permute-start(bf16[2,128,768]{2,1,0:T(8,128)(2,1)S(1)} %shard_map.288), channel_id=1, source_target_pairs={{2,4},{3,5},{10,12},{11,13},{18,20},{19,21},{26,28},{27,29}} | collective-permute-start | bytes 1179656 | tf_op jit(solution)/shard_map/ppermute | solution.py:730
  206.3 8.6 %collective-permute-start.27 = (f32[2,8,512]{2,1,0:T(8,128)S(1)}, f32[2,8,512]{2,1,0:T(8,128)S(1)}, u32[]{:S(2)}, u32[]{:S(2)}) collective-permute-start(f32[2,8,512]{2,1,0:T(8,128)S(1)} %get-tuple-element.172), channel_id=1, source_target_pairs={{0,8},{8,0},{1,9},{9,1},{2,10},{10,2},{3,11},{11,3},{4,12},{12,4},... | collective-permute-start | bytes 98312 | tf_op jit(solution)/shard_map/ppermute | solution.py:691
  221.3 75.1 %collective-permute-start.32 = (bf16[512,1536]{1,0:T(8,128)(2,1)}, bf16[512,1536]{1,0:T(8,128)(2,1)}, u32[]{:S(2)}, u32[]{:S(2)}) collective-permute-start(bf16[512,1536]{1,0:T(8,128)(2,1)} %slice_bitcast_fusion.7), channel_id=1, source_target_pairs={{0,8},{8,0},{1,9},{9,1},{2,10},{10,2},{3,11},{11,3},{4,12},{12,4},... | collective-permute-start | bytes 4718600 | tf_op jit(solution)/shard_map/ppermute | solution.py:691
  231.5 34.0 %collective-permute-start.33 = (bf16[2,144,768]{2,1,0:T(8,128)(2,1)S(1)}, bf16[2,144,768]{2,1,0:T(8,128)(2,1)S(1)}, u32[]{:S(2)}, u32[]{:S(2)}) collective-permute-start(bf16[2,144,768]{2,1,0:T(8,128)(2,1)S(1)} %get-tuple-element.187.refs_10_), channel_id=1, source_target_pairs={{2,0},{3,1},{6,4},{7,5},{10,8},{11,9},{14,12},{15,13},{18,16},{19,... | collective-permute-start | bytes 1327112 | tf_op jit(solution)/shard_map/ppermute | solution.py:724
  248.0 9.2 %collective-permute-start.37 = (f32[2,8,512]{2,1,0:T(8,128)S(1)}, f32[2,8,512]{2,1,0:T(8,128)S(1)}, u32[]{:S(2)}, u32[]{:S(2)}) collective-permute-start(f32[2,8,512]{2,1,0:T(8,128)S(1)} %reverse_add_fusion), channel_id=1, source_target_pairs={{0,1},{1,0},{2,3},{3,2},{4,5},{5,4},{6,7},{7,6},{8,9},{9,8},{10,11... | collective-permute-start | bytes 98312 | tf_op jit(solution)/shard_map/ppermute | solution.py:691
  252.7 47.8 %collective-permute-start.38 = (bf16[512,1536]{1,0:T(8,128)(2,1)}, bf16[512,1536]{1,0:T(8,128)(2,1)}, u32[]{:S(2)}, u32[]{:S(2)}) collective-permute-start(bf16[512,1536]{1,0:T(8,128)(2,1)} %slice_bitcast_fusion.5), channel_id=1, source_target_pairs={{0,8},{8,0},{1,9},{9,1},{2,10},{10,2},{3,11},{11,3},{4,12},{12,4},... | collective-permute-start | bytes 4718600 | tf_op jit(solution)/shard_map/ppermute | solution.py:691
  266.0 23.7 %collective-permute-start.41 = (bf16[2,128,768]{2,1,0:T(8,128)(2,1)S(1)}, bf16[2,128,768]{2,1,0:T(8,128)(2,1)S(1)}, u32[]{:S(2)}, u32[]{:S(2)}) collective-permute-start(bf16[2,128,768]{2,1,0:T(8,128)(2,1)S(1)} %shard_map.293), channel_id=1, source_target_pairs={{4,0},{5,1},{12,8},{13,9},{20,16},{21,17},{28,24},{29,25}} | collective-permute-start | bytes 1179656 | tf_op jit(solution)/shard_map/ppermute | solution.py:730
  267.3 22.4 %collective-permute-start.40 = (bf16[2,128,768]{2,1,0:T(8,128)(2,1)S(1)}, bf16[2,128,768]{2,1,0:T(8,128)(2,1)S(1)}, u32[]{:S(2)}, u32[]{:S(2)}) collective-permute-start(bf16[2,128,768]{2,1,0:T(8,128)(2,1)S(1)} %shard_map.293), channel_id=1, source_target_pairs={{4,2},{5,3},{12,10},{13,11},{20,18},{21,19},{28,26},{29,27}} | collective-permute-start | bytes 1179656 | tf_op jit(solution)/shard_map/ppermute | solution.py:730
  268.0 27.4 %collective-permute-start.42 = (bf16[2,144,768]{2,1,0:T(8,128)(2,1)S(1)}, bf16[2,144,768]{2,1,0:T(8,128)(2,1)S(1)}, u32[]{:S(2)}, u32[]{:S(2)}) collective-permute-start(bf16[2,144,768]{2,1,0:T(8,128)(2,1)S(1)} %get-tuple-element.216), channel_id=1, source_target_pairs={{2,0},{3,1},{6,4},{7,5},{10,8},{11,9},{14,12},{15,13},{18,16},{19,... | collective-permute-start | bytes 1327112 | tf_op jit(solution)/shard_map/ppermute | solution.py:724
  290.9 39.6 %collective-permute-start.46 = (bf16[2,2,192,768]{3,2,1,0:T(8,128)(2,1)}, bf16[2,2,192,768]{3,2,1,0:T(8,128)(2,1)}, u32[]{:S(2)}, u32[]{:S(2)}) collective-permute-start(bf16[2,2,192,768]{3,2,1,0:T(8,128)(2,1)} %pad_maximum_fusion.6.refs_20_), channel_id=1, source_target_pairs={{0,4},{4,0},{1,5},{5,1},{2,6},{6,2},{3,7},{7,3},{8,12},{12,8},{9,1... | collective-permute-start | bytes 3538952 | tf_op jit(solution)/shard_map/ppermute | solution.py:691
  294.4 36.1 %collective-permute-start.45 = (bf16[2,2,192,768]{3,2,1,0:T(8,128)(2,1)S(1)}, bf16[2,2,192,768]{3,2,1,0:T(8,128)(2,1)}, u32[]{:S(2)}, u32[]{:S(2)}) collective-permute-start(bf16[2,2,192,768]{3,2,1,0:T(8,128)(2,1)S(1)} %pad_maximum_fusion.5.refs_19_), channel_id=1, source_target_pairs={{0,16},{16,0},{1,17},{17,1},{2,18},{18,2},{3,19},{19,3},{4,20},{20... | collective-permute-start | bytes 3538952 | tf_op jit(solution)/shard_map/ppermute | solution.py:691
  295.7 34.7 %collective-permute-start.43 = (bf16[2,128,768]{2,1,0:T(8,128)(2,1)S(1)}, bf16[2,128,768]{2,1,0:T(8,128)(2,1)S(1)}, u32[]{:S(2)}, u32[]{:S(2)}) collective-permute-start(bf16[2,128,768]{2,1,0:T(8,128)(2,1)S(1)} %shard_map.294.refs_17_), channel_id=1, source_target_pairs={{4,2},{5,3},{12,10},{13,11},{20,18},{21,19},{28,26},{29,27}} | collective-permute-start | bytes 1179656 | tf_op jit(solution)/shard_map/ppermute | solution.py:730
  296.4 34.0 %collective-permute-start.44 = (bf16[2,128,768]{2,1,0:T(8,128)(2,1)S(1)}, bf16[2,128,768]{2,1,0:T(8,128)(2,1)S(1)}, u32[]{:S(2)}, u32[]{:S(2)}) collective-permute-start(bf16[2,128,768]{2,1,0:T(8,128)(2,1)S(1)} %shard_map.294.refs_17_), channel_id=1, source_target_pairs={{4,0},{5,1},{12,8},{13,9},{20,16},{21,17},{28,24},{29,25}} | collective-permute-start | bytes 1179656 | tf_op jit(solution)/shard_map/ppermute | solution.py:730
  304.2 35.8 %collective-permute-start.39 = (bf16[2,256,1536]{2,1,0:T(8,128)(2,1)}, bf16[2,256,1536]{2,1,0:T(8,128)(2,1)}, u32[]{:S(2)}, u32[]{:S(2)}) collective-permute-start(bf16[2,256,1536]{2,1,0:T(8,128)(2,1)} %pad_maximum_fusion.1.refs_18_), channel_id=1, source_target_pairs={{0,1},{1,0},{2,3},{3,2},{4,5},{5,4},{6,7},{7,6},{8,9},{9,8},{10,11... | collective-permute-start | bytes 4718600 | tf_op jit(solution)/shard_map/ppermute | solution.py:691
  343.3 30.4 %collective-permute-start.51 = (bf16[2,192,768]{2,1,0:T(8,128)(2,1)S(1)}, bf16[2,192,768]{2,1,0:T(8,128)(2,1)S(1)}, u32[]{:S(2)}, u32[]{:S(2)}) collective-permute-start(bf16[2,192,768]{2,1,0:T(8,128)(2,1)S(1)} %pad_maximum_fusion.11), channel_id=1, source_target_pairs={{0,16},{16,0},{1,17},{17,1},{2,18},{18,2},{3,19},{19,3},{4,20},{20... | collective-permute-start | bytes 1769480 | tf_op jit(solution)/shard_map/ppermute | solution.py:691
  346.2 27.5 %collective-permute-start.50 = (bf16[2,192,768]{2,1,0:T(8,128)(2,1)S(1)}, bf16[2,192,768]{2,1,0:T(8,128)(2,1)S(1)}, u32[]{:S(2)}, u32[]{:S(2)}) collective-permute-start(bf16[2,192,768]{2,1,0:T(8,128)(2,1)S(1)} %pad_maximum_fusion.10), channel_id=1, source_target_pairs={{0,4},{4,0},{1,5},{5,1},{2,6},{6,2},{3,7},{7,3},{8,12},{12,8},{9,1... | collective-permute-start | bytes 1769480 | tf_op jit(solution)/shard_map/ppermute | solution.py:691
  360.8 15.5 %collective-permute-start.48 = (bf16[512,1536]{1,0:T(8,128)(2,1)S(1)}, bf16[512,1536]{1,0:T(8,128)(2,1)S(1)}, u32[]{:S(2)}, u32[]{:S(2)}) collective-permute-start(bf16[512,1536]{1,0:T(8,128)(2,1)S(1)} %slice_bitcast_fusion.3), channel_id=1, source_target_pairs={{0,8},{8,0},{1,9},{9,1},{2,10},{10,2},{3,11},{11,3},{4,12},{12,4},... | collective-permute-start | bytes 4718600 | tf_op jit(solution)/shard_map/ppermute | solution.py:691
  374.1 33.2 %collective-permute-start.52 = (bf16[2,192,768]{2,1,0:T(8,128)(2,1)S(1)}, bf16[2,192,768]{2,1,0:T(8,128)(2,1)}, u32[]{:S(2)}, u32[]{:S(2)}) collective-permute-start(bf16[2,192,768]{2,1,0:T(8,128)(2,1)S(1)} %get-tuple-element.339.refs_19_), channel_id=1, source_target_pairs={{2,0},{8,10},{10,2},{0,8},{3,1},{9,11},{11,3},{1,9},{6,4},{12,14},... | collective-permute-start | bytes 1769480 | tf_op jit(solution)/shard_map/ppermute | solution.py:834
  374.5 32.9 %collective-permute-start.53 = (bf16[2,192,768]{2,1,0:T(8,128)(2,1)S(1)}, bf16[2,192,768]{2,1,0:T(8,128)(2,1)}, u32[]{:S(2)}, u32[]{:S(2)}) collective-permute-start(bf16[2,192,768]{2,1,0:T(8,128)(2,1)S(1)} %get-tuple-element.338.refs_20_), channel_id=1, source_target_pairs={{2,8},{8,2},{3,9},{9,3},{6,12},{12,6},{7,13},{13,7},{18,24},{24,18... | collective-permute-start | bytes 1769480 | tf_op jit(solution)/shard_map/ppermute | solution.py:835
  376.8 34.8 %collective-permute-start.49 = (bf16[256,1536]{1,0:T(8,128)(2,1)S(1)}, bf16[256,1536]{1,0:T(8,128)(2,1)S(1)}, u32[]{:S(2)}, u32[]{:S(2)}) collective-permute-start(bf16[256,1536]{1,0:T(8,128)(2,1)S(1)} %constant_dynamic-slice_fusion.8.refs_17_), channel_id=1, source_target_pairs={{0,1},{1,0},{2,3},{3,2},{4,5},{5,4},{6,7},{7,6},{8,9},{9,8},{10,11... | collective-permute-start | bytes 2359304 | tf_op jit(solution)/shard_map/ppermute | solution.py:691
  409.9 12.8 %collective-permute-start.54 = (f32[2,8,1024]{2,1,0:T(8,128)S(1)}, f32[2,8,1024]{2,1,0:T(8,128)S(1)}, u32[]{:S(2)}, u32[]{:S(2)}) collective-permute-start(f32[2,8,1024]{2,1,0:T(8,128)S(1)} %get-tuple-element.245), channel_id=1, source_target_pairs={{2,0},{4,2},{6,4},{3,1},{5,3},{7,5},{10,8},{12,10},{14,12},{11,9},... | collective-permute-start | bytes 196616 | tf_op jit(solution)/shard_map/ppermute | solution.py:720
  430.7 12.0 %collective-permute-start.55 = (bf16[512,1536]{1,0:T(8,128)(2,1)}, bf16[512,1536]{1,0:T(8,128)(2,1)}, u32[]{:S(2)}, u32[]{:S(2)}) collective-permute-start(bf16[512,1536]{1,0:T(8,128)(2,1)} %slice_bitcast_fusion.1), channel_id=1, source_target_pairs={{0,8},{8,0},{1,9},{9,1},{2,10},{10,2},{3,11},{11,3},{4,12},{12,4},... | collective-permute-start | bytes 4718600 | tf_op jit(solution)/shard_map/ppermute | solution.py:691
  439.0 21.7 %collective-permute-start.58 = (bf16[1,2,192,1152]{3,2,1,0:T(8,128)(2,1)}, bf16[1,2,192,1152]{3,2,1,0:T(8,128)(2,1)}, u32[]{:S(2)}, u32[]{:S(2)}) collective-permute-start(bf16[1,2,192,1152]{3,2,1,0:T(8,128)(2,1)} %dynamic-slice_bitcast_fusion), channel_id=1, source_target_pairs={{0,4},{4,0},{1,5},{5,1},{2,6},{6,2},{3,7},{7,3},{8,12},{12,8},{9,1... | collective-permute-start | bytes 2654216 | tf_op jit(solution)/shard_map/ppermute | solution.py:691
  441.7 21.2 %collective-permute-start.57 = (bf16[1,2,192,1152]{3,2,1,0:T(8,128)(2,1)}, bf16[1,2,192,1152]{3,2,1,0:T(8,128)(2,1)}, u32[]{:S(2)}, u32[]{:S(2)}) collective-permute-start(bf16[1,2,192,1152]{3,2,1,0:T(8,128)(2,1)} %dynamic-slice_bitcast_fusion.1), channel_id=1, source_target_pairs={{0,16},{16,0},{1,17},{17,1},{2,18},{18,2},{3,19},{19,3},{4,20},{20... | collective-permute-start | bytes 2654216 | tf_op jit(solution)/shard_map/ppermute | solution.py:691
  446.2 22.2 %collective-permute-start.56 = (bf16[256,1536]{1,0:T(8,128)(2,1)}, bf16[256,1536]{1,0:T(8,128)(2,1)}, u32[]{:S(2)}, u32[]{:S(2)}) collective-permute-start(bf16[256,1536]{1,0:T(8,128)(2,1)} %constant_dynamic-slice_fusion.2), channel_id=1, source_target_pairs={{0,1},{1,0},{2,3},{3,2},{4,5},{5,4},{6,7},{7,6},{8,9},{9,8},{10,11... | collective-permute-start | bytes 2359304 | tf_op jit(solution)/shard_map/ppermute | solution.py:691
  465.7 10.8 %collective-permute-start.60 = (bf16[1,192,1152]{2,1,0:T(8,128)(2,1)}, bf16[1,192,1152]{2,1,0:T(8,128)(2,1)}, u32[]{:S(2)}, u32[]{:S(2)}) collective-permute-start(bf16[1,192,1152]{2,1,0:T(8,128)(2,1)} %constant_dynamic-slice_fusion), channel_id=1, source_target_pairs={{0,16},{16,0},{1,17},{17,1},{2,18},{18,2},{3,19},{19,3},{4,20},{20... | collective-permute-start | bytes 1327112 | tf_op jit(solution)/shard_map/ppermute | solution.py:691
  467.5 10.5 %collective-permute-start.59 = (bf16[1,192,1152]{2,1,0:T(8,128)(2,1)}, bf16[1,192,1152]{2,1,0:T(8,128)(2,1)}, u32[]{:S(2)}, u32[]{:S(2)}) collective-permute-start(bf16[1,192,1152]{2,1,0:T(8,128)(2,1)} %constant_dynamic-slice_fusion.1), channel_id=1, source_target_pairs={{0,4},{4,0},{1,5},{5,1},{2,6},{6,2},{3,7},{7,3},{8,12},{12,8},{9,1... | collective-permute-start | bytes 1327112 | tf_op jit(solution)/shard_map/ppermute | solution.py:691
  480.6 20.3 %collective-permute-start.63 = (bf16[1,192,1152]{2,1,0:T(8,128)(2,1)}, bf16[1,192,1152]{2,1,0:T(8,128)(2,1)}, u32[]{:S(2)}, u32[]{:S(2)}) collective-permute-start(bf16[1,192,1152]{2,1,0:T(8,128)(2,1)} %get-tuple-element.320), channel_id=1, source_target_pairs={{2,0},{8,10},{10,2},{0,8},{3,1},{9,11},{11,3},{1,9},{6,4},{12,14},... | collective-permute-start | bytes 1327112 | tf_op jit(solution)/shard_map/ppermute | solution.py:834
  480.6 20.3 %collective-permute-start.64 = (bf16[1,192,1152]{2,1,0:T(8,128)(2,1)}, bf16[1,192,1152]{2,1,0:T(8,128)(2,1)}, u32[]{:S(2)}, u32[]{:S(2)}) collective-permute-start(bf16[1,192,1152]{2,1,0:T(8,128)(2,1)} %get-tuple-element.321), channel_id=1, source_target_pairs={{2,8},{8,2},{3,9},{9,3},{6,12},{12,6},{7,13},{13,7},{18,24},{24,18... | collective-permute-start | bytes 1327112 | tf_op jit(solution)/shard_map/ppermute | solution.py:835
  502.4 13.1 %collective-permute-start.65 = (f32[7460]{0:T(1024)S(1)}, f32[7460]{0:T(1024)S(1)}, u32[]{:S(2)}, u32[]{:S(2)}) collective-permute-start(f32[7460]{0:T(1024)S(1)} %add.420), channel_id=1, source_target_pairs={{0,2},{2,0},{1,3},{3,1},{4,6},{6,4},{5,7},{7,5},{8,10},{10,8},{9,1... | collective-permute-start | bytes 89528 | tf_op jit(solution)/shard_map/ppermute | solution.py:691
  508.6 15.8 %collective-permute-start.68 = (f32[192,256]{1,0:T(8,128)S(1)}, f32[192,256]{1,0:T(8,128)S(1)}, u32[]{:S(2)}, u32[]{:S(2)}) collective-permute-start(f32[192,256]{1,0:T(8,128)S(1)} %slice.418), channel_id=1, source_target_pairs={{0,1},{1,0},{2,3},{3,2},{4,5},{5,4},{6,7},{7,6},{8,9},{9,8},{10,11... | collective-permute-start | bytes 589832 | tf_op jit(solution)/shard_map/ppermute | solution.py:691
  511.5 16.2 %collective-permute-start.69 = (f32[192,256]{1,0:T(8,128)S(1)}, f32[192,256]{1,0:T(8,128)S(1)}, u32[]{:S(2)}, u32[]{:S(2)}) collective-permute-start(f32[192,256]{1,0:T(8,128)S(1)} %slice.418), channel_id=1, source_target_pairs={{0,2},{2,0},{1,3},{3,1},{4,6},{6,4},{5,7},{7,5},{8,10},{10,8},{9,1... | collective-permute-start | bytes 589832 | tf_op jit(solution)/shard_map/ppermute | solution.py:691
  511.5 16.2 %collective-permute-start.70 = (f32[192,256]{1,0:T(8,128)S(1)}, f32[192,256]{1,0:T(8,128)S(1)}, u32[]{:S(2)}, u32[]{:S(2)}) collective-permute-start(f32[192,256]{1,0:T(8,128)S(1)} %slice.418), channel_id=1, source_target_pairs={{0,3},{3,0},{1,2},{2,1},{4,7},{7,4},{5,6},{6,5},{8,11},{11,8},{9,1... | collective-permute-start | bytes 589832 | tf_op jit(solution)/shard_map/ppermute | solution.py:1198
  (92 other events, 787.0 us)

commit v6 on v3

--- a/solution.py
+++ b/solution.py
@@ -199,7 +199,7 @@
         gained = gated * rows_ref[1:2, cols]
         mixed_ref[0, :, cols] = gained.astype(BF16)
         squares = squares + gated * gated
-        crossed = crossed + gained * gm_ref[0, :, cols]
+        crossed = crossed + gained * gm_ref[0, :, cols].astype(F32)
     ones = jnp.ones((8, STRIP), BF16)
     square_row = sum(dot_nt(ones, term) for term in pieces(squares, 3))
     cross_row = sum(dot_nt(ones, term) for term in pieces(crossed, 3))
@@ -236,7 +236,7 @@
         silu = gate * sigmoid
         gated = y * silu
         scaled = gated * scale
-        gm = gm_ref[0, :, cols]
+        gm = gm_ref[0, :, cols].astype(F32)
         gain = rows_ref[1:2, cols]
         gg = scale * gm * gain - gated * bent
         gy = (gg * silu).astype(BF16)
@@ -1016,7 +1016,7 @@
     cot = [whole_cot(0, gate[-1])]
 
     w_down_held = hold(w_down, found[0][1])
-    gm = [matmul(cot[0], w_down_held, ((2,), (0,)))]
+    gm = [matmul(cot[0], w_down_held, ((2,), (0,)), BF16)]
     mixes, stats, branches, gates = [], [], [], []
     g_gate = g_down = 0.0
     tokens = ((0, 1), (0, 1))
@@ -1031,10 +1031,10 @@
             following = hold(packed[part + 1], found[part][1])
             found.append(hop(part + 1, following, local[part + 1][3], 1, y))
             cot.append(whole_cot(part + 1, found[-1][1]))
-            gm.append(matmul(cot[-1], w_down, ((2,), (0,))))
+            gm.append(matmul(cot[-1], w_down, ((2,), (0,)), BF16))
             other = hold(other, cot[-1])
         else:
-            g_gate = matmul(normed[0], hold(gates[0][1], y), tokens)
+            g_gate = matmul(normed[0], hold(gates[0][1], y), tokens, BF16)
             other = hold(other, g_gate)
         stat = stat + jnp.flip(other, 0)
         other = swap(stat, "zq")
@@ -1051,7 +1051,7 @@
 
     found = [hop(0, back_packed[0], gates[0][3], -1, back_packed[-1])]
     for part in parts:
-        g_down = g_down + matmul(cot[part], hold(gates[part][2], found[0][1]), tokens)
+        g_down = (g_down + matmul(cot[part], hold(gates[part][2], found[0][1]), tokens)).astype(BF16)
         if part == 0:
             branch_cut = [
                 cut(added(branch[0], hold(got, g_down)), "zq", 0) for branch, got in branches
@@ -1061,7 +1061,7 @@
         else:
             g_gate = g_gate + matmul(normed[part], hold(gates[part][1], g_down), tokens)
     g_gate, g_down = g_gate.astype(BF16), g_down.astype(BF16)
-    g_normed_gate = [matmul(hold(gates[0][1], g_gate), w_gate, ((2,), (1,)))]
+    g_normed_gate = [matmul(hold(gates[0][1], g_gate), w_gate, ((2,), (1,)), BF16)]
     gin = entering(found[0], -1, g_normed_gate[0])
     for part in parts[1:]:
         following = hold(back_packed[part], found[part - 1][1])
@@ -1133,7 +1133,7 @@
         gmix = lax.dynamic_update_slice_in_dim(gmix, last.astype(BF16), length - RIM, 1)
 
         def for_weights(gmix):
-            return g_first + matmul(normed[part], gmix, tokens)
+            return (g_first + matmul(normed[part], gmix, tokens)).astype(BF16)
 
         def for_tokens(gmix):
             total = g_normed_gate[part] + matmul(gmix, w_first, ((2,), (1,)))
@@ -1149,7 +1149,7 @@
                 moved_first = swap(first[2], "x"), swap(first[3], "y")
         else:
             g_normed_gate.append(
-                matmul(hold(gates[part + 1][1], g_first), w_gate, ((2,), (1,)))
+                matmul(hold(gates[part + 1][1], g_first), w_gate, ((2,), (1,)), BF16)
             )
             kept, sent = cut(added(total[0], hold(other, g_first)), "zq", 0)
             norm_cut = kept, swap(sent, "zq")

time: 536 us -> 525 us (0.979)
  matrix products: 102 us -> 90.8 us
    dot_general x18, matrix products: 102 us -> 90.8 us  [matmul(): lax.dot_general(left, right, (contract, ((), ())), preferred_element_type...]
  transfers between devices with their start and end apart: 73 -> 73, of which waited for: 21 -> 22; matrix products, arithmetic and copies ran while one was open for 30% -> 28% of each run, Pallas kernels for 25% -> 25%
where the time goes in v6:
time: 525 us; the launch traced here: 516 us
  Pallas kernels  131 us (25%)
  waiting for transfers between devices  116 us (22%)
  starting transfers between devices  93.4 us (18%)
  matrix products  90.8 us (17%)
  other arithmetic  47.5 us (9%)
  local copies, waits for them, and re-layouts  33.6 us (6%)
    pallas_call x8, Pallas kernels, run(): pl.pallas_call(body, grid=grid, in_specs=[spec for _, spec in ins] + [pl....  105 us
    ppermute x48, waiting for transfers between devices, swap(): return lax.ppermute(value, axis, [(0, 1), (1, 0)])  101 us
    dot_general x18, matrix products, matmul(): lax.dot_general(left, right, (contract, ((), ())), preferred_element_type...  90.8 us
    ppermute x48, starting transfers between devices, swap(): return lax.ppermute(value, axis, [(0, 1), (1, 0)])  55.2 us
    pallas_call x4, Pallas kernels, joined(): pl.pallas_call(join_kernel, grid_spec=pltpu.PrefetchScalarGridSpec(num_sc...  13 us
    convert_element_type x8, other arithmetic, added(): return (kept.astype(F32) + got.astype(F32)).astype(dtype)  12.2 us
    pallas_call x2, Pallas kernels, place(): pl.pallas_call(place_kernel, grid_spec=pltpu.PrefetchScalarGridSpec(num_s...  11.5 us
  transfers between devices with their start and end apart: 73, of which 22 were waited for; matrix products, arithmetic and copies ran while one was open for 28% of the time, Pallas kernels for 25%

profile of v6, /device:TPU:0, one launch (start us, length us, event | category | flops | bytes accessed | tf_op | source)
XLA Modules:
  0.0 515.6 jit_solution(10660439716322819348)
XLA Ops:
  2.6 4.1 collective-permute-start.3
  21.5 18.8 %collective-permute-done.got = bf16[1,256,1536]{2,1,0:T(8,128)(2,1)} collective-permute-done((bf16[1,256,1536]{2,1,0:T(8,128)(2,1)S(1)}, bf16[1,256,1536]{2,1,0:T(8,128)(2,1)}, u32[]{:S(2)}, u32[]{:S(2)}) %collective-permute-start) | collective-permute-done | bytes 786464 | tf_op jit(solution)/shard_map/ppermute | solution.py:691
  49.2 16.9 %collective-permute-done.18.got = bf16[1,256,1536]{2,1,0:T(8,128)(2,1)} collective-permute-done((bf16[1,256,1536]{2,1,0:T(8,128)(2,1)S(1)}, bf16[1,256,1536]{2,1,0:T(8,128)(2,1)}, u32[]{:S(2)}, u32[]{:S(2)}) %collective-permute-start.18) | collective-permute-done | bytes 786464 | tf_op jit(solution)/shard_map/ppermute | solution.py:691
  71.4 3.8 shard_map.279
  75.7 7.1 %shard_map.280 = bf16[2,2,2,192,1152]{4,3,2,1,0:T(8,128)(2,1)} custom-call(s32[3]{0:T(128)S(1)} %pad_add_fusion.at_ref, bf16[2,192,1152]{2,1,0:T(8,128)(2,1)S(1)} %pad_maximum_fusion.7.first, bf16[2,192,1152]{2,1,0:T(8,128)(2,1)} %collective-permute-done.7.first_y, bf16[2,192,1152]{2,1,0:T(8,128)(2,1)S(1)} %pad_maximum_fusion.8.second, ...), custom_call_target="tpu_custom_call" | custom-call | bytes 221184 | tf_op jit(solution)/shard_map/pallas_call | solution.py:637
  87.4 6.5 %convolution_convert_fusion.5.refs_0_.refs_2_.refs_9_.refs_10_.refs_12_ = bf16[2,512,1152]{2,1,0:T(8,128)(2,1)S(1)} fusion(bf16[2,512,1536]{2,1,0:T(8,128)(2,1)S(1)} %copy-done.37, bf16[1536,1152,1]{1,0,2:T(8,128)(2,1)} %bitcast.277), kind=kOutput, calls=%fused_computation.17 | convolution fusion | flops 3625058304 | bytes 9043968 | tf_op jit(solution)/shard_map/dot_general | solution.py:889
  94.1 2.7 collective-permute-start.9
  96.8 3.3 collective-permute-done.14
  102.8 2.5 collective-permute-start.16
  105.4 3.4 shard_map.282
  108.8 7.2 %convolution_convert_fusion.4.refs_0_.refs_2_.refs_9_.refs_10_.refs_12_ = bf16[2,512,1152]{2,1,0:T(8,128)(2,1)S(1)} fusion(bf16[2,512,1536]{2,1,0:T(8,128)(2,1)} %shard_map.282, bf16[1536,1152,1]{1,0,2:T(8,128)(2,1)} %bitcast.278), kind=kOutput, calls=%fused_computation.16 | convolution fusion | flops 3625058304 | bytes 9043968 | tf_op jit(solution)/shard_map/dot_general | solution.py:889
  117.3 8.9 %shard_map.281 = (bf16[2,512,1024]{2,1,0:T(8,128)(2,1)S(1)}, f32[2,512,128]{2,1,0:T(8,128)S(1)}, f32[2,512,128]{2,1,0:T(8,128)S(1)}, f32[2,128,768]{2,1,0:T(8,12...) custom-call(bf16[2,512,1152]{2,1,0:T(8,128)(2,1)} %copy-done.70, ...), custom_call_target="tpu_custom_call" | custom-call | flops 6000000000 | bytes 8000000 | tf_op jit(solution)/shard_map/pallas_call | solution.py:419
  126.3 5.1 collective-permute-start.11
  133.1 8.9 %shard_map.283 = (bf16[2,512,1024]{2,1,0:T(8,128)(2,1)S(1)}, f32[2,512,128]{2,1,0:T(8,128)S(1)}, f32[2,512,128]{2,1,0:T(8,128)S(1)}, f32[2,128,768]{2,1,0:T(8,12...) custom-call(bf16[2,512,1152]{2,1,0:T(8,128)(2,1)} %copy-done.69, ...), custom_call_target="tpu_custom_call" | custom-call | flops 6000000000 | bytes 8000000 | tf_op jit(solution)/shard_map/pallas_call | solution.py:419
  144.8 4.4 shard_map.284
  149.7 6.5 %convolution_convert_fusion.7.refs_6_.refs_2_ = bf16[2,512,768]{2,1,0:T(8,128)(2,1)} fusion(bf16[2,512,1536]{2,1,0:T(8,128)(2,1)} %shard_map.279, bf16[1536,1536]{1,0:T(8,128)(2,1)} %bitcast.261), kind=kOutput, calls=%fused_computation.42 | convolution fusion | flops 2416705536 | bytes 7077888 | tf_op jit(solution)/shard_map/dot_general | solution.py:889
  156.2 2.4 collective-permute-done.23.got
  158.9 3.5 slice.387
  163.9 5.3 %convolution_convert_fusion.6.refs_6_.refs_2_ = bf16[2,512,768]{2,1,0:T(8,128)(2,1)} fusion(bf16[2,512,1536]{2,1,0:T(8,128)(2,1)S(1)} %copy-done.34, bf16[1536,1536]{1,0:T(8,128)(2,1)} %bitcast.263), kind=kOutput, calls=%fused_computation.41 | convolution fusion | flops 2416705536 | bytes 7077888 | tf_op jit(solution)/shard_map/dot_general | solution.py:889
  169.2 4.5 collective-permute-done.28.got
  176.3 3.7 shard_map.286
  180.0 5.8 %fusion.15.refs_7_.refs_10_.refs_3_ = bf16[2,512,768]{2,1,0:T(8,128)(2,1)} fusion(bf16[2,512,1536]{2,1,0:T(8,128)(2,1)} %shard_map.286, bf16[1536,768]{1,0:T(8,128)(2,1)S(1)} %copy-done.46), kind=kOutput, calls=%fused_computation.39 | convolution fusion | flops 2416705536 | bytes 7077888 | tf_op jit(solution)/shard_map/dot_general | solution.py:889
  185.8 10.2 %shard_map.287 = (f32[2,512,768]{2,1,0:T(8,128)}, bf16[2,512,768]{2,1,0:T(8,128)(2,1)S(1)}, bf16[2,2,128,768]{3,2,1,0:T(8,128)(2,1)S(1)}, f32[2,8,512]{2,1,0:T(8,128)S(1)}) custom-call(bf16[2,512,1024]{2,1,0:T(8,128)(2,1)} %copy-done.7, f32[2,512,128]{2,1,0:T(8,128)S(1)} %copy-done.13, f32[2,512,128]{2,1,0:T(8,128)S(1)} %copy-done.17, ...), custom_call_target="tpu_custom_call" | custom-call | flops 10000000000 | bytes 16000000 | tf_op jit(solution)/shard_map/pallas_call | solution.py:419
  202.0 6.4 %fusion.18.refs_7_.refs_11_.refs_3_ = bf16[2,512,768]{2,1,0:T(8,128)(2,1)} fusion(bf16[2,512,1536]{2,1,0:T(8,128)(2,1)} %shard_map.289, bf16[1536,1536]{1,0:T(8,128)(2,1)} %bitcast.264), kind=kOutput, calls=%fused_computation.40 | convolution fusion | flops 2416705536 | bytes 7077888 | tf_op jit(solution)/shard_map/dot_general | solution.py:889
  208.4 2.5 collective-permute-start.31
  210.9 4.5 convolution_convert_fusion.3.refs_9_
  217.7 8.0 %shard_map.290 = (bf16[2,512,768]{2,1,0:T(8,128)(2,1)S(1)}, bf16[2,512,768]{2,1,0:T(8,128)(2,1)S(1)}, bf16[2,512,768]{2,1,0:T(8,128)(2,1)}, f32[2,128,768]{2,1,0...) custom-call(f32[2,512,768]{2,1,0:T(8,128)} %get-tuple-element.181.refs_0_.refs_4_, ...), custom_call_target="tpu_custom_call" | custom-call | flops 6000000000 | bytes 18000000 | tf_op jit(solution)/shard_map/pallas_call | solution.py:419
  228.2 10.3 %shard_map.291 = (f32[2,512,768]{2,1,0:T(8,128)}, bf16[2,512,768]{2,1,0:T(8,128)(2,1)S(1)}, bf16[2,2,128,768]{3,2,1,0:T(8,128)(2,1)S(1)}, f32[2,8,512]{2,1,0:T(8,128)S(1)}) custom-call(bf16[2,512,1024]{2,1,0:T(8,128)(2,1)} %copy-done.6, f32[2,512,128]{2,1,0:T(8,128)S(1)} %copy-done.11, f32[2,512,128]{2,1,0:T(8,128)S(1)} %copy-done.15, ...), custom_call_target="tpu_custom_call" | custom-call | flops 10000000000 | bytes 16000000 | tf_op jit(solution)/shard_map/pallas_call | solution.py:419
  238.6 4.0 bitcast_convert_fusion.1
  242.7 2.9 convolution_convert_fusion.2.refs_9_
  247.4 4.0 collective-permute-done.37
  251.4 7.9 %shard_map.292 = (bf16[2,512,768]{2,1,0:T(8,128)(2,1)S(1)}, bf16[2,512,768]{2,1,0:T(8,128)(2,1)S(1)}, bf16[2,512,768]{2,1,0:T(8,128)(2,1)}, f32[2,128,768]{2,1,0...) custom-call(f32[2,512,768]{2,1,0:T(8,128)} %get-tuple-element.197.refs_0_.refs_4_, ...), custom_call_target="tpu_custom_call" | custom-call | flops 6000000000 | bytes 18000000 | tf_op jit(solution)/shard_map/pallas_call | solution.py:419
  263.5 5.2 %bitcast_convert_fusion = bf16[1536,768]{1,0:T(8,128)(2,1)S(1)} fusion(bf16[2,512,1536]{2,1,0:T(8,128)(2,1)} %shard_map.286, bf16[2,512,768]{2,1,0:T(8,128)(2,1)} %get-tuple-element.207), kind=kOutput, calls=%fused_computation.10 | convolution fusion | flops 2417098752 | bytes 7077888 | tf_op jit(solution)/shard_map/dot_general | solution.py:889
  268.8 2.9 fusion.2
  271.8 3.0 fusion.1
  274.8 4.1 convolution_convert_fusion.1
  280.1 3.3 collective-permute-start.46
  287.8 2.4 fusion.6
  294.9 25.3 %shard_map.295 = (bf16[2,512,1152]{2,1,0:T(8,128)(2,1)}, f32[2,8,1024]{2,1,0:T(8,128)S(1)}, f32[8,1024]{1,0:T(8,128)S(1)}, f32[8,128]{1,0:T(8,128)S(1)}, f32[8,768]{1,0:T(8,128)S(1)}) custom-call(bf16[2,512,1024]{2,1,0:T(8,128)(2,1)} %copy-done.7, f32[2,512,128]{2,1,0:T(8,128)S(1)} %copy-done.13, f32[2,512,128]{2,1,0:T(8,128)S(1)} %copy-done.17, ...), custom_call_target="tpu_custom_call" | custom-call | flops 32000000000 | bytes 24000000 | tf_op jit(solution)/shard_map/pallas_call | solution.py:419
  320.3 10.4 %collective-permute-done.39 = bf16[2,256,1536]{2,1,0:T(8,128)(2,1)} collective-permute-done((bf16[2,256,1536]{2,1,0:T(8,128)(2,1)}, bf16[2,256,1536]{2,1,0:T(8,128)(2,1)}, u32[]{:S(2)}, u32[]{:S(2)}) %collective-permute-start.39) | collective-permute-done | bytes 1572896 | tf_op jit(solution)/shard_map/ppermute | solution.py:691
  330.7 3.0 fusion.39
  337.1 5.3 %collective-permute-start.50 = (bf16[2,192,768]{2,1,0:T(8,128)(2,1)S(1)}, bf16[2,192,768]{2,1,0:T(8,128)(2,1)S(1)}, u32[]{:S(2)}, u32[]{:S(2)}) collective-permute-start(bf16[2,192,768]{2,1,0:T(8,128)(2,1)S(1)} %pad_maximum_fusion.10), channel_id=1, source_target_pairs={{0,4},{4,0},{1,5},{5,1},{2,6},{6,2},{3,7},{7,3},{8,12},{12,8},{9,1... | collective-permute-start | bytes 1769480 | tf_op jit(solution)/shard_map/ppermute | solution.py:691
  343.1 6.1 %add_convert_fusion.2 = bf16[2,512,1536]{2,1,0:T(8,128)(2,1)S(1)} fusion(bf16[2,512,1536]{2,1,0:T(8,128)(2,1)} %convolution_convert_fusion.1, bf16[2,512,1152]{2,1,0:T(8,128)(2,1)S(1)} %fusion.51, bf16[1536,1152,1]{1,0,2:T(8,128)(2,1)S(1)} %bitcast.279), kind=kOutput, calls=%fused_computation.5 | convolution fusion | flops 3628597248 | bytes 12189696 | tf_op jit(solution)/shard_map/dot_general | solution.py:889
  349.4 5.8 %fusion = bf16[1536,1152]{1,0:T(8,128)(2,1)} fusion(bf16[2,512,1536]{2,1,0:T(8,128)(2,1)S(1)} %copy-done.39, bf16[2,512,1152]{2,1,0:T(8,128)(2,1)S(1)} %fusion.51), kind=kOutput, calls=%fused_computation.2 | convolution fusion | flops 3625648128 | bytes 9043968 | tf_op jit(solution)/shard_map/dot_general | solution.py:889
  355.2 4.1 convolution_convert_fusion
  366.9 25.3 %shard_map.296 = (bf16[2,512,1152]{2,1,0:T(8,128)(2,1)}, f32[2,8,1024]{2,1,0:T(8,128)S(1)}, f32[8,1024]{1,0:T(8,128)S(1)}, f32[8,128]{1,0:T(8,128)S(1)}, f32[8,768]{1,0:T(8,128)S(1)}) custom-call(bf16[2,512,1024]{2,1,0:T(8,128)(2,1)} %copy-done.6, f32[2,512,128]{2,1,0:T(8,128)S(1)} %copy-done.11, f32[2,512,128]{2,1,0:T(8,128)S(1)} %copy-done.15, ...), custom_call_target="tpu_custom_call" | custom-call | flops 32000000000 | bytes 24000000 | tf_op jit(solution)/shard_map/pallas_call | solution.py:419
  395.3 2.3 fusion.36
  397.7 3.3 fusion.22
  400.9 5.6 %collective-permute-done.54 = f32[2,8,1024]{2,1,0:T(8,128)S(1)} collective-permute-done((f32[2,8,1024]{2,1,0:T(8,128)S(1)}, f32[2,8,1024]{2,1,0:T(8,128)S(1)}, u32[]{:S(2)}, u32[]{:S(2)}) %collective-permute-start.54) | collective-permute-done | bytes 65568 | tf_op jit(solution)/shard_map/ppermute | solution.py:720
  406.7 6.1 %add_convert_fusion.1 = bf16[2,512,1536]{2,1,0:T(8,128)(2,1)S(1)} fusion(bf16[2,512,1536]{2,1,0:T(8,128)(2,1)} %convolution_convert_fusion, bf16[2,512,1152]{2,1,0:T(8,128)(2,1)S(1)} %fusion.52, bf16[1536,1152,1]{1,0,2:T(8,128)(2,1)S(1)} %bitcast.280), kind=kOutput, calls=%fused_computation.4 | convolution fusion | flops 3628597248 | bytes 12189696 | tf_op jit(solution)/shard_map/dot_general | solution.py:889
  414.0 2.3 copy-done.36
  416.4 4.6 add_convert_fusion
  422.1 3.6 collective-permute-start.58
  427.8 2.4 fusion.3
  432.8 12.5 %collective-permute-done.58 = bf16[1,2,192,1152]{3,2,1,0:T(8,128)(2,1)} collective-permute-done((bf16[1,2,192,1152]{3,2,1,0:T(8,128)(2,1)}, bf16[1,2,192,1152]{3,2,1,0:T(8,128)(2,1)}, u32[]{:S(2)}, u32[]{:S(2)}) %collective-permute-start.58) | collective-permute-done | bytes 884768 | tf_op jit(solution)/shard_map/ppermute | solution.py:691
  445.3 2.5 collective-permute-done.57
  453.8 8.0 %collective-permute-done.60 = bf16[1,192,1152]{2,1,0:T(8,128)(2,1)} collective-permute-done((bf16[1,192,1152]{2,1,0:T(8,128)(2,1)}, bf16[1,192,1152]{2,1,0:T(8,128)(2,1)}, u32[]{:S(2)}, u32[]{:S(2)}) %collective-permute-start.60) | collective-permute-done | bytes 442400 | tf_op jit(solution)/shard_map/ppermute | solution.py:691
  464.0 2.6 broadcast_select_fusion.2
  470.2 3.6 collective-permute-done.61
  477.8 7.8 %collective-permute-done.63 = bf16[1,192,1152]{2,1,0:T(8,128)(2,1)} collective-permute-done((bf16[1,192,1152]{2,1,0:T(8,128)(2,1)}, bf16[1,192,1152]{2,1,0:T(8,128)(2,1)}, u32[]{:S(2)}, u32[]{:S(2)}) %collective-permute-start.63) | collective-permute-done | bytes 442400 | tf_op jit(solution)/shard_map/ppermute | solution.py:834
  487.1 4.3 collective-permute-start.65
  493.3 3.8 collective-permute-start.68
  497.2 2.4 collective-permute-start.70
  506.0 6.5 %collective-permute-done.67 = f32[2816]{0:T(1024)S(1)} collective-permute-done((f32[2816]{0:T(1024)S(1)}, f32[2816]{0:T(1024)S(1)}, u32[]{:S(2)}, u32[]{:S(2)}) %collective-permute-start.67) | collective-permute-done | bytes 11296 | tf_op jit(solution)/shard_map/ppermute | solution.py:691
  (436 shorter events, 126.0 us)
Async XLA Ops:
  2.6 13.2 %collective-permute-start.3 = (bf16[192,1152]{1,0:T(8,128)(2,1)S(1)}, bf16[192,1152]{1,0:T(8,128)(2,1)S(1)}, u32[]{:S(2)}, u32[]{:S(2)}) collective-permute-start(bf16[192,1152]{1,0:T(8,128)(2,1)S(1)} %concatenate.24), channel_id=1, source_target_pairs={{0,2},{10,8},{2,10},{8,0},{1,3},{11,9},{3,11},{9,1},{4,6},{14,12},... | collective-permute-start | bytes 1327112 | tf_op jit(solution)/shard_map/ppermute | solution.py:763
  6.7 9.1 %collective-permute-start.5 = (bf16[192,1152]{1,0:T(8,128)(2,1)S(1)}, bf16[192,1152]{1,0:T(8,128)(2,1)}, u32[]{:S(2)}, u32[]{:S(2)}) collective-permute-start(bf16[192,1152]{1,0:T(8,128)(2,1)S(1)} %concatenate.24), channel_id=1, source_target_pairs={{2,8},{8,2},{3,9},{9,3},{6,12},{12,6},{7,13},{13,7},{18,24},{24,18... | collective-permute-start | bytes 1327112 | tf_op jit(solution)/shard_map/ppermute | solution.py:763
  11.6 28.6 %collective-permute-start = (bf16[1,256,1536]{2,1,0:T(8,128)(2,1)S(1)}, bf16[1,256,1536]{2,1,0:T(8,128)(2,1)}, u32[]{:S(2)}, u32[]{:S(2)}) collective-permute-start(bf16[1,256,1536]{2,1,0:T(8,128)(2,1)S(1)} %get-tuple-element.330.own), channel_id=1, source_target_pairs={{0,1},{1,0},{2,3},{3,2},{4,5},{5,4},{6,7},{7,6},{8,9},{9,8},{10,11... | collective-permute-start | bytes 2359304 | tf_op jit(solution)/shard_map/ppermute | solution.py:691
  13.2 34.2 %collective-permute-start.1 = (bf16[1,256,1536]{2,1,0:T(8,128)(2,1)S(1)}, bf16[1,256,1536]{2,1,0:T(8,128)(2,1)}, u32[]{:S(2)}, u32[]{:S(2)}) collective-permute-start(bf16[1,256,1536]{2,1,0:T(8,128)(2,1)S(1)} %get-tuple-element.330.own), channel_id=1, source_target_pairs={{0,8},{8,0},{1,9},{9,1},{2,10},{10,2},{3,11},{11,3},{4,12},{12,4},... | collective-permute-start | bytes 2359304 | tf_op jit(solution)/shard_map/ppermute | solution.py:691
  15.9 24.4 %collective-permute-start.4 = (bf16[192,1152]{1,0:T(8,128)(2,1)S(1)}, bf16[192,1152]{1,0:T(8,128)(2,1)S(1)}, u32[]{:S(2)}, u32[]{:S(2)}) collective-permute-start(bf16[192,1152]{1,0:T(8,128)(2,1)S(1)} %get-tuple-element.351), channel_id=1, source_target_pairs={{0,16},{16,0},{1,17},{17,1},{2,18},{18,2},{3,19},{19,3},{4,20},{20... | collective-permute-start | bytes 1327112 | tf_op jit(solution)/shard_map/ppermute | solution.py:691
  17.4 22.8 %collective-permute-start.6 = (bf16[192,1152]{1,0:T(8,128)(2,1)S(1)}, bf16[192,1152]{1,0:T(8,128)(2,1)S(1)}, u32[]{:S(2)}, u32[]{:S(2)}) collective-permute-start(bf16[192,1152]{1,0:T(8,128)(2,1)S(1)} %get-tuple-element.350), channel_id=1, source_target_pairs={{0,4},{4,0},{1,5},{5,1},{2,6},{6,2},{3,7},{7,3},{8,12},{12,8},{9,1... | collective-permute-start | bytes 1327112 | tf_op jit(solution)/shard_map/ppermute | solution.py:691
  40.2 25.9 %collective-permute-start.18 = (bf16[1,256,1536]{2,1,0:T(8,128)(2,1)S(1)}, bf16[1,256,1536]{2,1,0:T(8,128)(2,1)}, u32[]{:S(2)}, u32[]{:S(2)}) collective-permute-start(bf16[1,256,1536]{2,1,0:T(8,128)(2,1)S(1)} %get-tuple-element.155.own), channel_id=1, source_target_pairs={{0,1},{1,0},{2,3},{3,2},{4,5},{5,4},{6,7},{7,6},{8,9},{9,8},{10,11... | collective-permute-start | bytes 2359304 | tf_op jit(solution)/shard_map/ppermute | solution.py:691
  42.4 32.8 %collective-permute-start.8 = (bf16[2,192,1152]{2,1,0:T(8,128)(2,1)S(1)}, bf16[2,192,1152]{2,1,0:T(8,128)(2,1)}, u32[]{:S(2)}, u32[]{:S(2)}) collective-permute-start(bf16[2,192,1152]{2,1,0:T(8,128)(2,1)S(1)} %pad_maximum_fusion.8.second), channel_id=1, source_target_pairs={{0,16},{16,0},{1,17},{17,1},{2,18},{18,2},{3,19},{19,3},{4,20},{20... | collective-permute-start | bytes 2654216 | tf_op jit(solution)/shard_map/ppermute | solution.py:691
  45.1 30.1 %collective-permute-start.7 = (bf16[2,192,1152]{2,1,0:T(8,128)(2,1)S(1)}, bf16[2,192,1152]{2,1,0:T(8,128)(2,1)}, u32[]{:S(2)}, u32[]{:S(2)}) collective-permute-start(bf16[2,192,1152]{2,1,0:T(8,128)(2,1)S(1)} %pad_maximum_fusion.7.first), channel_id=1, source_target_pairs={{0,4},{4,0},{1,5},{5,1},{2,6},{6,2},{3,7},{7,3},{8,12},{12,8},{9,1... | collective-permute-start | bytes 2654216 | tf_op jit(solution)/shard_map/ppermute | solution.py:691
  46.8 22.5 %collective-permute-start.2 = (bf16[1,256,1536]{2,1,0:T(8,128)(2,1)}, bf16[1,256,1536]{2,1,0:T(8,128)(2,1)}, u32[]{:S(2)}, u32[]{:S(2)}) collective-permute-start(bf16[1,256,1536]{2,1,0:T(8,128)(2,1)} %collective-permute-done.got), channel_id=1, source_target_pairs={{0,8},{8,0},{1,9},{9,1},{2,10},{10,2},{3,11},{11,3},{4,12},{12,4},... | collective-permute-start | bytes 2359304 | tf_op jit(solution)/shard_map/ppermute | solution.py:691
  47.4 35.5 %collective-permute-start.12 = (bf16[192,1536]{1,0:T(8,128)(2,1)}, bf16[192,1536]{1,0:T(8,128)(2,1)}, u32[]{:S(2)}, u32[]{:S(2)}) collective-permute-start(bf16[192,1536]{1,0:T(8,128)(2,1)} %pad_maximum_fusion.9), channel_id=1, source_target_pairs={{0,2},{10,8},{2,10},{8,0},{1,3},{11,9},{3,11},{9,1},{4,6},{14,12},... | collective-permute-start | bytes 1769480 | tf_op jit(solution)/shard_map/ppermute | solution.py:763
  66.1 16.7 %collective-permute-start.13 = (bf16[192,1536]{1,0:T(8,128)(2,1)}, bf16[192,1536]{1,0:T(8,128)(2,1)}, u32[]{:S(2)}, u32[]{:S(2)}) collective-permute-start(bf16[192,1536]{1,0:T(8,128)(2,1)} %pad_maximum_fusion.9), channel_id=1, source_target_pairs={{2,8},{8,2},{3,9},{9,3},{6,12},{12,6},{7,13},{13,7},{18,24},{24,18... | collective-permute-start | bytes 1769480 | tf_op jit(solution)/shard_map/ppermute | solution.py:763
  69.2 18.0 %collective-permute-start.10 = (f32[8,768]{1,0:T(8,128)S(1)}, f32[8,768]{1,0:T(8,128)S(1)}, u32[]{:S(2)}, u32[]{:S(2)}) collective-permute-start(f32[8,768]{1,0:T(8,128)S(1)} %maximum_maximum_fusion), channel_id=1, source_target_pairs={{0,2},{2,0},{1,3},{3,1},{4,6},{6,4},{5,7},{7,5},{8,10},{10,8},{9,1... | collective-permute-start | bytes 73736 | tf_op jit(solution)/shard_map/ppermute | solution.py:691
  75.2 30.2 %collective-permute-start.19 = (bf16[1,256,1536]{2,1,0:T(8,128)(2,1)S(1)}, bf16[1,256,1536]{2,1,0:T(8,128)(2,1)S(1)}, u32[]{:S(2)}, u32[]{:S(2)}) collective-permute-start(bf16[1,256,1536]{2,1,0:T(8,128)(2,1)S(1)} %get-tuple-element.155.own), channel_id=1, source_target_pairs={{0,8},{8,0},{1,9},{9,1},{2,10},{10,2},{3,11},{11,3},{4,12},{12,4},... | collective-permute-start | bytes 2359304 | tf_op jit(solution)/shard_map/ppermute | solution.py:691
  75.2 30.2 %collective-permute-start.20 = (bf16[1,256,1536]{2,1,0:T(8,128)(2,1)}, bf16[1,256,1536]{2,1,0:T(8,128)(2,1)S(1)}, u32[]{:S(2)}, u32[]{:S(2)}) collective-permute-start(bf16[1,256,1536]{2,1,0:T(8,128)(2,1)} %collective-permute-done.18.got), channel_id=1, source_target_pairs={{0,8},{8,0},{1,9},{9,1},{2,10},{10,2},{3,11},{11,3},{4,12},{12,4},... | collective-permute-start | bytes 2359304 | tf_op jit(solution)/shard_map/ppermute | solution.py:691
  84.2 16.0 %collective-permute-start.14 = (bf16[192,1536]{1,0:T(8,128)(2,1)S(1)}, bf16[192,1536]{1,0:T(8,128)(2,1)S(1)}, u32[]{:S(2)}, u32[]{:S(2)}) collective-permute-start(bf16[192,1536]{1,0:T(8,128)(2,1)S(1)} %get-tuple-element.349), channel_id=1, source_target_pairs={{0,16},{16,0},{1,17},{17,1},{2,18},{18,2},{3,19},{19,3},{4,20},{20... | collective-permute-start | bytes 1769480 | tf_op jit(solution)/shard_map/ppermute | solution.py:691
  85.7 16.3 %collective-permute-start.15 = (bf16[192,1536]{1,0:T(8,128)(2,1)S(1)}, bf16[192,1536]{1,0:T(8,128)(2,1)S(1)}, u32[]{:S(2)}, u32[]{:S(2)}) collective-permute-start(bf16[192,1536]{1,0:T(8,128)(2,1)S(1)} %get-tuple-element.348), channel_id=1, source_target_pairs={{0,4},{4,0},{1,5},{5,1},{2,6},{6,2},{3,7},{7,3},{8,12},{12,8},{9,1... | collective-permute-start | bytes 1769480 | tf_op jit(solution)/shard_map/ppermute | solution.py:691
  94.1 23.2 %collective-permute-start.9 = (bf16[2,16,1024]{2,1,0:T(8,128)(2,1)S(1)}, bf16[2,16,1024]{2,1,0:T(8,128)(2,1)S(1)}, u32[]{:S(2)}, u32[]{:S(2)}) collective-permute-start(bf16[2,16,1024]{2,1,0:T(8,128)(2,1)S(1)} %slice.379), channel_id=1, source_target_pairs={{0,2},{2,4},{4,6},{1,3},{3,5},{5,7},{8,10},{10,12},{12,14},{9,11},... | collective-permute-start | bytes 196616 | tf_op jit(solution)/shard_map/ppermute | solution.py:720
  102.1 40.7 %collective-permute-start.17 = (bf16[2,192,1536]{2,1,0:T(8,128)(2,1)S(1)}, bf16[2,192,1536]{2,1,0:T(8,128)(2,1)S(1)}, u32[]{:S(2)}, u32[]{:S(2)}) collective-permute-start(bf16[2,192,1536]{2,1,0:T(8,128)(2,1)S(1)} %pad_maximum_fusion.4.second), channel_id=1, source_target_pairs={{0,16},{16,0},{1,17},{17,1},{2,18},{18,2},{3,19},{19,3},{4,20},{20... | collective-permute-start | bytes 3538952 | tf_op jit(solution)/shard_map/ppermute | solution.py:691
  102.8 42.0 %collective-permute-start.16 = (bf16[2,192,1536]{2,1,0:T(8,128)(2,1)S(1)}, bf16[2,192,1536]{2,1,0:T(8,128)(2,1)S(1)}, u32[]{:S(2)}, u32[]{:S(2)}) collective-permute-start(bf16[2,192,1536]{2,1,0:T(8,128)(2,1)S(1)} %pad_maximum_fusion.3.first), channel_id=1, source_target_pairs={{0,4},{4,0},{1,5},{5,1},{2,6},{6,2},{3,7},{7,3},{8,12},{12,8},{9,1... | collective-permute-start | bytes 3538952 | tf_op jit(solution)/shard_map/ppermute | solution.py:691
  116.0 15.5 %collective-permute-start.21 = (bf16[2,16,1024]{2,1,0:T(8,128)(2,1)S(1)}, bf16[2,16,1024]{2,1,0:T(8,128)(2,1)S(1)}, u32[]{:S(2)}, u32[]{:S(2)}) collective-permute-start(bf16[2,16,1024]{2,1,0:T(8,128)(2,1)S(1)} %slice.385), channel_id=1, source_target_pairs={{0,2},{2,4},{4,6},{1,3},{3,5},{5,7},{8,10},{10,12},{12,14},{9,11},... | collective-permute-start | bytes 196616 | tf_op jit(solution)/shard_map/ppermute | solution.py:720
  126.3 22.9 %collective-permute-start.11 = (bf16[2,144,768]{2,1,0:T(8,128)(2,1)S(1)}, bf16[2,144,768]{2,1,0:T(8,128)(2,1)S(1)}, u32[]{:S(2)}, u32[]{:S(2)}) collective-permute-start(bf16[2,144,768]{2,1,0:T(8,128)(2,1)S(1)} %get-tuple-element.149.refs_6_), channel_id=1, source_target_pairs={{0,2},{1,3},{4,6},{5,7},{8,10},{9,11},{12,14},{13,15},{16,18},{17,... | collective-permute-start | bytes 1327112 | tf_op jit(solution)/shard_map/ppermute | solution.py:724
  131.4 42.4 %collective-permute-start.24 = (bf16[2,256,1536]{2,1,0:T(8,128)(2,1)}, bf16[2,256,1536]{2,1,0:T(8,128)(2,1)}, u32[]{:S(2)}, u32[]{:S(2)}) collective-permute-start(bf16[2,256,1536]{2,1,0:T(8,128)(2,1)} %param.17), channel_id=1, source_target_pairs={{0,8},{8,0},{1,9},{9,1},{2,10},{10,2},{3,11},{11,3},{4,12},{12,4},... | collective-permute-start | bytes 4718600 | tf_op jit(solution)/shard_map/ppermute | solution.py:691
  133.0 25.7 %collective-permute-start.23 = (bf16[1,256,1536]{2,1,0:T(8,128)(2,1)S(1)}, bf16[1,256,1536]{2,1,0:T(8,128)(2,1)}, u32[]{:S(2)}, u32[]{:S(2)}) collective-permute-start(bf16[1,256,1536]{2,1,0:T(8,128)(2,1)S(1)} %get-tuple-element.339.own), channel_id=1, source_target_pairs={{0,1},{1,0},{2,3},{3,2},{4,5},{5,4},{6,7},{7,6},{8,9},{9,8},{10,11... | collective-permute-start | bytes 2359304 | tf_op jit(solution)/shard_map/ppermute | solution.py:691
  142.8 31.0 %collective-permute-start.28 = (bf16[1,256,1536]{2,1,0:T(8,128)(2,1)S(1)}, bf16[1,256,1536]{2,1,0:T(8,128)(2,1)S(1)}, u32[]{:S(2)}, u32[]{:S(2)}) collective-permute-start(bf16[1,256,1536]{2,1,0:T(8,128)(2,1)S(1)} %get-tuple-element.338.own), channel_id=1, source_target_pairs={{0,1},{1,0},{2,3},{3,2},{4,5},{5,4},{6,7},{7,6},{8,9},{9,8},{10,11... | collective-permute-start | bytes 2359304 | tf_op jit(solution)/shard_map/ppermute | solution.py:691
  158.7 16.4 %collective-permute-start.25 = (bf16[1,256,1536]{2,1,0:T(8,128)(2,1)}, bf16[1,256,1536]{2,1,0:T(8,128)(2,1)}, u32[]{:S(2)}, u32[]{:S(2)}) collective-permute-start(bf16[1,256,1536]{2,1,0:T(8,128)(2,1)} %collective-permute-done.23.got), channel_id=1, source_target_pairs={{0,8},{8,0},{1,9},{9,1},{2,10},{10,2},{3,11},{11,3},{4,12},{12,4},... | collective-permute-start | bytes 2359304 | tf_op jit(solution)/shard_map/ppermute | solution.py:691
  162.4 23.4 %collective-permute-start.26 = (bf16[2,128,768]{2,1,0:T(8,128)(2,1)S(1)}, bf16[2,128,768]{2,1,0:T(8,128)(2,1)S(1)}, u32[]{:S(2)}, u32[]{:S(2)}) collective-permute-start(bf16[2,128,768]{2,1,0:T(8,128)(2,1)S(1)} %copy-done.3), channel_id=1, source_target_pairs={{2,6},{3,7},{10,14},{11,15},{18,22},{19,23},{26,30},{27,31}} | collective-permute-start | bytes 1179656 | tf_op jit(solution)/shard_map/ppermute | solution.py:730
  163.2 22.6 %collective-permute-start.22 = (bf16[2,128,768]{2,1,0:T(8,128)(2,1)S(1)}, bf16[2,128,768]{2,1,0:T(8,128)(2,1)S(1)}, u32[]{:S(2)}, u32[]{:S(2)}) collective-permute-start(bf16[2,128,768]{2,1,0:T(8,128)(2,1)S(1)} %copy-done.3), channel_id=1, source_target_pairs={{2,4},{3,5},{10,12},{11,13},{18,20},{19,21},{26,28},{27,29}} | collective-permute-start | bytes 1179656 | tf_op jit(solution)/shard_map/ppermute | solution.py:730
  173.8 24.3 %collective-permute-start.29 = (bf16[1,256,1536]{2,1,0:T(8,128)(2,1)S(1)}, bf16[1,256,1536]{2,1,0:T(8,128)(2,1)S(1)}, u32[]{:S(2)}, u32[]{:S(2)}) collective-permute-start(bf16[1,256,1536]{2,1,0:T(8,128)(2,1)S(1)} %collective-permute-done.28.got), channel_id=1, source_target_pairs={{0,8},{8,0},{1,9},{9,1},{2,10},{10,2},{3,11},{11,3},{4,12},{12,4},... | collective-permute-start | bytes 2359304 | tf_op jit(solution)/shard_map/ppermute | solution.py:691
  173.8 22.3 %collective-permute-start.30 = (bf16[2,144,768]{2,1,0:T(8,128)(2,1)S(1)}, bf16[2,144,768]{2,1,0:T(8,128)(2,1)S(1)}, u32[]{:S(2)}, u32[]{:S(2)}) collective-permute-start(bf16[2,144,768]{2,1,0:T(8,128)(2,1)S(1)} %copy-done.5), channel_id=1, source_target_pairs={{0,2},{1,3},{4,6},{5,7},{8,10},{9,11},{12,14},{13,15},{16,18},{17,... | collective-permute-start | bytes 1327112 | tf_op jit(solution)/shard_map/ppermute | solution.py:724
  196.4 31.7 %collective-permute-start.35 = (bf16[2,128,768]{2,1,0:T(8,128)(2,1)S(1)}, bf16[2,128,768]{2,1,0:T(8,128)(2,1)S(1)}, u32[]{:S(2)}, u32[]{:S(2)}) collective-permute-start(bf16[2,128,768]{2,1,0:T(8,128)(2,1)S(1)} %shard_map.288), channel_id=1, source_target_pairs={{2,6},{3,7},{10,14},{11,15},{18,22},{19,23},{26,30},{27,31}} | collective-permute-start | bytes 1179656 | tf_op jit(solution)/shard_map/ppermute | solution.py:730
  197.1 31.0 %collective-permute-start.34 = (bf16[2,128,768]{2,1,0:T(8,128)(2,1)S(1)}, bf16[2,128,768]{2,1,0:T(8,128)(2,1)S(1)}, u32[]{:S(2)}, u32[]{:S(2)}) collective-permute-start(bf16[2,128,768]{2,1,0:T(8,128)(2,1)S(1)} %shard_map.288), channel_id=1, source_target_pairs={{2,4},{3,5},{10,12},{11,13},{18,20},{19,21},{26,28},{27,29}} | collective-permute-start | bytes 1179656 | tf_op jit(solution)/shard_map/ppermute | solution.py:730
  199.2 9.1 %collective-permute-start.27 = (f32[2,8,512]{2,1,0:T(8,128)S(1)}, f32[2,8,512]{2,1,0:T(8,128)S(1)}, u32[]{:S(2)}, u32[]{:S(2)}) collective-permute-start(f32[2,8,512]{2,1,0:T(8,128)S(1)} %get-tuple-element.176), channel_id=1, source_target_pairs={{0,8},{8,0},{1,9},{9,1},{2,10},{10,2},{3,11},{11,3},{4,12},{12,4},... | collective-permute-start | bytes 98312 | tf_op jit(solution)/shard_map/ppermute | solution.py:691
  208.4 9.2 %collective-permute-start.31 = (f32[2,8,512]{2,1,0:T(8,128)S(1)}, f32[2,8,512]{2,1,0:T(8,128)S(1)}, u32[]{:S(2)}, u32[]{:S(2)}) collective-permute-start(f32[2,8,512]{2,1,0:T(8,128)S(1)} %reverse_add_fusion.1), channel_id=1, source_target_pairs={{0,1},{1,0},{2,3},{3,2},{4,5},{5,4},{6,7},{7,6},{8,9},{9,8},{10,11... | collective-permute-start | bytes 98312 | tf_op jit(solution)/shard_map/ppermute | solution.py:691
  216.9 69.5 %collective-permute-start.32 = (bf16[512,1536]{1,0:T(8,128)(2,1)}, bf16[512,1536]{1,0:T(8,128)(2,1)}, u32[]{:S(2)}, u32[]{:S(2)}) collective-permute-start(bf16[512,1536]{1,0:T(8,128)(2,1)} %slice_bitcast_fusion.7), channel_id=1, source_target_pairs={{0,8},{8,0},{1,9},{9,1},{2,10},{10,2},{3,11},{11,3},{4,12},{12,4},... | collective-permute-start | bytes 4718600 | tf_op jit(solution)/shard_map/ppermute | solution.py:691
  226.8 32.5 %collective-permute-start.33 = (bf16[2,144,768]{2,1,0:T(8,128)(2,1)S(1)}, bf16[2,144,768]{2,1,0:T(8,128)(2,1)S(1)}, u32[]{:S(2)}, u32[]{:S(2)}) collective-permute-start(bf16[2,144,768]{2,1,0:T(8,128)(2,1)S(1)} %get-tuple-element.191.refs_10_), channel_id=1, source_target_pairs={{2,0},{3,1},{6,4},{7,5},{10,8},{11,9},{14,12},{15,13},{18,16},{19,... | collective-permute-start | bytes 1327112 | tf_op jit(solution)/shard_map/ppermute | solution.py:724
  246.9 43.4 %collective-permute-start.38 = (bf16[512,1536]{1,0:T(8,128)(2,1)}, bf16[512,1536]{1,0:T(8,128)(2,1)}, u32[]{:S(2)}, u32[]{:S(2)}) collective-permute-start(bf16[512,1536]{1,0:T(8,128)(2,1)} %slice_bitcast_fusion.5), channel_id=1, source_target_pairs={{0,8},{8,0},{1,9},{9,1},{2,10},{10,2},{3,11},{11,3},{4,12},{12,4},... | collective-permute-start | bytes 4718600 | tf_op jit(solution)/shard_map/ppermute | solution.py:691
  259.8 19.1 %collective-permute-start.41 = (bf16[2,128,768]{2,1,0:T(8,128)(2,1)S(1)}, bf16[2,128,768]{2,1,0:T(8,128)(2,1)S(1)}, u32[]{:S(2)}, u32[]{:S(2)}) collective-permute-start(bf16[2,128,768]{2,1,0:T(8,128)(2,1)S(1)} %shard_map.293), channel_id=1, source_target_pairs={{4,0},{5,1},{12,8},{13,9},{20,16},{21,17},{28,24},{29,25}} | collective-permute-start | bytes 1179656 | tf_op jit(solution)/shard_map/ppermute | solution.py:730
  261.1 17.8 %collective-permute-start.40 = (bf16[2,128,768]{2,1,0:T(8,128)(2,1)S(1)}, bf16[2,128,768]{2,1,0:T(8,128)(2,1)S(1)}, u32[]{:S(2)}, u32[]{:S(2)}) collective-permute-start(bf16[2,128,768]{2,1,0:T(8,128)(2,1)S(1)} %shard_map.293), channel_id=1, source_target_pairs={{4,2},{5,3},{12,10},{13,11},{20,18},{21,19},{28,26},{29,27}} | collective-permute-start | bytes 1179656 | tf_op jit(solution)/shard_map/ppermute | solution.py:730
  261.8 23.4 %collective-permute-start.42 = (bf16[2,144,768]{2,1,0:T(8,128)(2,1)S(1)}, bf16[2,144,768]{2,1,0:T(8,128)(2,1)S(1)}, u32[]{:S(2)}, u32[]{:S(2)}) collective-permute-start(bf16[2,144,768]{2,1,0:T(8,128)(2,1)S(1)} %get-tuple-element.220), channel_id=1, source_target_pairs={{2,0},{3,1},{6,4},{7,5},{10,8},{11,9},{14,12},{15,13},{18,16},{19,... | collective-permute-start | bytes 1327112 | tf_op jit(solution)/shard_map/ppermute | solution.py:724
  280.1 40.1 %collective-permute-start.46 = (bf16[2,2,192,768]{3,2,1,0:T(8,128)(2,1)}, bf16[2,2,192,768]{3,2,1,0:T(8,128)(2,1)}, u32[]{:S(2)}, u32[]{:S(2)}) collective-permute-start(bf16[2,2,192,768]{3,2,1,0:T(8,128)(2,1)} %pad_maximum_fusion.6.refs_20_), channel_id=1, source_target_pairs={{0,4},{4,0},{1,5},{5,1},{2,6},{6,2},{3,7},{7,3},{8,12},{12,8},{9,1... | collective-permute-start | bytes 3538952 | tf_op jit(solution)/shard_map/ppermute | solution.py:691
  283.6 36.6 %collective-permute-start.45 = (bf16[2,2,192,768]{3,2,1,0:T(8,128)(2,1)S(1)}, bf16[2,2,192,768]{3,2,1,0:T(8,128)(2,1)}, u32[]{:S(2)}, u32[]{:S(2)}) collective-permute-start(bf16[2,2,192,768]{3,2,1,0:T(8,128)(2,1)S(1)} %pad_maximum_fusion.5.refs_19_), channel_id=1, source_target_pairs={{0,16},{16,0},{1,17},{17,1},{2,18},{18,2},{3,19},{19,3},{4,20},{20... | collective-permute-start | bytes 3538952 | tf_op jit(solution)/shard_map/ppermute | solution.py:691
  285.7 34.6 %collective-permute-start.43 = (bf16[2,128,768]{2,1,0:T(8,128)(2,1)S(1)}, bf16[2,128,768]{2,1,0:T(8,128)(2,1)S(1)}, u32[]{:S(2)}, u32[]{:S(2)}) collective-permute-start(bf16[2,128,768]{2,1,0:T(8,128)(2,1)S(1)} %shard_map.294.refs_17_), channel_id=1, source_target_pairs={{4,2},{5,3},{12,10},{13,11},{20,18},{21,19},{28,26},{29,27}} | collective-permute-start | bytes 1179656 | tf_op jit(solution)/shard_map/ppermute | solution.py:730
  286.4 33.9 %collective-permute-start.44 = (bf16[2,128,768]{2,1,0:T(8,128)(2,1)S(1)}, bf16[2,128,768]{2,1,0:T(8,128)(2,1)S(1)}, u32[]{:S(2)}, u32[]{:S(2)}) collective-permute-start(bf16[2,128,768]{2,1,0:T(8,128)(2,1)S(1)} %shard_map.294.refs_17_), channel_id=1, source_target_pairs={{4,0},{5,1},{12,8},{13,9},{20,16},{21,17},{28,24},{29,25}} | collective-permute-start | bytes 1179656 | tf_op jit(solution)/shard_map/ppermute | solution.py:730
  294.2 36.5 %collective-permute-start.39 = (bf16[2,256,1536]{2,1,0:T(8,128)(2,1)}, bf16[2,256,1536]{2,1,0:T(8,128)(2,1)}, u32[]{:S(2)}, u32[]{:S(2)}) collective-permute-start(bf16[2,256,1536]{2,1,0:T(8,128)(2,1)} %pad_maximum_fusion.1.refs_18_), channel_id=1, source_target_pairs={{0,1},{1,0},{2,3},{3,2},{4,5},{5,4},{6,7},{7,6},{8,9},{9,8},{10,11... | collective-permute-start | bytes 4718600 | tf_op jit(solution)/shard_map/ppermute | solution.py:691
  333.9 25.4 %collective-permute-start.51 = (bf16[2,192,768]{2,1,0:T(8,128)(2,1)S(1)}, bf16[2,192,768]{2,1,0:T(8,128)(2,1)S(1)}, u32[]{:S(2)}, u32[]{:S(2)}) collective-permute-start(bf16[2,192,768]{2,1,0:T(8,128)(2,1)S(1)} %pad_maximum_fusion.11), channel_id=1, source_target_pairs={{0,16},{16,0},{1,17},{17,1},{2,18},{18,2},{3,19},{19,3},{4,20},{20... | collective-permute-start | bytes 1769480 | tf_op jit(solution)/shard_map/ppermute | solution.py:691
  337.1 22.2 %collective-permute-start.50 = (bf16[2,192,768]{2,1,0:T(8,128)(2,1)S(1)}, bf16[2,192,768]{2,1,0:T(8,128)(2,1)S(1)}, u32[]{:S(2)}, u32[]{:S(2)}) collective-permute-start(bf16[2,192,768]{2,1,0:T(8,128)(2,1)S(1)} %pad_maximum_fusion.10), channel_id=1, source_target_pairs={{0,4},{4,0},{1,5},{5,1},{2,6},{6,2},{3,7},{7,3},{8,12},{12,8},{9,1... | collective-permute-start | bytes 1769480 | tf_op jit(solution)/shard_map/ppermute | solution.py:691
  349.3 11.9 %collective-permute-start.48 = (bf16[512,1536]{1,0:T(8,128)(2,1)S(1)}, bf16[512,1536]{1,0:T(8,128)(2,1)S(1)}, u32[]{:S(2)}, u32[]{:S(2)}) collective-permute-start(bf16[512,1536]{1,0:T(8,128)(2,1)S(1)} %slice_bitcast_fusion.3), channel_id=1, source_target_pairs={{0,8},{8,0},{1,9},{9,1},{2,10},{10,2},{3,11},{11,3},{4,12},{12,4},... | collective-permute-start | bytes 4718600 | tf_op jit(solution)/shard_map/ppermute | solution.py:691
  359.7 32.5 %collective-permute-start.52 = (bf16[2,192,768]{2,1,0:T(8,128)(2,1)S(1)}, bf16[2,192,768]{2,1,0:T(8,128)(2,1)S(1)}, u32[]{:S(2)}, u32[]{:S(2)}) collective-permute-start(bf16[2,192,768]{2,1,0:T(8,128)(2,1)S(1)} %get-tuple-element.343.refs_19_), channel_id=1, source_target_pairs={{2,0},{8,10},{10,2},{0,8},{3,1},{9,11},{11,3},{1,9},{6,4},{12,14},... | collective-permute-start | bytes 1769480 | tf_op jit(solution)/shard_map/ppermute | solution.py:834
  360.3 32.0 %collective-permute-start.53 = (bf16[2,192,768]{2,1,0:T(8,128)(2,1)S(1)}, bf16[2,192,768]{2,1,0:T(8,128)(2,1)S(1)}, u32[]{:S(2)}, u32[]{:S(2)}) collective-permute-start(bf16[2,192,768]{2,1,0:T(8,128)(2,1)S(1)} %get-tuple-element.342.refs_20_), channel_id=1, source_target_pairs={{2,8},{8,2},{3,9},{9,3},{6,12},{12,6},{7,13},{13,7},{18,24},{24,18... | collective-permute-start | bytes 1769480 | tf_op jit(solution)/shard_map/ppermute | solution.py:835
  361.7 33.6 %collective-permute-start.49 = (bf16[256,1536]{1,0:T(8,128)(2,1)S(1)}, bf16[256,1536]{1,0:T(8,128)(2,1)S(1)}, u32[]{:S(2)}, u32[]{:S(2)}) collective-permute-start(bf16[256,1536]{1,0:T(8,128)(2,1)S(1)} %constant_dynamic-slice_fusion.8.refs_17_), channel_id=1, source_target_pairs={{0,1},{1,0},{2,3},{3,2},{4,5},{5,4},{6,7},{7,6},{8,9},{9,8},{10,11... | collective-permute-start | bytes 2359304 | tf_op jit(solution)/shard_map/ppermute | solution.py:691
  393.5 13.1 %collective-permute-start.54 = (f32[2,8,1024]{2,1,0:T(8,128)S(1)}, f32[2,8,1024]{2,1,0:T(8,128)S(1)}, u32[]{:S(2)}, u32[]{:S(2)}) collective-permute-start(f32[2,8,1024]{2,1,0:T(8,128)S(1)} %get-tuple-element.249), channel_id=1, source_target_pairs={{2,0},{4,2},{6,4},{3,1},{5,3},{7,5},{10,8},{12,10},{14,12},{11,9},... | collective-permute-start | bytes 196616 | tf_op jit(solution)/shard_map/ppermute | solution.py:720
  414.0 13.7 %collective-permute-start.55 = (bf16[512,1536]{1,0:T(8,128)(2,1)}, bf16[512,1536]{1,0:T(8,128)(2,1)}, u32[]{:S(2)}, u32[]{:S(2)}) collective-permute-start(bf16[512,1536]{1,0:T(8,128)(2,1)} %slice_bitcast_fusion.1), channel_id=1, source_target_pairs={{0,8},{8,0},{1,9},{9,1},{2,10},{10,2},{3,11},{11,3},{4,12},{12,4},... | collective-permute-start | bytes 4718600 | tf_op jit(solution)/shard_map/ppermute | solution.py:691
  422.1 23.2 %collective-permute-start.58 = (bf16[1,2,192,1152]{3,2,1,0:T(8,128)(2,1)}, bf16[1,2,192,1152]{3,2,1,0:T(8,128)(2,1)}, u32[]{:S(2)}, u32[]{:S(2)}) collective-permute-start(bf16[1,2,192,1152]{3,2,1,0:T(8,128)(2,1)} %dynamic-slice_bitcast_fusion), channel_id=1, source_target_pairs={{0,4},{4,0},{1,5},{5,1},{2,6},{6,2},{3,7},{7,3},{8,12},{12,8},{9,1... | collective-permute-start | bytes 2654216 | tf_op jit(solution)/shard_map/ppermute | solution.py:691
  426.7 21.1 %collective-permute-start.57 = (bf16[1,2,192,1152]{3,2,1,0:T(8,128)(2,1)}, bf16[1,2,192,1152]{3,2,1,0:T(8,128)(2,1)}, u32[]{:S(2)}, u32[]{:S(2)}) collective-permute-start(bf16[1,2,192,1152]{3,2,1,0:T(8,128)(2,1)} %dynamic-slice_bitcast_fusion.1), channel_id=1, source_target_pairs={{0,16},{16,0},{1,17},{17,1},{2,18},{18,2},{3,19},{19,3},{4,20},{20... | collective-permute-start | bytes 2654216 | tf_op jit(solution)/shard_map/ppermute | solution.py:691
  431.2 22.6 %collective-permute-start.56 = (bf16[256,1536]{1,0:T(8,128)(2,1)}, bf16[256,1536]{1,0:T(8,128)(2,1)}, u32[]{:S(2)}, u32[]{:S(2)}) collective-permute-start(bf16[256,1536]{1,0:T(8,128)(2,1)} %constant_dynamic-slice_fusion.2), channel_id=1, source_target_pairs={{0,1},{1,0},{2,3},{3,2},{4,5},{5,4},{6,7},{7,6},{8,9},{9,8},{10,11... | collective-permute-start | bytes 2359304 | tf_op jit(solution)/shard_map/ppermute | solution.py:691
  450.6 11.2 %collective-permute-start.60 = (bf16[1,192,1152]{2,1,0:T(8,128)(2,1)}, bf16[1,192,1152]{2,1,0:T(8,128)(2,1)}, u32[]{:S(2)}, u32[]{:S(2)}) collective-permute-start(bf16[1,192,1152]{2,1,0:T(8,128)(2,1)} %constant_dynamic-slice_fusion), channel_id=1, source_target_pairs={{0,16},{16,0},{1,17},{17,1},{2,18},{18,2},{3,19},{19,3},{4,20},{20... | collective-permute-start | bytes 1327112 | tf_op jit(solution)/shard_map/ppermute | solution.py:691
  453.0 11.0 %collective-permute-start.59 = (bf16[1,192,1152]{2,1,0:T(8,128)(2,1)}, bf16[1,192,1152]{2,1,0:T(8,128)(2,1)}, u32[]{:S(2)}, u32[]{:S(2)}) collective-permute-start(bf16[1,192,1152]{2,1,0:T(8,128)(2,1)} %constant_dynamic-slice_fusion.1), channel_id=1, source_target_pairs={{0,4},{4,0},{1,5},{5,1},{2,6},{6,2},{3,7},{7,3},{8,12},{12,8},{9,1... | collective-permute-start | bytes 1327112 | tf_op jit(solution)/shard_map/ppermute | solution.py:691
  466.6 19.0 %collective-permute-start.63 = (bf16[1,192,1152]{2,1,0:T(8,128)(2,1)}, bf16[1,192,1152]{2,1,0:T(8,128)(2,1)}, u32[]{:S(2)}, u32[]{:S(2)}) collective-permute-start(bf16[1,192,1152]{2,1,0:T(8,128)(2,1)} %get-tuple-element.324), channel_id=1, source_target_pairs={{2,0},{8,10},{10,2},{0,8},{3,1},{9,11},{11,3},{1,9},{6,4},{12,14},... | collective-permute-start | bytes 1327112 | tf_op jit(solution)/shard_map/ppermute | solution.py:834
  466.6 19.0 %collective-permute-start.64 = (bf16[1,192,1152]{2,1,0:T(8,128)(2,1)}, bf16[1,192,1152]{2,1,0:T(8,128)(2,1)}, u32[]{:S(2)}, u32[]{:S(2)}) collective-permute-start(bf16[1,192,1152]{2,1,0:T(8,128)(2,1)} %get-tuple-element.325), channel_id=1, source_target_pairs={{2,8},{8,2},{3,9},{9,3},{6,12},{12,6},{7,13},{13,7},{18,24},{24,18... | collective-permute-start | bytes 1327112 | tf_op jit(solution)/shard_map/ppermute | solution.py:835
  487.1 14.1 %collective-permute-start.65 = (f32[7460]{0:T(1024)S(1)}, f32[7460]{0:T(1024)S(1)}, u32[]{:S(2)}, u32[]{:S(2)}) collective-permute-start(f32[7460]{0:T(1024)S(1)} %add.420), channel_id=1, source_target_pairs={{0,2},{2,0},{1,3},{3,1},{4,6},{6,4},{5,7},{7,5},{8,10},{10,8},{9,1... | collective-permute-start | bytes 89528 | tf_op jit(solution)/shard_map/ppermute | solution.py:691
  493.3 21.0 %collective-permute-start.68 = (f32[192,256]{1,0:T(8,128)S(1)}, f32[192,256]{1,0:T(8,128)S(1)}, u32[]{:S(2)}, u32[]{:S(2)}) collective-permute-start(f32[192,256]{1,0:T(8,128)S(1)} %slice.418), channel_id=1, source_target_pairs={{0,1},{1,0},{2,3},{3,2},{4,5},{5,4},{6,7},{7,6},{8,9},{9,8},{10,11... | collective-permute-start | bytes 589832 | tf_op jit(solution)/shard_map/ppermute | solution.py:691
  497.1 17.2 %collective-permute-start.69 = (f32[192,256]{1,0:T(8,128)S(1)}, f32[192,256]{1,0:T(8,128)S(1)}, u32[]{:S(2)}, u32[]{:S(2)}) collective-permute-start(f32[192,256]{1,0:T(8,128)S(1)} %slice.418), channel_id=1, source_target_pairs={{0,2},{2,0},{1,3},{3,1},{4,6},{6,4},{5,7},{7,5},{8,10},{10,8},{9,1... | collective-permute-start | bytes 589832 | tf_op jit(solution)/shard_map/ppermute | solution.py:691
  497.2 17.2 %collective-permute-start.70 = (f32[192,256]{1,0:T(8,128)S(1)}, f32[192,256]{1,0:T(8,128)S(1)}, u32[]{:S(2)}, u32[]{:S(2)}) collective-permute-start(f32[192,256]{1,0:T(8,128)S(1)} %slice.418), channel_id=1, source_target_pairs={{0,3},{3,0},{1,2},{2,1},{4,7},{7,4},{5,6},{6,5},{8,11},{11,8},{9,1... | collective-permute-start | bytes 589832 | tf_op jit(solution)/shard_map/ppermute | solution.py:1202
  (94 other events, 688.6 us)

commit v7 on v6

--- a/solution.py
+++ b/solution.py
@@ -16,7 +16,7 @@
 EPS = 1e-05
 F32 = jnp.float32
 BF16 = jnp.bfloat16
-VMEM_BYTES = 48 * 1024 * 1024
+VMEM_BYTES = 32 * 1024 * 1024
 
 
 def dot(left, right):

time: 525 us -> 518 us (0.987)
  starting transfers between devices: 93.4 us -> 122 us
  Pallas kernels: 131 us -> 103 us
  matrix products: 90.8 us -> 68.7 us
  local copies, waits for them, and re-layouts: 33.6 us -> 55.3 us
    unnamed x172 -> x284, local copies, waits for them, and re-layouts: 10.2 us -> 32.6 us
    dot_general x18, matrix products: 90.8 us -> 68.7 us  [matmul(): lax.dot_general(left, right, (contract, ((), ())), preferred_element_type...]
    ppermute x48, starting transfers between devices: 55.2 us -> 72.9 us  [swap(): return lax.ppermute(value, axis, [(0, 1), (1, 0)])]
    pallas_call x8, Pallas kernels: 105 us -> 88.9 us  [run(): pl.pallas_call(body, grid=grid, in_specs=[spec for _, spec in ins] + [pl....]
    ppermute x4, starting transfers between devices: 7.35 us -> 15.1 us  [shift(): return lax.ppermute(value, ('y', 'zp'), pairs)]
    pallas_call x4, Pallas kernels: 13 us -> 6.87 us  [joined(): pl.pallas_call(join_kernel, grid_spec=pltpu.PrefetchScalarGridSpec(num_sc...]
    pallas_call x2, Pallas kernels: 11.5 us -> 5.51 us  [place(): pl.pallas_call(place_kernel, grid_spec=pltpu.PrefetchScalarGridSpec(num_s...]
  transfers between devices with their start and end apart: 73 -> 73, of which waited for: 22 -> 22; matrix products, arithmetic and copies ran while one was open for 28% -> 24% of each run, Pallas kernels for 25% -> 20%
where the time goes in v7:
time: 518 us; the launch traced here: 509 us
  starting transfers between devices  122 us (24%)
  waiting for transfers between devices  111 us (21%)
  Pallas kernels  103 us (20%)
  matrix products  68.7 us (13%)
  local copies, waits for them, and re-layouts  55.3 us (11%)
  other arithmetic  44.9 us (9%)
    ppermute x48, waiting for transfers between devices, swap(): return lax.ppermute(value, axis, [(0, 1), (1, 0)])  95.8 us
    pallas_call x8, Pallas kernels, run(): pl.pallas_call(body, grid=grid, in_specs=[spec for _, spec in ins] + [pl....  88.9 us
    ppermute x48, starting transfers between devices, swap(): return lax.ppermute(value, axis, [(0, 1), (1, 0)])  72.9 us
    dot_general x18, matrix products, matmul(): lax.dot_general(left, right, (contract, ((), ())), preferred_element_type...  68.7 us
    unnamed x284, local copies, waits for them, and re-layouts  32.6 us
    ppermute x4, starting transfers between devices, shift(): return lax.ppermute(value, ('y', 'zp'), pairs)  15.1 us
    convert_element_type x8, other arithmetic, added(): return (kept.astype(F32) + got.astype(F32)).astype(dtype)  12.2 us
    ppermute x4, starting transfers between devices, row_hop(): lax.ppermute(packed, 'zp', [(0, 1)] if way == 1 else [(1, 0)])  11.3 us
  transfers between devices with their start and end apart: 73, of which 22 were waited for; matrix products, arithmetic and copies ran while one was open for 24% of the time, Pallas kernels for 20%

profile of v7, /device:TPU:0, one launch (start us, length us, event | category | flops | bytes accessed | tf_op | source)
XLA Modules:
  0.0 508.9 jit_solution(10618222007998706274)
XLA Ops:
  2.6 4.1 collective-permute-start.3
  21.5 18.8 %collective-permute-done.got = bf16[1,256,1536]{2,1,0:T(8,128)(2,1)} collective-permute-done((bf16[1,256,1536]{2,1,0:T(8,128)(2,1)S(1)}, bf16[1,256,1536]{2,1,0:T(8,128)(2,1)}, u32[]{:S(2)}, u32[]{:S(2)}) %collective-permute-start) | collective-permute-done | bytes 786464 | tf_op jit(solution)/shard_map/ppermute | solution.py:691
  49.3 16.8 %collective-permute-done.18.got = bf16[1,256,1536]{2,1,0:T(8,128)(2,1)} collective-permute-done((bf16[1,256,1536]{2,1,0:T(8,128)(2,1)S(1)}, bf16[1,256,1536]{2,1,0:T(8,128)(2,1)}, u32[]{:S(2)}, u32[]{:S(2)}) %collective-permute-start.18) | collective-permute-done | bytes 786464 | tf_op jit(solution)/shard_map/ppermute | solution.py:691
  69.3 2.2 collective-permute-start.10
  74.0 4.2 shard_map.280
  78.3 2.2 broadcast_select_fusion
  84.0 4.4 convolution_convert_fusion.5.refs_0_.refs_2_.refs_9_.refs_10_.refs_12_
  88.6 5.9 %collective-permute-start.9 = (bf16[2,16,1024]{2,1,0:T(8,128)(2,1)S(1)}, bf16[2,16,1024]{2,1,0:T(8,128)(2,1)S(1)}, u32[]{:S(2)}, u32[]{:S(2)}) collective-permute-start(bf16[2,16,1024]{2,1,0:T(8,128)(2,1)S(1)} %slice.379), channel_id=1, source_target_pairs={{0,2},{2,4},{4,6},{1,3},{3,5},{5,7},{8,10},{10,12},{12,14},{9,11},... | collective-permute-start | bytes 196616 | tf_op jit(solution)/shard_map/ppermute | solution.py:720
  99.0 4.5 convolution_convert_fusion.4.refs_0_.refs_2_.refs_9_.refs_10_.refs_12_
  103.5 6.0 %collective-permute-start.21 = (bf16[2,16,1024]{2,1,0:T(8,128)(2,1)S(1)}, bf16[2,16,1024]{2,1,0:T(8,128)(2,1)S(1)}, u32[]{:S(2)}, u32[]{:S(2)}) collective-permute-start(bf16[2,16,1024]{2,1,0:T(8,128)(2,1)S(1)} %slice.385), channel_id=1, source_target_pairs={{0,2},{2,4},{4,6},{1,3},{3,5},{5,7},{8,10},{10,12},{12,14},{9,11},... | collective-permute-start | bytes 196616 | tf_op jit(solution)/shard_map/ppermute | solution.py:720
  109.5 8.1 %shard_map.281 = (bf16[2,512,1024]{2,1,0:T(8,128)(2,1)S(1)}, f32[2,512,128]{2,1,0:T(8,128)S(1)}, f32[2,512,128]{2,1,0:T(8,128)S(1)}, f32[2,128,768]{2,1,0:T(8,12...) custom-call(bf16[2,512,1152]{2,1,0:T(8,128)(2,1)S(1)} %convolution_convert_fusion.5.refs_0_.refs_2_.refs_9_.refs_10_.refs, ...), custom_call_target="tpu_custom_call" | custom-call | flops 6000000000 | bytes 8000000 | tf_op jit(solution)/shard_map/pallas_call | solution.py:419
  118.5 2.1 collective-permute-start.11
  120.6 3.1 collective-permute-start.24
  123.7 2.4 fusion.74
  126.1 8.1 %shard_map.283 = (bf16[2,512,1024]{2,1,0:T(8,128)(2,1)S(1)}, f32[2,512,128]{2,1,0:T(8,128)S(1)}, f32[2,512,128]{2,1,0:T(8,128)S(1)}, f32[2,128,768]{2,1,0:T(8,12...) custom-call(bf16[2,512,1152]{2,1,0:T(8,128)(2,1)S(1)} %convolution_convert_fusion.4.refs_0_.refs_2_.refs_9_.refs_10_.refs, ...), custom_call_target="tpu_custom_call" | custom-call | flops 6000000000 | bytes 8000000 | tf_op jit(solution)/shard_map/pallas_call | solution.py:419
  138.2 3.7 convolution_convert_fusion.7.refs_6_.refs_2_
  141.9 4.7 collective-permute-done.23.got
  146.6 3.7 collective-permute-start.25
  154.0 3.7 convolution_convert_fusion.6.refs_6_.refs_2_
  157.7 7.2 %collective-permute-done.28.got = bf16[1,256,1536]{2,1,0:T(8,128)(2,1)} collective-permute-done((bf16[1,256,1536]{2,1,0:T(8,128)(2,1)}, bf16[1,256,1536]{2,1,0:T(8,128)(2,1)}, u32[]{:S(2)}, u32[]{:S(2)}) %collective-permute-start.28) | collective-permute-done | bytes 786464 | tf_op jit(solution)/shard_map/ppermute | solution.py:691
  164.9 6.1 %collective-permute-start.30 = (bf16[2,144,768]{2,1,0:T(8,128)(2,1)S(1)}, bf16[2,144,768]{2,1,0:T(8,128)(2,1)S(1)}, u32[]{:S(2)}, u32[]{:S(2)}) collective-permute-start(bf16[2,144,768]{2,1,0:T(8,128)(2,1)S(1)} %copy-done.29), channel_id=1, source_target_pairs={{0,2},{1,3},{4,6},{5,7},{8,10},{9,11},{12,14},{13,15},{16,18},{17,... | collective-permute-start | bytes 1327112 | tf_op jit(solution)/shard_map/ppermute | solution.py:724
  174.0 2.6 fusion.15.refs_7_.refs_10_.refs_3_
  176.7 8.2 %shard_map.287 = (f32[2,512,768]{2,1,0:T(8,128)S(1)}, bf16[2,512,768]{2,1,0:T(8,128)(2,1)S(1)}, bf16[2,2,128,768]{3,2,1,0:T(8,128)(2,1)S(1)}, f32[2,8,512]{2,1,0:T(8,128)S(1)}) custom-call(bf16[2,512,1024]{2,1,0:T(8,128)(2,1)S(1)} %copy-done.51, f32[2,512,128]{2,1,0:T(8,128)S(1)} %copy-done.73, f32[2,512,128]{2,1,0:T(8,128)S(1)} %copy-done.80, ...), custom_call_target="tpu_custom_call" | custom-call | flops 10000000000 | bytes 16000000 | tf_op jit(solution)/shard_map/pallas_call | solution.py:419
  190.2 3.7 fusion.18.refs_7_.refs_11_.refs_3_
  193.9 7.0 %collective-permute-start.31 = (f32[2,8,512]{2,1,0:T(8,128)S(1)}, f32[2,8,512]{2,1,0:T(8,128)S(1)}, u32[]{:S(2)}, u32[]{:S(2)}) collective-permute-start(f32[2,8,512]{2,1,0:T(8,128)S(1)} %reverse_add_fusion.1), channel_id=1, source_target_pairs={{0,1},{1,0},{2,3},{3,2},{4,5},{5,4},{6,7},{7,6},{8,9},{9,8},{10,11... | collective-permute-start | bytes 98312 | tf_op jit(solution)/shard_map/ppermute | solution.py:691
  200.9 2.9 convolution_convert_fusion.3.refs_9_
  208.9 5.3 %shard_map.290 = (bf16[2,512,768]{2,1,0:T(8,128)(2,1)S(1)}, bf16[2,512,768]{2,1,0:T(8,128)(2,1)S(1)}, bf16[2,512,768]{2,1,0:T(8,128)(2,1)S(1)}, f32[2,128,768]{2...) custom-call(f32[2,512,768]{2,1,0:T(8,128)S(1)} %copy-done.39, ...), custom_call_target="tpu_custom_call" | custom-call | flops 6000000000 | bytes 18000000 | tf_op jit(solution)/shard_map/pallas_call | solution.py:419
  227.2 8.1 %shard_map.291 = (f32[2,512,768]{2,1,0:T(8,128)S(1)}, bf16[2,512,768]{2,1,0:T(8,128)(2,1)S(1)}, bf16[2,2,128,768]{3,2,1,0:T(8,128)(2,1)S(1)}, f32[2,8,512]{2,1,0:T(8,128)S(1)}) custom-call(bf16[2,512,1024]{2,1,0:T(8,128)(2,1)S(1)} %copy-done.47, f32[2,512,128]{2,1,0:T(8,128)S(1)} %copy-done.69, f32[2,512,128]{2,1,0:T(8,128)S(1)} %copy-done.77, ...), custom_call_target="tpu_custom_call" | custom-call | flops 10000000000 | bytes 16000000 | tf_op jit(solution)/shard_map/pallas_call | solution.py:419
  235.7 3.9 bitcast_convert_fusion.1
  239.8 2.9 convolution_convert_fusion.2.refs_9_
  249.2 5.3 %shard_map.292 = (bf16[2,512,768]{2,1,0:T(8,128)(2,1)S(1)}, bf16[2,512,768]{2,1,0:T(8,128)(2,1)S(1)}, bf16[2,512,768]{2,1,0:T(8,128)(2,1)S(1)}, f32[2,128,768]{2...) custom-call(f32[2,512,768]{2,1,0:T(8,128)S(1)} %get-tuple-element.197.refs_0_.refs_4_, ...), custom_call_target="tpu_custom_call" | custom-call | flops 6000000000 | bytes 18000000 | tf_op jit(solution)/shard_map/pallas_call | solution.py:419
  259.0 2.9 bitcast_convert_fusion
  262.0 2.9 fusion.2
  265.0 2.9 fusion.1
  268.0 4.1 convolution_convert_fusion.1
  272.3 6.8 %collective-permute-start.46 = (bf16[2,2,192,768]{3,2,1,0:T(8,128)(2,1)S(1)}, bf16[2,2,192,768]{3,2,1,0:T(8,128)(2,1)}, u32[]{:S(2)}, u32[]{:S(2)}) collective-permute-start(bf16[2,2,192,768]{3,2,1,0:T(8,128)(2,1)S(1)} %pad_maximum_fusion.6.refs_20_), channel_id=1, source_target_pairs={{0,4},{4,0},{1,5},{5,1},{2,6},{6,2},{3,7},{7,3},{8,12},{12,8},{9,1... | collective-permute-start | bytes 3538952 | tf_op jit(solution)/shard_map/ppermute | solution.py:691
  280.6 2.7 collective-permute-done.42.packed_ref.refs_6_
  288.0 2.3 fusion.5
  293.3 22.9 %shard_map.295 = (bf16[2,512,1152]{2,1,0:T(8,128)(2,1)S(1)}, f32[2,8,1024]{2,1,0:T(8,128)S(1)}, f32[8,1024]{1,0:T(8,128)S(1)}, f32[8,128]{1,0:T(8,128)S(1)}, f32[8,768]{1,0:T(8,128)S(1)}) custom-call(bf16[2,512,1024]{2,1,0:T(8,128)(2,1)S(1)} %copy-done.53, f32[2,512,128]{2,1,0:T(8,128)S(1)} %copy-done.75, f32[2,512,128]{2,1,0:T(8,128)S(1)} %copy-done.81, ...), custom_call_target="tpu_custom_call" | custom-call | flops 32000000000 | bytes 24000000 | tf_op jit(solution)/shard_map/pallas_call | solution.py:419
  316.3 11.4 %collective-permute-done.39 = bf16[2,256,1536]{2,1,0:T(8,128)(2,1)S(1)} collective-permute-done((bf16[2,256,1536]{2,1,0:T(8,128)(2,1)S(1)}, bf16[2,256,1536]{2,1,0:T(8,128)(2,1)S(1)}, u32[]{:S(2)}, u32[]{:S(2)}) %collective-permute-start.39) | collective-permute-done | bytes 1572896 | tf_op jit(solution)/shard_map/ppermute | solution.py:691
  327.6 3.5 fusion.39
  334.2 5.8 %collective-permute-start.50 = (bf16[2,192,768]{2,1,0:T(8,128)(2,1)S(1)}, bf16[2,192,768]{2,1,0:T(8,128)(2,1)S(1)}, u32[]{:S(2)}, u32[]{:S(2)}) collective-permute-start(bf16[2,192,768]{2,1,0:T(8,128)(2,1)S(1)} %pad_maximum_fusion.10), channel_id=1, source_target_pairs={{0,4},{4,0},{1,5},{5,1},{2,6},{6,2},{3,7},{7,3},{8,12},{12,8},{9,1... | collective-permute-start | bytes 1769480 | tf_op jit(solution)/shard_map/ppermute | solution.py:691
  340.5 4.5 add_convert_fusion.2
  347.0 5.8 %fusion = bf16[1536,1152]{1,0:T(8,128)(2,1)} fusion(bf16[2,512,1536]{2,1,0:T(8,128)(2,1)S(1)} %copy-done.6, bf16[2,512,1152]{2,1,0:T(8,128)(2,1)S(1)} %fusion.51), kind=kOutput, calls=%fused_computation.2 | convolution fusion | flops 3625648128 | bytes 9043968 | tf_op jit(solution)/shard_map/dot_general | solution.py:889
  352.8 4.1 convolution_convert_fusion
  366.6 22.9 %shard_map.296 = (bf16[2,512,1152]{2,1,0:T(8,128)(2,1)S(1)}, f32[2,8,1024]{2,1,0:T(8,128)S(1)}, f32[8,1024]{1,0:T(8,128)S(1)}, f32[8,128]{1,0:T(8,128)S(1)}, f32[8,768]{1,0:T(8,128)S(1)}) custom-call(bf16[2,512,1024]{2,1,0:T(8,128)(2,1)S(1)} %copy-done.49, f32[2,512,128]{2,1,0:T(8,128)S(1)} %copy-done.71, f32[2,512,128]{2,1,0:T(8,128)S(1)} %copy-done.78, ...), custom_call_target="tpu_custom_call" | custom-call | flops 32000000000 | bytes 24000000 | tf_op jit(solution)/shard_map/pallas_call | solution.py:419
  389.5 2.4 add_bitcast_fusion.1
  393.7 2.3 fusion.36
  396.0 3.2 fusion.22
  399.2 3.1 collective-permute-done.54
  402.5 4.5 add_convert_fusion.1
  410.3 4.6 add_convert_fusion
  416.0 5.3 %collective-permute-start.58 = (bf16[1,2,192,1152]{3,2,1,0:T(8,128)(2,1)}, bf16[1,2,192,1152]{3,2,1,0:T(8,128)(2,1)}, u32[]{:S(2)}, u32[]{:S(2)}) collective-permute-start(bf16[1,2,192,1152]{3,2,1,0:T(8,128)(2,1)} %dynamic-slice_bitcast_fusion), channel_id=1, source_target_pairs={{0,4},{4,0},{1,5},{5,1},{2,6},{6,2},{3,7},{7,3},{8,12},{12,8},{9,1... | collective-permute-start | bytes 2654216 | tf_op jit(solution)/shard_map/ppermute | solution.py:691
  428.9 12.5 %collective-permute-done.58 = bf16[1,2,192,1152]{3,2,1,0:T(8,128)(2,1)} collective-permute-done((bf16[1,2,192,1152]{3,2,1,0:T(8,128)(2,1)}, bf16[1,2,192,1152]{3,2,1,0:T(8,128)(2,1)}, u32[]{:S(2)}, u32[]{:S(2)}) %collective-permute-start.58) | collective-permute-done | bytes 884768 | tf_op jit(solution)/shard_map/ppermute | solution.py:691
  441.4 2.5 collective-permute-done.57
  450.3 7.6 %collective-permute-done.60 = bf16[1,192,1152]{2,1,0:T(8,128)(2,1)} collective-permute-done((bf16[1,192,1152]{2,1,0:T(8,128)(2,1)}, bf16[1,192,1152]{2,1,0:T(8,128)(2,1)}, u32[]{:S(2)}, u32[]{:S(2)}) %collective-permute-start.60) | collective-permute-done | bytes 442400 | tf_op jit(solution)/shard_map/ppermute | solution.py:691
  459.9 2.6 broadcast_select_fusion.2
  466.6 3.4 collective-permute-done.61
  471.3 2.2 fusion.21
  474.0 7.5 %collective-permute-done.63 = bf16[1,192,1152]{2,1,0:T(8,128)(2,1)} collective-permute-done((bf16[1,192,1152]{2,1,0:T(8,128)(2,1)}, bf16[1,192,1152]{2,1,0:T(8,128)(2,1)}, u32[]{:S(2)}, u32[]{:S(2)}) %collective-permute-start.63) | collective-permute-done | bytes 442400 | tf_op jit(solution)/shard_map/ppermute | solution.py:834
  483.0 4.3 collective-permute-start.65
  490.5 3.2 collective-permute-start.70
  499.4 3.6 collective-permute-done.67
  504.7 2.9 collective-permute-done.69
  (545 shorter events, 150.1 us)
Async XLA Ops:
  2.6 13.2 %collective-permute-start.3 = (bf16[192,1152]{1,0:T(8,128)(2,1)S(1)}, bf16[192,1152]{1,0:T(8,128)(2,1)S(1)}, u32[]{:S(2)}, u32[]{:S(2)}) collective-permute-start(bf16[192,1152]{1,0:T(8,128)(2,1)S(1)} %concatenate.24), channel_id=1, source_target_pairs={{0,2},{10,8},{2,10},{8,0},{1,3},{11,9},{3,11},{9,1},{4,6},{14,12},... | collective-permute-start | bytes 1327112 | tf_op jit(solution)/shard_map/ppermute | solution.py:763
  6.7 9.1 %collective-permute-start.5 = (bf16[192,1152]{1,0:T(8,128)(2,1)S(1)}, bf16[192,1152]{1,0:T(8,128)(2,1)}, u32[]{:S(2)}, u32[]{:S(2)}) collective-permute-start(bf16[192,1152]{1,0:T(8,128)(2,1)S(1)} %concatenate.24), channel_id=1, source_target_pairs={{2,8},{8,2},{3,9},{9,3},{6,12},{12,6},{7,13},{13,7},{18,24},{24,18... | collective-permute-start | bytes 1327112 | tf_op jit(solution)/shard_map/ppermute | solution.py:763
  11.6 28.6 %collective-permute-start = (bf16[1,256,1536]{2,1,0:T(8,128)(2,1)S(1)}, bf16[1,256,1536]{2,1,0:T(8,128)(2,1)}, u32[]{:S(2)}, u32[]{:S(2)}) collective-permute-start(bf16[1,256,1536]{2,1,0:T(8,128)(2,1)S(1)} %get-tuple-element.330.own), channel_id=1, source_target_pairs={{0,1},{1,0},{2,3},{3,2},{4,5},{5,4},{6,7},{7,6},{8,9},{9,8},{10,11... | collective-permute-start | bytes 2359304 | tf_op jit(solution)/shard_map/ppermute | solution.py:691
  13.3 34.1 %collective-permute-start.1 = (bf16[1,256,1536]{2,1,0:T(8,128)(2,1)S(1)}, bf16[1,256,1536]{2,1,0:T(8,128)(2,1)}, u32[]{:S(2)}, u32[]{:S(2)}) collective-permute-start(bf16[1,256,1536]{2,1,0:T(8,128)(2,1)S(1)} %get-tuple-element.330.own), channel_id=1, source_target_pairs={{0,8},{8,0},{1,9},{9,1},{2,10},{10,2},{3,11},{11,3},{4,12},{12,4},... | collective-permute-start | bytes 2359304 | tf_op jit(solution)/shard_map/ppermute | solution.py:691
  15.9 24.4 %collective-permute-start.4 = (bf16[192,1152]{1,0:T(8,128)(2,1)S(1)}, bf16[192,1152]{1,0:T(8,128)(2,1)S(1)}, u32[]{:S(2)}, u32[]{:S(2)}) collective-permute-start(bf16[192,1152]{1,0:T(8,128)(2,1)S(1)} %get-tuple-element.351), channel_id=1, source_target_pairs={{0,16},{16,0},{1,17},{17,1},{2,18},{18,2},{3,19},{19,3},{4,20},{20... | collective-permute-start | bytes 1327112 | tf_op jit(solution)/shard_map/ppermute | solution.py:691
  17.4 22.9 %collective-permute-start.6 = (bf16[192,1152]{1,0:T(8,128)(2,1)S(1)}, bf16[192,1152]{1,0:T(8,128)(2,1)S(1)}, u32[]{:S(2)}, u32[]{:S(2)}) collective-permute-start(bf16[192,1152]{1,0:T(8,128)(2,1)S(1)} %get-tuple-element.350), channel_id=1, source_target_pairs={{0,4},{4,0},{1,5},{5,1},{2,6},{6,2},{3,7},{7,3},{8,12},{12,8},{9,1... | collective-permute-start | bytes 1327112 | tf_op jit(solution)/shard_map/ppermute | solution.py:691
  40.3 25.9 %collective-permute-start.18 = (bf16[1,256,1536]{2,1,0:T(8,128)(2,1)S(1)}, bf16[1,256,1536]{2,1,0:T(8,128)(2,1)}, u32[]{:S(2)}, u32[]{:S(2)}) collective-permute-start(bf16[1,256,1536]{2,1,0:T(8,128)(2,1)S(1)} %get-tuple-element.155.own), channel_id=1, source_target_pairs={{0,1},{1,0},{2,3},{3,2},{4,5},{5,4},{6,7},{7,6},{8,9},{9,8},{10,11... | collective-permute-start | bytes 2359304 | tf_op jit(solution)/shard_map/ppermute | solution.py:691
  42.4 31.0 %collective-permute-start.8 = (bf16[2,192,1152]{2,1,0:T(8,128)(2,1)S(1)}, bf16[2,192,1152]{2,1,0:T(8,128)(2,1)}, u32[]{:S(2)}, u32[]{:S(2)}) collective-permute-start(bf16[2,192,1152]{2,1,0:T(8,128)(2,1)S(1)} %pad_maximum_fusion.8.second), channel_id=1, source_target_pairs={{0,16},{16,0},{1,17},{17,1},{2,18},{18,2},{3,19},{19,3},{4,20},{20... | collective-permute-start | bytes 2654216 | tf_op jit(solution)/shard_map/ppermute | solution.py:691
  45.1 28.4 %collective-permute-start.7 = (bf16[2,192,1152]{2,1,0:T(8,128)(2,1)S(1)}, bf16[2,192,1152]{2,1,0:T(8,128)(2,1)}, u32[]{:S(2)}, u32[]{:S(2)}) collective-permute-start(bf16[2,192,1152]{2,1,0:T(8,128)(2,1)S(1)} %pad_maximum_fusion.7.first), channel_id=1, source_target_pairs={{0,4},{4,0},{1,5},{5,1},{2,6},{6,2},{3,7},{7,3},{8,12},{12,8},{9,1... | collective-permute-start | bytes 2654216 | tf_op jit(solution)/shard_map/ppermute | solution.py:691
  46.8 22.5 %collective-permute-start.2 = (bf16[1,256,1536]{2,1,0:T(8,128)(2,1)}, bf16[1,256,1536]{2,1,0:T(8,128)(2,1)}, u32[]{:S(2)}, u32[]{:S(2)}) collective-permute-start(bf16[1,256,1536]{2,1,0:T(8,128)(2,1)} %collective-permute-done.got), channel_id=1, source_target_pairs={{0,8},{8,0},{1,9},{9,1},{2,10},{10,2},{3,11},{11,3},{4,12},{12,4},... | collective-permute-start | bytes 2359304 | tf_op jit(solution)/shard_map/ppermute | solution.py:691
  47.4 30.9 %collective-permute-start.12 = (bf16[192,1536]{1,0:T(8,128)(2,1)}, bf16[192,1536]{1,0:T(8,128)(2,1)}, u32[]{:S(2)}, u32[]{:S(2)}) collective-permute-start(bf16[192,1536]{1,0:T(8,128)(2,1)} %pad_maximum_fusion.9), channel_id=1, source_target_pairs={{0,2},{10,8},{2,10},{8,0},{1,3},{11,9},{3,11},{9,1},{4,6},{14,12},... | collective-permute-start | bytes 1769480 | tf_op jit(solution)/shard_map/ppermute | solution.py:763
  66.1 12.1 %collective-permute-start.13 = (bf16[192,1536]{1,0:T(8,128)(2,1)}, bf16[192,1536]{1,0:T(8,128)(2,1)}, u32[]{:S(2)}, u32[]{:S(2)}) collective-permute-start(bf16[192,1536]{1,0:T(8,128)(2,1)} %pad_maximum_fusion.9), channel_id=1, source_target_pairs={{2,8},{8,2},{3,9},{9,3},{6,12},{12,6},{7,13},{13,7},{18,24},{24,18... | collective-permute-start | bytes 1769480 | tf_op jit(solution)/shard_map/ppermute | solution.py:763
  69.3 14.6 %collective-permute-start.10 = (f32[8,768]{1,0:T(8,128)S(1)}, f32[8,768]{1,0:T(8,128)S(1)}, u32[]{:S(2)}, u32[]{:S(2)}) collective-permute-start(f32[8,768]{1,0:T(8,128)S(1)} %maximum_maximum_fusion), channel_id=1, source_target_pairs={{0,2},{2,0},{1,3},{3,1},{4,6},{6,4},{5,7},{7,5},{8,10},{10,8},{9,1... | collective-permute-start | bytes 73736 | tf_op jit(solution)/shard_map/ppermute | solution.py:691
  73.4 24.0 %collective-permute-start.19 = (bf16[1,256,1536]{2,1,0:T(8,128)(2,1)S(1)}, bf16[1,256,1536]{2,1,0:T(8,128)(2,1)S(1)}, u32[]{:S(2)}, u32[]{:S(2)}) collective-permute-start(bf16[1,256,1536]{2,1,0:T(8,128)(2,1)S(1)} %get-tuple-element.155.own), channel_id=1, source_target_pairs={{0,8},{8,0},{1,9},{9,1},{2,10},{10,2},{3,11},{11,3},{4,12},{12,4},... | collective-permute-start | bytes 2359304 | tf_op jit(solution)/shard_map/ppermute | solution.py:691
  73.5 23.9 %collective-permute-start.20 = (bf16[1,256,1536]{2,1,0:T(8,128)(2,1)}, bf16[1,256,1536]{2,1,0:T(8,128)(2,1)S(1)}, u32[]{:S(2)}, u32[]{:S(2)}) collective-permute-start(bf16[1,256,1536]{2,1,0:T(8,128)(2,1)} %collective-permute-done.18.got), channel_id=1, source_target_pairs={{0,8},{8,0},{1,9},{9,1},{2,10},{10,2},{3,11},{11,3},{4,12},{12,4},... | collective-permute-start | bytes 2359304 | tf_op jit(solution)/shard_map/ppermute | solution.py:691
  80.5 14.0 %collective-permute-start.14 = (bf16[192,1536]{1,0:T(8,128)(2,1)S(1)}, bf16[192,1536]{1,0:T(8,128)(2,1)S(1)}, u32[]{:S(2)}, u32[]{:S(2)}) collective-permute-start(bf16[192,1536]{1,0:T(8,128)(2,1)S(1)} %get-tuple-element.349), channel_id=1, source_target_pairs={{0,16},{16,0},{1,17},{17,1},{2,18},{18,2},{3,19},{19,3},{4,20},{20... | collective-permute-start | bytes 1769480 | tf_op jit(solution)/shard_map/ppermute | solution.py:691
  82.1 12.9 %collective-permute-start.15 = (bf16[192,1536]{1,0:T(8,128)(2,1)S(1)}, bf16[192,1536]{1,0:T(8,128)(2,1)S(1)}, u32[]{:S(2)}, u32[]{:S(2)}) collective-permute-start(bf16[192,1536]{1,0:T(8,128)(2,1)S(1)} %get-tuple-element.348), channel_id=1, source_target_pairs={{0,4},{4,0},{1,5},{5,1},{2,6},{6,2},{3,7},{7,3},{8,12},{12,8},{9,1... | collective-permute-start | bytes 1769480 | tf_op jit(solution)/shard_map/ppermute | solution.py:691
  88.6 20.9 %collective-permute-start.9 = (bf16[2,16,1024]{2,1,0:T(8,128)(2,1)S(1)}, bf16[2,16,1024]{2,1,0:T(8,128)(2,1)S(1)}, u32[]{:S(2)}, u32[]{:S(2)}) collective-permute-start(bf16[2,16,1024]{2,1,0:T(8,128)(2,1)S(1)} %slice.379), channel_id=1, source_target_pairs={{0,2},{2,4},{4,6},{1,3},{3,5},{5,7},{8,10},{10,12},{12,14},{9,11},... | collective-permute-start | bytes 196616 | tf_op jit(solution)/shard_map/ppermute | solution.py:720
  95.1 39.2 %collective-permute-start.17 = (bf16[2,192,1536]{2,1,0:T(8,128)(2,1)S(1)}, bf16[2,192,1536]{2,1,0:T(8,128)(2,1)S(1)}, u32[]{:S(2)}, u32[]{:S(2)}) collective-permute-start(bf16[2,192,1536]{2,1,0:T(8,128)(2,1)S(1)} %pad_maximum_fusion.4.second), channel_id=1, source_target_pairs={{0,16},{16,0},{1,17},{17,1},{2,18},{18,2},{3,19},{19,3},{4,20},{20... | collective-permute-start | bytes 3538952 | tf_op jit(solution)/shard_map/ppermute | solution.py:691
  95.9 40.4 %collective-permute-start.16 = (bf16[2,192,1536]{2,1,0:T(8,128)(2,1)S(1)}, bf16[2,192,1536]{2,1,0:T(8,128)(2,1)S(1)}, u32[]{:S(2)}, u32[]{:S(2)}) collective-permute-start(bf16[2,192,1536]{2,1,0:T(8,128)(2,1)S(1)} %pad_maximum_fusion.3.first), channel_id=1, source_target_pairs={{0,4},{4,0},{1,5},{5,1},{2,6},{6,2},{3,7},{7,3},{8,12},{12,8},{9,1... | collective-permute-start | bytes 3538952 | tf_op jit(solution)/shard_map/ppermute | solution.py:691
  103.5 20.2 %collective-permute-start.21 = (bf16[2,16,1024]{2,1,0:T(8,128)(2,1)S(1)}, bf16[2,16,1024]{2,1,0:T(8,128)(2,1)S(1)}, u32[]{:S(2)}, u32[]{:S(2)}) collective-permute-start(bf16[2,16,1024]{2,1,0:T(8,128)(2,1)S(1)} %slice.385), channel_id=1, source_target_pairs={{0,2},{2,4},{4,6},{1,3},{3,5},{5,7},{8,10},{10,12},{12,14},{9,11},... | collective-permute-start | bytes 196616 | tf_op jit(solution)/shard_map/ppermute | solution.py:720
  118.5 19.3 %collective-permute-start.11 = (bf16[2,144,768]{2,1,0:T(8,128)(2,1)S(1)}, bf16[2,144,768]{2,1,0:T(8,128)(2,1)S(1)}, u32[]{:S(2)}, u32[]{:S(2)}) collective-permute-start(bf16[2,144,768]{2,1,0:T(8,128)(2,1)S(1)} %get-tuple-element.149.refs_6_), channel_id=1, source_target_pairs={{0,2},{1,3},{4,6},{5,7},{8,10},{9,11},{12,14},{13,15},{16,18},{17,... | collective-permute-start | bytes 1327112 | tf_op jit(solution)/shard_map/ppermute | solution.py:724
  120.6 44.3 %collective-permute-start.24 = (bf16[2,256,1536]{2,1,0:T(8,128)(2,1)}, bf16[2,256,1536]{2,1,0:T(8,128)(2,1)}, u32[]{:S(2)}, u32[]{:S(2)}) collective-permute-start(bf16[2,256,1536]{2,1,0:T(8,128)(2,1)} %param.17), channel_id=1, source_target_pairs={{0,8},{8,0},{1,9},{9,1},{2,10},{10,2},{3,11},{11,3},{4,12},{12,4},... | collective-permute-start | bytes 4718600 | tf_op jit(solution)/shard_map/ppermute | solution.py:691
  126.1 20.5 %collective-permute-start.23 = (bf16[1,256,1536]{2,1,0:T(8,128)(2,1)S(1)}, bf16[1,256,1536]{2,1,0:T(8,128)(2,1)}, u32[]{:S(2)}, u32[]{:S(2)}) collective-permute-start(bf16[1,256,1536]{2,1,0:T(8,128)(2,1)S(1)} %get-tuple-element.339.own), channel_id=1, source_target_pairs={{0,1},{1,0},{2,3},{3,2},{4,5},{5,4},{6,7},{7,6},{8,9},{9,8},{10,11... | collective-permute-start | bytes 2359304 | tf_op jit(solution)/shard_map/ppermute | solution.py:691
  134.3 30.6 %collective-permute-start.28 = (bf16[1,256,1536]{2,1,0:T(8,128)(2,1)}, bf16[1,256,1536]{2,1,0:T(8,128)(2,1)}, u32[]{:S(2)}, u32[]{:S(2)}) collective-permute-start(bf16[1,256,1536]{2,1,0:T(8,128)(2,1)} %get-tuple-element.338.own), channel_id=1, source_target_pairs={{0,1},{1,0},{2,3},{3,2},{4,5},{5,4},{6,7},{7,6},{8,9},{9,8},{10,11... | collective-permute-start | bytes 2359304 | tf_op jit(solution)/shard_map/ppermute | solution.py:691
  146.6 24.4 %collective-permute-start.25 = (bf16[1,256,1536]{2,1,0:T(8,128)(2,1)}, bf16[1,256,1536]{2,1,0:T(8,128)(2,1)}, u32[]{:S(2)}, u32[]{:S(2)}) collective-permute-start(bf16[1,256,1536]{2,1,0:T(8,128)(2,1)} %collective-permute-done.23.got), channel_id=1, source_target_pairs={{0,8},{8,0},{1,9},{9,1},{2,10},{10,2},{3,11},{11,3},{4,12},{12,4},... | collective-permute-start | bytes 2359304 | tf_op jit(solution)/shard_map/ppermute | solution.py:691
  152.5 24.1 %collective-permute-start.26 = (bf16[2,128,768]{2,1,0:T(8,128)(2,1)}, bf16[2,128,768]{2,1,0:T(8,128)(2,1)S(1)}, u32[]{:S(2)}, u32[]{:S(2)}) collective-permute-start(bf16[2,128,768]{2,1,0:T(8,128)(2,1)} %copy-done.23), channel_id=1, source_target_pairs={{2,6},{3,7},{10,14},{11,15},{18,22},{19,23},{26,30},{27,31}} | collective-permute-start | bytes 1179656 | tf_op jit(solution)/shard_map/ppermute | solution.py:730
  153.3 23.3 %collective-permute-start.22 = (bf16[2,128,768]{2,1,0:T(8,128)(2,1)}, bf16[2,128,768]{2,1,0:T(8,128)(2,1)S(1)}, u32[]{:S(2)}, u32[]{:S(2)}) collective-permute-start(bf16[2,128,768]{2,1,0:T(8,128)(2,1)} %copy-done.23), channel_id=1, source_target_pairs={{2,4},{3,5},{10,12},{11,13},{18,20},{19,21},{26,28},{27,29}} | collective-permute-start | bytes 1179656 | tf_op jit(solution)/shard_map/ppermute | solution.py:730
  164.9 22.1 %collective-permute-start.29 = (bf16[1,256,1536]{2,1,0:T(8,128)(2,1)}, bf16[1,256,1536]{2,1,0:T(8,128)(2,1)S(1)}, u32[]{:S(2)}, u32[]{:S(2)}) collective-permute-start(bf16[1,256,1536]{2,1,0:T(8,128)(2,1)} %collective-permute-done.28.got), channel_id=1, source_target_pairs={{0,8},{8,0},{1,9},{9,1},{2,10},{10,2},{3,11},{11,3},{4,12},{12,4},... | collective-permute-start | bytes 2359304 | tf_op jit(solution)/shard_map/ppermute | solution.py:691
  164.9 20.0 %collective-permute-start.30 = (bf16[2,144,768]{2,1,0:T(8,128)(2,1)S(1)}, bf16[2,144,768]{2,1,0:T(8,128)(2,1)S(1)}, u32[]{:S(2)}, u32[]{:S(2)}) collective-permute-start(bf16[2,144,768]{2,1,0:T(8,128)(2,1)S(1)} %copy-done.29), channel_id=1, source_target_pairs={{0,2},{1,3},{4,6},{5,7},{8,10},{9,11},{12,14},{13,15},{16,18},{17,... | collective-permute-start | bytes 1327112 | tf_op jit(solution)/shard_map/ppermute | solution.py:724
  185.4 33.6 %collective-permute-start.35 = (bf16[2,128,768]{2,1,0:T(8,128)(2,1)S(1)}, bf16[2,128,768]{2,1,0:T(8,128)(2,1)S(1)}, u32[]{:S(2)}, u32[]{:S(2)}) collective-permute-start(bf16[2,128,768]{2,1,0:T(8,128)(2,1)S(1)} %shard_map.288), channel_id=1, source_target_pairs={{2,6},{3,7},{10,14},{11,15},{18,22},{19,23},{26,30},{27,31}} | collective-permute-start | bytes 1179656 | tf_op jit(solution)/shard_map/ppermute | solution.py:730
  186.1 32.9 %collective-permute-start.34 = (bf16[2,128,768]{2,1,0:T(8,128)(2,1)S(1)}, bf16[2,128,768]{2,1,0:T(8,128)(2,1)S(1)}, u32[]{:S(2)}, u32[]{:S(2)}) collective-permute-start(bf16[2,128,768]{2,1,0:T(8,128)(2,1)S(1)} %shard_map.288), channel_id=1, source_target_pairs={{2,4},{3,5},{10,12},{11,13},{18,20},{19,21},{26,28},{27,29}} | collective-permute-start | bytes 1179656 | tf_op jit(solution)/shard_map/ppermute | solution.py:730
  193.9 13.0 %collective-permute-start.31 = (f32[2,8,512]{2,1,0:T(8,128)S(1)}, f32[2,8,512]{2,1,0:T(8,128)S(1)}, u32[]{:S(2)}, u32[]{:S(2)}) collective-permute-start(f32[2,8,512]{2,1,0:T(8,128)S(1)} %reverse_add_fusion.1), channel_id=1, source_target_pairs={{0,1},{1,0},{2,3},{3,2},{4,5},{5,4},{6,7},{7,6},{8,9},{9,8},{10,11... | collective-permute-start | bytes 98312 | tf_op jit(solution)/shard_map/ppermute | solution.py:691
  206.7 77.7 %collective-permute-start.32 = (bf16[512,1536]{1,0:T(8,128)(2,1)}, bf16[512,1536]{1,0:T(8,128)(2,1)}, u32[]{:S(2)}, u32[]{:S(2)}) collective-permute-start(bf16[512,1536]{1,0:T(8,128)(2,1)} %slice_bitcast_fusion.7), channel_id=1, source_target_pairs={{0,8},{8,0},{1,9},{9,1},{2,10},{10,2},{3,11},{11,3},{4,12},{12,4},... | collective-permute-start | bytes 4718600 | tf_op jit(solution)/shard_map/ppermute | solution.py:691
  217.7 36.9 %collective-permute-start.33 = (bf16[2,144,768]{2,1,0:T(8,128)(2,1)S(1)}, bf16[2,144,768]{2,1,0:T(8,128)(2,1)S(1)}, u32[]{:S(2)}, u32[]{:S(2)}) collective-permute-start(bf16[2,144,768]{2,1,0:T(8,128)(2,1)S(1)} %get-tuple-element.191.refs_10_), channel_id=1, source_target_pairs={{2,0},{3,1},{6,4},{7,5},{10,8},{11,9},{14,12},{15,13},{18,16},{19,... | collective-permute-start | bytes 1327112 | tf_op jit(solution)/shard_map/ppermute | solution.py:724
  245.7 42.3 %collective-permute-start.38 = (bf16[512,1536]{1,0:T(8,128)(2,1)}, bf16[512,1536]{1,0:T(8,128)(2,1)}, u32[]{:S(2)}, u32[]{:S(2)}) collective-permute-start(bf16[512,1536]{1,0:T(8,128)(2,1)} %slice_bitcast_fusion.5), channel_id=1, source_target_pairs={{0,8},{8,0},{1,9},{9,1},{2,10},{10,2},{3,11},{11,3},{4,12},{12,4},... | collective-permute-start | bytes 4718600 | tf_op jit(solution)/shard_map/ppermute | solution.py:691
  255.0 17.1 %collective-permute-start.41 = (bf16[2,128,768]{2,1,0:T(8,128)(2,1)S(1)}, bf16[2,128,768]{2,1,0:T(8,128)(2,1)S(1)}, u32[]{:S(2)}, u32[]{:S(2)}) collective-permute-start(bf16[2,128,768]{2,1,0:T(8,128)(2,1)S(1)} %shard_map.293), channel_id=1, source_target_pairs={{4,0},{5,1},{12,8},{13,9},{20,16},{21,17},{28,24},{29,25}} | collective-permute-start | bytes 1179656 | tf_op jit(solution)/shard_map/ppermute | solution.py:730
  256.5 15.5 %collective-permute-start.40 = (bf16[2,128,768]{2,1,0:T(8,128)(2,1)S(1)}, bf16[2,128,768]{2,1,0:T(8,128)(2,1)S(1)}, u32[]{:S(2)}, u32[]{:S(2)}) collective-permute-start(bf16[2,128,768]{2,1,0:T(8,128)(2,1)S(1)} %shard_map.293), channel_id=1, source_target_pairs={{4,2},{5,3},{12,10},{13,11},{20,18},{21,19},{28,26},{29,27}} | collective-permute-start | bytes 1179656 | tf_op jit(solution)/shard_map/ppermute | solution.py:730
  257.2 26.1 %collective-permute-start.42 = (bf16[2,144,768]{2,1,0:T(8,128)(2,1)S(1)}, bf16[2,144,768]{2,1,0:T(8,128)(2,1)S(1)}, u32[]{:S(2)}, u32[]{:S(2)}) collective-permute-start(bf16[2,144,768]{2,1,0:T(8,128)(2,1)S(1)} %get-tuple-element.220), channel_id=1, source_target_pairs={{2,0},{3,1},{6,4},{7,5},{10,8},{11,9},{14,12},{15,13},{18,16},{19,... | collective-permute-start | bytes 1327112 | tf_op jit(solution)/shard_map/ppermute | solution.py:724
  272.3 44.0 %collective-permute-start.46 = (bf16[2,2,192,768]{3,2,1,0:T(8,128)(2,1)S(1)}, bf16[2,2,192,768]{3,2,1,0:T(8,128)(2,1)}, u32[]{:S(2)}, u32[]{:S(2)}) collective-permute-start(bf16[2,2,192,768]{3,2,1,0:T(8,128)(2,1)S(1)} %pad_maximum_fusion.6.refs_20_), channel_id=1, source_target_pairs={{0,4},{4,0},{1,5},{5,1},{2,6},{6,2},{3,7},{7,3},{8,12},{12,8},{9,1... | collective-permute-start | bytes 3538952 | tf_op jit(solution)/shard_map/ppermute | solution.py:691
  279.3 37.0 %collective-permute-start.45 = (bf16[2,2,192,768]{3,2,1,0:T(8,128)(2,1)S(1)}, bf16[2,2,192,768]{3,2,1,0:T(8,128)(2,1)}, u32[]{:S(2)}, u32[]{:S(2)}) collective-permute-start(bf16[2,2,192,768]{3,2,1,0:T(8,128)(2,1)S(1)} %pad_maximum_fusion.5.refs_19_), channel_id=1, source_target_pairs={{0,16},{16,0},{1,17},{17,1},{2,18},{18,2},{3,19},{19,3},{4,20},{20... | collective-permute-start | bytes 3538952 | tf_op jit(solution)/shard_map/ppermute | solution.py:691
  283.7 32.5 %collective-permute-start.43 = (bf16[2,128,768]{2,1,0:T(8,128)(2,1)S(1)}, bf16[2,128,768]{2,1,0:T(8,128)(2,1)S(1)}, u32[]{:S(2)}, u32[]{:S(2)}) collective-permute-start(bf16[2,128,768]{2,1,0:T(8,128)(2,1)S(1)} %shard_map.294.refs_17_), channel_id=1, source_target_pairs={{4,2},{5,3},{12,10},{13,11},{20,18},{21,19},{28,26},{29,27}} | collective-permute-start | bytes 1179656 | tf_op jit(solution)/shard_map/ppermute | solution.py:730
  284.4 31.8 %collective-permute-start.44 = (bf16[2,128,768]{2,1,0:T(8,128)(2,1)S(1)}, bf16[2,128,768]{2,1,0:T(8,128)(2,1)S(1)}, u32[]{:S(2)}, u32[]{:S(2)}) collective-permute-start(bf16[2,128,768]{2,1,0:T(8,128)(2,1)S(1)} %shard_map.294.refs_17_), channel_id=1, source_target_pairs={{4,0},{5,1},{12,8},{13,9},{20,16},{21,17},{28,24},{29,25}} | collective-permute-start | bytes 1179656 | tf_op jit(solution)/shard_map/ppermute | solution.py:730
  291.5 36.2 %collective-permute-start.39 = (bf16[2,256,1536]{2,1,0:T(8,128)(2,1)S(1)}, bf16[2,256,1536]{2,1,0:T(8,128)(2,1)S(1)}, u32[]{:S(2)}, u32[]{:S(2)}) collective-permute-start(bf16[2,256,1536]{2,1,0:T(8,128)(2,1)S(1)} %pad_maximum_fusion.1.refs_18_), channel_id=1, source_target_pairs={{0,1},{1,0},{2,3},{3,2},{4,5},{5,4},{6,7},{7,6},{8,9},{9,8},{10,11... | collective-permute-start | bytes 4718600 | tf_op jit(solution)/shard_map/ppermute | solution.py:691
  331.3 25.5 %collective-permute-start.51 = (bf16[2,192,768]{2,1,0:T(8,128)(2,1)S(1)}, bf16[2,192,768]{2,1,0:T(8,128)(2,1)S(1)}, u32[]{:S(2)}, u32[]{:S(2)}) collective-permute-start(bf16[2,192,768]{2,1,0:T(8,128)(2,1)S(1)} %pad_maximum_fusion.11), channel_id=1, source_target_pairs={{0,16},{16,0},{1,17},{17,1},{2,18},{18,2},{3,19},{19,3},{4,20},{20... | collective-permute-start | bytes 1769480 | tf_op jit(solution)/shard_map/ppermute | solution.py:691
  332.6 7.8 %collective-permute-start.47 = (f32[2,8,1024]{2,1,0:T(8,128)S(1)}, f32[2,8,1024]{2,1,0:T(8,128)S(1)}, u32[]{:S(2)}, u32[]{:S(2)}) collective-permute-start(f32[2,8,1024]{2,1,0:T(8,128)S(1)} %get-tuple-element.230), channel_id=1, source_target_pairs={{2,0},{4,2},{6,4},{3,1},{5,3},{7,5},{10,8},{12,10},{14,12},{11,9},... | collective-permute-start | bytes 196616 | tf_op jit(solution)/shard_map/ppermute | solution.py:720
  334.2 22.6 %collective-permute-start.50 = (bf16[2,192,768]{2,1,0:T(8,128)(2,1)S(1)}, bf16[2,192,768]{2,1,0:T(8,128)(2,1)S(1)}, u32[]{:S(2)}, u32[]{:S(2)}) collective-permute-start(bf16[2,192,768]{2,1,0:T(8,128)(2,1)S(1)} %pad_maximum_fusion.10), channel_id=1, source_target_pairs={{0,4},{4,0},{1,5},{5,1},{2,6},{6,2},{3,7},{7,3},{8,12},{12,8},{9,1... | collective-permute-start | bytes 1769480 | tf_op jit(solution)/shard_map/ppermute | solution.py:691
  345.2 14.4 %collective-permute-start.48 = (bf16[512,1536]{1,0:T(8,128)(2,1)S(1)}, bf16[512,1536]{1,0:T(8,128)(2,1)S(1)}, u32[]{:S(2)}, u32[]{:S(2)}) collective-permute-start(bf16[512,1536]{1,0:T(8,128)(2,1)S(1)} %slice_bitcast_fusion.3), channel_id=1, source_target_pairs={{0,8},{8,0},{1,9},{9,1},{2,10},{10,2},{3,11},{11,3},{4,12},{12,4},... | collective-permute-start | bytes 4718600 | tf_op jit(solution)/shard_map/ppermute | solution.py:691
  357.7 31.8 %collective-permute-start.52 = (bf16[2,192,768]{2,1,0:T(8,128)(2,1)S(1)}, bf16[2,192,768]{2,1,0:T(8,128)(2,1)}, u32[]{:S(2)}, u32[]{:S(2)}) collective-permute-start(bf16[2,192,768]{2,1,0:T(8,128)(2,1)S(1)} %get-tuple-element.343.refs_19_), channel_id=1, source_target_pairs={{2,0},{8,10},{10,2},{0,8},{3,1},{9,11},{11,3},{1,9},{6,4},{12,14},... | collective-permute-start | bytes 1769480 | tf_op jit(solution)/shard_map/ppermute | solution.py:834
  357.7 31.8 %collective-permute-start.53 = (bf16[2,192,768]{2,1,0:T(8,128)(2,1)S(1)}, bf16[2,192,768]{2,1,0:T(8,128)(2,1)}, u32[]{:S(2)}, u32[]{:S(2)}) collective-permute-start(bf16[2,192,768]{2,1,0:T(8,128)(2,1)S(1)} %get-tuple-element.342.refs_20_), channel_id=1, source_target_pairs={{2,8},{8,2},{3,9},{9,3},{6,12},{12,6},{7,13},{13,7},{18,24},{24,18... | collective-permute-start | bytes 1769480 | tf_op jit(solution)/shard_map/ppermute | solution.py:835
  360.1 33.6 %collective-permute-start.49 = (bf16[256,1536]{1,0:T(8,128)(2,1)S(1)}, bf16[256,1536]{1,0:T(8,128)(2,1)}, u32[]{:S(2)}, u32[]{:S(2)}) collective-permute-start(bf16[256,1536]{1,0:T(8,128)(2,1)S(1)} %constant_dynamic-slice_fusion.8.refs_17_), channel_id=1, source_target_pairs={{0,1},{1,0},{2,3},{3,2},{4,5},{5,4},{6,7},{7,6},{8,9},{9,8},{10,11... | collective-permute-start | bytes 2359304 | tf_op jit(solution)/shard_map/ppermute | solution.py:691
  392.0 10.4 %collective-permute-start.54 = (f32[2,8,1024]{2,1,0:T(8,128)S(1)}, f32[2,8,1024]{2,1,0:T(8,128)S(1)}, u32[]{:S(2)}, u32[]{:S(2)}) collective-permute-start(f32[2,8,1024]{2,1,0:T(8,128)S(1)} %get-tuple-element.249), channel_id=1, source_target_pairs={{2,0},{4,2},{6,4},{3,1},{5,3},{7,5},{10,8},{12,10},{14,12},{11,9},... | collective-permute-start | bytes 196616 | tf_op jit(solution)/shard_map/ppermute | solution.py:720
  408.4 15.4 %collective-permute-start.55 = (bf16[512,1536]{1,0:T(8,128)(2,1)}, bf16[512,1536]{1,0:T(8,128)(2,1)}, u32[]{:S(2)}, u32[]{:S(2)}) collective-permute-start(bf16[512,1536]{1,0:T(8,128)(2,1)} %slice_bitcast_fusion.1), channel_id=1, source_target_pairs={{0,8},{8,0},{1,9},{9,1},{2,10},{10,2},{3,11},{11,3},{4,12},{12,4},... | collective-permute-start | bytes 4718600 | tf_op jit(solution)/shard_map/ppermute | solution.py:691
  416.0 25.4 %collective-permute-start.58 = (bf16[1,2,192,1152]{3,2,1,0:T(8,128)(2,1)}, bf16[1,2,192,1152]{3,2,1,0:T(8,128)(2,1)}, u32[]{:S(2)}, u32[]{:S(2)}) collective-permute-start(bf16[1,2,192,1152]{3,2,1,0:T(8,128)(2,1)} %dynamic-slice_bitcast_fusion), channel_id=1, source_target_pairs={{0,4},{4,0},{1,5},{5,1},{2,6},{6,2},{3,7},{7,3},{8,12},{12,8},{9,1... | collective-permute-start | bytes 2654216 | tf_op jit(solution)/shard_map/ppermute | solution.py:691
  422.2 21.6 %collective-permute-start.57 = (bf16[1,2,192,1152]{3,2,1,0:T(8,128)(2,1)}, bf16[1,2,192,1152]{3,2,1,0:T(8,128)(2,1)}, u32[]{:S(2)}, u32[]{:S(2)}) collective-permute-start(bf16[1,2,192,1152]{3,2,1,0:T(8,128)(2,1)} %dynamic-slice_bitcast_fusion.1), channel_id=1, source_target_pairs={{0,16},{16,0},{1,17},{17,1},{2,18},{18,2},{3,19},{19,3},{4,20},{20... | collective-permute-start | bytes 2654216 | tf_op jit(solution)/shard_map/ppermute | solution.py:691
  426.8 23.4 %collective-permute-start.56 = (bf16[256,1536]{1,0:T(8,128)(2,1)}, bf16[256,1536]{1,0:T(8,128)(2,1)}, u32[]{:S(2)}, u32[]{:S(2)}) collective-permute-start(bf16[256,1536]{1,0:T(8,128)(2,1)} %constant_dynamic-slice_fusion.2), channel_id=1, source_target_pairs={{0,1},{1,0},{2,3},{3,2},{4,5},{5,4},{6,7},{7,6},{8,9},{9,8},{10,11... | collective-permute-start | bytes 2359304 | tf_op jit(solution)/shard_map/ppermute | solution.py:691
  446.7 11.2 %collective-permute-start.60 = (bf16[1,192,1152]{2,1,0:T(8,128)(2,1)}, bf16[1,192,1152]{2,1,0:T(8,128)(2,1)}, u32[]{:S(2)}, u32[]{:S(2)}) collective-permute-start(bf16[1,192,1152]{2,1,0:T(8,128)(2,1)} %constant_dynamic-slice_fusion), channel_id=1, source_target_pairs={{0,16},{16,0},{1,17},{17,1},{2,18},{18,2},{3,19},{19,3},{4,20},{20... | collective-permute-start | bytes 1327112 | tf_op jit(solution)/shard_map/ppermute | solution.py:691
  449.0 10.9 %collective-permute-start.59 = (bf16[1,192,1152]{2,1,0:T(8,128)(2,1)}, bf16[1,192,1152]{2,1,0:T(8,128)(2,1)}, u32[]{:S(2)}, u32[]{:S(2)}) collective-permute-start(bf16[1,192,1152]{2,1,0:T(8,128)(2,1)} %constant_dynamic-slice_fusion.1), channel_id=1, source_target_pairs={{0,4},{4,0},{1,5},{5,1},{2,6},{6,2},{3,7},{7,3},{8,12},{12,8},{9,1... | collective-permute-start | bytes 1327112 | tf_op jit(solution)/shard_map/ppermute | solution.py:691
  462.5 19.0 %collective-permute-start.63 = (bf16[1,192,1152]{2,1,0:T(8,128)(2,1)}, bf16[1,192,1152]{2,1,0:T(8,128)(2,1)}, u32[]{:S(2)}, u32[]{:S(2)}) collective-permute-start(bf16[1,192,1152]{2,1,0:T(8,128)(2,1)} %get-tuple-element.324), channel_id=1, source_target_pairs={{2,0},{8,10},{10,2},{0,8},{3,1},{9,11},{11,3},{1,9},{6,4},{12,14},... | collective-permute-start | bytes 1327112 | tf_op jit(solution)/shard_map/ppermute | solution.py:834
  462.5 19.0 %collective-permute-start.64 = (bf16[1,192,1152]{2,1,0:T(8,128)(2,1)}, bf16[1,192,1152]{2,1,0:T(8,128)(2,1)}, u32[]{:S(2)}, u32[]{:S(2)}) collective-permute-start(bf16[1,192,1152]{2,1,0:T(8,128)(2,1)} %get-tuple-element.325), channel_id=1, source_target_pairs={{2,8},{8,2},{3,9},{9,3},{6,12},{12,6},{7,13},{13,7},{18,24},{24,18... | collective-permute-start | bytes 1327112 | tf_op jit(solution)/shard_map/ppermute | solution.py:835
  483.0 12.2 %collective-permute-start.65 = (f32[7460]{0:T(1024)S(1)}, f32[7460]{0:T(1024)S(1)}, u32[]{:S(2)}, u32[]{:S(2)}) collective-permute-start(f32[7460]{0:T(1024)S(1)} %add.420), channel_id=1, source_target_pairs={{0,2},{2,0},{1,3},{3,1},{4,6},{6,4},{5,7},{7,5},{8,10},{10,8},{9,1... | collective-permute-start | bytes 89528 | tf_op jit(solution)/shard_map/ppermute | solution.py:691
  489.2 15.5 %collective-permute-start.68 = (f32[192,256]{1,0:T(8,128)S(1)}, f32[192,256]{1,0:T(8,128)S(1)}, u32[]{:S(2)}, u32[]{:S(2)}) collective-permute-start(f32[192,256]{1,0:T(8,128)S(1)} %slice.418), channel_id=1, source_target_pairs={{0,1},{1,0},{2,3},{3,2},{4,5},{5,4},{6,7},{7,6},{8,9},{9,8},{10,11... | collective-permute-start | bytes 589832 | tf_op jit(solution)/shard_map/ppermute | solution.py:691
  490.5 17.2 %collective-permute-start.69 = (f32[192,256]{1,0:T(8,128)S(1)}, f32[192,256]{1,0:T(8,128)S(1)}, u32[]{:S(2)}, u32[]{:S(2)}) collective-permute-start(f32[192,256]{1,0:T(8,128)S(1)} %slice.418), channel_id=1, source_target_pairs={{0,2},{2,0},{1,3},{3,1},{4,6},{6,4},{5,7},{7,5},{8,10},{10,8},{9,1... | collective-permute-start | bytes 589832 | tf_op jit(solution)/shard_map/ppermute | solution.py:691
  490.5 17.1 %collective-permute-start.70 = (f32[192,256]{1,0:T(8,128)S(1)}, f32[192,256]{1,0:T(8,128)S(1)}, u32[]{:S(2)}, u32[]{:S(2)}) collective-permute-start(f32[192,256]{1,0:T(8,128)S(1)} %slice.418), channel_id=1, source_target_pairs={{0,3},{3,0},{1,2},{2,1},{4,7},{7,4},{5,6},{6,5},{8,11},{11,8},{9,1... | collective-permute-start | bytes 589832 | tf_op jit(solution)/shard_map/ppermute | solution.py:1202
  (150 other events, 1450.2 us)
